TPU v7x, 32 devices: a whole 2x2x4 slice. The times are simulated.
32 devices in a mesh: rows: 4 (over z), cols: 8 (over y, x, core).
Axes of the slice: x: 2, y: 2, z: 4, core: 2. Of those that a mesh axis runs over, the one named last changes fastest.
Arguments:
- global_in: bfloat16 [8, 32, 1024], P('rows', None, 'cols'), may hold values from -6 to 6
- global_first: bfloat16 [3, 3, 1024, 1024], P(None, None, None, 'cols'), may hold values from -0.0625 to 0.0625
- global_second: bfloat16 [3, 3, 1024, 1024], P(None, None, None, 'cols'), may hold values from -0.0625 to 0.0625
- project_weight: bfloat16 [1024, 128], replicated, may hold values from -0.1875 to 0.1875
- enhancer_input: bfloat16 [128, 512, 128], P('rows', 'cols'), may hold values from -6 to 6
- instance_map: int32 [128, 512], P('rows', 'cols'), may hold values from 0 to 255, as said below
- encoder_features: float32 [16, 128, 512], P(None, 'rows', 'cols'), may hold values from -5 to 5
- instance_weight: float32 [16, 128], replicated, may hold values from -4 to 4
- enhancer_first: bfloat16 [3, 3, 128, 128], replicated, may hold values from -0.1875 to 0.1875
- enhancer_second: bfloat16 [3, 3, 128, 128], replicated, may hold values from -0.1875 to 0.1875
- output_cotangent: bfloat16 [128, 512, 128], P('rows', 'cols'), may hold values from -6 to 6
Outputs:
- enhanced: bfloat16 [128, 512, 128], P('rows', 'cols')
- gradient_first: float32 [3, 3, 128, 128], replicated
- gradient_second: float32 [3, 3, 128, 128], replicated
- global_gradient: float32 [8, 32, 128], P('rows', 'cols')
Inputs may be any that keep to these rules, and one draw needn't show every extreme that they name: `instance_map`: constant on each aligned 16 x 16 block of fine pixels.
All inputs are finite; a program needn't handle non-finite values.
Results may differ from a plain program's by a relative error of at most 0.0075.
Values may be sent and summed in bfloat16 or wider, within the bound.
No kernel may reach another device: no remote copies, remote signals or barrier semaphores. Data moves between devices by JAX's collectives and lax.ppermute only.
A program may use at most 64 MiB of HBM per device.

v0:
```python
import math

import jax
import jax.numpy as jnp
from jax import lax
from jax.sharding import PartitionSpec as P

INSTANCES = 256
UPSCALE = 16


norm_eps = 1e-05


def padded_2(array, sides, width):
    for axis, dim in sides:
        devices, length = (lax.axis_size(axis), array.shape[dim])
        up = [(i, (i + 1) % devices) for i in range(devices - 1)]
        down = [(j, i) for i, j in up]
        last = lax.slice_in_dim(array, length - width, length, axis=dim)
        initial = lax.slice_in_dim(array, 0, width, axis=dim)
        before = lax.ppermute(last, axis, up)
        after = lax.ppermute(initial, axis, down)
        array = jnp.concatenate([before, array, after], axis=dim)
    return array


def conv_taps(padded, weight, row_count, col_count):
    summed = jnp.zeros((row_count * col_count, weight.shape[3]), jnp.float32)
    for tap_row in range(3):
        for tap_col in range(3):
            window = padded[tap_row : tap_row + row_count, tap_col : tap_col + col_count]
            summed = summed + jnp.dot(
                window.reshape(row_count * col_count, window.shape[2]),
                weight[tap_row, tap_col],
                preferred_element_type=jnp.float32,
            )
    return summed


def back_taps(padded, weight, row_count, col_count):
    summed = jnp.zeros((row_count * col_count, weight.shape[2]), jnp.float32)
    for tap_row in range(3):
        for tap_col in range(3):
            window = padded[
                2 - tap_row : 2 - tap_row + row_count, 2 - tap_col : 2 - tap_col + col_count
            ]
            summed = summed + jnp.dot(
                window.reshape(row_count * col_count, window.shape[2]),
                weight[tap_row, tap_col].T,
                preferred_element_type=jnp.float32,
            )
    return summed


def weight_taps(padded, gradient, row_count, col_count):
    flattened = gradient.reshape(row_count * col_count, gradient.shape[2])
    stacked = []
    for tap_row in range(3):
        line = []
        for tap_col in range(3):
            window = padded[tap_row : tap_row + row_count, tap_col : tap_col + col_count]
            line.append(
                lax.dot_general(
                    window.reshape(row_count * col_count, window.shape[2]),
                    flattened,
                    (((0,), (0,)), ((), ())),
                    preferred_element_type=jnp.float32,
                )
            )
        stacked.append(jnp.stack(line))
    return jnp.stack(stacked)


def band_conv(band_field, weight):
    band_rows, band_cols, width_share = band_field.shape
    gathered = lax.all_gather(band_field, "cols", axis=2, tiled=True)
    rimmed = padded_2(gathered, (("rows", 0),), 1)
    rimmed = jnp.pad(rimmed, ((0, 0), (1, 1), (0, 0)))
    result = conv_taps(rimmed, weight, band_rows, band_cols)
    return result


def tile_conv(field, weight):
    padded = padded_2(field, (("rows", 0), ("cols", 1)), 1)
    return (padded, conv_taps(padded, weight, field.shape[0], field.shape[1]))


def grad_halo(field):
    return padded_2(field, (("rows", 0), ("cols", 1)), 1)


def per_device(
    global_in,
    global_first,
    global_second,
    project_weight,
    enhancer_input,
    instance_map,
    encoder_features,
    instance_weight,
    enhancer_first,
    enhancer_second,
    output_cotangent,
):
    band_rows, band_cols, width_share = global_in.shape
    tile_rows, tile_cols, local_width = enhancer_input.shape
    first_raw = band_conv(global_in, global_first)
    band_sum, band_square = lax.psum(
        (jnp.sum(first_raw, 0), jnp.sum(first_raw * first_raw, 0)), "rows"
    )
    band_total = band_rows * band_cols * lax.axis_size("rows")
    band_mean = band_sum / band_total
    band_var = band_square / band_total - band_mean * band_mean
    normed = (first_raw - band_mean) * lax.rsqrt(band_var + norm_eps)
    hidden = (
        jnp.maximum(normed, 0.0).astype(jnp.bfloat16).reshape(band_rows, band_cols, width_share)
    )
    second_raw = band_conv(hidden, global_second)
    global_out = (
        (global_in.astype(jnp.float32).reshape(-1, width_share) + second_raw)
        .astype(jnp.bfloat16)
        .reshape(band_rows, band_cols, width_share)
    )
    weight_rows = lax.dynamic_slice_in_dim(
        project_weight, lax.axis_index("cols") * width_share, width_share, 0
    )
    reduced = lax.psum_scatter(
        jnp.einsum("bwc,cd->wbd", global_out, weight_rows, preferred_element_type=jnp.float32),
        "cols",
        scatter_dimension=0,
        tiled=True,
    )
    coarse = jnp.transpose(reduced, (1, 0, 2)).astype(jnp.bfloat16)
    block_rows = tile_rows // UPSCALE
    block_cols = tile_cols // UPSCALE
    block_labels = instance_map[::UPSCALE, ::UPSCALE].reshape(-1)
    one_hot = (block_labels[:, None] == jnp.arange(INSTANCES, dtype=jnp.int32)[None, :]).astype(
        jnp.float32
    )
    encoder_width = encoder_features.shape[0]
    block_sums = (
        encoder_features.reshape(encoder_width, block_rows, UPSCALE, block_cols, UPSCALE)
        .sum(axis=(2, 4))
        .reshape(encoder_width, -1)
    )
    feature_sums = jnp.dot(block_sums, one_hot, precision=lax.Precision.HIGHEST)
    member_counts = jnp.sum(one_hot, 0) * float(UPSCALE * UPSCALE)
    feature_sums, member_counts = lax.psum((feature_sums, member_counts), ("rows", "cols"))
    averages = feature_sums / jnp.maximum(member_counts, 1.0)
    lookup = jnp.dot(averages.T, instance_weight, precision=lax.Precision.HIGHEST)
    pooled_blocks = jnp.dot(one_hot, lookup, precision=lax.Precision.HIGHEST).reshape(
        block_rows, block_cols, local_width
    )
    block_terms = coarse.astype(jnp.float32) + pooled_blocks
    upsampled = jnp.repeat(jnp.repeat(block_terms, UPSCALE, 0), UPSCALE, 1)
    mixed = (enhancer_input.astype(jnp.float32) + upsampled).astype(jnp.bfloat16)
    mixed_padded, first_act = tile_conv(mixed, enhancer_first)
    pixel_total = tile_rows * tile_cols * lax.axis_size("rows") * lax.axis_size("cols")
    act_sum, act_square = lax.psum(
        (jnp.sum(first_act, 0), jnp.sum(first_act * first_act, 0)), ("rows", "cols")
    )
    act_mean = act_sum / pixel_total
    inverse_dev = lax.rsqrt(act_square / pixel_total - act_mean * act_mean + norm_eps)
    normed_act = (first_act - act_mean) * inverse_dev
    activated = (
        jax.nn.silu(normed_act).astype(jnp.bfloat16).reshape(tile_rows, tile_cols, local_width)
    )
    active_padded, second_act = tile_conv(activated, enhancer_second)
    enhanced = (
        (mixed.astype(jnp.float32).reshape(-1, local_width) + second_act)
        .astype(jnp.bfloat16)
        .reshape(tile_rows, tile_cols, local_width)
    )
    cotangent_padded = grad_halo(output_cotangent)
    second_local = weight_taps(active_padded, output_cotangent, tile_rows, tile_cols)
    act_grad = back_taps(cotangent_padded, enhancer_second, tile_rows, tile_cols)
    gate_value = jax.nn.sigmoid(normed_act)
    normed_grad = act_grad * gate_value * (1.0 + normed_act * (1.0 - gate_value))
    grad_sum, cross_sum = lax.psum(
        (jnp.sum(normed_grad, 0), jnp.sum(normed_grad * normed_act, 0)), ("rows", "cols")
    )
    first_grad = (
        (
            inverse_dev
            * (normed_grad - grad_sum / pixel_total - normed_act * (cross_sum / pixel_total))
        )
        .astype(jnp.bfloat16)
        .reshape(tile_rows, tile_cols, local_width)
    )
    first_local = weight_taps(mixed_padded, first_grad, tile_rows, tile_cols)
    first_padded = grad_halo(first_grad)
    mixed_grad = output_cotangent.astype(jnp.float32).reshape(-1, local_width) + back_taps(
        first_padded, enhancer_first, tile_rows, tile_cols
    )
    global_gradient = (
        mixed_grad.reshape(block_rows, UPSCALE, block_cols, UPSCALE, local_width).sum(axis=(1, 3))
        / UPSCALE
    )
    first_total, second_total = lax.psum((first_local, second_local), ("rows", "cols"))
    rescale = 1.0 / math.sqrt(pixel_total)
    return (enhanced, first_total * rescale, second_total * rescale, global_gradient)


def solution(mesh):
    return jax.shard_map(
        per_device,
        mesh=mesh,
        in_specs=(
            P("rows", None, "cols"),
            P(None, None, None, "cols"),
            P(None, None, None, "cols"),
            P(),
            P("rows", "cols", None),
            P("rows", "cols"),
            P(None, "rows", "cols"),
            P(),
            P(),
            P(),
            P("rows", "cols", None),
        ),
        out_specs=(P("rows", "cols", None), P(), P(), P("rows", "cols", None)),
        check_vma=False,
    )
```

profile of v0, /device:TPU:0, one launch (start us, length us, event | category | flops | bytes accessed | tf_op | source)
XLA Modules:
  0.0 439.8 jit_solution(5252399451311661370)
XLA Ops:
  7.2 10.8 %all_gather.6 = bf16[2,32,1024]{2,1,0:T(8,128)(2,1)S(1)} all-gather(bf16[2,32,128]{2,1,0:T(8,128)(2,1)} %param.11), channel_id=1, replica_groups=mesh['rows'=4,'cols'=8] {'cols'}, dimensions={2}, use_global_device_ids=true | all-gather | bytes 147456 | tf_op jit(solution)/shard_map/all_gather | solution.py:77
  18.7 3.5 collective-permute-start
  22.2 1.3 collective-permute-start.1
  24.2 4.7 %collective-permute-start.12 = (bf16[1,64,128]{2,1,0:T(8,128)(2,1)S(1)}, bf16[1,64,128]{2,1,0:T(8,128)(2,1)S(1)}, u32[]{:S(2)}, u32[]{:S(2)}) collective-permute-start(bf16[1,64,128]{2,1,0:T(8,128)(2,1)S(1)} %get-tuple-element.71), channel_id=1, source_target_pairs={{0,8},{8,16},{16,24},{1,9},{9,17},{17,25},{2,10},{10,18},{18,26},{... | collective-permute-start | bytes 49160 | tf_op jit(solution)/shard_map/ppermute | solution.py:22
  28.9 1.3 collective-permute-start.13
  31.1 1.4 reshape.263
  33.2 40.9 %all-reduce.5 = (f32[16,256]{1,0:T(8,128)S(1)}, f32[256]{0:T(256)S(1)}) all-reduce(f32[16,256]{1,0:T(8,128)S(1)} %fusion.158, f32[256]{0:T(256)S(1)} %broadcast_multiply_fusion.3), channel_id=1, replica_groups=mesh['rows'=4,'cols'=8] {'rows','cols'}, use_global_device_ids=true, to_apply=%region_6.7 | all-reduce | flops 4352 | bytes 34816 | tf_op jit(solution)/shard_map/psum | solution.py:149
  76.4 1.3 collective-permute-start.14
  77.7 3.0 collective-permute-start.15
  81.0 1.3 fusion.75
  82.3 1.4 pad_maximum_fusion.9
  85.2 1.1 copy-done.13
  88.0 10.6 %all-reduce.7 = (f32[128]{0:T(128)S(1)}, f32[128]{0:T(128)S(1)}) all-reduce(f32[128]{0:T(128)S(1)} %get-tuple-element.9, f32[128]{0:T(128)S(1)} %get-tuple-element.8), channel_id=1, replica_groups=mesh['rows'=4,'cols'=8] {'rows'}, use_global_device_ids=true, to_apply=%region_3.4 | all-reduce | flops 256 | bytes 2048 | tf_op jit(solution)/shard_map/psum | solution.py:109
  98.6 11.8 %all_gather.7 = bf16[2,32,1024]{2,1,0:T(8,128)(2,1)S(1)} all-gather(bf16[2,32,128]{2,1,0:T(8,128)(2,1)S(1)} %bitcast.452), channel_id=1, replica_groups=mesh['rows'=4,'cols'=8] {'cols'}, dimensions={2}, use_global_device_ids=true | all-gather | bytes 147456 | tf_op jit(solution)/shard_map/all_gather | solution.py:77
  110.4 1.7 collective-permute-start.2
  112.1 1.3 collective-permute-start.3
  113.4 2.2 convolution_add_fusion.8
  115.6 2.7 collective-permute-done.3
  120.4 22.4 %all-reduce.2 = bf16[32,2,128]{2,0,1:T(8,128)(2,1)S(1)} all-reduce(f32[32,2,128]{2,0,1:T(8,128)S(1)} %convolution_bitcast_fusion.18), channel_id=2, replica_groups=mesh['rows'=4,'cols'=8] {'cols'}, use_global_device_ids=true, to_apply=%region_4.5.clone | all-reduce | flops 8192 | bytes 49152
  142.9 2.6 collective-permute-start.4
  145.5 1.3 collective-permute-start.5
  146.8 2.0 fusion.71
  148.8 2.3 collective-permute-done.5
  151.2 1.3 collective-permute-start.6
  152.5 1.3 collective-permute-start.7
  154.2 1.4 collective-permute-done.7
  158.9 1.3 fusion.171
  160.2 41.8 %all-reduce.4 = (f32[128]{0:T(128)S(1)}, f32[128]{0:T(128)S(1)}) all-reduce(f32[128]{0:T(128)S(1)} %get-tuple-element.7, f32[128]{0:T(128)S(1)} %get-tuple-element.6), channel_id=1, replica_groups=mesh['rows'=4,'cols'=8] {'rows','cols'}, use_global_device_ids=true, to_apply=%region_12.13 | all-reduce | flops 256 | bytes 2048 | tf_op jit(solution)/shard_map/psum | solution.py:160
  202.1 3.8 fusion.170
  205.9 40.1 %all-reduce.3 = (f32[128]{0:T(128)S(1)}, f32[128]{0:T(128)S(1)}) all-reduce(f32[128]{0:T(128)S(1)} %get-tuple-element.5, f32[128]{0:T(128)S(1)} %get-tuple-element.4), channel_id=1, replica_groups=mesh['rows'=4,'cols'=8] {'rows','cols'}, use_global_device_ids=true, to_apply=%region_16.17 | all-reduce | flops 256 | bytes 2048 | tf_op jit(solution)/shard_map/psum | solution.py:180
  246.0 2.0 multiply_convert_fusion
  252.6 2.4 collective-permute-start.16
  255.0 1.3 collective-permute-start.17
  256.3 4.5 %collective-permute-start.8 = (bf16[1,64,128]{2,1,0:T(8,128)(2,1)S(1)}, bf16[1,64,128]{2,1,0:T(8,128)(2,1)S(1)}, u32[]{:S(2)}, u32[]{:S(2)}) collective-permute-start(bf16[1,64,128]{2,1,0:T(8,128)(2,1)S(1)} %get-tuple-element.74), channel_id=1, source_target_pairs={{0,8},{8,16},{16,24},{1,9},{9,17},{17,25},{2,10},{10,18},{18,26},{... | collective-permute-start | bytes 49160 | tf_op jit(solution)/shard_map/ppermute | solution.py:22
  260.8 1.3 collective-permute-start.9
  262.2 0.9 pad_maximum_fusion.3
  263.5 1.3 collective-permute-start.18
  264.8 3.0 collective-permute-start.19
  267.9 3.8 collective-permute-start.10
  271.7 1.5 collective-permute-start.11
  273.3 1.0 fusion.90
  274.4 1.0 convolution_bitcast_fusion.1
  276.1 1.0 convolution_bitcast_fusion.7
  277.0 1.0 convolution_bitcast_fusion.4
  278.0 1.0 convolution_bitcast_fusion.8
  279.0 1.0 convolution_bitcast_fusion.6
  279.9 1.0 convolution_bitcast_fusion.2
  280.9 1.3 fusion.175
  282.2 1.4 fusion.176
  283.6 1.0 convolution_bitcast_fusion.3
  287.9 1.3 fusion.1
  289.2 1.4 reduce_sum.89
  290.6 1.1 convolution_add_fusion.19
  291.7 1.1 convolution_add_fusion.18
  292.8 1.0 convolution_add_fusion.17
  294.0 1.1 convolution_add_fusion.16
  295.3 0.9 pad_maximum_fusion.4
  296.5 1.1 convolution_add_fusion.15
  297.6 1.1 convolution_add_fusion.14
  299.3 1.0 fusion.73
  300.4 1.9 fusion.9
  302.3 127.9 %all-reduce.10.cloned.1.call-done = (f32[3,3,128,128]{3,2,1,0:T(8,128)}, f32[3,3,128,128]{3,2,1,0:T(8,128)}) async-done(((f32[3,3,128,128]{3,2,1,0:T(8,128)}, f32[3,3,128,128]{3,2,1,0:T(8,128)}), (f32[3,3,128,128]{3,2,1,0:T(8,128)}, f32[3,3,128,128]{3,2,1,0:T(8,128)})) %all-reduce.10.cloned.1.call-update) | async-done | bytes 1179664 | tf_op jit(solution)/shard_map/psum | solution.py:200
  430.1 2.0 broadcast_multiply_fusion
  432.1 0.9 broadcast_multiply_fusion.1
  (197 shorter events, 23.7 us)
Async XLA Ops:
  7.2 113.0 %copy-start = (bf16[1024,128]{1,0:T(8,128)(2,1)S(1)}, bf16[1024,128]{1,0:T(8,128)(2,1)}, u32[]{:S(2)}) copy-start(bf16[1024,128]{1,0:T(8,128)(2,1)} %param.14) | copy-start | bytes 786436
  7.2 423.0 %all-reduce.10.cloned.1.call-start = ((), (), s32[]{:S(2)}) async-start(), calls=%async_computation | async-start | bytes 2359296 | tf_op jit(solution)/shard_map/psum | solution.py:200
  18.7 66.3 %collective-permute-start = (bf16[1,32,1024]{2,1,0:T(8,128)(2,1)}, bf16[1,32,1024]{2,1,0:T(8,128)(2,1)S(1)}, u32[]{:S(2)}, u32[]{:S(2)}) collective-permute-start(bf16[1,32,1024]{2,1,0:T(8,128)(2,1)} %get-tuple-element.98), channel_id=1, source_target_pairs={{0,8},{8,16},{16,24},{1,9},{9,17},{17,25},{2,10},{10,18},{18,26},{... | collective-permute-start | bytes 196616 | tf_op jit(solution)/shard_map/ppermute | solution.py:22
  22.2 62.8 %collective-permute-start.1 = (bf16[1,32,1024]{2,1,0:T(8,128)(2,1)S(1)}, bf16[1,32,1024]{2,1,0:T(8,128)(2,1)S(1)}, u32[]{:S(2)}, u32[]{:S(2)}) collective-permute-start(bf16[1,32,1024]{2,1,0:T(8,128)(2,1)S(1)} %get-tuple-element.99), channel_id=1, source_target_pairs={{8,0},{16,8},{24,16},{9,1},{17,9},{25,17},{10,2},{18,10},{26,18},{... | collective-permute-start | bytes 196616 | tf_op jit(solution)/shard_map/ppermute | solution.py:23
  24.2 49.9 %copy-start.35 = (f32[16,128]{1,0:T(8,128)S(1)}, f32[16,128]{1,0:T(8,128)}, u32[]{:S(2)}) copy-start(f32[16,128]{1,0:T(8,128)} %param.18) | copy-start | bytes 24580
  24.2 51.7 %collective-permute-start.12 = (bf16[1,64,128]{2,1,0:T(8,128)(2,1)S(1)}, bf16[1,64,128]{2,1,0:T(8,128)(2,1)S(1)}, u32[]{:S(2)}, u32[]{:S(2)}) collective-permute-start(bf16[1,64,128]{2,1,0:T(8,128)(2,1)S(1)} %get-tuple-element.71), channel_id=1, source_target_pairs={{0,8},{8,16},{16,24},{1,9},{9,17},{17,25},{2,10},{10,18},{18,26},{... | collective-permute-start | bytes 49160 | tf_op jit(solution)/shard_map/ppermute | solution.py:22
  28.9 47.1 %collective-permute-start.13 = (bf16[1,64,128]{2,1,0:T(8,128)(2,1)S(1)}, bf16[1,64,128]{2,1,0:T(8,128)(2,1)S(1)}, u32[]{:S(2)}, u32[]{:S(2)}) collective-permute-start(bf16[1,64,128]{2,1,0:T(8,128)(2,1)S(1)} %get-tuple-element.70), channel_id=1, source_target_pairs={{8,0},{16,8},{24,16},{9,1},{17,9},{25,17},{10,2},{18,10},{26,18},{... | collective-permute-start | bytes 49160 | tf_op jit(solution)/shard_map/ppermute | solution.py:23
  31.1 43.6 %copy-start.36 = (u32[32]{0:T(128)S(1)}, u32[32]{0:T(128)}, u32[]{:S(2)}) copy-start(u32[32]{0:T(128)} %constant.45) | copy-start | bytes 388
  31.1 44.9 %copy-start.2 = (bf16[32,64,128]{2,1,0:T(8,128)(2,1)S(1)}, bf16[32,64,128]{2,1,0:T(8,128)(2,1)}, u32[]{:S(2)}) copy-start(bf16[32,64,128]{2,1,0:T(8,128)(2,1)} %param.21) | copy-start | bytes 1572868
  74.5 6.2 %copy-start.23 = (bf16[3,3,128,128]{3,2,1,0:T(8,128)(2,1)S(1)}, bf16[3,3,128,128]{3,2,1,0:T(8,128)(2,1)}, u32[]{:S(2)}) copy-start(bf16[3,3,128,128]{3,2,1,0:T(8,128)(2,1)} %param.20) | copy-start | bytes 884740
  76.4 5.9 %collective-permute-start.14 = (bf16[34,1,128]{2,1,0:T(2,128)(2,1)S(1)}, bf16[34,1,128]{2,1,0:T(2,128)(2,1)S(1)}, u32[]{:S(2)}, u32[]{:S(2)}) collective-permute-start(bf16[34,1,128]{2,1,0:T(2,128)(2,1)S(1)} %get-tuple-element.53), channel_id=1, source_target_pairs={{1,0},{2,1},{3,2},{4,3},{5,4},{6,5},{7,6},{9,8},{10,9},{11,10},{12... | collective-permute-start | bytes 26120 | tf_op jit(solution)/shard_map/ppermute | solution.py:23
  77.7 4.7 %collective-permute-start.15 = (bf16[34,1,128]{2,1,0:T(2,128)(2,1)S(1)}, bf16[34,1,128]{2,1,0:T(2,128)(2,1)S(1)}, u32[]{:S(2)}, u32[]{:S(2)}) collective-permute-start(bf16[34,1,128]{2,1,0:T(2,128)(2,1)S(1)} %get-tuple-element.54), channel_id=1, source_target_pairs={{0,1},{1,2},{2,3},{3,4},{4,5},{5,6},{6,7},{8,9},{9,10},{10,11},{11... | collective-permute-start | bytes 26120 | tf_op jit(solution)/shard_map/ppermute | solution.py:22
  84.7 1.7 copy-start.13
  110.4 5.2 %collective-permute-start.2 = (bf16[1,32,1024]{2,1,0:T(8,128)(2,1)S(1)}, bf16[1,32,1024]{2,1,0:T(8,128)(2,1)S(1)}, u32[]{:S(2)}, u32[]{:S(2)}) collective-permute-start(bf16[1,32,1024]{2,1,0:T(8,128)(2,1)S(1)} %get-tuple-element.94), channel_id=1, source_target_pairs={{0,8},{8,16},{16,24},{1,9},{9,17},{17,25},{2,10},{10,18},{18,26},{... | collective-permute-start | bytes 196616 | tf_op jit(solution)/shard_map/ppermute | solution.py:22
  112.1 6.2 %collective-permute-start.3 = (bf16[1,32,1024]{2,1,0:T(8,128)(2,1)S(1)}, bf16[1,32,1024]{2,1,0:T(8,128)(2,1)S(1)}, u32[]{:S(2)}, u32[]{:S(2)}) collective-permute-start(bf16[1,32,1024]{2,1,0:T(8,128)(2,1)S(1)} %get-tuple-element.95), channel_id=1, source_target_pairs={{8,0},{16,8},{24,16},{9,1},{17,9},{25,17},{10,2},{18,10},{26,18},{... | collective-permute-start | bytes 196616 | tf_op jit(solution)/shard_map/ppermute | solution.py:23
  113.4 5.1 %copy-start.14 = (bf16[3,3,1024,128]{3,2,1,0:T(8,128)(2,1)S(1)}, bf16[3,3,1024,128]{3,2,1,0:T(8,128)(2,1)}, u32[]{:S(2)}) copy-start(bf16[3,3,1024,128]{3,2,1,0:T(8,128)(2,1)} %param.13) | copy-start | bytes 7077892
  119.1 0.9 copy-start.27
  119.3 23.5 %copy-start.26 = (bf16[32,64,128]{2,1,0:T(8,128)(2,1)S(1)}, bf16[32,64,128]{2,1,0:T(8,128)(2,1)}, u32[]{:S(2)}) copy-start(bf16[32,64,128]{2,1,0:T(8,128)(2,1)} %param.15) | copy-start | bytes 1572868
  142.9 5.9 %collective-permute-start.4 = (bf16[1,64,128]{2,1,0:T(8,128)(2,1)S(1)}, bf16[1,64,128]{2,1,0:T(8,128)(2,1)S(1)}, u32[]{:S(2)}, u32[]{:S(2)}) collective-permute-start(bf16[1,64,128]{2,1,0:T(8,128)(2,1)S(1)} %get-tuple-element.78), channel_id=1, source_target_pairs={{0,8},{8,16},{16,24},{1,9},{9,17},{17,25},{2,10},{10,18},{18,26},{... | collective-permute-start | bytes 49160 | tf_op jit(solution)/shard_map/ppermute | solution.py:22
  145.5 5.6 %collective-permute-start.5 = (bf16[1,64,128]{2,1,0:T(8,128)(2,1)S(1)}, bf16[1,64,128]{2,1,0:T(8,128)(2,1)S(1)}, u32[]{:S(2)}, u32[]{:S(2)}) collective-permute-start(bf16[1,64,128]{2,1,0:T(8,128)(2,1)S(1)} %get-tuple-element.79), channel_id=1, source_target_pairs={{8,0},{16,8},{24,16},{9,1},{17,9},{25,17},{10,2},{18,10},{26,18},{... | collective-permute-start | bytes 49160 | tf_op jit(solution)/shard_map/ppermute | solution.py:23
  148.8 5.0 %copy-start.21 = (bf16[3,3,128,128]{3,2,1,0:T(8,128)(2,1)S(1)}, bf16[3,3,128,128]{3,2,1,0:T(8,128)(2,1)}, u32[]{:S(2)}) copy-start(bf16[3,3,128,128]{3,2,1,0:T(8,128)(2,1)} %param.19) | copy-start | bytes 884740
  151.2 3.0 collective-permute-start.6
  152.5 3.1 collective-permute-start.7
  156.5 0.8 copy-start.9
  156.5 1.0 copy-start.11
  156.5 1.2 copy-start.5
  156.5 1.8 copy-start.7
  156.5 2.1 copy-start.3
  158.9 43.2 %copy-start.25 = (bf16[32,64,128]{2,1,0:T(8,128)(2,1)S(1)}, bf16[32,64,128]{2,1,0:T(8,128)(2,1)}, u32[]{:S(2)}) copy-start(bf16[32,64,128]{2,1,0:T(8,128)(2,1)} %get-tuple-element.40) | copy-start | bytes 1572868
  248.0 1.0 copy-start.12
  248.4 1.1 copy-start.10
  249.0 1.1 copy-start.8
  249.4 1.1 copy-start.6
  250.9 1.0 copy-start.4
  252.6 10.5 %collective-permute-start.16 = (bf16[1,64,128]{2,1,0:T(8,128)(2,1)S(1)}, bf16[1,64,128]{2,1,0:T(8,128)(2,1)S(1)}, u32[]{:S(2)}, u32[]{:S(2)}) collective-permute-start(bf16[1,64,128]{2,1,0:T(8,128)(2,1)S(1)} %get-tuple-element.65), channel_id=1, source_target_pairs={{0,8},{8,16},{16,24},{1,9},{9,17},{17,25},{2,10},{10,18},{18,26},{... | collective-permute-start | bytes 49160 | tf_op jit(solution)/shard_map/ppermute | solution.py:22
  255.0 8.1 %collective-permute-start.17 = (bf16[1,64,128]{2,1,0:T(8,128)(2,1)S(1)}, bf16[1,64,128]{2,1,0:T(8,128)(2,1)S(1)}, u32[]{:S(2)}, u32[]{:S(2)}) collective-permute-start(bf16[1,64,128]{2,1,0:T(8,128)(2,1)S(1)} %get-tuple-element.66), channel_id=1, source_target_pairs={{8,0},{16,8},{24,16},{9,1},{17,9},{25,17},{10,2},{18,10},{26,18},{... | collective-permute-start | bytes 49160 | tf_op jit(solution)/shard_map/ppermute | solution.py:23
  256.3 11.6 %collective-permute-start.8 = (bf16[1,64,128]{2,1,0:T(8,128)(2,1)S(1)}, bf16[1,64,128]{2,1,0:T(8,128)(2,1)S(1)}, u32[]{:S(2)}, u32[]{:S(2)}) collective-permute-start(bf16[1,64,128]{2,1,0:T(8,128)(2,1)S(1)} %get-tuple-element.74), channel_id=1, source_target_pairs={{0,8},{8,16},{16,24},{1,9},{9,17},{17,25},{2,10},{10,18},{18,26},{... | collective-permute-start | bytes 49160 | tf_op jit(solution)/shard_map/ppermute | solution.py:22
  260.8 7.0 %collective-permute-start.9 = (bf16[1,64,128]{2,1,0:T(8,128)(2,1)S(1)}, bf16[1,64,128]{2,1,0:T(8,128)(2,1)S(1)}, u32[]{:S(2)}, u32[]{:S(2)}) collective-permute-start(bf16[1,64,128]{2,1,0:T(8,128)(2,1)S(1)} %get-tuple-element.75), channel_id=1, source_target_pairs={{8,0},{16,8},{24,16},{9,1},{17,9},{25,17},{10,2},{18,10},{26,18},{... | collective-permute-start | bytes 49160 | tf_op jit(solution)/shard_map/ppermute | solution.py:23
  262.2 1.0 copy-start.22
  263.5 21.1 %collective-permute-start.18 = (bf16[34,1,128]{2,1,0:T(2,128)(2,1)S(1)}, bf16[34,1,128]{2,1,0:T(2,128)(2,1)S(1)}, u32[]{:S(2)}, u32[]{:S(2)}) collective-permute-start(bf16[34,1,128]{2,1,0:T(2,128)(2,1)S(1)} %get-tuple-element.48), channel_id=1, source_target_pairs={{1,0},{2,1},{3,2},{4,3},{5,4},{6,5},{7,6},{9,8},{10,9},{11,10},{12... | collective-permute-start | bytes 26120 | tf_op jit(solution)/shard_map/ppermute | solution.py:23
  264.8 19.8 %collective-permute-start.19 = (bf16[34,1,128]{2,1,0:T(2,128)(2,1)S(1)}, bf16[34,1,128]{2,1,0:T(2,128)(2,1)S(1)}, u32[]{:S(2)}, u32[]{:S(2)}) collective-permute-start(bf16[34,1,128]{2,1,0:T(2,128)(2,1)S(1)} %get-tuple-element.49), channel_id=1, source_target_pairs={{0,1},{1,2},{2,3},{3,4},{4,5},{5,6},{6,7},{8,9},{9,10},{10,11},{11... | collective-permute-start | bytes 26120 | tf_op jit(solution)/shard_map/ppermute | solution.py:22
  267.9 7.8 %collective-permute-start.10 = (bf16[34,1,128]{2,1,0:T(2,128)(2,1)S(1)}, bf16[34,1,128]{2,1,0:T(2,128)(2,1)S(1)}, u32[]{:S(2)}, u32[]{:S(2)}) collective-permute-start(bf16[34,1,128]{2,1,0:T(2,128)(2,1)S(1)} %get-tuple-element.57), channel_id=1, source_target_pairs={{0,1},{1,2},{2,3},{3,4},{4,5},{5,6},{6,7},{8,9},{9,10},{10,11},{11... | collective-permute-start | bytes 26120 | tf_op jit(solution)/shard_map/ppermute | solution.py:22
  271.7 4.0 collective-permute-start.11
  289.2 1.4 copy-start.19
  290.6 1.1 copy-start.20
  291.7 1.1 copy-start.18
  293.9 1.2 copy-start.28
  293.9 1.2 copy-start.32
  293.9 1.2 copy-start.33
  293.9 1.2 copy-start.29
  293.9 1.2 copy-start.31
  293.9 1.3 copy-start.30
  294.0 1.3 copy-start.34
  295.2 1.3 copy-start.17
  296.5 1.1 copy-start.16
  297.6 1.7 copy-start.15
  300.4 132.6 %copy-start.1 = (bf16[1024,128]{1,0:T(8,128)(2,1)S(1)}, bf16[1024,128]{1,0:T(8,128)(2,1)}, u32[]{:S(2)}) copy-start(bf16[1024,128]{1,0:T(8,128)(2,1)} %param.14) | copy-start | bytes 786436
  430.1 2.0 copy-start.24
Sparse Core Ops, SparseCore 0:
  296.3 133.8 all-reduce.9
where the time goes:
time: 442 us; the launch traced here: 440 us
  blocking collectives  178 us (40%)
  waiting for transfers between devices  134 us (30%)
  starting transfers between devices  43.6 us (10%)
  matrix products  43.2 us (10%)
  between operations  15.9 us (4%)
  other arithmetic  12.6 us (3%)
  local copies, waits for them, and re-layouts  11.9 us (3%)
    psum x1, waiting for transfers between devices, per_device(): lax.psum((first_local, second_local), ('rows', 'cols'))  128 us
    psum x1, blocking collectives, per_device(): lax.psum((jnp.sum(first_act, 0), jnp.sum(first_act * first_act, 0)), ('ro...  41.8 us
    psum x1, blocking collectives, per_device(): lax.psum((feature_sums, member_counts), ('rows', 'cols'))  40.9 us
    psum x1, blocking collectives, per_device(): lax.psum((jnp.sum(normed_grad, 0), jnp.sum(normed_grad * normed_act, 0)),...  40.1 us
    ppermute x10, starting transfers between devices, padded_2(): before = lax.ppermute(last, axis, up)  30.5 us
    all_gather x2, blocking collectives, band_conv(): gathered = lax.all_gather(band_field, 'cols', axis=2, tiled=True)  22.7 us
    unnamed x1, blocking collectives  22.4 us
    dot_general x36, matrix products, conv_taps(): jnp.dot(window.reshape(row_count * col_count, window.shape[2]), weight[ta...  17.2 us
  transfers between devices with their start and end apart: 21, of which 4 were waited for; matrix products, arithmetic and copies ran while one was open for 7% of the time, Pallas kernels for 0%

commit v1 on v0

v1 whole, which is shorter than its diff:
```python
import math

import jax
import jax.numpy as jnp
from jax import lax
from jax.sharding import PartitionSpec as P

INSTANCES = 256
UPSCALE = 16
BOTH = ("rows", "cols")

norm_eps = 1e-05


def halo_2(array, axis, dim, width):
    devices, length = (lax.axis_size(axis), array.shape[dim])
    up = [(i, i + 1) for i in range(devices - 1)]
    down = [(j, i) for i, j in up]
    last = lax.slice_in_dim(array, length - width, length, axis=dim)
    initial = lax.slice_in_dim(array, 0, width, axis=dim)
    before = lax.ppermute(last, axis, up)
    after = lax.ppermute(initial, axis, down)
    return jnp.concatenate([before, array, after], axis=dim)


def conv_taps(padded, weight, row_count, col_count):
    summed = jnp.zeros((row_count * col_count, weight.shape[3]), jnp.float32)
    for tap_row in range(3):
        for tap_col in range(3):
            window = padded[tap_row : tap_row + row_count, tap_col : tap_col + col_count]
            summed = summed + jnp.dot(
                window.reshape(row_count * col_count, window.shape[2]),
                weight[tap_row, tap_col],
                preferred_element_type=jnp.float32,
            )
    return summed


def back_taps(padded, weight, row_count, col_count):
    summed = jnp.zeros((row_count * col_count, weight.shape[2]), jnp.float32)
    for tap_row in range(3):
        for tap_col in range(3):
            window = padded[
                2 - tap_row : 2 - tap_row + row_count, 2 - tap_col : 2 - tap_col + col_count
            ]
            summed = summed + jnp.dot(
                window.reshape(row_count * col_count, window.shape[2]),
                weight[tap_row, tap_col].T,
                preferred_element_type=jnp.float32,
            )
    return summed


def weight_taps(padded, gradient, row_count, col_count):
    flattened = gradient.reshape(row_count * col_count, gradient.shape[2])
    stacked = []
    for tap_row in range(3):
        for tap_col in range(3):
            window = padded[tap_row : tap_row + row_count, tap_col : tap_col + col_count]
            stacked.append(
                lax.dot_general(
                    window.reshape(row_count * col_count, window.shape[2]),
                    flattened,
                    (((0,), (0,)), ((), ())),
                    preferred_element_type=jnp.float32,
                )
            )
    return jnp.concatenate(stacked)


def pieces(array):
    high = array.astype(jnp.bfloat16)
    rest = array - high.astype(jnp.float32)
    middle = rest.astype(jnp.bfloat16)
    return high, middle, (rest - middle.astype(jnp.float32)).astype(jnp.bfloat16)


def per_device(
    global_in,
    global_first,
    global_second,
    project_weight,
    enhancer_input,
    instance_map,
    encoder_features,
    instance_weight,
    enhancer_first,
    enhancer_second,
    output_cotangent,
):
    row_devices, col_devices = lax.axis_size("rows"), lax.axis_size("cols")
    devices = row_devices * col_devices
    my_row, my_col = lax.axis_index("rows"), lax.axis_index("cols")
    band_rows, band_cols, width_share = global_in.shape
    tile_rows, tile_cols, local_width = enhancer_input.shape
    coarse_rows = band_rows * row_devices
    block_rows = tile_rows // UPSCALE
    block_cols = tile_cols // UPSCALE
    blocks = block_rows * block_cols
    encoder_width = encoder_features.shape[0]

    block_labels = instance_map[::UPSCALE, ::UPSCALE].reshape(-1)
    block_sums = (
        encoder_features.reshape(encoder_width, block_rows, UPSCALE, block_cols, UPSCALE)
        .sum(axis=(2, 4))
        .reshape(-1)
    )
    extra = jnp.concatenate([*pieces(block_sums), block_labels.astype(jnp.bfloat16)])
    extra_rows = -(-extra.shape[0] // 2048) * 16
    extra = jnp.pad(extra, (0, extra_rows * 128 - extra.shape[0])).reshape(extra_rows, 128)
    packed = jnp.concatenate([global_in.reshape(-1, 128), extra])
    everything = lax.all_gather(packed, BOTH, axis=0)
    main_rows = packed.shape[0] - extra_rows
    gathered = everything[:, :main_rows].reshape(
        row_devices, col_devices, band_rows, band_cols, width_share
    )
    tail = everything[:, main_rows:].reshape(devices, -1)
    sums = blocks * encoder_width
    all_sums = sum(tail[:, k * sums : (k + 1) * sums].astype(jnp.float32) for k in (2, 1, 0))
    all_sums = (
        all_sums.reshape(row_devices, col_devices, encoder_width, block_rows, block_cols)
        .transpose(0, 3, 1, 4, 2)
        .reshape(-1, encoder_width)
    )
    all_labels = (
        tail[:, 3 * sums : 3 * sums + blocks]
        .reshape(row_devices, col_devices, block_rows, block_cols)
        .transpose(0, 2, 1, 3)
    )
    label_map = jnp.pad(
        all_labels.reshape(coarse_rows, band_cols), 1, constant_values=-1.0
    )
    near_labels = lax.dynamic_slice(
        label_map,
        (my_row * block_rows, my_col * block_cols),
        (block_rows + 2, block_cols + 2),
    ).reshape(-1)
    same = (near_labels[:, None] == all_labels.reshape(-1)[None, :]).astype(jnp.float32)
    near_sums = jnp.dot(same, all_sums, precision=lax.Precision.HIGHEST)
    near_counts = jnp.sum(same, 1, keepdims=True) * float(UPSCALE * UPSCALE)
    pooled = jnp.dot(
        near_sums / jnp.maximum(near_counts, 1.0),
        instance_weight,
        precision=lax.Precision.HIGHEST,
    ).reshape(block_rows + 2, block_cols + 2, local_width)

    both = jnp.stack([enhancer_input, output_cotangent])
    both = halo_2(both, "rows", 1, 2)
    both = halo_2(both, "cols", 2, 2)
    input_padded, cotangent_padded = both[0], both[1]

    whole_in = gathered.transpose(0, 2, 3, 1, 4).reshape(coarse_rows, band_cols, -1)
    rimmed = jnp.pad(whole_in, ((1, 1), (1, 1), (0, 0)))
    first_raw = conv_taps(rimmed, global_first, coarse_rows, band_cols)
    band_total = coarse_rows * band_cols
    band_mean = jnp.sum(first_raw, 0) / band_total
    band_var = jnp.sum(first_raw * first_raw, 0) / band_total - band_mean * band_mean
    normed = (first_raw - band_mean) * lax.rsqrt(band_var + norm_eps)
    hidden = (
        jnp.maximum(normed, 0.0).astype(jnp.bfloat16).reshape(coarse_rows, band_cols, width_share)
    )
    hidden = jnp.pad(hidden, ((2, 2), (0, 0), (0, 0)))
    near_hidden = lax.dynamic_slice_in_dim(hidden, my_row * band_rows, band_rows + 4, 0)
    near_hidden = lax.all_gather(near_hidden, "cols", axis=2, tiled=True)
    second_raw = conv_taps(
        jnp.pad(near_hidden, ((0, 0), (1, 1), (0, 0))), global_second, band_rows + 2, band_cols
    )
    mine = lax.dynamic_index_in_dim(gathered, my_col, 1, keepdims=False)
    mine = jnp.pad(
        mine.reshape(coarse_rows, band_cols, width_share), ((1, 1), (0, 0), (0, 0))
    )
    near_in = lax.dynamic_slice_in_dim(mine, my_row * band_rows, band_rows + 2, 0)
    global_out = (
        near_in.astype(jnp.float32).reshape(-1, width_share) + second_raw
    ).astype(jnp.bfloat16)
    weight_rows = lax.dynamic_slice_in_dim(project_weight, my_col * width_share, width_share, 0)
    partial = jnp.dot(global_out, weight_rows, preferred_element_type=jnp.float32)
    partial = jnp.pad(
        partial.reshape(band_rows + 2, band_cols, local_width), ((0, 0), (1, 1), (0, 0))
    )
    outgoing = jnp.stack(
        [partial[:, j * block_cols : (j + 1) * block_cols + 2] for j in range(col_devices)]
    )
    incoming = lax.all_to_all(outgoing, "cols", 0, 0)
    coarse = jnp.sum(incoming, 0).astype(jnp.bfloat16)

    block_terms = coarse.astype(jnp.float32) + pooled
    upsampled = jnp.repeat(jnp.repeat(block_terms, UPSCALE, 0), UPSCALE, 1)
    cut = UPSCALE - 2
    upsampled = upsampled[cut:-cut, cut:-cut]
    row_ids = my_row * tile_rows - 2 + jnp.arange(tile_rows + 4)
    col_ids = my_col * tile_cols - 2 + jnp.arange(tile_cols + 4)
    inside = (
        ((row_ids >= 0) & (row_ids < tile_rows * row_devices))[:, None]
        & ((col_ids >= 0) & (col_ids < tile_cols * col_devices))[None, :]
    )[:, :, None]
    mixed = jnp.where(inside, input_padded.astype(jnp.float32) + upsampled, 0.0).astype(
        jnp.bfloat16
    )
    near_rows, near_cols = tile_rows + 2, tile_cols + 2
    inside = inside[1:-1, 1:-1]
    first_act = conv_taps(mixed, enhancer_first, near_rows, near_cols).reshape(
        near_rows, near_cols, local_width
    )
    pixel_total = tile_rows * tile_cols * devices
    own_act = first_act[1:-1, 1:-1]
    act_sums = jnp.stack([jnp.sum(own_act, (0, 1)), jnp.sum(own_act * own_act, (0, 1))])
    act_sums = jnp.sum(lax.all_gather(act_sums, BOTH, axis=0), 0)
    act_mean = act_sums[0] / pixel_total
    inverse_dev = lax.rsqrt(act_sums[1] / pixel_total - act_mean * act_mean + norm_eps)
    normed_act = (first_act - act_mean) * inverse_dev
    activated = jnp.where(inside, jax.nn.silu(normed_act), 0.0).astype(jnp.bfloat16)
    second_act = conv_taps(activated, enhancer_second, tile_rows, tile_cols)
    own_mixed = mixed[2:-2, 2:-2]
    enhanced = (
        (own_mixed.astype(jnp.float32).reshape(-1, local_width) + second_act)
        .astype(jnp.bfloat16)
        .reshape(tile_rows, tile_cols, local_width)
    )
    second_local = weight_taps(activated, output_cotangent, tile_rows, tile_cols)
    act_grad = back_taps(cotangent_padded, enhancer_second, near_rows, near_cols).reshape(
        near_rows, near_cols, local_width
    )
    gate_value = jax.nn.sigmoid(normed_act)
    normed_grad = act_grad * gate_value * (1.0 + normed_act * (1.0 - gate_value))
    own_grad = normed_grad[1:-1, 1:-1]
    grad_sums = jnp.stack(
        [jnp.sum(own_grad, (0, 1)), jnp.sum(own_grad * normed_act[1:-1, 1:-1], (0, 1))]
    )
    grad_sums = jnp.sum(
        lax.all_to_all(
            jnp.broadcast_to(grad_sums, (devices, 2, local_width)), BOTH, 0, 0
        ),
        0,
    )
    first_grad = jnp.where(
        inside,
        inverse_dev
        * (normed_grad - grad_sums[0] / pixel_total - normed_act * (grad_sums[1] / pixel_total)),
        0.0,
    ).astype(jnp.bfloat16)
    first_local = weight_taps(mixed[1:-1, 1:-1], first_grad[1:-1, 1:-1], tile_rows, tile_cols)
    windows = []
    for tap_row in range(3):
        for tap_col in range(3):
            window = first_grad[
                2 - tap_row : 2 - tap_row + tile_rows, 2 - tap_col : 2 - tap_col + tile_cols
            ].astype(jnp.float32)
            windows.append(
                window.reshape(block_rows, UPSCALE, block_cols, UPSCALE, local_width)
                .sum(axis=(1, 3))
                .reshape(blocks, local_width)
            )
    cot_blocks = (
        output_cotangent.astype(jnp.float32)
        .reshape(block_rows, UPSCALE, block_cols, UPSCALE, local_width)
        .sum(axis=(1, 3))
    )
    turned = jnp.swapaxes(enhancer_first, 2, 3).reshape(-1, local_width)
    spread = jnp.dot(
        jnp.concatenate(windows, 1), turned.astype(jnp.float32), precision=lax.Precision.HIGHEST
    )
    global_gradient = (
        cot_blocks + spread.reshape(block_rows, block_cols, local_width)
    ) / UPSCALE

    rescale = 1.0 / math.sqrt(pixel_total)
    locals_both = jnp.concatenate([first_local, second_local]).astype(jnp.bfloat16)
    share = locals_both.shape[0] // devices
    received = lax.all_to_all(
        locals_both.reshape(devices, share, local_width), BOTH, 0, 0
    )
    summed = jnp.sum(received.astype(jnp.float32), 0) * rescale
    totals = lax.all_gather(summed.astype(jnp.bfloat16), BOTH, axis=0, tiled=True).astype(
        jnp.float32
    )
    totals = totals.reshape(2, 3, 3, local_width, local_width)
    return (enhanced, totals[0], totals[1], global_gradient)


def solution(mesh):
    return jax.shard_map(
        per_device,
        mesh=mesh,
        in_specs=(
            P("rows", None, "cols"),
            P(None, None, None, "cols"),
            P(None, None, None, "cols"),
            P(),
            P("rows", "cols", None),
            P("rows", "cols"),
            P(None, "rows", "cols"),
            P(),
            P(),
            P(),
            P("rows", "cols", None),
        ),
        out_specs=(P("rows", "cols", None), P(), P(), P("rows", "cols", None)),
        check_vma=False,
    )
```

time: 442 us -> 300 us (0.68)
  waiting for transfers between devices: 134 us -> 16.9 us
  local copies, waits for them, and re-layouts: 11.9 us -> 77 us
  blocking collectives: 178 us -> 134 us
  starting transfers between devices: 43.6 us -> 14.3 us
  between operations: 15.9 us -> 1.63 us
  other arithmetic: 12.6 us -> 7.25 us
    psum x4 -> x0, blocking collectives: 133 us -> none  [the longest x1 41.8 us: per_device(): lax.psum((jnp.sum(first_act, 0), jnp.sum(first_act * first_act, 0)), ('ro...]
    psum x1 -> x0, waiting for transfers between devices: 128 us -> none  [per_device(): lax.psum((first_local, second_local), ('rows', 'cols'))]
    all_gather x2 -> x4, blocking collectives: 22.7 us -> 134 us  [the longest x1 45 us: per_device(): everything = lax.all_gather(packed, BOTH, axis=0)]
    ppermute x20 -> x4, starting transfers between devices: 43.6 us -> 5.53 us  [the longest x2 2.76 us: halo_2(): after = lax.ppermute(initial, axis, down)]
    reshape x0 -> x28, local copies, waits for them, and re-layouts: none -> 36 us  [the longest x9 16.2 us: conv_taps(): window.reshape(row_count * col_count, window.shape[2])]
    unnamed x1 -> x0, blocking collectives: 22.4 us -> none
    unnamed x76 -> x100, local copies, waits for them, and re-layouts: 3.72 us -> 21.1 us
    dot_general x36 -> x35, matrix products: 17.2 us -> 31 us  [conv_taps(): jnp.dot(window.reshape(row_count * col_count, window.shape[2]), weight[ta...]
  transfers between devices with their start and end apart: 21 -> 7, of which waited for: 4 -> 4; matrix products, arithmetic and copies ran while one was open for 7% -> 4% of each run, Pallas kernels for 0% -> 0%
where the time goes in v1:
time: 300 us; the launch traced here: 298 us
  blocking collectives  134 us (45%)
  local copies, waits for them, and re-layouts  77 us (26%)
  matrix products  47 us (16%)
  waiting for transfers between devices  16.9 us (6%)
  starting transfers between devices  14.3 us (5%)
  other arithmetic  7.25 us (2%)
    all_gather x1, blocking collectives, per_device(): everything = lax.all_gather(packed, BOTH, axis=0)  45 us
    all_gather x1, blocking collectives, per_device(): lax.all_gather(summed.astype(jnp.bfloat16), BOTH, axis=0, tiled=True)  40.9 us
    all_gather x1, blocking collectives, per_device(): act_sums = jnp.sum(lax.all_gather(act_sums, BOTH, axis=0), 0)  39.2 us
    dot_general x35, matrix products, conv_taps(): jnp.dot(window.reshape(row_count * col_count, window.shape[2]), weight[ta...  31 us
    unnamed x100, local copies, waits for them, and re-layouts  21.1 us
    reshape x9, local copies, waits for them, and re-layouts, conv_taps(): window.reshape(row_count * col_count, window.shape[2])  16.2 us
    reshape x9, local copies, waits for them, and re-layouts, back_taps(): window.reshape(row_count * col_count, window.shape[2])  15.3 us
    all_gather x1, blocking collectives, per_device(): near_hidden = lax.all_gather(near_hidden, 'cols', axis=2, tiled=True)  8.49 us
  transfers between devices with their start and end apart: 7, of which 4 were waited for; matrix products, arithmetic and copies ran while one was open for 4% of the time, Pallas kernels for 0%

profile of v1, /device:TPU:0, one launch (start us, length us, event | category | flops | bytes accessed | tf_op | source)
XLA Modules:
  0.0 297.7 jit_solution(9575846571176483737)
XLA Ops:
  0.7 1.4 reshape.461
  2.8 45.0 %all-gather = bf16[2560,128]{1,0:T(8,128)(2,1)S(1)} all-gather(bf16[80,128]{1,0:T(8,128)(2,1)S(1)} %pad_maximum_fusion.7), channel_id=2, replica_groups=mesh['rows'=4,'cols'=8] {'rows','cols'}, dimensions={0}, use_global_device_ids=true | all-gather | bytes 675840 | tf_op jit(solution)/shard_map/all_gather | solution.py:112
  50.0 5.0 %pad_slice_fusion = (bf16[8,32,1024]{2,1,0:T(8,128)(2,1)S(1)}, bf16[8,32,1024]{2,1,0:T(8,128)(2,1)}, bf16[8,32,1024]{2,1,0:T(8,128)(2,1)}, bf16[8,32,1024]{2,1,0...) fusion(bf16[8,32,1024]{2,1,0:T(8,128)(2,1)} %reshape.468), kind=kLoop, calls=%fused_computation.36 | loop fusion | bytes 4718592 | tf_op jit(solution)/shard_map/slice | solution.py:30
  55.0 1.3 fusion.74
  56.3 1.4 convolution_add_fusion.31
  57.8 1.3 convolution_add_fusion.30
  59.1 1.3 convolution_add_fusion.29
  60.4 1.2 convolution_add_fusion.28
  61.6 1.2 convolution_add_fusion.27
  62.9 1.2 convolution_add_fusion.26
  64.1 1.2 convolution_add_fusion.25
  65.4 1.3 fusion.191
  66.7 8.5 %all_gather.20 = bf16[6,32,1024]{2,1,0:T(8,128)(2,1)S(1)} all-gather(bf16[6,32,128]{2,1,0:T(8,128)(2,1)S(1)} %pad_dynamic-slice_fusion), channel_id=1, replica_groups=mesh['rows'=4,'cols'=8] {'cols'}, dimensions={2}, use_global_device_ids=true | all-gather | bytes 442368 | tf_op jit(solution)/shard_map/all_gather | solution.py:164
  76.2 1.2 fusion.64
  77.5 1.2 convolution_add_fusion.39
  78.6 1.2 convolution_add_fusion.38
  79.8 1.2 convolution_add_fusion.37
  81.0 1.2 convolution_add_fusion.36
  82.2 1.2 convolution_add_fusion.35
  83.3 1.2 convolution_add_fusion.34
  84.5 1.3 convolution_add_fusion.33
  85.9 1.3 fusion.42
  92.0 3.4 %all-to-all-start = ((f32[8,4,6,128]{3,1,2,0:T(4,128)}), f32[8,4,6,128]{3,1,2,0:T(4,128)S(1)}, u32[]{:S(2)}, u32[]{:S(2)}) async-start(f32[8,4,6,128]{3,1,2,0:T(4,128)} %constant_dynamic-update-slice_fusion), calls=%async_computation | async-start | bytes 196608 | tf_op jit(solution)/shard_map/all_to_all | solution.py:184
  95.4 1.3 collective-permute-start
  96.7 1.3 collective-permute-start.1
  100.4 2.6 collective-permute-done.1
  103.1 1.5 collective-permute-start.2
  104.6 1.5 collective-permute-start.3
  106.1 3.4 %collective-permute-done.3 = bf16[2,36,2,128]{3,2,1,0:T(2,128)(2,1)S(1)} collective-permute-done((bf16[2,36,2,128]{3,2,1,0:T(2,128)(2,1)S(1)}, bf16[2,36,2,128]{3,2,1,0:T(2,128)(2,1)S(1)}, u32[]{:S(2)}, u32[]{:S(2)}) %collective-permute-start.3) | collective-permute-done | bytes 36896 | tf_op jit(solution)/shard_map/ppermute | solution.py:22
  109.5 1.5 pad_maximum_fusion
  111.9 2.3 fusion.192
  114.2 2.0 reshape.499
  116.2 2.0 reshape.500
  118.2 2.0 reshape.501
  120.2 2.0 reshape.502
  122.3 2.0 reshape.503
  124.3 2.1 reshape.504
  126.4 2.0 reshape.505
  130.4 1.3 fusion.124
  139.1 1.5 convolution_add_fusion.8
  140.6 1.4 reshape.508
  142.3 39.2 %all-gather.2 = f32[32,2,128]{2,1,0:T(2,128)S(1)} all-gather(f32[1,2,128]{2,1,0:T(2,128)S(1)} %maximum_bitcast_fusion), channel_id=3, replica_groups=mesh['rows'=4,'cols'=8] {'rows','cols'}, dimensions={0}, use_global_device_ids=true | all-gather | bytes 33792 | tf_op jit(solution)/shard_map/all_gather | solution.py:208
  181.6 2.3 fusion.193
  183.9 2.0 reshape.519
  185.9 2.0 reshape.520
  187.9 2.0 reshape.521
  190.0 2.0 reshape.522
  192.0 2.0 reshape.523
  194.0 2.1 reshape.524
  196.1 2.0 reshape.525
  199.3 1.6 fusion.112
  207.7 1.5 convolution_add_fusion
  209.2 1.4 reshape.528
  213.1 2.8 all-to-all-start.1
  216.0 1.1 convert_reduce_fusion.10
  217.1 1.8 copy.104
  219.9 3.0 %all-to-all-done.1 = f32[32,2,128]{2,1,0:T(2,128)S(1)} async-done(((f32[32,2,128]{2,1,0:T(2,128)}), f32[32,2,128]{2,1,0:T(2,128)S(1)}, u32[]{:S(2)}, u32[]{:S(2)}) %all-to-all-start.1) | async-done | bytes 32800 | tf_op jit(solution)/shard_map/all_to_all | solution.py:231
  224.4 2.8 fusion.194
  236.2 2.6 all-to-all-start.2
  238.9 1.1 fusion.114
  246.6 1.1 fusion.1
  247.7 7.8 %all-to-all-done.2 = bf16[32,72,128]{2,1,0:T(8,128)(2,1)S(1)} async-done(((bf16[32,72,128]{2,1,0:T(8,128)(2,1)}), bf16[32,72,128]{2,1,0:T(8,128)(2,1)S(1)}, u32[]{:S(2)}, u32[]{:S(2)}) %all-to-all-start.2) | async-done | bytes 589856 | tf_op jit(solution)/shard_map/all_to_all | solution.py:270
  255.7 40.9 %all_gather.23 = bf16[2304,128]{1,0:T(8,128)(2,1)S(1)} all-gather(bf16[72,128]{1,0:T(8,128)(2,1)S(1)} %multiply_convert_fusion), channel_id=1, replica_groups=mesh['rows'=4,'cols'=8] {'rows','cols'}, dimensions={0}, use_global_device_ids=true | all-gather | bytes 608256 | tf_op jit(solution)/shard_map/all_gather | solution.py:274
  296.6 1.1 fusion.196
  (222 shorter events, 50.5 us)
Async XLA Ops:
  0.6 85.2 %copy-start = (bf16[1024,128]{1,0:T(8,128)(2,1)S(1)}, bf16[1024,128]{1,0:T(8,128)(2,1)}, u32[]{:S(2)}) copy-start(bf16[1024,128]{1,0:T(8,128)(2,1)} %param.14) | copy-start | bytes 786436
  0.6 1.9 copy-start.39
  0.7 2.1 copy-start.40
  48.2 0.8 copy-start.30
  55.0 2.8 copy-start.25
  56.3 2.8 copy-start.24
  57.7 2.6 copy-start.31
  59.1 2.6 copy-start.23
  84.5 10.9 %copy-start.4 = (bf16[32,64,128]{2,1,0:T(8,128)(2,1)S(1)}, bf16[32,64,128]{2,1,0:T(8,128)(2,1)}, u32[]{:S(2)}) copy-start(bf16[32,64,128]{2,1,0:T(8,128)(2,1)} %param.21) | copy-start | bytes 1572868
  84.5 10.9 %copy-start.6 = (bf16[32,64,128]{2,1,0:T(8,128)(2,1)S(1)}, bf16[32,64,128]{2,1,0:T(8,128)(2,1)}, u32[]{:S(2)}) copy-start(bf16[32,64,128]{2,1,0:T(8,128)(2,1)} %param.15) | copy-start | bytes 1572868
  92.0 14.0 %all-to-all-start = ((f32[8,4,6,128]{3,1,2,0:T(4,128)}), f32[8,4,6,128]{3,1,2,0:T(4,128)S(1)}, u32[]{:S(2)}, u32[]{:S(2)}) async-start(f32[8,4,6,128]{3,1,2,0:T(4,128)} %constant_dynamic-update-slice_fusion), calls=%async_computation | async-start | bytes 196608 | tf_op jit(solution)/shard_map/all_to_all | solution.py:184
  95.4 4.7 %copy-start.41 = (f32[16,128]{1,0:T(8,128)S(1)}, f32[16,128]{1,0:T(8,128)}, u32[]{:S(2)}) copy-start(f32[16,128]{1,0:T(8,128)} %param.18) | copy-start | bytes 24580
  95.4 5.0 %collective-permute-start = (bf16[2,2,64,128]{3,2,1,0:T(8,128)(2,1)S(1)}, bf16[2,2,64,128]{3,2,1,0:T(8,128)(2,1)S(1)}, u32[]{:S(2)}, u32[]{:S(2)}) collective-permute-start(bf16[2,2,64,128]{3,2,1,0:T(8,128)(2,1)S(1)} %get-tuple-element.16), channel_id=1, source_target_pairs={{0,8},{8,16},{16,24},{1,9},{9,17},{17,25},{2,10},{10,18},{18,26},{... | collective-permute-start | bytes 196616 | tf_op jit(solution)/shard_map/ppermute | solution.py:21
  96.7 6.3 %collective-permute-start.1 = (bf16[2,2,64,128]{3,2,1,0:T(8,128)(2,1)S(1)}, bf16[2,2,64,128]{3,2,1,0:T(8,128)(2,1)S(1)}, u32[]{:S(2)}, u32[]{:S(2)}) collective-permute-start(bf16[2,2,64,128]{3,2,1,0:T(8,128)(2,1)S(1)} %get-tuple-element.17), channel_id=1, source_target_pairs={{8,0},{16,8},{24,16},{9,1},{17,9},{25,17},{10,2},{18,10},{26,18},{... | collective-permute-start | bytes 196616 | tf_op jit(solution)/shard_map/ppermute | solution.py:22
  103.0 3.1 %copy-start.38 = (bf16[2,2,64,128]{3,2,1,0:T(8,128)(2,1)}, bf16[2,2,64,128]{3,2,1,0:T(8,128)(2,1)S(1)}, u32[]{:S(2)}) copy-start(bf16[2,2,64,128]{3,2,1,0:T(8,128)(2,1)S(1)} %collective-permute-done.1) | copy-start | bytes 196612
  103.1 3.0 %collective-permute-start.2 = (bf16[2,36,2,128]{3,2,1,0:T(2,128)(2,1)S(1)}, bf16[2,36,2,128]{3,2,1,0:T(2,128)(2,1)S(1)}, u32[]{:S(2)}, u32[]{:S(2)}) collective-permute-start(bf16[2,36,2,128]{3,2,1,0:T(2,128)(2,1)S(1)} %get-tuple-element.14), channel_id=1, source_target_pairs={{0,1},{1,2},{2,3},{3,4},{4,5},{5,6},{6,7},{8,9},{9,10},{10,11},{11... | collective-permute-start | bytes 110600 | tf_op jit(solution)/shard_map/ppermute | solution.py:21
  104.6 5.0 %collective-permute-start.3 = (bf16[2,36,2,128]{3,2,1,0:T(2,128)(2,1)S(1)}, bf16[2,36,2,128]{3,2,1,0:T(2,128)(2,1)S(1)}, u32[]{:S(2)}, u32[]{:S(2)}) collective-permute-start(bf16[2,36,2,128]{3,2,1,0:T(2,128)(2,1)S(1)} %get-tuple-element.15), channel_id=1, source_target_pairs={{1,0},{2,1},{3,2},{4,3},{5,4},{6,5},{7,6},{9,8},{10,9},{11,10},{12... | collective-permute-start | bytes 110600 | tf_op jit(solution)/shard_map/ppermute | solution.py:22
  129.4 1.1 copy-start.22
  130.4 1.3 copy-start.20
  130.4 1.3 copy-start.33
  131.7 1.1 copy-start.18
  132.8 1.1 copy-start.16
  133.8 1.1 copy-start.14
  134.9 1.1 copy-start.12
  136.0 1.1 copy-start.10
  137.0 1.1 copy-start.7
  138.1 1.1 copy-start.8
  199.2 1.6 copy-start.21
  199.3 1.6 copy-start.34
  200.9 1.1 copy-start.19
  201.9 1.1 copy-start.17
  203.0 1.1 copy-start.15
  204.1 1.1 copy-start.13
  205.1 1.1 copy-start.11
  206.2 1.1 copy-start.9
  211.0 1.0 copy-start.2
  212.5 10.5 %copy-start.3 = (f32[34,66,128]{2,1,0:T(8,128)S(1)}, f32[34,66,128]{2,1,0:T(8,128)}, u32[]{:S(2)}) copy-start(f32[34,66,128]{2,1,0:T(8,128)} %copy-done.2) | copy-start | bytes 3446788
  213.1 9.8 %all-to-all-start.1 = ((f32[32,2,128]{2,1,0:T(2,128)}), f32[32,2,128]{2,1,0:T(2,128)S(1)}, u32[]{:S(2)}, u32[]{:S(2)}) async-start(f32[32,2,128]{2,1,0:T(2,128)} %broadcast_in_dim.57), calls=%async_computation.1 | async-start | bytes 65536 | tf_op jit(solution)/shard_map/all_to_all | solution.py:231
  231.0 1.0 copy-start.5
  235.4 0.8 copy-start.37
  236.2 19.4 %all-to-all-start.2 = ((bf16[32,72,128]{2,1,0:T(8,128)(2,1)}), bf16[32,72,128]{2,1,0:T(8,128)(2,1)S(1)}, u32[]{:S(2)}, u32[]{:S(2)}) async-start(bf16[32,72,128]{2,1,0:T(8,128)(2,1)} %bitcast.502), calls=%async_computation.2 | async-start | bytes 1179648 | tf_op jit(solution)/shard_map/all_to_all | solution.py:270
  238.8 1.2 copy-start.29
  238.8 1.2 copy-start.35
  240.1 1.0 copy-start.28
  241.1 1.0 copy-start.27
  242.2 1.0 copy-start.26
  243.2 1.0 copy-start.36
  245.6 1.0 copy-start.32
  255.7 42.0 %copy-start.1 = (bf16[1024,128]{1,0:T(8,128)(2,1)S(1)}, bf16[1024,128]{1,0:T(8,128)(2,1)}, u32[]{:S(2)}) copy-start(bf16[1024,128]{1,0:T(8,128)(2,1)} %param.14) | copy-start | bytes 786436

commit v2 on v1

--- a/solution.py
+++ b/solution.py
@@ -10,6 +10,11 @@
 BOTH = ("rows", "cols")
 
 norm_eps = 1e-05
+
+
+def spread_to(array, axis):
+    devices = lax.axis_size(axis)
+    return lax.all_to_all(jnp.broadcast_to(array, (devices, *array.shape)), axis, 0, 0)
 
 
 def halo_2(array, axis, dim, width):
@@ -109,7 +114,7 @@
     extra_rows = -(-extra.shape[0] // 2048) * 16
     extra = jnp.pad(extra, (0, extra_rows * 128 - extra.shape[0])).reshape(extra_rows, 128)
     packed = jnp.concatenate([global_in.reshape(-1, 128), extra])
-    everything = lax.all_gather(packed, BOTH, axis=0)
+    everything = spread_to(packed, BOTH)
     main_rows = packed.shape[0] - extra_rows
     gathered = everything[:, :main_rows].reshape(
         row_devices, col_devices, band_rows, band_cols, width_share
@@ -161,7 +166,8 @@
     )
     hidden = jnp.pad(hidden, ((2, 2), (0, 0), (0, 0)))
     near_hidden = lax.dynamic_slice_in_dim(hidden, my_row * band_rows, band_rows + 4, 0)
-    near_hidden = lax.all_gather(near_hidden, "cols", axis=2, tiled=True)
+    near_hidden = spread_to(near_hidden, "cols")
+    near_hidden = near_hidden.transpose(1, 2, 0, 3).reshape(band_rows + 4, band_cols, -1)
     second_raw = conv_taps(
         jnp.pad(near_hidden, ((0, 0), (1, 1), (0, 0))), global_second, band_rows + 2, band_cols
     )
@@ -205,7 +211,7 @@
     pixel_total = tile_rows * tile_cols * devices
     own_act = first_act[1:-1, 1:-1]
     act_sums = jnp.stack([jnp.sum(own_act, (0, 1)), jnp.sum(own_act * own_act, (0, 1))])
-    act_sums = jnp.sum(lax.all_gather(act_sums, BOTH, axis=0), 0)
+    act_sums = jnp.sum(spread_to(act_sums, BOTH), 0)
     act_mean = act_sums[0] / pixel_total
     inverse_dev = lax.rsqrt(act_sums[1] / pixel_total - act_mean * act_mean + norm_eps)
     normed_act = (first_act - act_mean) * inverse_dev
@@ -227,12 +233,7 @@
     grad_sums = jnp.stack(
         [jnp.sum(own_grad, (0, 1)), jnp.sum(own_grad * normed_act[1:-1, 1:-1], (0, 1))]
     )
-    grad_sums = jnp.sum(
-        lax.all_to_all(
-            jnp.broadcast_to(grad_sums, (devices, 2, local_width)), BOTH, 0, 0
-        ),
-        0,
-    )
+    grad_sums = jnp.sum(spread_to(grad_sums, BOTH), 0)
     first_grad = jnp.where(
         inside,
         inverse_dev
@@ -271,9 +272,7 @@
         locals_both.reshape(devices, share, local_width), BOTH, 0, 0
     )
     summed = jnp.sum(received.astype(jnp.float32), 0) * rescale
-    totals = lax.all_gather(summed.astype(jnp.bfloat16), BOTH, axis=0, tiled=True).astype(
-        jnp.float32
-    )
+    totals = spread_to(summed.astype(jnp.bfloat16), BOTH).astype(jnp.float32)
     totals = totals.reshape(2, 3, 3, local_width, local_width)
     return (enhanced, totals[0], totals[1], global_gradient)
 

time: 300 us -> 211 us (0.70)
  blocking collectives: 134 us -> 0 us
  waiting for transfers between devices: 16.9 us -> 54.1 us
  starting transfers between devices: 14.3 us -> 40.6 us
  local copies, waits for them, and re-layouts: 77 us -> 67.7 us
  matrix products: 47 us -> 38.7 us
    all_gather x4 -> x0, blocking collectives: 134 us -> none  [the longest x1 45 us: per_device(): everything = lax.all_gather(packed, BOTH, axis=0)]
    all_to_all x1 -> x5, starting transfers between devices: 2.83 us -> 26.5 us  [spread_to(): lax.all_to_all(jnp.broadcast_to(array, (devices, *array.shape)), axis, 0, 0)]
    all_to_all x1 -> x5, waiting for transfers between devices: 3.01 us -> 26.6 us  [spread_to(): lax.all_to_all(jnp.broadcast_to(array, (devices, *array.shape)), axis, 0, 0)]
    dot_general x35, matrix products: 31 us -> 14.9 us  [conv_taps(): jnp.dot(window.reshape(row_count * col_count, window.shape[2]), weight[ta...]
    dot_general x9, matrix products: 6.24 us -> 14.2 us  [back_taps(): jnp.dot(window.reshape(row_count * col_count, window.shape[2]), weight[ta...]
    ppermute x2, waiting for transfers between devices: 0.02 us -> 7.39 us  [halo_2(): before = lax.ppermute(last, axis, up)]
    all_to_all x1, waiting for transfers between devices: 0.01 us -> 4.9 us  [per_device(): incoming = lax.all_to_all(outgoing, 'cols', 0, 0)]
    slice x3 -> x7, local copies, waits for them, and re-layouts: 8.27 us -> 3.39 us  [conv_taps(): window = padded[tap_row:tap_row + row_count, tap_col:tap_col + col_count]]
  transfers between devices with their start and end apart: 7 -> 11, of which waited for: 4 -> 8; matrix products, arithmetic and copies ran while one was open for 4% -> 22% of each run, Pallas kernels for 0% -> 0%
where the time goes in v2:
time: 211 us; the launch traced here: 209 us
  local copies, waits for them, and re-layouts  67.7 us (32%)
  waiting for transfers between devices  54.1 us (26%)
  starting transfers between devices  40.6 us (19%)
  matrix products  38.7 us (18%)
  other arithmetic  6.45 us (3%)
    all_to_all x5, waiting for transfers between devices, spread_to(): lax.all_to_all(jnp.broadcast_to(array, (devices, *array.shape)), axis, 0, 0)  26.6 us
    all_to_all x5, starting transfers between devices, spread_to(): lax.all_to_all(jnp.broadcast_to(array, (devices, *array.shape)), axis, 0, 0)  26.5 us
    unnamed x88, local copies, waits for them, and re-layouts  17.5 us
    reshape x9, local copies, waits for them, and re-layouts, back_taps(): window.reshape(row_count * col_count, window.shape[2])  16.1 us
    dot_general x35, matrix products, conv_taps(): jnp.dot(window.reshape(row_count * col_count, window.shape[2]), weight[ta...  14.9 us
    dot_general x9, matrix products, back_taps(): jnp.dot(window.reshape(row_count * col_count, window.shape[2]), weight[ta...  14.2 us
    all_to_all x1, waiting for transfers between devices, per_device(): lax.all_to_all(locals_both.reshape(devices, share, local_width), BOTH, 0, 0)  12.1 us
    reshape x9, local copies, waits for them, and re-layouts, conv_taps(): window.reshape(row_count * col_count, window.shape[2])  11.6 us
  transfers between devices with their start and end apart: 11, of which 8 were waited for; matrix products, arithmetic and copies ran while one was open for 22% of the time, Pallas kernels for 0%

profile of v2, /device:TPU:0, one launch (start us, length us, event | category | flops | bytes accessed | tf_op | source)
XLA Modules:
  0.0 209.2 jit_solution(5427172536042966883)
XLA Ops:
  0.7 1.4 reshape.470
  2.8 1.0 broadcast_in_dim.63
  3.7 7.3 %all-to-all-start = ((bf16[32,80,128]{2,1,0:T(8,128)(2,1)}), bf16[32,80,128]{2,1,0:T(8,128)(2,1)S(1)}, u32[]{:S(2)}, u32[]{:S(2)}) async-start(bf16[32,80,128]{2,1,0:T(8,128)(2,1)} %broadcast_in_dim.63), calls=%async_computation | async-start | bytes 1310720 | tf_op jit(solution)/shard_map/all_to_all | solution.py:17
  11.1 3.7 %collective-permute-start = (bf16[2,2,64,128]{3,2,1,0:T(8,128)(2,1)S(1)}, bf16[2,2,64,128]{3,2,1,0:T(8,128)(2,1)S(1)}, u32[]{:S(2)}, u32[]{:S(2)}) collective-permute-start(bf16[2,2,64,128]{3,2,1,0:T(8,128)(2,1)S(1)} %get-tuple-element.16), channel_id=1, source_target_pairs={{0,8},{8,16},{16,24},{1,9},{9,17},{17,25},{2,10},{10,18},{18,26},{... | collective-permute-start | bytes 196616 | tf_op jit(solution)/shard_map/ppermute | solution.py:26
  14.8 1.3 collective-permute-start.1
  16.3 7.4 %collective-permute-done = bf16[2,2,64,128]{3,2,1,0:T(8,128)(2,1)S(1)} collective-permute-done((bf16[2,2,64,128]{3,2,1,0:T(8,128)(2,1)S(1)}, bf16[2,2,64,128]{3,2,1,0:T(8,128)(2,1)S(1)}, u32[]{:S(2)}, u32[]{:S(2)}) %collective-permute-start) | collective-permute-done | bytes 65568 | tf_op jit(solution)/shard_map/ppermute | solution.py:26
  23.8 1.7 collective-permute-start.2
  25.5 1.3 collective-permute-start.3
  26.9 3.2 %collective-permute-done.3 = bf16[2,36,2,128]{3,2,1,0:T(2,128)(2,1)S(1)} collective-permute-done((bf16[2,36,2,128]{3,2,1,0:T(2,128)(2,1)S(1)}, bf16[2,36,2,128]{3,2,1,0:T(2,128)(2,1)S(1)}, u32[]{:S(2)}, u32[]{:S(2)}) %collective-permute-start.3) | collective-permute-done | bytes 36896 | tf_op jit(solution)/shard_map/ppermute | solution.py:27
  30.8 2.3 %fusion.199 = (bf16[34,66,128]{2,1,0:T(8,128)(2,1)}, bf16[34,66,128]{2,1,0:T(8,128)(2,1)}, bf16[34,66,128]{2,1,0:T(8,128)(2,1)}, bf16[34,66,128]{2,1,0:T(8,128)(...) fusion(bf16[36,68,128]{2,1,0:T(8,128)(2,1)S(1)} %slice_bitcast_, ...), kind=kLoop, calls=%fused_computation.354 | loop fusion | bytes 10340352 | tf_op jit(solution)/shard_map/slice | solution.py:48
  33.1 2.0 reshape.529
  35.1 2.0 reshape.530
  37.1 1.0 reshape.531
  38.1 1.0 reshape.532
  39.1 1.5 fusion.118
  40.6 1.3 convolution_add_fusion.7
  41.9 1.3 convolution_add_fusion.6
  43.2 1.2 convolution_add_fusion.5
  44.4 2.0 reshape.533
  46.4 2.0 reshape.534
  48.5 2.0 reshape.535
  50.5 2.1 reshape.536
  52.5 2.0 reshape.537
  54.6 1.6 convolution_add_fusion.4
  56.2 1.3 convolution_add_fusion.3
  57.5 1.3 convolution_add_fusion.2
  58.8 2.2 %convolution_add_fusion.1 = f32[2244,128]{1,0:T(8,128)} fusion(f32[2244,128]{1,0:T(8,128)S(1)} %convolution_add_fusion.2, bf16[2244,128]{1,0:T(8,128)(2,1)S(1)} %copy-done.13, bf16[3,3,128,128]{3,2,1,0:T(8,128)(2,1)} %param.20), kind=kOutput, calls=%fused_computation.1 | convolution fusion | flops 73818624 | bytes 2905088 | tf_op jit(solution)/shard_map/dot_general | solution.py:51
  63.8 1.1 copy-done.27
  68.9 5.9 %all-to-all-start.1 = ((bf16[8,6,32,128]{3,2,1,0:T(8,128)(2,1)}), bf16[8,6,32,128]{3,2,1,0:T(8,128)(2,1)S(1)}, u32[]{:S(2)}, u32[]{:S(2)}) async-start(bf16[8,6,32,128]{3,2,1,0:T(8,128)(2,1)} %broadcast_in_dim.64), calls=%async_computation.1 | async-start | bytes 786432 | tf_op jit(solution)/shard_map/all_to_all | solution.py:17
  75.9 7.3 %all-to-all-done.1 = bf16[8,6,32,128]{3,2,1,0:T(8,128)(2,1)S(1)} async-done(((bf16[8,6,32,128]{3,2,1,0:T(8,128)(2,1)}), bf16[8,6,32,128]{3,2,1,0:T(8,128)(2,1)S(1)}, u32[]{:S(2)}, u32[]{:S(2)}) %all-to-all-start.1) | async-done | bytes 393248 | tf_op jit(solution)/shard_map/all_to_all | solution.py:17
  84.1 1.0 copy-done.31
  86.9 1.3 fusion.42
  93.1 3.4 %all-to-all-start.2 = ((f32[8,4,6,128]{3,1,2,0:T(4,128)}), f32[8,4,6,128]{3,1,2,0:T(4,128)S(1)}, u32[]{:S(2)}, u32[]{:S(2)}) async-start(f32[8,4,6,128]{3,1,2,0:T(4,128)} %constant_dynamic-update-slice_fusion), calls=%async_computation.2 | async-start | bytes 196608 | tf_op jit(solution)/shard_map/all_to_all | solution.py:190
  96.7 4.9 %all-to-all-done.2 = f32[8,4,6,128]{3,1,2,0:T(4,128)S(1)} async-done(((f32[8,4,6,128]{3,1,2,0:T(4,128)}), f32[8,4,6,128]{3,1,2,0:T(4,128)S(1)}, u32[]{:S(2)}, u32[]{:S(2)}) %all-to-all-start.2) | async-done | bytes 98336 | tf_op jit(solution)/shard_map/all_to_all | solution.py:190
  102.5 2.0 fusion.198
  104.5 2.0 reshape.509
  106.5 2.0 reshape.510
  108.6 2.0 reshape.511
  110.6 2.0 reshape.512
  112.6 2.0 reshape.513
  114.7 1.0 reshape.514
  116.2 1.6 fusion.130
  123.3 1.5 convolution_add_fusion.8
  124.8 1.5 reshape.518
  127.2 7.3 %all-to-all-start.3 = ((f32[32,2,128]{2,1,0:T(2,128)}), f32[32,2,128]{2,1,0:T(2,128)S(1)}, u32[]{:S(2)}, u32[]{:S(2)}) async-start(f32[32,2,128]{2,1,0:T(2,128)} %broadcast_in_dim.70), calls=%async_computation.3 | async-start | bytes 65536 | tf_op jit(solution)/shard_map/all_to_all | solution.py:17
  134.5 2.5 %convolution_add_fusion = f32[2244,128]{1,0:T(8,128)} fusion(f32[2244,128]{1,0:T(8,128)S(1)} %copy-done.7, bf16[2244,128]{1,0:T(8,128)(2,1)} %reshape.537, bf16[3,3,128,128]{3,2,1,0:T(8,128)(2,1)} %param.20), kind=kOutput, calls=%fused_computation | convolution fusion | flops 73818624 | bytes 2906112 | tf_op jit(solution)/shard_map/dot_general | solution.py:51
  137.1 1.4 reshape.538
  138.5 3.3 %all-to-all-done.3 = f32[32,2,128]{2,1,0:T(2,128)S(1)} async-done(((f32[32,2,128]{2,1,0:T(2,128)}), f32[32,2,128]{2,1,0:T(2,128)S(1)}, u32[]{:S(2)}, u32[]{:S(2)}) %all-to-all-start.3) | async-done | bytes 32800 | tf_op jit(solution)/shard_map/all_to_all | solution.py:17
  142.3 1.0 copy-done.2
  144.4 2.8 %all-to-all-start.4 = ((f32[32,2,128]{2,1,0:T(2,128)}), f32[32,2,128]{2,1,0:T(2,128)S(1)}, u32[]{:S(2)}, u32[]{:S(2)}) async-start(f32[32,2,128]{2,1,0:T(2,128)} %broadcast_in_dim.72), calls=%async_computation.4 | async-start | bytes 65536 | tf_op jit(solution)/shard_map/all_to_all | solution.py:17
  147.2 1.1 convert_reduce_fusion.10
  148.4 1.9 copy.120
  150.2 1.0 slice.583
  151.2 3.0 %all-to-all-done.4 = f32[32,2,128]{2,1,0:T(2,128)S(1)} async-done(((f32[32,2,128]{2,1,0:T(2,128)}), f32[32,2,128]{2,1,0:T(2,128)S(1)}, u32[]{:S(2)}, u32[]{:S(2)}) %all-to-all-start.4) | async-done | bytes 32800 | tf_op jit(solution)/shard_map/all_to_all | solution.py:17
  154.3 1.0 select_convert_fusion
  155.7 3.0 %fusion.200 = (bf16[32,64,128]{2,1,0:T(8,128)(2,1)S(1)}, bf16[32,64,128]{2,1,0:T(8,128)(2,1)S(1)}, bf16[32,64,128]{2,1,0:T(8,128)(2,1)S(1)}, bf16[32,64,128]{2,1...) fusion(bf16[34,66,128]{2,1,0:T(8,128)(2,1)S(1)} %get-tuple-elem, ...), kind=kLoop, calls=%fused_computation.355 | loop fusion | bytes 18874368 | tf_op jit(solution)/shard_map/slice | solution.py:247
  167.7 2.7 %all-to-all-start.5 = ((bf16[32,72,128]{2,1,0:T(8,128)(2,1)}), bf16[32,72,128]{2,1,0:T(8,128)(2,1)S(1)}, u32[]{:S(2)}, u32[]{:S(2)}) async-start(bf16[32,72,128]{2,1,0:T(8,128)(2,1)} %bitcast.510), calls=%async_computation.5 | async-start | bytes 1179648 | tf_op jit(solution)/shard_map/all_to_all | solution.py:271
  175.2 12.1 %all-to-all-done.5 = bf16[32,72,128]{2,1,0:T(8,128)(2,1)S(1)} async-done(((bf16[32,72,128]{2,1,0:T(8,128)(2,1)}), bf16[32,72,128]{2,1,0:T(8,128)(2,1)S(1)}, u32[]{:S(2)}, u32[]{:S(2)}) %all-to-all-start.5) | async-done | bytes 589856 | tf_op jit(solution)/shard_map/all_to_all | solution.py:271
  187.3 0.9 broadcast_in_dim.73
  188.2 3.2 %all-to-all-start.6 = ((bf16[32,72,128]{2,1,0:T(8,128)(2,1)}), bf16[32,72,128]{2,1,0:T(8,128)(2,1)S(1)}, u32[]{:S(2)}, u32[]{:S(2)}) async-start(bf16[32,72,128]{2,1,0:T(8,128)(2,1)} %broadcast_in_dim.73), calls=%async_computation.6 | async-start | bytes 1179648 | tf_op jit(solution)/shard_map/all_to_all | solution.py:17
  191.4 1.4 convolution_add_fusion.19
  194.2 1.1 fusion.1
  195.2 12.9 %all-to-all-done.6 = bf16[32,72,128]{2,1,0:T(8,128)(2,1)S(1)} async-done(((bf16[32,72,128]{2,1,0:T(8,128)(2,1)}), bf16[32,72,128]{2,1,0:T(8,128)(2,1)S(1)}, u32[]{:S(2)}, u32[]{:S(2)}) %all-to-all-start.6) | async-done | bytes 589856 | tf_op jit(solution)/shard_map/all_to_all | solution.py:17
  208.2 1.1 fusion.202
  (223 shorter events, 42.0 us)
Async XLA Ops:
  0.6 86.3 %copy-start = (bf16[1024,128]{1,0:T(8,128)(2,1)S(1)}, bf16[1024,128]{1,0:T(8,128)(2,1)}, u32[]{:S(2)}) copy-start(bf16[1024,128]{1,0:T(8,128)(2,1)} %param.14) | copy-start | bytes 786436
  0.6 1.9 copy-start.33
  0.7 2.1 %copy-start.34 = (bf16[2,32,128]{2,1,0:T(8,128)(2,1)S(1)}, bf16[2,32,128]{2,1,0:T(8,128)(2,1)}, u32[]{:S(2)}) copy-start(bf16[2,32,128]{2,1,0:T(8,128)(2,1)} %param.11) | copy-start | bytes 49156
  2.4 8.6 %copy-start.4 = (bf16[32,64,128]{2,1,0:T(8,128)(2,1)S(1)}, bf16[32,64,128]{2,1,0:T(8,128)(2,1)}, u32[]{:S(2)}) copy-start(bf16[32,64,128]{2,1,0:T(8,128)(2,1)} %param.21) | copy-start | bytes 1572868
  2.4 8.6 %copy-start.6 = (bf16[32,64,128]{2,1,0:T(8,128)(2,1)S(1)}, bf16[32,64,128]{2,1,0:T(8,128)(2,1)}, u32[]{:S(2)}) copy-start(bf16[32,64,128]{2,1,0:T(8,128)(2,1)} %param.15) | copy-start | bytes 1572868
  3.7 57.3 %all-to-all-start = ((bf16[32,80,128]{2,1,0:T(8,128)(2,1)}), bf16[32,80,128]{2,1,0:T(8,128)(2,1)S(1)}, u32[]{:S(2)}, u32[]{:S(2)}) async-start(bf16[32,80,128]{2,1,0:T(8,128)(2,1)} %broadcast_in_dim.63), calls=%async_computation | async-start | bytes 1310720 | tf_op jit(solution)/shard_map/all_to_all | solution.py:17
  11.1 12.6 %collective-permute-start = (bf16[2,2,64,128]{3,2,1,0:T(8,128)(2,1)S(1)}, bf16[2,2,64,128]{3,2,1,0:T(8,128)(2,1)S(1)}, u32[]{:S(2)}, u32[]{:S(2)}) collective-permute-start(bf16[2,2,64,128]{3,2,1,0:T(8,128)(2,1)S(1)} %get-tuple-element.16), channel_id=1, source_target_pairs={{0,8},{8,16},{16,24},{1,9},{9,17},{17,25},{2,10},{10,18},{18,26},{... | collective-permute-start | bytes 196616 | tf_op jit(solution)/shard_map/ppermute | solution.py:26
  14.8 9.0 %collective-permute-start.1 = (bf16[2,2,64,128]{3,2,1,0:T(8,128)(2,1)S(1)}, bf16[2,2,64,128]{3,2,1,0:T(8,128)(2,1)S(1)}, u32[]{:S(2)}, u32[]{:S(2)}) collective-permute-start(bf16[2,2,64,128]{3,2,1,0:T(8,128)(2,1)S(1)} %get-tuple-element.17), channel_id=1, source_target_pairs={{8,0},{16,8},{24,16},{9,1},{17,9},{25,17},{10,2},{18,10},{26,18},{... | collective-permute-start | bytes 196616 | tf_op jit(solution)/shard_map/ppermute | solution.py:27
  23.8 3.1 %collective-permute-start.2 = (bf16[2,36,2,128]{3,2,1,0:T(2,128)(2,1)S(1)}, bf16[2,36,2,128]{3,2,1,0:T(2,128)(2,1)S(1)}, u32[]{:S(2)}, u32[]{:S(2)}) collective-permute-start(bf16[2,36,2,128]{3,2,1,0:T(2,128)(2,1)S(1)} %get-tuple-element.14), channel_id=1, source_target_pairs={{0,1},{1,2},{2,3},{3,4},{4,5},{5,6},{6,7},{8,9},{9,10},{10,11},{11... | collective-permute-start | bytes 110600 | tf_op jit(solution)/shard_map/ppermute | solution.py:26
  25.5 4.6 %collective-permute-start.3 = (bf16[2,36,2,128]{3,2,1,0:T(2,128)(2,1)S(1)}, bf16[2,36,2,128]{3,2,1,0:T(2,128)(2,1)S(1)}, u32[]{:S(2)}, u32[]{:S(2)}) collective-permute-start(bf16[2,36,2,128]{3,2,1,0:T(2,128)(2,1)S(1)} %get-tuple-element.15), channel_id=1, source_target_pairs={{1,0},{2,1},{3,2},{4,3},{5,4},{6,5},{7,6},{9,8},{10,9},{11,10},{12... | collective-permute-start | bytes 110600 | tf_op jit(solution)/shard_map/ppermute | solution.py:27
  38.1 2.5 %copy-start.18 = (bf16[2244,128]{1,0:T(8,128)(2,1)S(1)}, bf16[2244,128]{1,0:T(8,128)(2,1)}, u32[]{:S(2)}) copy-start(bf16[2244,128]{1,0:T(8,128)(2,1)} %reshape.530) | copy-start | bytes 1723396
  40.6 1.3 copy-start.17
  41.9 1.3 copy-start.16
  54.6 1.6 copy-start.15
  56.2 1.3 copy-start.14
  57.5 1.3 copy-start.13
  62.2 0.8 copy-start.24
  63.2 1.7 copy-start.27
  65.5 1.0 copy-start.25
  68.9 14.3 %all-to-all-start.1 = ((bf16[8,6,32,128]{3,2,1,0:T(8,128)(2,1)}), bf16[8,6,32,128]{3,2,1,0:T(8,128)(2,1)S(1)}, u32[]{:S(2)}, u32[]{:S(2)}) async-start(bf16[8,6,32,128]{3,2,1,0:T(8,128)(2,1)} %broadcast_in_dim.64), calls=%async_computation.1 | async-start | bytes 786432 | tf_op jit(solution)/shard_map/all_to_all | solution.py:17
  83.4 1.7 copy-start.31
  86.5 10.0 %copy-start.35 = (f32[16,128]{1,0:T(8,128)S(1)}, f32[16,128]{1,0:T(8,128)}, u32[]{:S(2)}) copy-start(f32[16,128]{1,0:T(8,128)} %param.18) | copy-start | bytes 24580
  93.1 8.5 %all-to-all-start.2 = ((f32[8,4,6,128]{3,1,2,0:T(4,128)}), f32[8,4,6,128]{3,1,2,0:T(4,128)S(1)}, u32[]{:S(2)}, u32[]{:S(2)}) async-start(f32[8,4,6,128]{3,1,2,0:T(4,128)} %constant_dynamic-update-slice_fusion), calls=%async_computation.2 | async-start | bytes 196608 | tf_op jit(solution)/shard_map/all_to_all | solution.py:190
  116.1 1.6 copy-start.12
  116.2 1.6 copy-start.28
  117.8 1.1 copy-start.11
  118.8 1.1 copy-start.10
  119.9 1.1 copy-start.9
  120.9 1.1 copy-start.8
  124.8 9.7 %copy-start.7 = (f32[2244,128]{1,0:T(8,128)S(1)}, f32[2244,128]{1,0:T(8,128)}, u32[]{:S(2)}) copy-start(f32[2244,128]{1,0:T(8,128)} %convolution_add_fusion.1) | copy-start | bytes 3446788
  127.2 14.6 %all-to-all-start.3 = ((f32[32,2,128]{2,1,0:T(2,128)}), f32[32,2,128]{2,1,0:T(2,128)S(1)}, u32[]{:S(2)}, u32[]{:S(2)}) async-start(f32[32,2,128]{2,1,0:T(2,128)} %broadcast_in_dim.70), calls=%async_computation.3 | async-start | bytes 65536 | tf_op jit(solution)/shard_map/all_to_all | solution.py:17
  142.3 1.0 copy-start.2
  143.8 10.5 %copy-start.3 = (f32[34,66,128]{2,1,0:T(8,128)S(1)}, f32[34,66,128]{2,1,0:T(8,128)}, u32[]{:S(2)}) copy-start(f32[34,66,128]{2,1,0:T(8,128)} %copy-done.2) | copy-start | bytes 3446788
  144.4 9.8 %all-to-all-start.4 = ((f32[32,2,128]{2,1,0:T(2,128)}), f32[32,2,128]{2,1,0:T(2,128)S(1)}, u32[]{:S(2)}, u32[]{:S(2)}) async-start(f32[32,2,128]{2,1,0:T(2,128)} %broadcast_in_dim.72), calls=%async_computation.4 | async-start | bytes 65536 | tf_op jit(solution)/shard_map/all_to_all | solution.py:17
  162.6 1.0 copy-start.5
  166.6 4.0 %copy-start.29 = (bf16[3,3,128,128]{3,2,1,0:T(8,128)(2,1)S(1)}, bf16[3,3,128,128]{3,2,1,0:T(8,128)(2,1)}, u32[]{:S(2)}) copy-start(bf16[3,3,128,128]{3,2,1,0:T(8,128)(2,1)} %param.20) | copy-start | bytes 884740
  166.9 0.8 copy-start.32
  167.7 3.2 %copy-start.30 = (bf16[3,3,128,128]{2,3,1,0:T(8,128)(2,1)S(1)}, bf16[3,3,128,128]{2,3,1,0:T(8,128)(2,1)}, u32[]{:S(2)}) copy-start(bf16[3,3,128,128]{2,3,1,0:T(8,128)(2,1)} %copy.120) | copy-start | bytes 884740
  167.7 19.5 %all-to-all-start.5 = ((bf16[32,72,128]{2,1,0:T(8,128)(2,1)}), bf16[32,72,128]{2,1,0:T(8,128)(2,1)S(1)}, u32[]{:S(2)}, u32[]{:S(2)}) async-start(bf16[32,72,128]{2,1,0:T(8,128)(2,1)} %bitcast.510), calls=%async_computation.5 | async-start | bytes 1179648 | tf_op jit(solution)/shard_map/all_to_all | solution.py:271
  170.5 1.3 copy-start.23
  171.8 1.0 copy-start.22
  172.8 1.0 copy-start.21
  173.8 1.0 copy-start.20
  188.2 19.9 %all-to-all-start.6 = ((bf16[32,72,128]{2,1,0:T(8,128)(2,1)}), bf16[32,72,128]{2,1,0:T(8,128)(2,1)S(1)}, u32[]{:S(2)}, u32[]{:S(2)}) async-start(bf16[32,72,128]{2,1,0:T(8,128)(2,1)} %broadcast_in_dim.73), calls=%async_computation.6 | async-start | bytes 1179648 | tf_op jit(solution)/shard_map/all_to_all | solution.py:17
  191.4 1.4 copy-start.19
  193.1 1.0 copy-start.26
  194.2 15.1 %copy-start.1 = (bf16[1024,128]{1,0:T(8,128)(2,1)S(1)}, bf16[1024,128]{1,0:T(8,128)(2,1)}, u32[]{:S(2)}) copy-start(bf16[1024,128]{1,0:T(8,128)(2,1)} %param.14) | copy-start | bytes 786436

commit v3 on v2

v3 whole, which is shorter than its diff:
```python
import functools
import math

import jax
import jax.numpy as jnp
import numpy as np
from jax import lax
from jax.experimental import pallas as pl
from jax.experimental.pallas import tpu as pltpu
from jax.sharding import PartitionSpec as P

INSTANCES = 256
UPSCALE = 16
BOTH = ("rows", "cols")

norm_eps = 1e-05


def spread_to(array, axis):
    devices = lax.axis_size(axis)
    return lax.all_to_all(jnp.broadcast_to(array, (devices, *array.shape)), axis, 0, 0)


def conv_taps(padded, weight, row_count, col_count):
    summed = jnp.zeros((row_count * col_count, weight.shape[3]), jnp.float32)
    for tap_row in range(3):
        for tap_col in range(3):
            window = padded[tap_row : tap_row + row_count, tap_col : tap_col + col_count]
            summed = summed + jnp.dot(
                window.reshape(row_count * col_count, window.shape[2]),
                weight[tap_row, tap_col],
                preferred_element_type=jnp.float32,
            )
    return summed


RIM = 8
MARGIN = 16
KERNEL_VMEM = 40 * 1024 * 1024


class Layout:
    def __init__(self, tile_rows, tile_cols):
        self.rows, self.cols = tile_rows, tile_cols
        self.wide = tile_cols + 2 * RIM
        self.flat = (tile_rows + 6) * self.wide + 2 * MARGIN
        self.out_rows = tile_rows + 3
        self.out = self.out_rows * self.wide
        self.z = self.out + 2 * MARGIN
        self.own = tile_rows * self.wide + 2 * MARGIN
        self.kept = -(-self.out // 128) * 128


def vmem(count):
    return [pl.BlockSpec(memory_space=pltpu.VMEM)] * count


def call(body, outs, ins, scratch=(), flops=0, **fixed):
    return pl.pallas_call(
        functools.partial(body, **fixed),
        out_shape=outs,
        in_specs=vmem(len(ins)),
        out_specs=jax.tree.map(lambda _: pl.BlockSpec(memory_space=pltpu.VMEM), outs),
        scratch_shapes=list(scratch),
        compiler_params=pltpu.CompilerParams(vmem_limit_bytes=KERNEL_VMEM),
        cost_estimate=pl.CostEstimate(flops=flops, bytes_accessed=4 << 20, transcendentals=0),
    )(*ins)


def put_tiles(flat_ref, lay, main_ref, top_ref, bottom_ref, strip_ref):
    flat_ref[...] = jnp.zeros_like(flat_ref)
    for k in range(lay.rows + 5):
        base = MARGIN + k * lay.wide
        i = k - 3
        if i >= -2:
            if i < 0:
                row = top_ref[i + 2]
            elif i < lay.rows:
                row = main_ref[i]
            else:
                row = bottom_ref[i - lay.rows]
            flat_ref[base : base + lay.cols] = row
        flat_ref[base + lay.cols : base + lay.wide] = strip_ref[k]


def taps_matmul(flat_ref, square_ref, z_refs, lay, turned):
    count = z_refs[0].shape[0]
    chunks = 3
    step = count // chunks
    width = z_refs[0].shape[1]

    @pl.loop(0, chunks)
    def _(c):
        begin = pl.multiple_of(c * step, 16)
        parts = [flat_ref[pl.ds(begin + shift, step)] for shift in (0, lay.wide, 2 * lay.wide)]
        if turned:
            left = jnp.concatenate(parts[::-1], 1)
            result = lax.dot_general(
                left, square_ref[...], (((1,), (1,)), ((), ())), preferred_element_type=jnp.float32
            )
        else:
            left = jnp.concatenate(parts, 1)
            result = jnp.dot(left, square_ref[...], preferred_element_type=jnp.float32)
        for b in range(3):
            z_refs[b][pl.ds(begin, step)] = result[:, b * width : (b + 1) * width]


def put_square(square_ref, weight_ref, turned):
    width = weight_ref.shape[2]
    for a in range(3):
        for b in range(3):
            r, c = (b, a) if turned else (a, b)
            square_ref[r * width : (r + 1) * width, c * width : (c + 1) * width] = weight_ref[a, b]


def taken(z_refs, begin, count, turned):
    early, late = (2, 0) if turned else (0, 2)
    return (
        z_refs[early][pl.ds(begin + MARGIN - 1, count)]
        + z_refs[1][pl.ds(begin + MARGIN, count)]
        + z_refs[late][pl.ds(begin + MARGIN + 1, count)]
    )


def folded(value):
    return value.reshape(-1, 8, value.shape[-1]).sum(0)


def send_stats(out_ref, first, second):
    sums = jnp.concatenate(
        [jnp.sum(first, 0, keepdims=True), jnp.sum(second, 0, keepdims=True)], 0
    )
    out_ref[...] = jnp.zeros_like(out_ref)
    for d in range(out_ref.shape[0]):
        out_ref[d, 0:2] = sums


def cot_kernel(main, top, bottom, strip, weight, grad_out, flat, square, z0, z1, z2, *, lay):
    put_tiles(flat, lay, main, top, bottom, strip)
    put_square(square, weight, True)
    taps_matmul(flat, square, (z0, z1, z2), lay, True)

    @pl.loop(0, lay.out_rows)
    def _(r):
        begin = pl.multiple_of(r * lay.wide, 16)
        grad_out[pl.ds(begin, lay.wide)] = taken((z0, z1, z2), begin, lay.wide, True)


def mixed_kernel(
    main, top, bottom, strip, terms, weight, flat, act_out, stats, square, z0, z1, z2, *, lay
):
    width = main.shape[2]
    flat[...] = jnp.zeros_like(flat)
    blocks = lay.cols // UPSCALE
    for k in range(lay.rows + 5):
        base = MARGIN + k * lay.wide
        i = k - 3
        own, following = (i + UPSCALE) // UPSCALE, (i + 1 + UPSCALE) // UPSCALE

        def spread(block_row, block_col, rows):
            return jnp.broadcast_to(
                terms[block_row, block_col : block_col + 1], (rows, width)
            )

        if i >= -2:
            if i < 0:
                row = top[i + 2]
            elif i < lay.rows:
                row = main[i]
            else:
                row = bottom[i - lay.rows]
            added = jnp.concatenate([spread(own, b + 2, UPSCALE) for b in range(blocks)], 0)
            flat[base : base + lay.cols] = (row.astype(jnp.float32) + added).astype(jnp.bfloat16)
        zero = jnp.zeros((RIM, width), jnp.float32)
        right = spread(own, blocks + 2, RIM) if i >= -2 else zero
        left = spread(following, 1, RIM) if i + 1 < lay.rows + 2 else zero
        flat[base + lay.cols : base + lay.wide] = (
            strip[k].astype(jnp.float32) + jnp.concatenate([right, left], 0)
        ).astype(jnp.bfloat16)
    put_square(square, weight, False)
    taps_matmul(flat, square, (z0, z1, z2), lay, False)

    def step(r, sums):
        begin = pl.multiple_of(r * lay.wide, 16)
        value = taken((z0, z1, z2), begin, lay.wide, False)
        act_out[pl.ds(begin, lay.wide)] = value
        mine = ((r >= 2) & (r < lay.rows + 2)).astype(jnp.float32)
        own_value = value[: lay.cols] * mine
        return sums[0] + folded(own_value), sums[1] + folded(own_value * own_value)

    zero = jnp.zeros((8, width), jnp.float32)
    sums = lax.fori_loop(0, lay.out_rows, step, (zero, zero))
    send_stats(stats, *sums)


def act_moments(stats, pixel_total):
    sums = jnp.sum(stats[...], 0)
    mean = sums[0:1] / pixel_total
    return mean, lax.rsqrt(sums[1:2] / pixel_total - mean * mean + norm_eps)


def inside_masks(lay, width, row_devices, col_devices):
    my_row, my_col = lax.axis_index("rows"), lax.axis_index("cols")
    column = lax.broadcasted_iota(jnp.int32, (lay.wide, width), 0)
    has_right = (my_col < col_devices - 1).astype(jnp.float32)
    has_left = (my_col > 0).astype(jnp.float32)
    near = jnp.where(
        column < lay.cols, 1.0, jnp.where(column < lay.cols + RIM, has_right, 0.0)
    )
    following = jnp.where(column >= lay.cols + RIM, has_left, 0.0)

    def row_inside(i):
        row = my_row * lay.rows + i
        return ((row >= 0) & (row < lay.rows * row_devices)).astype(jnp.float32)

    return lambda r: near * row_inside(r - 2) + following * row_inside(r - 1)


def norm_kernel(
    act, stats, act_grad, activated, normed_out, grad_out, grad_stats, *, lay, grid, pixel_total
):
    width = act.shape[1]
    mean, inverse = act_moments(stats, pixel_total)
    mask = inside_masks(lay, width, *grid)
    activated[...] = jnp.zeros_like(activated)

    def step(r, sums):
        begin = pl.multiple_of(r * lay.wide, 16)
        normed = (act[pl.ds(begin, lay.wide)] - mean) * inverse
        gate = 1.0 / (1.0 + jnp.exp(-normed))
        inside = mask(r)
        activated[pl.ds(pl.multiple_of(begin + MARGIN + lay.wide, 16), lay.wide)] = (
            normed * gate * inside
        ).astype(jnp.bfloat16)
        grad = act_grad[pl.ds(begin, lay.wide)] * gate * (1.0 + normed * (1.0 - gate))
        normed_out[pl.ds(begin, lay.wide)] = normed
        grad_out[pl.ds(begin, lay.wide)] = grad
        mine = ((r >= 2) & (r < lay.rows + 2)).astype(jnp.float32)
        own_grad = grad[: lay.cols] * mine
        return sums[0] + folded(own_grad), sums[1] + folded(own_grad * normed[: lay.cols])

    zero = jnp.zeros((8, width), jnp.float32)
    sums = lax.fori_loop(0, lay.out_rows, step, (zero, zero))
    send_stats(grad_stats, *sums)


def weight_matmul(flat_ref, own_ref, total_ref, sent_ref, lay, chunk):
    count = lay.own
    first = MARGIN + 3 * lay.wide - MARGIN
    chunks = 3
    step = count // chunks
    width = own_ref.shape[1]
    total = None
    for c in range(chunks):
        begin = c * step
        left = jnp.concatenate(
            [
                flat_ref[first + begin + a * lay.wide : first + begin + a * lay.wide + step]
                for a in (-1, 0, 1)
            ],
            1,
        )
        right = jnp.concatenate(
            [
                own_ref[MARGIN + begin - b : MARGIN + begin - b + step].astype(jnp.bfloat16)
                for b in (-1, 0, 1)
            ],
            1,
        )
        part = lax.dot_general(
            left, right, (((0,), (0,)), ((), ())), preferred_element_type=jnp.float32
        )
        total = part if total is None else total + part
    for a in range(3):
        for b in range(3):
            total_ref[(a * 3 + b) * width : (a * 3 + b + 1) * width] = total[
                a * width : (a + 1) * width, b * width : (b + 1) * width
            ]
    padded = sent_ref.shape[1]
    for d in range(sent_ref.shape[0]):
        sent_ref[d] = total_ref[d * chunk : d * chunk + padded].astype(jnp.bfloat16)


def second_kernel(
    activated, mixed, main, weight, enhanced, sent, square, z0, z1, z2, own, total, *, lay, chunk
):
    put_square(square, weight, False)
    taps_matmul(activated, square, (z0, z1, z2), lay, False)

    @pl.loop(0, lay.rows)
    def _(i):
        begin = pl.multiple_of((i + 2) * lay.wide, 16)
        value = taken((z0, z1, z2), begin, lay.cols, False)
        place = pl.multiple_of((i + 3) * lay.wide + MARGIN, 16)
        enhanced[i] = (mixed[pl.ds(place, lay.cols)].astype(jnp.float32) + value).astype(
            jnp.bfloat16
        )

    own[...] = jnp.zeros_like(own)

    @pl.loop(0, lay.rows)
    def _(i):
        place = pl.multiple_of(i * lay.wide + 2 * MARGIN, 16)
        own[pl.ds(place, lay.cols)] = main[i].astype(jnp.float32)

    weight_matmul(activated, own, total, sent, lay, chunk)


def first_kernel(
    stats, grad_stats, normed_ref, grad_ref, mixed, sent, kept, own, total, *, lay, grid, chunk,
    pixel_total
):
    width = normed_ref.shape[1]
    _, inverse = act_moments(stats, pixel_total)
    sums = jnp.sum(grad_stats[...], 0)
    grad_mean, cross_mean = sums[0:1] / pixel_total, sums[1:2] / pixel_total
    mask = inside_masks(lay, width, *grid)
    own[...] = jnp.zeros_like(own)
    kept[...] = jnp.zeros_like(kept)

    @pl.loop(0, lay.out_rows)
    def _(r):
        begin = pl.multiple_of(r * lay.wide, 16)
        value = inverse * (
            grad_ref[pl.ds(begin, lay.wide)]
            - grad_mean
            - normed_ref[pl.ds(begin, lay.wide)] * cross_mean
        )
        value = (value * mask(r)).astype(jnp.bfloat16)
        kept[pl.ds(begin, lay.wide)] = value

        @pl.when((r >= 2) & (r < lay.rows + 2))
        def _():
            place = pl.multiple_of((r - 2) * lay.wide + 2 * MARGIN, 16)
            own[pl.ds(place, lay.cols)] = value[: lay.cols].astype(jnp.float32)

    weight_matmul(mixed, own, total, sent, lay, chunk)


def coarse_kernel(kept, picked, main, weight, out, *, lay):
    width = weight.shape[2]
    windows = jnp.dot(picked[...], kept[...], preferred_element_type=jnp.float32)
    block_rows, block_cols = lay.rows // UPSCALE, lay.cols // UPSCALE
    blocks = block_rows * block_cols
    summed = jnp.zeros((blocks, width), jnp.float32)
    for tap in range(9):
        summed = summed + lax.dot_general(
            windows[tap * blocks : (tap + 1) * blocks],
            weight[tap // 3, tap % 3].astype(jnp.float32),
            (((1,), (1,)), ((), ())),
            precision=lax.Precision.HIGHEST,
            preferred_element_type=jnp.float32,
        )
    for bi in range(block_rows):
        rows = jnp.zeros((lay.cols, width), jnp.float32)
        for i in range(UPSCALE):
            rows = rows + main[bi * UPSCALE + i].astype(jnp.float32)
        for bj in range(block_cols):
            k = bi * block_cols + bj
            cot = jnp.sum(rows[bj * UPSCALE : (bj + 1) * UPSCALE], 0, keepdims=True)
            out[k : k + 1] = (cot + summed[k : k + 1]) / UPSCALE


def share_kernel(received, sent, *, rescale):
    total = received[0].astype(jnp.float32)
    for d in range(1, received.shape[0]):
        total = total + received[d].astype(jnp.float32)
    total = (total * rescale).astype(jnp.bfloat16)
    for d in range(sent.shape[0]):
        sent[d] = total


def join_kernel(received, out, *, chunk):
    for d in range(received.shape[0]):
        out[d * chunk : (d + 1) * chunk] = received[d].astype(jnp.float32)[:chunk]


def window_picks(lay):
    place = np.arange(lay.kept)
    slot, column = place // lay.wide + 1, place % lay.wide
    behind = column >= lay.cols + RIM
    i = np.where(behind, slot - 2, slot - 3)
    j = np.where(behind, column - lay.wide, column)
    rows = []
    for a in range(3):
        for b in range(3):
            y, x = i + a - 1, j + b - 1
            for bi in range(lay.rows // UPSCALE):
                for bj in range(lay.cols // UPSCALE):
                    rows.append((y // UPSCALE == bi) & (x // UPSCALE == bj) & (place < lay.out))
    return jnp.asarray(np.stack(rows), jnp.bfloat16)


def to_all(payload, axis):
    return lax.all_to_all(payload, axis, 0, 0)


def pieces(array):
    high = array.astype(jnp.bfloat16)
    rest = array - high.astype(jnp.float32)
    middle = rest.astype(jnp.bfloat16)
    return high, middle, (rest - middle.astype(jnp.float32)).astype(jnp.bfloat16)


def per_device(
    global_in,
    global_first,
    global_second,
    project_weight,
    enhancer_input,
    instance_map,
    encoder_features,
    instance_weight,
    enhancer_first,
    enhancer_second,
    output_cotangent,
):
    row_devices, col_devices = lax.axis_size("rows"), lax.axis_size("cols")
    devices = row_devices * col_devices
    my_row, my_col = lax.axis_index("rows"), lax.axis_index("cols")
    band_rows, band_cols, width_share = global_in.shape
    tile_rows, tile_cols, local_width = enhancer_input.shape
    coarse_rows = band_rows * row_devices
    block_rows = tile_rows // UPSCALE
    block_cols = tile_cols // UPSCALE
    blocks = block_rows * block_cols
    encoder_width = encoder_features.shape[0]

    block_labels = instance_map[::UPSCALE, ::UPSCALE].reshape(-1)
    block_sums = (
        encoder_features.reshape(encoder_width, block_rows, UPSCALE, block_cols, UPSCALE)
        .sum(axis=(2, 4))
        .reshape(-1)
    )
    extra = jnp.concatenate([*pieces(block_sums), block_labels.astype(jnp.bfloat16)])
    extra_rows = -(-extra.shape[0] // 2048) * 16
    extra = jnp.pad(extra, (0, extra_rows * 128 - extra.shape[0])).reshape(extra_rows, 128)
    packed = jnp.concatenate([global_in.reshape(-1, 128), extra])
    everything = spread_to(packed, BOTH)
    main_rows = packed.shape[0] - extra_rows
    gathered = everything[:, :main_rows].reshape(
        row_devices, col_devices, band_rows, band_cols, width_share
    )
    tail = everything[:, main_rows:].reshape(devices, -1)
    sums = blocks * encoder_width
    all_sums = sum(tail[:, k * sums : (k + 1) * sums].astype(jnp.float32) for k in (2, 1, 0))
    all_sums = (
        all_sums.reshape(row_devices, col_devices, encoder_width, block_rows, block_cols)
        .transpose(0, 3, 1, 4, 2)
        .reshape(-1, encoder_width)
    )
    all_labels = (
        tail[:, 3 * sums : 3 * sums + blocks]
        .reshape(row_devices, col_devices, block_rows, block_cols)
        .transpose(0, 2, 1, 3)
    )
    label_map = jnp.pad(
        all_labels.reshape(coarse_rows, band_cols), 1, constant_values=-1.0
    )
    near_labels = lax.dynamic_slice(
        label_map,
        (my_row * block_rows, my_col * block_cols),
        (block_rows + 2, block_cols + 2),
    ).reshape(-1)
    same = (near_labels[:, None] == all_labels.reshape(-1)[None, :]).astype(jnp.float32)
    near_sums = jnp.dot(same, all_sums, precision=lax.Precision.HIGHEST)
    near_counts = jnp.sum(same, 1, keepdims=True) * float(UPSCALE * UPSCALE)
    pooled = jnp.dot(
        near_sums / jnp.maximum(near_counts, 1.0),
        instance_weight,
        precision=lax.Precision.HIGHEST,
    ).reshape(block_rows + 2, block_cols + 2, local_width)

    row_up = [(i, i + 1) for i in range(row_devices - 1)]
    row_down = [(j, i) for i, j in row_up]
    col_up = [(i, i + 1) for i in range(col_devices - 1)]
    col_down = [(j, i) for i, j in col_up]
    top = lax.ppermute(
        jnp.stack([enhancer_input[-2:], output_cotangent[-2:]]), "rows", row_up
    )
    bottom = lax.ppermute(
        jnp.stack([enhancer_input[:2], output_cotangent[:2]]), "rows", row_down
    )
    both = jnp.stack([enhancer_input, output_cotangent])
    tall_last = jnp.concatenate([top[:, :, -RIM:], both[:, :, -RIM:], bottom[:, :, -RIM:]], 1)
    tall_first = jnp.concatenate([top[:, :, :RIM], both[:, :, :RIM], bottom[:, :, :RIM]], 1)
    left = lax.ppermute(tall_last, "cols", col_up)
    right = lax.ppermute(tall_first, "cols", col_down)
    strip = jnp.concatenate(
        [
            jnp.pad(right, ((0, 0), (1, 0), (0, 0), (0, 0))),
            jnp.pad(left, ((0, 0), (0, 1), (0, 0), (0, 0))),
        ],
        2,
    )
    lay = Layout(tile_rows, tile_cols)
    width = local_width
    grid = (row_devices, col_devices)
    pixel_total = float(tile_rows * tile_cols * devices)
    chunk = 9 * width // devices
    padded_chunk = -(-chunk // 8) * 8
    square = pltpu.VMEM((3 * width, 3 * width), jnp.bfloat16)
    z = [pltpu.VMEM((lay.z, width), jnp.float32)] * 3
    own = pltpu.VMEM((lay.own + 2 * MARGIN, width), jnp.float32)
    total = pltpu.VMEM((9 * width + 64, width), jnp.float32)
    flat_shape = jax.ShapeDtypeStruct((lay.flat, width), jnp.bfloat16)
    out_shape = jax.ShapeDtypeStruct((lay.out, width), jnp.float32)
    stats_shape = jax.ShapeDtypeStruct((devices, 8, width), jnp.float32)
    sent_shape = jax.ShapeDtypeStruct((devices, padded_chunk, width), jnp.bfloat16)
    conv_flops = 18 * width * width * lay.out

    act_grad = call(
        cot_kernel,
        out_shape,
        (output_cotangent, top[1], bottom[1], strip[1], enhancer_second),
        [pltpu.VMEM((lay.flat, width), jnp.bfloat16), square, *z],
        conv_flops,
        lay=lay,
    )

    whole_in = gathered.transpose(0, 2, 3, 1, 4).reshape(coarse_rows, band_cols, -1)
    rimmed = jnp.pad(whole_in, ((1, 1), (1, 1), (0, 0)))
    first_raw = conv_taps(rimmed, global_first, coarse_rows, band_cols)
    band_total = coarse_rows * band_cols
    band_mean = jnp.sum(first_raw, 0) / band_total
    band_var = jnp.sum(first_raw * first_raw, 0) / band_total - band_mean * band_mean
    normed = (first_raw - band_mean) * lax.rsqrt(band_var + norm_eps)
    hidden = (
        jnp.maximum(normed, 0.0).astype(jnp.bfloat16).reshape(coarse_rows, band_cols, width_share)
    )
    hidden = jnp.pad(hidden, ((2, 2), (0, 0), (0, 0)))
    near_hidden = lax.dynamic_slice_in_dim(hidden, my_row * band_rows, band_rows + 4, 0)
    near_hidden = spread_to(near_hidden, "cols")
    near_hidden = near_hidden.transpose(1, 2, 0, 3).reshape(band_rows + 4, band_cols, -1)
    second_raw = conv_taps(
        jnp.pad(near_hidden, ((0, 0), (1, 1), (0, 0))), global_second, band_rows + 2, band_cols
    )
    mine = lax.dynamic_index_in_dim(gathered, my_col, 1, keepdims=False)
    mine = jnp.pad(
        mine.reshape(coarse_rows, band_cols, width_share), ((1, 1), (0, 0), (0, 0))
    )
    near_in = lax.dynamic_slice_in_dim(mine, my_row * band_rows, band_rows + 2, 0)
    global_out = (
        near_in.astype(jnp.float32).reshape(-1, width_share) + second_raw
    ).astype(jnp.bfloat16)
    weight_rows = lax.dynamic_slice_in_dim(project_weight, my_col * width_share, width_share, 0)
    partial = jnp.dot(global_out, weight_rows, preferred_element_type=jnp.float32)
    partial = jnp.pad(
        partial.reshape(band_rows + 2, band_cols, local_width), ((0, 0), (1, 1), (0, 0))
    )
    outgoing = jnp.stack(
        [partial[:, j * block_cols : (j + 1) * block_cols + 2] for j in range(col_devices)]
    )
    incoming = lax.all_to_all(outgoing, "cols", 0, 0)
    coarse = jnp.sum(incoming, 0).astype(jnp.bfloat16)

    block_terms = coarse.astype(jnp.float32) + pooled
    row_ids = my_row * block_rows - 1 + jnp.arange(block_rows + 2)
    col_ids = my_col * block_cols - 1 + jnp.arange(block_cols + 2)
    inside = ((row_ids >= 0) & (row_ids < coarse_rows))[:, None] & (
        (col_ids >= 0) & (col_ids < band_cols)
    )[None, :]
    terms = jnp.where(inside[:, :, None], block_terms, 0.0)
    terms = jnp.pad(terms, ((0, 0), (1, 1), (0, 0)))

    mixed, first_act, stats = call(
        mixed_kernel,
        (flat_shape, out_shape, stats_shape),
        (enhancer_input, top[0], bottom[0], strip[0], terms, enhancer_first),
        [square, *z],
        conv_flops,
        lay=lay,
    )
    stats = to_all(stats, BOTH)
    activated, normed_act, normed_grad, grad_stats = call(
        norm_kernel,
        (flat_shape, out_shape, out_shape, stats_shape),
        (first_act, stats, act_grad),
        lay=lay,
        grid=grid,
        pixel_total=pixel_total,
    )
    grad_stats = to_all(grad_stats, BOTH)
    enhanced, second_sent = call(
        second_kernel,
        (jax.ShapeDtypeStruct((tile_rows, tile_cols, width), jnp.bfloat16), sent_shape),
        (activated, mixed, output_cotangent, enhancer_second),
        [square, *z, own, total],
        2 * conv_flops,
        lay=lay,
        chunk=chunk,
    )
    second_part = to_all(second_sent, BOTH)
    first_sent, kept = call(
        first_kernel,
        (sent_shape, jax.ShapeDtypeStruct((lay.kept, width), jnp.bfloat16)),
        (stats, grad_stats, normed_act, normed_grad, mixed),
        [own, total],
        conv_flops,
        lay=lay,
        grid=grid,
        chunk=chunk,
        pixel_total=pixel_total,
    )
    first_part = to_all(first_sent, BOTH)
    rescale = 1.0 / math.sqrt(pixel_total)
    second_share = to_all(call(share_kernel, sent_shape, (second_part,), rescale=rescale), BOTH)
    global_gradient = call(
        coarse_kernel,
        jax.ShapeDtypeStruct((blocks, width), jnp.float32),
        (kept, window_picks(lay), output_cotangent, enhancer_first),
        (),
        lay=lay,
    )
    first_share = to_all(call(share_kernel, sent_shape, (first_part,), rescale=rescale), BOTH)
    whole_shape = jax.ShapeDtypeStruct((9 * width, width), jnp.float32)
    second_total = call(join_kernel, whole_shape, (second_share,), chunk=chunk)
    first_total = call(join_kernel, whole_shape, (first_share,), chunk=chunk)
    return (
        enhanced,
        first_total.reshape(3, 3, width, width),
        second_total.reshape(3, 3, width, width),
        global_gradient.reshape(block_rows, block_cols, width),
    )


def solution(mesh):
    return jax.shard_map(
        per_device,
        mesh=mesh,
        in_specs=(
            P("rows", None, "cols"),
            P(None, None, None, "cols"),
            P(None, None, None, "cols"),
            P(),
            P("rows", "cols", None),
            P("rows", "cols"),
            P(None, "rows", "cols"),
            P(),
            P(),
            P(),
            P("rows", "cols", None),
        ),
        out_specs=(P("rows", "cols", None), P(), P(), P("rows", "cols", None)),
        check_vma=False,
    )
```

time: 211 us -> 177 us (0.84)
  matrix products: 38.7 us -> 6.09 us
  local copies, waits for them, and re-layouts: 67.7 us -> 39.1 us
  Pallas kernels: 0 us -> 19.3 us
  waiting for transfers between devices: 54.1 us -> 64.3 us
  other arithmetic: 6.45 us -> 2.24 us
  starting transfers between devices: 40.6 us -> 43 us
    reshape x20 -> x0, local copies, waits for them, and re-layouts: 30.6 us -> none  [the longest x9 16.1 us: back_taps(): window.reshape(row_count * col_count, window.shape[2])]
    all_to_all x1 -> x6, waiting for transfers between devices: 12.1 us -> 41 us  [to_all(): return lax.all_to_all(payload, axis, 0, 0)]
    dot_general x28 -> x0, matrix products: 22.1 us -> none  [the longest x9 14.2 us: back_taps(): jnp.dot(window.reshape(row_count * col_count, window.shape[2]), weight[ta...]
    pallas_call x0 -> x10, Pallas kernels: none -> 19.3 us  [call(): pl.pallas_call(functools.partial(body, **fixed), out_shape=outs, in_specs...]
    all_to_all x5 -> x2, starting transfers between devices: 26.5 us -> 10.5 us  [spread_to(): lax.all_to_all(jnp.broadcast_to(array, (devices, *array.shape)), axis, 0, 0)]
    all_to_all x1 -> x6, starting transfers between devices: 2.74 us -> 18.5 us  [to_all(): return lax.all_to_all(payload, axis, 0, 0)]
    ppermute x4, waiting for transfers between devices: 10.6 us -> 0.01 us  [the longest x1 0.01 us: per_device(): lax.ppermute(jnp.stack([enhancer_input[-2:], output_cotangent[-2:]]), 'ro...]
    dot_general x35 -> x17, matrix products: 14.9 us -> 4.33 us  [conv_taps(): jnp.dot(window.reshape(row_count * col_count, window.shape[2]), weight[ta...]
  transfers between devices with their start and end apart: 11 -> 13, of which waited for: 8 -> 9; matrix products, arithmetic and copies ran while one was open for 22% -> 4% of each run, Pallas kernels for 0% -> 8%
where the time goes in v3:
time: 177 us; the launch traced here: 175 us
  waiting for transfers between devices  64.3 us (36%)
  starting transfers between devices  43 us (24%)
  local copies, waits for them, and re-layouts  39.1 us (22%)
  Pallas kernels  19.3 us (11%)
  matrix products  6.09 us (3%)
  other arithmetic  2.24 us (1%)
    all_to_all x6, waiting for transfers between devices, to_all(): return lax.all_to_all(payload, axis, 0, 0)  41 us
    unnamed x77, local copies, waits for them, and re-layouts  23.9 us
    pallas_call x10, Pallas kernels, call(): pl.pallas_call(functools.partial(body, **fixed), out_shape=outs, in_specs...  19.3 us
    all_to_all x6, starting transfers between devices, to_all(): return lax.all_to_all(payload, axis, 0, 0)  18.5 us
    all_to_all x2, waiting for transfers between devices, spread_to(): lax.all_to_all(jnp.broadcast_to(array, (devices, *array.shape)), axis, 0, 0)  18.4 us
    all_to_all x2, starting transfers between devices, spread_to(): lax.all_to_all(jnp.broadcast_to(array, (devices, *array.shape)), axis, 0, 0)  10.5 us
    slice x6, local copies, waits for them, and re-layouts, conv_taps(): window = padded[tap_row:tap_row + row_count, tap_col:tap_col + col_count]  4.93 us
    ppermute x1, starting transfers between devices, per_device(): lax.ppermute(jnp.stack([enhancer_input[-2:], output_cotangent[-2:]]), 'ro...  4.93 us
  transfers between devices with their start and end apart: 13, of which 9 were waited for; matrix products, arithmetic and copies ran while one was open for 4% of the time, Pallas kernels for 8%

profile of v3, /device:TPU:0, one launch (start us, length us, event | category | flops | bytes accessed | tf_op | source)
XLA Modules:
  0.0 175.5 jit_solution(11126294913848054667)
XLA Ops:
  0.7 0.9 slice_bitcast_fusion.6
  1.5 4.9 %collective-permute-start = (bf16[2,2,64,128]{3,2,1,0:T(8,128)(2,1)S(1)}, bf16[2,2,64,128]{3,2,1,0:T(8,128)(2,1)S(1)}, u32[]{:S(2)}, u32[]{:S(2)}) collective-permute-start(bf16[2,2,64,128]{3,2,1,0:T(8,128)(2,1)S(1)} %pad_maximum_fusion.2), channel_id=1, source_target_pairs={{0,8},{8,16},{16,24},{1,9},{9,17},{17,25},{2,10},{10,18},{18,26},{... | collective-permute-start | bytes 196616 | tf_op jit(solution)/shard_map/ppermute | solution.py:478
  6.5 1.4 collective-permute-start.1
  8.0 0.7 convert.4
  8.9 1.4 reshape.197
  10.7 0.9 broadcast_in_dim.25
  11.7 6.9 %all-to-all-start = ((bf16[32,80,128]{2,1,0:T(8,128)(2,1)}), bf16[32,80,128]{2,1,0:T(8,128)(2,1)S(1)}, u32[]{:S(2)}, u32[]{:S(2)}) async-start(bf16[32,80,128]{2,1,0:T(8,128)(2,1)} %broadcast_in_dim.25), calls=%async_computation | async-start | bytes 1310720 | tf_op jit(solution)/shard_map/all_to_all | solution.py:21
  18.8 1.3 collective-permute-start.2
  20.1 3.0 %collective-permute-start.3 = (bf16[2,36,8,128]{3,2,1,0:T(8,128)(2,1)S(1)}, bf16[2,36,8,128]{3,2,1,0:T(8,128)(2,1)S(1)}, u32[]{:S(2)}, u32[]{:S(2)}) collective-permute-start(bf16[2,36,8,128]{3,2,1,0:T(8,128)(2,1)S(1)} %get-tuple-element.29), channel_id=1, source_target_pairs={{0,1},{1,2},{2,3},{3,4},{4,5},{5,6},{6,7},{8,9},{9,10},{10,11},{11... | collective-permute-start | bytes 442376 | tf_op jit(solution)/shard_map/ppermute | solution.py:487
  24.4 0.7 slice_bitcast_fusion
  25.1 11.4 %all-to-all-done = bf16[32,80,128]{2,1,0:T(8,128)(2,1)S(1)} async-done(((bf16[32,80,128]{2,1,0:T(8,128)(2,1)}), bf16[32,80,128]{2,1,0:T(8,128)(2,1)S(1)}, u32[]{:S(2)}, u32[]{:S(2)}) %all-to-all-start) | async-done | bytes 655392 | tf_op jit(solution)/shard_map/all_to_all | solution.py:21
  36.8 0.6 convert_add_fusion
  38.7 0.8 copy-done.27
  39.5 1.0 reshape.204
  40.5 4.1 %pad_slice_fusion = (bf16[8,32,1024]{2,1,0:T(8,128)(2,1)S(1)}, bf16[8,32,1024]{2,1,0:T(8,128)(2,1)S(1)}, bf16[8,32,1024]{2,1,0:T(8,128)(2,1)S(1)}, bf16[8,32,102...) fusion(bf16[8,32,1024]{2,1,0:T(8,128)(2,1)} %reshape.204), kind=kLoop, calls=%fused_computation | loop fusion | bytes 4718592 | tf_op jit(solution)/shard_map/slice | solution.py:28
  47.4 0.8 broadcast_in_dim.26
  48.2 3.6 %all-to-all-start.1 = ((bf16[8,6,32,128]{3,2,1,0:T(8,128)(2,1)}), bf16[8,6,32,128]{3,2,1,0:T(8,128)(2,1)S(1)}, u32[]{:S(2)}, u32[]{:S(2)}) async-start(bf16[8,6,32,128]{3,2,1,0:T(8,128)(2,1)} %broadcast_in_dim.26), calls=%async_computation.1 | async-start | bytes 786432 | tf_op jit(solution)/shard_map/all_to_all | solution.py:21
  52.1 0.6 pad_dynamic-slice_fusion.1
  53.0 7.0 %all-to-all-done.1 = bf16[8,6,32,128]{3,2,1,0:T(8,128)(2,1)S(1)} async-done(((bf16[8,6,32,128]{3,2,1,0:T(8,128)(2,1)}), bf16[8,6,32,128]{3,2,1,0:T(8,128)(2,1)S(1)}, u32[]{:S(2)}, u32[]{:S(2)}) %all-to-all-start.1) | async-done | bytes 393248 | tf_op jit(solution)/shard_map/all_to_all | solution.py:21
  61.0 0.8 copy-done.30
  63.7 1.3 fusion.2
  69.9 3.4 %all-to-all-start.2 = ((f32[8,4,6,128]{3,1,2,0:T(4,128)}), f32[8,4,6,128]{3,1,2,0:T(4,128)S(1)}, u32[]{:S(2)}, u32[]{:S(2)}) async-start(f32[8,4,6,128]{3,1,2,0:T(4,128)} %constant_dynamic-update-slice_fusion), calls=%async_computation.2 | async-start | bytes 196608 | tf_op jit(solution)/shard_map/all_to_all | solution.py:554
  73.4 4.9 %all-to-all-done.2 = f32[8,4,6,128]{3,1,2,0:T(4,128)S(1)} async-done(((f32[8,4,6,128]{3,1,2,0:T(4,128)}), f32[8,4,6,128]{3,1,2,0:T(4,128)S(1)}, u32[]{:S(2)}, u32[]{:S(2)}) %all-to-all-start.2) | async-done | bytes 98336 | tf_op jit(solution)/shard_map/all_to_all | solution.py:554
  78.5 1.0 copy-done.11
  79.5 0.8 copy-done.21
  80.3 0.8 copy-done.22
  81.0 2.8 %shard_map.147 = (bf16[3072,128]{1,0:T(8,128)(2,1)S(1)}, f32[2800,128]{1,0:T(8,128)S(1)}, f32[32,8,128]{2,1,0:T(8,128)S(1)}) custom-call(bf16[32,64,128]{2,1,0:T(8,128)(2,1)S(1)} %copy-done.11, bf16[2,64,128]{2,1,0:T(8,128)(2,1)S(1)} %copy-done.21, bf16[2,64,128]{2,1,0:T(8,128)(2,1)S(1)} %copy-done.22, bf16[37,16,128]{2,1,0:T(8,128)(2,1)S(1)} %get-tuple-element.52.strip, ...), custom_call_target="tpu_custom_call" | custom-call | flops 825753600 | bytes 4194304 | tf_op jit(solution)/shard_map/pallas_call | solution.py:59
  83.9 0.6 copy-done.20
  84.6 2.6 %all-to-all-start.3 = ((f32[32,8,128]{2,1,0:T(8,128)}), f32[32,8,128]{2,1,0:T(8,128)S(1)}, u32[]{:S(2)}, u32[]{:S(2)}) async-start(f32[32,8,128]{2,1,0:T(8,128)} %copy-done.20), calls=%async_computation.3 | async-start | bytes 262144 | tf_op jit(solution)/shard_map/all_to_all | solution.py:395
  87.2 0.9 copy-done.19
  88.1 1.0 copy-done.25
  89.0 2.6 %shard_map.148.act_grad = f32[2800,128]{1,0:T(8,128)S(1)} custom-call(bf16[32,64,128]{2,1,0:T(8,128)(2,1)S(1)} %copy-done.1, bf16[2,64,128]{2,1,0:T(8,128)(2,1)S(1)} %get-tuple-element.55.top, bf16[2,64,128]{2,1,0:T(8,128)(2,1)S(1)} %get-tuple-element.53.bottom, bf16[37,16,128]{2,1,0:T(8,128)(2,1)S(1)} %copy-done.19, bf16[3,3,128,128]{3,2,1,0:T(8,128)(2,1)S(1)} %copy-done.25), custom_call_target="tpu_custom_call" | custom-call | flops 825753600 | bytes 4194304 | tf_op jit(solution)/shard_map/pallas_call | solution.py:59
  91.7 1.1 copy-done.2
  92.8 2.6 %all-to-all-done.3.stats = f32[32,8,128]{2,1,0:T(8,128)S(1)} async-done(((f32[32,8,128]{2,1,0:T(8,128)}), f32[32,8,128]{2,1,0:T(8,128)S(1)}, u32[]{:S(2)}, u32[]{:S(2)}) %all-to-all-start.3) | async-done | bytes 131104 | tf_op jit(solution)/shard_map/all_to_all | solution.py:395
  95.4 1.4 copy-done.3
  96.7 2.1 %shard_map.149 = (bf16[3072,128]{1,0:T(8,128)(2,1)S(1)}, f32[2800,128]{1,0:T(8,128)S(1)}, f32[2800,128]{1,0:T(8,128)S(1)}, f32[32,8,128]{2,1,0:T(8,128)}) custom-call(f32[2800,128]{1,0:T(8,128)S(1)} %get-tuple-element.15.act, f32[32,8,128]{2,1,0:T(8,128)S(1)} %all-to-all-done.3.stats, f32[2800,128]{1,0:T(8,128)S(1)} %copy-done.3), custom_call_target="tpu_custom_call" | custom-call | bytes 4194304 | tf_op jit(solution)/shard_map/pallas_call | solution.py:59
  98.8 1.1 copy-done.4
  100.0 1.1 copy-done.6
  101.1 0.9 copy-done.23
  102.0 3.4 %all-to-all-start.4 = ((f32[32,8,128]{2,1,0:T(8,128)}), f32[32,8,128]{2,1,0:T(8,128)S(1)}, u32[]{:S(2)}, u32[]{:S(2)}) async-start(f32[32,8,128]{2,1,0:T(8,128)} %get-tuple-element.20), calls=%async_computation.4 | async-start | bytes 262144 | tf_op jit(solution)/shard_map/all_to_all | solution.py:395
  105.4 1.1 copy-done.24
  106.5 1.0 copy-done.26
  107.5 4.2 %shard_map.150 = (bf16[32,64,128]{2,1,0:T(8,128)(2,1)}, bf16[32,40,128]{2,1,0:T(8,128)(2,1)S(1)}) custom-call(bf16[3072,128]{1,0:T(8,128)(2,1)S(1)} %copy-done.24, bf16[3072,128]{1,0:T(8,128)(2,1)S(1)} %get-tuple-element.18.mixed, bf16[32,64,128]{2,1,0:T(8,128)(2,1)S(1)} %copy-done.1, bf16[3,3,128,128]{3,2,1,0:T(8,128)(2,1)S(1)} %copy-done.26), custom_call_target="tpu_custom_call" | custom-call | flops 1651507200 | bytes 4194304 | tf_op jit(solution)/shard_map/pallas_call | solution.py:59
  111.7 0.7 copy-done.15
  112.4 1.1 all-to-all-done.4.grad_stats
  113.5 0.7 copy-done.12
  114.1 4.6 %all-to-all-start.7 = ((bf16[32,40,128]{2,1,0:T(8,128)(2,1)}), bf16[32,40,128]{2,1,0:T(8,128)(2,1)S(1)}, u32[]{:S(2)}, u32[]{:S(2)}) async-start(bf16[32,40,128]{2,1,0:T(8,128)(2,1)} %copy-done.15), calls=%async_computation.7 | async-start | bytes 655360 | tf_op jit(solution)/shard_map/all_to_all | solution.py:395
  118.7 1.4 copy-done.7
  120.1 0.9 copy-done.13
  121.0 2.3 %shard_map.151 = (bf16[32,40,128]{2,1,0:T(8,128)(2,1)S(1)}, bf16[2816,128]{1,0:T(8,128)(2,1)S(1)}) custom-call(f32[32,8,128]{2,1,0:T(8,128)S(1)} %all-to-all-done.3.stats, f32[32,8,128]{2,1,0:T(8,128)S(1)} %copy-done.13, f32[2800,128]{1,0:T(8,128)S(1)} %copy-done.5, f32[2800,128]{1,0:T(8,128)S(1)} %copy-done.7, bf16[3072,128]{1,0:T(8,128)(2,1)S(1)} %get-tuple-element.18.mixed), custom_call_target="tpu_custom_call" | custom-call | flops 825753600 | bytes 4194304 | tf_op jit(solution)/shard_map/pallas_call | solution.py:59
  123.3 0.9 copy-done.8
  124.2 0.7 copy-done.16
  124.9 5.8 %all-to-all-done.7.received = bf16[32,40,128]{2,1,0:T(8,128)(2,1)S(1)} async-done(((bf16[32,40,128]{2,1,0:T(8,128)(2,1)}), bf16[32,40,128]{2,1,0:T(8,128)(2,1)S(1)}, u32[]{:S(2)}, u32[]{:S(2)}) %all-to-all-start.7) | async-done | bytes 327712 | tf_op jit(solution)/shard_map/all_to_all | solution.py:395
  130.7 2.7 %all-to-all-start.5 = ((bf16[32,40,128]{2,1,0:T(8,128)(2,1)}), bf16[32,40,128]{2,1,0:T(8,128)(2,1)S(1)}, u32[]{:S(2)}, u32[]{:S(2)}) async-start(bf16[32,40,128]{2,1,0:T(8,128)(2,1)} %copy-done.16), calls=%async_computation.5 | async-start | bytes 655360 | tf_op jit(solution)/shard_map/all_to_all | solution.py:395
  133.5 0.8 shard_map.154
  134.2 11.2 %all-to-all-done.5.received = bf16[32,40,128]{2,1,0:T(8,128)(2,1)S(1)} async-done(((bf16[32,40,128]{2,1,0:T(8,128)(2,1)}), bf16[32,40,128]{2,1,0:T(8,128)(2,1)S(1)}, u32[]{:S(2)}, u32[]{:S(2)}) %all-to-all-start.5) | async-done | bytes 327712 | tf_op jit(solution)/shard_map/all_to_all | solution.py:395
  145.4 2.6 %all-to-all-start.8 = ((bf16[32,40,128]{2,1,0:T(8,128)(2,1)}), bf16[32,40,128]{2,1,0:T(8,128)(2,1)S(1)}, u32[]{:S(2)}, u32[]{:S(2)}) async-start(bf16[32,40,128]{2,1,0:T(8,128)(2,1)} %shard_map.154), calls=%async_computation.8 | async-start | bytes 655360 | tf_op jit(solution)/shard_map/all_to_all | solution.py:395
  148.0 0.8 shard_map.152
  148.8 11.2 %all-to-all-done.8.received = bf16[32,40,128]{2,1,0:T(8,128)(2,1)S(1)} async-done(((bf16[32,40,128]{2,1,0:T(8,128)(2,1)}), bf16[32,40,128]{2,1,0:T(8,128)(2,1)S(1)}, u32[]{:S(2)}, u32[]{:S(2)}) %all-to-all-start.8) | async-done | bytes 327712 | tf_op jit(solution)/shard_map/all_to_all | solution.py:395
  160.0 2.6 %all-to-all-start.6 = ((bf16[32,40,128]{2,1,0:T(8,128)(2,1)}), bf16[32,40,128]{2,1,0:T(8,128)(2,1)S(1)}, u32[]{:S(2)}, u32[]{:S(2)}) async-start(bf16[32,40,128]{2,1,0:T(8,128)(2,1)} %shard_map.152), calls=%async_computation.6 | async-start | bytes 655360 | tf_op jit(solution)/shard_map/all_to_all | solution.py:395
  162.7 1.9 %shard_map.156 = f32[8,128]{1,0:T(8,128)} custom-call(bf16[2816,128]{1,0:T(8,128)(2,1)S(1)} %copy-done.9, bf16[72,2816]{1,0:T(8,128)(2,1)S(1)} %copy-done.14, bf16[32,64,128]{2,1,0:T(8,128)(2,1)S(1)} %copy-done.1, bf16[3,3,128,128]{3,2,1,0:T(8,128)(2,1)S(1)} %copy-done.18), custom_call_target="tpu_custom_call" | custom-call | bytes 4194304 | tf_op jit(solution)/shard_map/pallas_call | solution.py:59
  164.6 0.9 shard_map.155
  165.5 9.2 %all-to-all-done.6.received = bf16[32,40,128]{2,1,0:T(8,128)(2,1)S(1)} async-done(((bf16[32,40,128]{2,1,0:T(8,128)(2,1)}), bf16[32,40,128]{2,1,0:T(8,128)(2,1)S(1)}, u32[]{:S(2)}, u32[]{:S(2)}) %all-to-all-start.6) | async-done | bytes 327712 | tf_op jit(solution)/shard_map/all_to_all | solution.py:395
  174.6 0.9 shard_map.153
  (128 shorter events, 14.8 us)
Async XLA Ops:
  0.6 63.0 %copy-start = (bf16[1024,128]{1,0:T(8,128)(2,1)S(1)}, bf16[1024,128]{1,0:T(8,128)(2,1)}, u32[]{:S(2)}) copy-start(bf16[1024,128]{1,0:T(8,128)(2,1)} %param.15) | copy-start | bytes 786436
  0.6 10.1 %copy-start.33 = (bf16[2,32,128]{2,1,0:T(8,128)(2,1)S(1)}, bf16[2,32,128]{2,1,0:T(8,128)(2,1)}, u32[]{:S(2)}) copy-start(bf16[2,32,128]{2,1,0:T(8,128)(2,1)} %param.12) | copy-start | bytes 49156
  1.5 17.2 %collective-permute-start = (bf16[2,2,64,128]{3,2,1,0:T(8,128)(2,1)S(1)}, bf16[2,2,64,128]{3,2,1,0:T(8,128)(2,1)S(1)}, u32[]{:S(2)}, u32[]{:S(2)}) collective-permute-start(bf16[2,2,64,128]{3,2,1,0:T(8,128)(2,1)S(1)} %pad_maximum_fusion.2), channel_id=1, source_target_pairs={{0,8},{8,16},{16,24},{1,9},{9,17},{17,25},{2,10},{10,18},{18,26},{... | collective-permute-start | bytes 196616 | tf_op jit(solution)/shard_map/ppermute | solution.py:478
  6.5 12.2 %copy-start.1 = (bf16[32,64,128]{2,1,0:T(8,128)(2,1)S(1)}, bf16[32,64,128]{2,1,0:T(8,128)(2,1)}, u32[]{:S(2)}) copy-start(bf16[32,64,128]{2,1,0:T(8,128)(2,1)} %main.7) | copy-start | bytes 1572868
  6.5 12.2 %copy-start.10 = (bf16[32,64,128]{2,1,0:T(8,128)(2,1)S(1)}, bf16[32,64,128]{2,1,0:T(8,128)(2,1)}, u32[]{:S(2)}) copy-start(bf16[32,64,128]{2,1,0:T(8,128)(2,1)} %main.4) | copy-start | bytes 1572868
  6.5 12.2 %collective-permute-start.1 = (bf16[2,2,64,128]{3,2,1,0:T(8,128)(2,1)S(1)}, bf16[2,2,64,128]{3,2,1,0:T(8,128)(2,1)S(1)}, u32[]{:S(2)}, u32[]{:S(2)}) collective-permute-start(bf16[2,2,64,128]{3,2,1,0:T(8,128)(2,1)S(1)} %pad_maximum_fusion.3), channel_id=1, source_target_pairs={{8,0},{16,8},{24,16},{9,1},{17,9},{25,17},{10,2},{18,10},{26,18},{... | collective-permute-start | bytes 196616 | tf_op jit(solution)/shard_map/ppermute | solution.py:481
  11.7 24.8 %all-to-all-start = ((bf16[32,80,128]{2,1,0:T(8,128)(2,1)}), bf16[32,80,128]{2,1,0:T(8,128)(2,1)S(1)}, u32[]{:S(2)}, u32[]{:S(2)}) async-start(bf16[32,80,128]{2,1,0:T(8,128)(2,1)} %broadcast_in_dim.25), calls=%async_computation | async-start | bytes 1310720 | tf_op jit(solution)/shard_map/all_to_all | solution.py:21
  18.8 5.6 %collective-permute-start.2 = (bf16[2,36,8,128]{3,2,1,0:T(8,128)(2,1)S(1)}, bf16[2,36,8,128]{3,2,1,0:T(8,128)(2,1)S(1)}, u32[]{:S(2)}, u32[]{:S(2)}) collective-permute-start(bf16[2,36,8,128]{3,2,1,0:T(8,128)(2,1)S(1)} %get-tuple-element.28), channel_id=1, source_target_pairs={{1,0},{2,1},{3,2},{4,3},{5,4},{6,5},{7,6},{9,8},{10,9},{11,10},{12... | collective-permute-start | bytes 442376 | tf_op jit(solution)/shard_map/ppermute | solution.py:488
  20.1 4.3 %collective-permute-start.3 = (bf16[2,36,8,128]{3,2,1,0:T(8,128)(2,1)S(1)}, bf16[2,36,8,128]{3,2,1,0:T(8,128)(2,1)S(1)}, u32[]{:S(2)}, u32[]{:S(2)}) collective-permute-start(bf16[2,36,8,128]{3,2,1,0:T(8,128)(2,1)S(1)} %get-tuple-element.29), channel_id=1, source_target_pairs={{0,1},{1,2},{2,3},{3,4},{4,5},{5,6},{6,7},{8,9},{9,10},{10,11},{11... | collective-permute-start | bytes 442376 | tf_op jit(solution)/shard_map/ppermute | solution.py:487
  38.7 0.8 copy-start.27
  40.5 4.1 %copy-start.29 = (bf16[3,3,1024,128]{3,2,1,0:T(8,128)(2,1)S(1)}, bf16[3,3,1024,128]{3,2,1,0:T(8,128)(2,1)}, u32[]{:S(2)}) copy-start(bf16[3,3,1024,128]{3,2,1,0:T(8,128)(2,1)} %param.13) | copy-start | bytes 7077892
  44.6 1.2 copy-start.28
  46.4 5.4 %copy-start.31 = (f32[32,128]{0,1:T(8,128)S(1)}, f32[32,128]{0,1:T(8,128)}, u32[]{:S(2)}) copy-start(f32[32,128]{0,1:T(8,128)} %convert_add_fusion) | copy-start | bytes 49156
  48.2 11.9 %all-to-all-start.1 = ((bf16[8,6,32,128]{3,2,1,0:T(8,128)(2,1)}), bf16[8,6,32,128]{3,2,1,0:T(8,128)(2,1)S(1)}, u32[]{:S(2)}, u32[]{:S(2)}) async-start(bf16[8,6,32,128]{3,2,1,0:T(8,128)(2,1)} %broadcast_in_dim.26), calls=%async_computation.1 | async-start | bytes 786432 | tf_op jit(solution)/shard_map/all_to_all | solution.py:21
  60.2 1.7 copy-start.30
  62.1 1.6 copy-start.32
  62.5 10.7 %copy-start.34 = (f32[16,128]{1,0:T(8,128)S(1)}, f32[16,128]{1,0:T(8,128)}, u32[]{:S(2)}) copy-start(f32[16,128]{1,0:T(8,128)} %param.19) | copy-start | bytes 24580
  62.5 15.9 %copy-start.17 = (bf16[3,3,128,128]{3,2,1,0:T(8,128)(2,1)S(1)}, bf16[3,3,128,128]{3,2,1,0:T(8,128)(2,1)}, u32[]{:S(2)}) copy-start(bf16[3,3,128,128]{3,2,1,0:T(8,128)(2,1)} %weight.7) | copy-start | bytes 884740
  69.9 8.5 %all-to-all-start.2 = ((f32[8,4,6,128]{3,1,2,0:T(4,128)}), f32[8,4,6,128]{3,1,2,0:T(4,128)S(1)}, u32[]{:S(2)}, u32[]{:S(2)}) async-start(f32[8,4,6,128]{3,1,2,0:T(4,128)} %constant_dynamic-update-slice_fusion), calls=%async_computation.2 | async-start | bytes 196608 | tf_op jit(solution)/shard_map/all_to_all | solution.py:554
  78.5 1.0 copy-start.11
  79.5 0.8 copy-start.21
  80.3 0.8 copy-start.22
  83.9 0.7 copy-start.20
  84.6 10.8 %all-to-all-start.3 = ((f32[32,8,128]{2,1,0:T(8,128)}), f32[32,8,128]{2,1,0:T(8,128)S(1)}, u32[]{:S(2)}, u32[]{:S(2)}) async-start(f32[32,8,128]{2,1,0:T(8,128)} %copy-done.20), calls=%async_computation.3 | async-start | bytes 262144 | tf_op jit(solution)/shard_map/all_to_all | solution.py:395
  87.1 0.9 copy-start.19
  88.1 1.0 copy-start.25
  91.7 1.1 copy-start.2
  95.4 1.4 copy-start.3
  98.8 1.1 copy-start.4
  100.0 1.1 copy-start.6
  101.1 0.9 copy-start.23
  102.0 11.5 %all-to-all-start.4 = ((f32[32,8,128]{2,1,0:T(8,128)}), f32[32,8,128]{2,1,0:T(8,128)S(1)}, u32[]{:S(2)}, u32[]{:S(2)}) async-start(f32[32,8,128]{2,1,0:T(8,128)} %get-tuple-element.20), calls=%async_computation.4 | async-start | bytes 262144 | tf_op jit(solution)/shard_map/all_to_all | solution.py:395
  105.4 1.1 copy-start.24
  106.5 1.0 copy-start.26
  107.5 11.2 %copy-start.5 = (f32[2800,128]{1,0:T(8,128)S(1)}, f32[2800,128]{1,0:T(8,128)}, u32[]{:S(2)}) copy-start(f32[2800,128]{1,0:T(8,128)} %copy-done.4) | copy-start | bytes 4300804
  111.7 0.7 copy-start.15
  113.5 0.7 copy-start.12
  114.1 16.6 %all-to-all-start.7 = ((bf16[32,40,128]{2,1,0:T(8,128)(2,1)}), bf16[32,40,128]{2,1,0:T(8,128)(2,1)S(1)}, u32[]{:S(2)}, u32[]{:S(2)}) async-start(bf16[32,40,128]{2,1,0:T(8,128)(2,1)} %copy-done.15), calls=%async_computation.7 | async-start | bytes 655360 | tf_op jit(solution)/shard_map/all_to_all | solution.py:395
  118.7 1.4 copy-start.7
  120.1 0.9 copy-start.13
  123.3 0.9 copy-start.8
  124.2 0.7 copy-start.16
  124.9 37.7 %copy-start.14 = (bf16[72,2816]{1,0:T(8,128)(2,1)S(1)}, bf16[72,2816]{1,0:T(8,128)(2,1)}, u32[]{:S(2)}) copy-start(bf16[72,2816]{1,0:T(8,128)(2,1)} %constant.59.clone.picked) | copy-start | bytes 1216516
  124.9 37.7 %copy-start.18 = (bf16[3,3,128,128]{3,2,1,0:T(8,128)(2,1)S(1)}, bf16[3,3,128,128]{3,2,1,0:T(8,128)(2,1)}, u32[]{:S(2)}) copy-start(bf16[3,3,128,128]{3,2,1,0:T(8,128)(2,1)} %weight.7) | copy-start | bytes 884740
  130.7 31.9 %copy-start.9 = (bf16[2816,128]{1,0:T(8,128)(2,1)S(1)}, bf16[2816,128]{1,0:T(8,128)(2,1)}, u32[]{:S(2)}) copy-start(bf16[2816,128]{1,0:T(8,128)(2,1)} %copy-done.8) | copy-start | bytes 2162692
  130.7 14.7 %all-to-all-start.5 = ((bf16[32,40,128]{2,1,0:T(8,128)(2,1)}), bf16[32,40,128]{2,1,0:T(8,128)(2,1)S(1)}, u32[]{:S(2)}, u32[]{:S(2)}) async-start(bf16[32,40,128]{2,1,0:T(8,128)(2,1)} %copy-done.16), calls=%async_computation.5 | async-start | bytes 655360 | tf_op jit(solution)/shard_map/all_to_all | solution.py:395
  145.4 14.6 %all-to-all-start.8 = ((bf16[32,40,128]{2,1,0:T(8,128)(2,1)}), bf16[32,40,128]{2,1,0:T(8,128)(2,1)S(1)}, u32[]{:S(2)}, u32[]{:S(2)}) async-start(bf16[32,40,128]{2,1,0:T(8,128)(2,1)} %shard_map.154), calls=%async_computation.8 | async-start | bytes 655360 | tf_op jit(solution)/shard_map/all_to_all | solution.py:395
  160.0 14.6 %all-to-all-start.6 = ((bf16[32,40,128]{2,1,0:T(8,128)(2,1)}), bf16[32,40,128]{2,1,0:T(8,128)(2,1)S(1)}, u32[]{:S(2)}, u32[]{:S(2)}) async-start(bf16[32,40,128]{2,1,0:T(8,128)(2,1)} %shard_map.152), calls=%async_computation.6 | async-start | bytes 655360 | tf_op jit(solution)/shard_map/all_to_all | solution.py:395

commit v4 on v3

--- a/solution.py
+++ b/solution.py
@@ -16,27 +16,9 @@
 norm_eps = 1e-05
 
 
-def spread_to(array, axis):
-    devices = lax.axis_size(axis)
-    return lax.all_to_all(jnp.broadcast_to(array, (devices, *array.shape)), axis, 0, 0)
-
-
-def conv_taps(padded, weight, row_count, col_count):
-    summed = jnp.zeros((row_count * col_count, weight.shape[3]), jnp.float32)
-    for tap_row in range(3):
-        for tap_col in range(3):
-            window = padded[tap_row : tap_row + row_count, tap_col : tap_col + col_count]
-            summed = summed + jnp.dot(
-                window.reshape(row_count * col_count, window.shape[2]),
-                weight[tap_row, tap_col],
-                preferred_element_type=jnp.float32,
-            )
-    return summed
-
-
 RIM = 8
 MARGIN = 16
-KERNEL_VMEM = 40 * 1024 * 1024
+KERNEL_VMEM = 20 * 1024 * 1024
 
 
 class Layout:
@@ -147,11 +129,16 @@
 
 
 def mixed_kernel(
-    main, top, bottom, strip, terms, weight, flat, act_out, stats, square, z0, z1, z2, *, lay
+    main, top, bottom, strip, coarse, pooled, valid, weight, flat, act_out, stats, square, terms, z0,
+    z1, z2, *, lay
 ):
     width = main.shape[2]
     flat[...] = jnp.zeros_like(flat)
     blocks = lay.cols // UPSCALE
+    near = coarse[0]
+    for c in range(1, coarse.shape[0]):
+        near = near + coarse[c]
+    terms[...] = near.astype(jnp.bfloat16).astype(jnp.float32) * valid[...] + pooled[...]
     for k in range(lay.rows + 5):
         base = MARGIN + k * lay.wide
         i = k - 3
@@ -277,7 +264,7 @@
                 a * width : (a + 1) * width, b * width : (b + 1) * width
             ]
     padded = sent_ref.shape[1]
-    for d in range(sent_ref.shape[0]):
+    for d in range(9 * width // chunk):
         sent_ref[d] = total_ref[d * chunk : d * chunk + padded].astype(jnp.bfloat16)
 
 
@@ -307,8 +294,8 @@
 
 
 def first_kernel(
-    stats, grad_stats, normed_ref, grad_ref, mixed, sent, kept, own, total, *, lay, grid, chunk,
-    pixel_total
+    stats, grad_stats, normed_ref, grad_ref, mixed, second, sent, kept, own, total, *, lay, grid,
+    chunk, pixel_total
 ):
     width = normed_ref.shape[1]
     _, inverse = act_moments(stats, pixel_total)
@@ -335,6 +322,8 @@
             own[pl.ds(place, lay.cols)] = value[: lay.cols].astype(jnp.float32)
 
     weight_matmul(mixed, own, total, sent, lay, chunk)
+    for d in range(second.shape[0]):
+        sent[second.shape[0] + d] = second[d]
 
 
 def coarse_kernel(kept, picked, main, weight, out, *, lay):
@@ -370,9 +359,11 @@
         sent[d] = total
 
 
-def join_kernel(received, out, *, chunk):
-    for d in range(received.shape[0]):
-        out[d * chunk : (d + 1) * chunk] = received[d].astype(jnp.float32)[:chunk]
+def join_kernel(received, first, second, *, chunk):
+    half = received.shape[0] // 2
+    for out, begin in ((first, 0), (second, half)):
+        for d in range(half):
+            out[d * chunk : (d + 1) * chunk] = received[begin + d].astype(jnp.float32)[:chunk]
 
 
 def window_picks(lay):
@@ -400,6 +391,162 @@
     rest = array - high.astype(jnp.float32)
     middle = rest.astype(jnp.bfloat16)
     return high, middle, (rest - middle.astype(jnp.float32)).astype(jnp.bfloat16)
+
+
+def lane_roll(value, shift):
+    return pltpu.roll(value, shift % value.shape[1], 1)
+
+
+def pack_kernel(features, labels, band, sent, sums):
+    encoder_width, tile_rows, tile_cols = features.shape
+    block_rows, block_cols = tile_rows // UPSCALE, tile_cols // UPSCALE
+    blocks = block_rows * block_cols
+    sums[...] = jnp.zeros_like(sums)
+    slot = lax.broadcasted_iota(jnp.int32, (blocks, tile_cols), 0)
+    column = lax.broadcasted_iota(jnp.int32, (blocks, tile_cols), 1)
+    total = jnp.zeros((blocks, 128), jnp.float32)
+    for r in range(block_rows):
+        sums[0:encoder_width] = jnp.sum(features[:, r * UPSCALE : (r + 1) * UPSCALE], 1)
+        sums[encoder_width : encoder_width + 1] = (
+            labels[r * UPSCALE : r * UPSCALE + 1].astype(jnp.float32) / UPSCALE
+        )
+        low = (slot - r * block_cols) * UPSCALE
+        picked = ((column >= low) & (column < low + UPSCALE)).astype(jnp.float32)
+        total = total + lax.dot_general(
+            picked,
+            sums[...],
+            (((1,), (1,)), ((), ())),
+            precision=lax.Precision.HIGHEST,
+            preferred_element_type=jnp.float32,
+        )
+    high, middle, low = pieces(total)
+    packed = (
+        high.astype(jnp.float32)
+        + lane_roll(middle.astype(jnp.float32), 32)
+        + lane_roll(low.astype(jnp.float32), 64)
+    )
+    value = jnp.concatenate([band[...].astype(jnp.float32), packed], 0).astype(jnp.bfloat16)
+    for d in range(sent.shape[0]):
+        sent[d] = value
+
+
+def pool_kernel(received, places, weight, pooled, valid, table, *, near, coarse):
+    block_rows, block_cols = near
+    coarse_rows, coarse_cols = coarse
+    encoder_width = weight.shape[0]
+    devices, rows, _ = received.shape
+    lane = lax.broadcasted_iota(jnp.int32, (8, 128), 1)
+    for d in range(devices):
+        packed = received[d].astype(jnp.float32)[rows - 8 :]
+        value = packed + lane_roll(packed, -32) + lane_roll(packed, -64)
+        table[d * 8 : (d + 1) * 8] = jnp.where(lane <= encoder_width, value, 0.0)
+    exact = dict(precision=lax.Precision.HIGHEST, preferred_element_type=jnp.float32)
+    row0 = lax.axis_index("rows") * block_rows - 1
+    col0 = lax.axis_index("cols") * block_cols - 2
+
+    def position(shape):
+        q = lax.broadcasted_iota(jnp.int32, shape, 0)
+        return row0 + (q >> 3), col0 + (q & 7)
+
+    count = pooled.shape[0]
+    row, col = position((count, devices * 8))
+    chosen = ((row == places[0:1]) & (col == places[1:2])).astype(jnp.float32)
+    mine = jnp.dot(chosen, table[...], **exact)[:, encoder_width : encoder_width + 1]
+    pick = (lane == encoder_width).astype(jnp.float32)
+    every = lax.dot_general(pick, table[...], (((1,), (1,)), ((), ())), **exact)[0:1]
+    same = (mine == every).astype(jnp.float32)
+    sums = jnp.dot(same, table[...], **exact)
+    members = jnp.sum(same, 1, keepdims=True) * float(UPSCALE * UPSCALE)
+    averages = sums / jnp.maximum(members, 1.0)
+    result = jnp.dot(averages[:, :encoder_width], weight[...], **exact)
+    row, col = position(pooled.shape)
+    inside = (row >= 0) & (row < coarse_rows) & (col >= 0) & (col < coarse_cols)
+    pooled[...] = jnp.where(inside, result, 0.0)
+    valid[...] = inside.astype(jnp.float32)
+
+
+def channel_conv(rows_ref, weight, shifted, out_rows, cols):
+    width = weight.shape[3]
+    count = out_rows * cols
+    sums = None
+    for a in range(3):
+        left = rows_ref[a * cols : a * cols + count]
+        if width % 128:
+            part = [
+                jnp.dot(left, weight[a, b], preferred_element_type=jnp.float32) for b in range(3)
+            ]
+        else:
+            right = jnp.concatenate([weight[a, b] for b in range(3)], 1)
+            part = jnp.dot(left, right, preferred_element_type=jnp.float32)
+            part = [part[:, b * width : (b + 1) * width] for b in range(3)]
+        sums = part if sums is None else [s + p for s, p in zip(sums, part)]
+    shifted[...] = jnp.zeros_like(shifted)
+    total = sums[1]
+    for b in (0, 2):
+        shifted[:, 8 : 8 + cols] = sums[b].reshape(out_rows, cols, width)
+        total = total + shifted[:, 7 + b : 7 + b + cols].reshape(count, width)
+    return total
+
+
+def hidden_kernel(source, weight, sent, rows_ref, shifted, kept, *, grid, band, direct):
+    row_devices, col_devices = grid
+    band_rows, cols = band
+    coarse_rows = row_devices * band_rows
+    width = weight.shape[3]
+    rows_ref[...] = jnp.zeros_like(rows_ref)
+    if direct:
+        for d in range(row_devices * col_devices):
+            r, c = d // col_devices, d % col_devices
+            begin = (1 + r * band_rows) * cols
+            rows_ref[begin : begin + band_rows * cols, c * width : (c + 1) * width] = source[
+                d, : band_rows * cols
+            ]
+    else:
+        rows_ref[cols : cols + coarse_rows * cols] = source[...]
+    raw = channel_conv(rows_ref, weight, shifted, coarse_rows, cols)
+    pixels = coarse_rows * cols
+    mean = jnp.sum(raw, 0, keepdims=True) / pixels
+    variance = jnp.sum(raw * raw, 0, keepdims=True) / pixels - mean * mean
+    hidden = jnp.maximum((raw - mean) * lax.rsqrt(variance + norm_eps), 0.0)
+    kept[...] = jnp.zeros_like(kept)
+    kept[2 : 2 + coarse_rows] = hidden.astype(jnp.bfloat16).reshape(coarse_rows, cols, width)
+    near = kept[pl.ds(lax.axis_index("rows") * band_rows, band_rows + 4)]
+    near = near.reshape((band_rows + 4) * cols, width)
+    for d in range(sent.shape[0]):
+        sent[d] = near
+
+
+def project_kernel(
+    received, weight, source, project, sent, rows_ref, shifted, residual, spread, *, grid, band,
+    direct
+):
+    row_devices, col_devices = grid
+    band_rows, cols = band
+    width = weight.shape[3]
+    my_col = lax.axis_index("cols")
+    for c in range(col_devices):
+        rows_ref[:, c * width : (c + 1) * width] = received[c]
+    raw = channel_conv(rows_ref, weight, shifted, band_rows + 2, cols)
+    count = (band_rows + 2) * cols
+    if direct:
+        residual[...] = jnp.zeros_like(residual)
+        for r in range(row_devices):
+            piece = source[r * col_devices + my_col, : band_rows * cols]
+            residual[1 + r * band_rows : 1 + (r + 1) * band_rows] = piece.reshape(
+                band_rows, cols, width
+            )
+        base = residual[pl.ds(lax.axis_index("rows") * band_rows, band_rows + 2)]
+        base = base.reshape(count, width)
+    else:
+        base = source[...]
+    result = (base.astype(jnp.float32) + raw).astype(jnp.bfloat16)
+    rows = project[pl.ds(pl.multiple_of(my_col * width, width), width)]
+    partial = jnp.dot(result, rows, preferred_element_type=jnp.float32)
+    spread[...] = jnp.zeros_like(spread)
+    spread[:, 8 : 8 + cols] = partial.reshape(band_rows + 2, cols, partial.shape[1])
+    step = cols // col_devices
+    for j in range(col_devices):
+        sent[j] = spread[:, 6 + j * step : 6 + j * step + sent.shape[2]]
 
 
 def per_device(
@@ -426,61 +573,30 @@
     blocks = block_rows * block_cols
     encoder_width = encoder_features.shape[0]
 
-    block_labels = instance_map[::UPSCALE, ::UPSCALE].reshape(-1)
-    block_sums = (
-        encoder_features.reshape(encoder_width, block_rows, UPSCALE, block_cols, UPSCALE)
-        .sum(axis=(2, 4))
-        .reshape(-1)
-    )
-    extra = jnp.concatenate([*pieces(block_sums), block_labels.astype(jnp.bfloat16)])
-    extra_rows = -(-extra.shape[0] // 2048) * 16
-    extra = jnp.pad(extra, (0, extra_rows * 128 - extra.shape[0])).reshape(extra_rows, 128)
-    packed = jnp.concatenate([global_in.reshape(-1, 128), extra])
-    everything = spread_to(packed, BOTH)
-    main_rows = packed.shape[0] - extra_rows
-    gathered = everything[:, :main_rows].reshape(
-        row_devices, col_devices, band_rows, band_cols, width_share
-    )
-    tail = everything[:, main_rows:].reshape(devices, -1)
-    sums = blocks * encoder_width
-    all_sums = sum(tail[:, k * sums : (k + 1) * sums].astype(jnp.float32) for k in (2, 1, 0))
-    all_sums = (
-        all_sums.reshape(row_devices, col_devices, encoder_width, block_rows, block_cols)
-        .transpose(0, 3, 1, 4, 2)
-        .reshape(-1, encoder_width)
-    )
-    all_labels = (
-        tail[:, 3 * sums : 3 * sums + blocks]
-        .reshape(row_devices, col_devices, block_rows, block_cols)
-        .transpose(0, 2, 1, 3)
-    )
-    label_map = jnp.pad(
-        all_labels.reshape(coarse_rows, band_cols), 1, constant_values=-1.0
-    )
-    near_labels = lax.dynamic_slice(
-        label_map,
-        (my_row * block_rows, my_col * block_cols),
-        (block_rows + 2, block_cols + 2),
-    ).reshape(-1)
-    same = (near_labels[:, None] == all_labels.reshape(-1)[None, :]).astype(jnp.float32)
-    near_sums = jnp.dot(same, all_sums, precision=lax.Precision.HIGHEST)
-    near_counts = jnp.sum(same, 1, keepdims=True) * float(UPSCALE * UPSCALE)
-    pooled = jnp.dot(
-        near_sums / jnp.maximum(near_counts, 1.0),
-        instance_weight,
-        precision=lax.Precision.HIGHEST,
-    ).reshape(block_rows + 2, block_cols + 2, local_width)
+    lay = Layout(tile_rows, tile_cols)
+    width = local_width
+    grid = (row_devices, col_devices)
+    band = (band_rows, band_cols)
+    direct = width_share == 128
+    main = global_in.reshape(-1, 128)
+    main_rows = main.shape[0]
+    sent_input = call(
+        pack_kernel,
+        jax.ShapeDtypeStruct((devices, main_rows + 8, 128), jnp.bfloat16),
+        (encoder_features, instance_map, main),
+        [pltpu.VMEM((128, tile_cols), jnp.float32)],
+    )
+    tops = jnp.stack([enhancer_input[-2:], output_cotangent[-2:]])
+    bottoms = jnp.stack([enhancer_input[:2], output_cotangent[:2]])
+    sent_input, tops, bottoms = lax.optimization_barrier((sent_input, tops, bottoms))
+    everything = to_all(sent_input, BOTH)
 
     row_up = [(i, i + 1) for i in range(row_devices - 1)]
     row_down = [(j, i) for i, j in row_up]
     col_up = [(i, i + 1) for i in range(col_devices - 1)]
     col_down = [(j, i) for i, j in col_up]
-    top = lax.ppermute(
-        jnp.stack([enhancer_input[-2:], output_cotangent[-2:]]), "rows", row_up
-    )
-    bottom = lax.ppermute(
-        jnp.stack([enhancer_input[:2], output_cotangent[:2]]), "rows", row_down
-    )
+    top = lax.ppermute(tops, "rows", row_up)
+    bottom = lax.ppermute(bottoms, "rows", row_down)
     both = jnp.stack([enhancer_input, output_cotangent])
     tall_last = jnp.concatenate([top[:, :, -RIM:], both[:, :, -RIM:], bottom[:, :, -RIM:]], 1)
     tall_first = jnp.concatenate([top[:, :, :RIM], both[:, :, :RIM], bottom[:, :, :RIM]], 1)
@@ -493,11 +609,8 @@
         ],
         2,
     )
-    lay = Layout(tile_rows, tile_cols)
-    width = local_width
-    grid = (row_devices, col_devices)
     pixel_total = float(tile_rows * tile_cols * devices)
-    chunk = 9 * width // devices
+    chunk = 18 * width // devices
     padded_chunk = -(-chunk // 8) * 8
     square = pltpu.VMEM((3 * width, 3 * width), jnp.bfloat16)
     z = [pltpu.VMEM((lay.z, width), jnp.float32)] * 3
@@ -507,6 +620,7 @@
     out_shape = jax.ShapeDtypeStruct((lay.out, width), jnp.float32)
     stats_shape = jax.ShapeDtypeStruct((devices, 8, width), jnp.float32)
     sent_shape = jax.ShapeDtypeStruct((devices, padded_chunk, width), jnp.bfloat16)
+    half_shape = jax.ShapeDtypeStruct((devices // 2, padded_chunk, width), jnp.bfloat16)
     conv_flops = 18 * width * width * lay.out
 
     act_grad = call(
@@ -518,56 +632,73 @@
         lay=lay,
     )
 
-    whole_in = gathered.transpose(0, 2, 3, 1, 4).reshape(coarse_rows, band_cols, -1)
-    rimmed = jnp.pad(whole_in, ((1, 1), (1, 1), (0, 0)))
-    first_raw = conv_taps(rimmed, global_first, coarse_rows, band_cols)
-    band_total = coarse_rows * band_cols
-    band_mean = jnp.sum(first_raw, 0) / band_total
-    band_var = jnp.sum(first_raw * first_raw, 0) / band_total - band_mean * band_mean
-    normed = (first_raw - band_mean) * lax.rsqrt(band_var + norm_eps)
-    hidden = (
-        jnp.maximum(normed, 0.0).astype(jnp.bfloat16).reshape(coarse_rows, band_cols, width_share)
-    )
-    hidden = jnp.pad(hidden, ((2, 2), (0, 0), (0, 0)))
-    near_hidden = lax.dynamic_slice_in_dim(hidden, my_row * band_rows, band_rows + 4, 0)
-    near_hidden = spread_to(near_hidden, "cols")
-    near_hidden = near_hidden.transpose(1, 2, 0, 3).reshape(band_rows + 4, band_cols, -1)
-    second_raw = conv_taps(
-        jnp.pad(near_hidden, ((0, 0), (1, 1), (0, 0))), global_second, band_rows + 2, band_cols
-    )
-    mine = lax.dynamic_index_in_dim(gathered, my_col, 1, keepdims=False)
-    mine = jnp.pad(
-        mine.reshape(coarse_rows, band_cols, width_share), ((1, 1), (0, 0), (0, 0))
-    )
-    near_in = lax.dynamic_slice_in_dim(mine, my_row * band_rows, band_rows + 2, 0)
-    global_out = (
-        near_in.astype(jnp.float32).reshape(-1, width_share) + second_raw
-    ).astype(jnp.bfloat16)
-    weight_rows = lax.dynamic_slice_in_dim(project_weight, my_col * width_share, width_share, 0)
-    partial = jnp.dot(global_out, weight_rows, preferred_element_type=jnp.float32)
-    partial = jnp.pad(
-        partial.reshape(band_rows + 2, band_cols, local_width), ((0, 0), (1, 1), (0, 0))
-    )
-    outgoing = jnp.stack(
-        [partial[:, j * block_cols : (j + 1) * block_cols + 2] for j in range(col_devices)]
-    )
-    incoming = lax.all_to_all(outgoing, "cols", 0, 0)
-    coarse = jnp.sum(incoming, 0).astype(jnp.bfloat16)
-
-    block_terms = coarse.astype(jnp.float32) + pooled
-    row_ids = my_row * block_rows - 1 + jnp.arange(block_rows + 2)
-    col_ids = my_col * block_cols - 1 + jnp.arange(block_cols + 2)
-    inside = ((row_ids >= 0) & (row_ids < coarse_rows))[:, None] & (
-        (col_ids >= 0) & (col_ids < band_cols)
-    )[None, :]
-    terms = jnp.where(inside[:, :, None], block_terms, 0.0)
-    terms = jnp.pad(terms, ((0, 0), (1, 1), (0, 0)))
+    place = np.arange(devices * blocks)
+    owner, slot = place // blocks, place % blocks
+    places = np.zeros((8, devices * blocks), np.int32)
+    places[0] = owner // col_devices * block_rows + slot // block_cols
+    places[1] = owner % col_devices * block_cols + slot % block_cols
+    near_shape = jax.ShapeDtypeStruct(((block_rows + 2) * 8, width), jnp.float32)
+    pooled, valid = call(
+        pool_kernel,
+        (near_shape, near_shape),
+        (everything, jnp.asarray(places), instance_weight),
+        [pltpu.VMEM((devices * 8, 128), jnp.float32)],
+        near=(block_rows, block_cols),
+        coarse=(coarse_rows, band_cols),
+    )
+    channels = width_share * col_devices
+    if direct:
+        source = base = everything
+    else:
+        gathered = everything[:, :main_rows].reshape(
+            row_devices, col_devices, band_rows, band_cols, width_share
+        )
+        source = gathered.transpose(0, 2, 3, 1, 4).reshape(coarse_rows * band_cols, channels)
+        mine = lax.dynamic_index_in_dim(gathered, my_col, 1, keepdims=False)
+        mine = jnp.pad(
+            mine.reshape(coarse_rows, band_cols, width_share), ((1, 1), (0, 0), (0, 0))
+        )
+        base = lax.dynamic_slice_in_dim(mine, my_row * band_rows, band_rows + 2, 0)
+        base = base.reshape(-1, width_share)
+    near_rows = band_rows + 4
+    sent_hidden = call(
+        hidden_kernel,
+        jax.ShapeDtypeStruct((col_devices, near_rows * band_cols, width_share), jnp.bfloat16),
+        (source, global_first),
+        [
+            pltpu.VMEM(((coarse_rows + 2) * band_cols, channels), jnp.bfloat16),
+            pltpu.VMEM((coarse_rows, band_cols + 16, width_share), jnp.float32),
+            pltpu.VMEM((coarse_rows + 4, band_cols, width_share), jnp.bfloat16),
+        ],
+        18 * coarse_rows * band_cols * channels * width_share,
+        grid=grid,
+        band=band,
+        direct=direct,
+    )
+    near_hidden = to_all(sent_hidden, "cols")
+    sent_coarse = call(
+        project_kernel,
+        jax.ShapeDtypeStruct((col_devices, band_rows + 2, 8, width), jnp.float32),
+        (near_hidden, global_second, base, project_weight),
+        [
+            pltpu.VMEM((near_rows * band_cols, channels), jnp.bfloat16),
+            pltpu.VMEM((band_rows + 2, band_cols + 16, width_share), jnp.float32),
+            pltpu.VMEM((coarse_rows + 2, band_cols, width_share), jnp.bfloat16),
+            pltpu.VMEM((band_rows + 2, band_cols + 16, width), jnp.float32),
+        ],
+        18 * (band_rows + 2) * band_cols * channels * width_share,
+        grid=grid,
+        band=band,
+        direct=direct,
+    )
+    near_coarse = to_all(sent_coarse, "cols")
+    terms = (near_coarse, pooled.reshape(-1, 8, width), valid.reshape(-1, 8, width))
 
     mixed, first_act, stats = call(
         mixed_kernel,
         (flat_shape, out_shape, stats_shape),
-        (enhancer_input, top[0], bottom[0], strip[0], terms, enhancer_first),
-        [square, *z],
+        (enhancer_input, top[0], bottom[0], strip[0], *terms, enhancer_first),
+        [square, pltpu.VMEM((block_rows + 2, 8, width), jnp.float32), *z],
         conv_flops,
         lay=lay,
     )
@@ -583,18 +714,17 @@
     grad_stats = to_all(grad_stats, BOTH)
     enhanced, second_sent = call(
         second_kernel,
-        (jax.ShapeDtypeStruct((tile_rows, tile_cols, width), jnp.bfloat16), sent_shape),
+        (jax.ShapeDtypeStruct((tile_rows, tile_cols, width), jnp.bfloat16), half_shape),
         (activated, mixed, output_cotangent, enhancer_second),
         [square, *z, own, total],
         2 * conv_flops,
         lay=lay,
         chunk=chunk,
     )
-    second_part = to_all(second_sent, BOTH)
-    first_sent, kept = call(
+    sent_both, kept = call(
         first_kernel,
         (sent_shape, jax.ShapeDtypeStruct((lay.kept, width), jnp.bfloat16)),
-        (stats, grad_stats, normed_act, normed_grad, mixed),
+        (stats, grad_stats, normed_act, normed_grad, mixed, second_sent),
         [own, total],
         conv_flops,
         lay=lay,
@@ -602,9 +732,8 @@
         chunk=chunk,
         pixel_total=pixel_total,
     )
-    first_part = to_all(first_sent, BOTH)
+    part = to_all(sent_both, BOTH)
     rescale = 1.0 / math.sqrt(pixel_total)
-    second_share = to_all(call(share_kernel, sent_shape, (second_part,), rescale=rescale), BOTH)
     global_gradient = call(
         coarse_kernel,
         jax.ShapeDtypeStruct((blocks, width), jnp.float32),
@@ -612,10 +741,11 @@
         (),
         lay=lay,
     )
-    first_share = to_all(call(share_kernel, sent_shape, (first_part,), rescale=rescale), BOTH)
+    share = to_all(call(share_kernel, sent_shape, (part,), rescale=rescale), BOTH)
     whole_shape = jax.ShapeDtypeStruct((9 * width, width), jnp.float32)
-    second_total = call(join_kernel, whole_shape, (second_share,), chunk=chunk)
-    first_total = call(join_kernel, whole_shape, (first_share,), chunk=chunk)
+    first_total, second_total = call(
+        join_kernel, (whole_shape, whole_shape), (share,), chunk=chunk
+    )
     return (
         enhanced,
         first_total.reshape(3, 3, width, width),

time: 177 us -> 148 us (0.84)
  waiting for transfers between devices: 64.3 us -> 33.9 us
  blocking collectives: 0 us -> 22.2 us
  local copies, waits for them, and re-layouts: 39.1 us -> 25 us
  matrix products: 6.09 us -> 0 us
  Pallas kernels: 19.3 us -> 23.7 us
  starting transfers between devices: 43 us -> 38.6 us
    all_to_all x3 -> x0, waiting for transfers between devices: 23.3 us -> none  [the longest x2 18.4 us: spread_to(): lax.all_to_all(jnp.broadcast_to(array, (devices, *array.shape)), axis, 0, 0)]
    all_to_all x0 -> x1, blocking collectives: none -> 22.2 us  [to_all(): return lax.all_to_all(payload, axis, 0, 0)]
    all_to_all x3 -> x0, starting transfers between devices: 13.8 us -> none  [the longest x2 10.5 us: spread_to(): lax.all_to_all(jnp.broadcast_to(array, (devices, *array.shape)), axis, 0, 0)]
    all_to_all x6, waiting for transfers between devices: 41 us -> 27.2 us  [to_all(): return lax.all_to_all(payload, axis, 0, 0)]
    all_to_all x6, starting transfers between devices: 18.5 us -> 28.6 us  [to_all(): return lax.all_to_all(payload, axis, 0, 0)]
    ppermute x2, waiting for transfers between devices: 0.01 us -> 6.64 us  [the longest x1 6.64 us: per_device(): top = lax.ppermute(tops, 'rows', row_up)]
    dot_general x20 -> x0, matrix products: 6.09 us -> none  [the longest x17 4.33 us: conv_taps(): jnp.dot(window.reshape(row_count * col_count, window.shape[2]), weight[ta...]
    slice x10 -> x0, local copies, waits for them, and re-layouts: 5.1 us -> none  [the longest x6 4.93 us: conv_taps(): window = padded[tap_row:tap_row + row_count, tap_col:tap_col + col_count]]
  transfers between devices with their start and end apart: 13 -> 10, of which waited for: 9 -> 6; matrix products, arithmetic and copies ran while one was open for 4% -> 3% of each run, Pallas kernels for 8% -> 7%
where the time goes in v4:
time: 148 us; the launch traced here: 147 us
  starting transfers between devices  38.6 us (26%)
  waiting for transfers between devices  33.9 us (23%)
  local copies, waits for them, and re-layouts  25 us (17%)
  Pallas kernels  23.7 us (16%)
  blocking collectives  22.2 us (15%)
  other arithmetic  2.51 us (2%)
    all_to_all x6, starting transfers between devices, to_all(): return lax.all_to_all(payload, axis, 0, 0)  28.6 us
    all_to_all x6, waiting for transfers between devices, to_all(): return lax.all_to_all(payload, axis, 0, 0)  27.2 us
    pallas_call x12, Pallas kernels, call(): pl.pallas_call(functools.partial(body, **fixed), out_shape=outs, in_specs...  23.7 us
    all_to_all x1, blocking collectives, to_all(): return lax.all_to_all(payload, axis, 0, 0)  22.2 us
    unnamed x70, local copies, waits for them, and re-layouts  21 us
    ppermute x1, waiting for transfers between devices, per_device(): top = lax.ppermute(tops, 'rows', row_up)  6.64 us
    ppermute x1, starting transfers between devices, per_device(): left = lax.ppermute(tall_last, 'cols', col_up)  3.7 us
    ppermute x1, starting transfers between devices, per_device(): top = lax.ppermute(tops, 'rows', row_up)  3.68 us
  transfers between devices with their start and end apart: 10, of which 6 were waited for; matrix products, arithmetic and copies ran while one was open for 3% of the time, Pallas kernels for 7%

profile of v4, /device:TPU:0, one launch (start us, length us, event | category | flops | bytes accessed | tf_op | source)
XLA Modules:
  0.0 146.8 jit_solution(6642710326768886444)
XLA Ops:
  0.6 0.0 copy-start.13
  0.6 0.0 copy-start
  0.7 0.9 slice_bitcast_fusion.7
  1.5 0.8 slice_bitcast_fusion.6
  2.3 0.9 copy-done.22
  3.3 0.7 copy-done.26
  4.0 0.7 copy-done.27
  4.7 1.3 shard_map.156
  6.0 7.3 %all-to-all-start = ((bf16[32,72,128]{2,1,0:T(8,128)(2,1)}), bf16[32,72,128]{2,1,0:T(8,128)(2,1)S(1)}, u32[]{:S(2)}, u32[]{:S(2)}) async-start(bf16[32,72,128]{2,1,0:T(8,128)(2,1)} %shard_map.156), calls=%async_computation | async-start | bytes 1179648 | tf_op jit(solution)/shard_map/all_to_all | solution.py:386
  13.3 3.7 %collective-permute-start = (bf16[2,2,64,128]{3,2,1,0:T(8,128)(2,1)S(1)}, bf16[2,2,64,128]{3,2,1,0:T(8,128)(2,1)S(1)}, u32[]{:S(2)}, u32[]{:S(2)}) collective-permute-start(bf16[2,2,64,128]{3,2,1,0:T(8,128)(2,1)S(1)} %get-tuple-element.22), channel_id=1, source_target_pairs={{0,8},{8,16},{16,24},{1,9},{9,17},{17,25},{2,10},{10,18},{18,26},{... | collective-permute-start | bytes 196616 | tf_op jit(solution)/shard_map/ppermute | solution.py:598
  17.0 1.3 collective-permute-start.1
  18.3 6.6 %collective-permute-done = bf16[2,2,64,128]{3,2,1,0:T(8,128)(2,1)S(1)} collective-permute-done((bf16[2,2,64,128]{3,2,1,0:T(8,128)(2,1)S(1)}, bf16[2,2,64,128]{3,2,1,0:T(8,128)(2,1)S(1)}, u32[]{:S(2)}, u32[]{:S(2)}) %collective-permute-start) | collective-permute-done | bytes 65568 | tf_op jit(solution)/shard_map/ppermute | solution.py:598
  24.9 0.6 copy-done.34
  25.6 0.7 fusion.6
  26.3 1.3 collective-permute-start.2
  27.6 3.7 %collective-permute-start.3 = (bf16[2,36,8,128]{3,2,1,0:T(8,128)(2,1)}, bf16[2,36,8,128]{3,2,1,0:T(8,128)(2,1)}, u32[]{:S(2)}, u32[]{:S(2)}) collective-permute-start(bf16[2,36,8,128]{3,2,1,0:T(8,128)(2,1)} %get-tuple-element.41), channel_id=1, source_target_pairs={{0,1},{1,2},{2,3},{3,4},{4,5},{5,6},{6,7},{8,9},{9,10},{10,11},{11... | collective-permute-start | bytes 442376 | tf_op jit(solution)/shard_map/ppermute | solution.py:603
  31.3 0.0 copy-start.2
  31.3 1.7 %copy-done.2 = bf16[3,3,1024,128]{3,2,1,0:T(8,128)(2,1)S(1)} copy-done((bf16[3,3,1024,128]{3,2,1,0:T(8,128)(2,1)S(1)}, bf16[3,3,1024,128]{3,2,1,0:T(8,128)(2,1)}, u32[]{:S(2)}) %copy-start.2) | copy-done | bytes 2359320
  33.0 1.1 shard_map.157
  34.1 0.0 copy-start.3
  34.1 0.7 copy-done.3
  34.9 4.1 %all-to-all-start.1 = ((bf16[8,192,128]{2,1,0:T(8,128)(2,1)}), bf16[8,192,128]{2,1,0:T(8,128)(2,1)}, u32[]{:S(2)}, u32[]{:S(2)}) async-start(bf16[8,192,128]{2,1,0:T(8,128)(2,1)} %copy-done.3), calls=%async_computation.1 | async-start | bytes 786432 | tf_op jit(solution)/shard_map/all_to_all | solution.py:386
  39.0 1.4 slice_bitcast_fusion.2
  40.4 1.8 %fusion.2 = bf16[2,37,16,128]{3,2,1,0:T(8,128)(2,1)} fusion(bf16[2,36,8,128]{3,2,1,0:T(8,128)(2,1)} %collective-permute-done.3, bf16[2,36,8,128]{3,2,1,0:T(8,128)(2,1)} %collective-permute-done.2), kind=kLoop, calls=%fused_computation.4 | loop fusion | flops 1212416 | bytes 598016 | tf_op jit(solution)/shard_map/concatenate | solution.py:605
  42.1 5.2 %all-to-all-done.1.received = bf16[8,192,128]{2,1,0:T(8,128)(2,1)} async-done(((bf16[8,192,128]{2,1,0:T(8,128)(2,1)}), bf16[8,192,128]{2,1,0:T(8,128)(2,1)}, u32[]{:S(2)}, u32[]{:S(2)}) %all-to-all-start.1) | async-done | bytes 393248 | tf_op jit(solution)/shard_map/all_to_all | solution.py:386
  47.3 0.9 copy-done.21
  48.3 1.8 %shard_map.158 = f32[8,4,8,128]{3,2,1,0:T(8,128)S(1)} custom-call(bf16[8,192,128]{2,1,0:T(8,128)(2,1)} %all-to-all-done.1.received, bf16[3,3,1024,128]{3,2,1,0:T(8,128)(2,1)S(1)} %copy-done.1, bf16[32,72,128]{2,1,0:T(8,128)(2,1)S(1)} %all-to-all-done.source.received, bf16[1024,128]{1,0:T(8,128)(2,1)S(1)} %copy-done.21), custom_call_target="tpu_custom_call" | custom-call | flops 301989888 | bytes 4194304 | tf_op jit(solution)/shard_map/pallas_call | solution.py:41
  50.1 0.0 copy-start.15
  50.1 0.6 copy-done.15
  50.7 3.5 %all-to-all-start.2 = ((f32[8,4,8,128]{3,2,1,0:T(8,128)}), f32[8,4,8,128]{3,2,1,0:T(8,128)S(1)}, u32[]{:S(2)}, u32[]{:S(2)}) async-start(f32[8,4,8,128]{3,2,1,0:T(8,128)} %copy-done.15), calls=%async_computation.2 | async-start | bytes 262144 | tf_op jit(solution)/shard_map/all_to_all | solution.py:386
  54.2 1.0 slice_bitcast_fusion
  55.3 0.8 shard_map.159
  56.1 3.6 %all-to-all-done.2.coarse = f32[8,4,8,128]{3,2,1,0:T(8,128)S(1)} async-done(((f32[8,4,8,128]{3,2,1,0:T(8,128)}), f32[8,4,8,128]{3,2,1,0:T(8,128)S(1)}, u32[]{:S(2)}, u32[]{:S(2)}) %all-to-all-start.2) | async-done | bytes 131104 | tf_op jit(solution)/shard_map/all_to_all | solution.py:386
  59.7 3.5 %shard_map.160 = (bf16[3072,128]{1,0:T(8,128)(2,1)S(1)}, f32[2800,128]{1,0:T(8,128)S(1)}, f32[32,8,128]{2,1,0:T(8,128)}) custom-call(bf16[32,64,128]{2,1,0:T(8,128)(2,1)S(1)} %copy-done.14, bf16[2,64,128]{2,1,0:T(8,128)(2,1)S(1)} %get-tuple-element.51.top, bf16[2,64,128]{2,1,0:T(8,128)(2,1)S(1)} %copy-done.25, ...), custom_call_target="tpu_custom_call" | custom-call | flops 825753600 | bytes 4194304 | tf_op jit(solution)/shard_map/pallas_call | solution.py:41
  63.3 0.9 copy-done.8
  64.1 7.1 %all-to-all-start.3 = ((f32[32,8,128]{2,1,0:T(8,128)}), f32[32,8,128]{2,1,0:T(8,128)S(1)}, u32[]{:S(2)}, u32[]{:S(2)}) async-start(f32[32,8,128]{2,1,0:T(8,128)} %get-tuple-element.28), calls=%async_computation.3 | async-start | bytes 262144 | tf_op jit(solution)/shard_map/all_to_all | solution.py:386
  71.3 0.0 copy-start.32
  71.3 1.0 copy-done.32
  72.2 2.6 %shard_map.161.act_grad = f32[2800,128]{1,0:T(8,128)S(1)} custom-call(bf16[32,64,128]{2,1,0:T(8,128)(2,1)S(1)} %copy-done, bf16[2,64,128]{2,1,0:T(8,128)(2,1)S(1)} %get-tuple-element.50.top, bf16[2,64,128]{2,1,0:T(8,128)(2,1)S(1)} %copy-done.24, bf16[37,16,128]{2,1,0:T(8,128)(2,1)S(1)} %get-tuple-element.46.strip, bf16[3,3,128,128]{3,2,1,0:T(8,128)(2,1)S(1)} %copy-done.32), custom_call_target="tpu_custom_call" | custom-call | flops 825753600 | bytes 4194304 | tf_op jit(solution)/shard_map/pallas_call | solution.py:41
  74.9 1.1 copy-done.6
  76.0 3.5 %all-to-all-done.3.stats = f32[32,8,128]{2,1,0:T(8,128)S(1)} async-done(((f32[32,8,128]{2,1,0:T(8,128)}), f32[32,8,128]{2,1,0:T(8,128)S(1)}, u32[]{:S(2)}, u32[]{:S(2)}) %all-to-all-start.3) | async-done | bytes 131104 | tf_op jit(solution)/shard_map/all_to_all | solution.py:386
  79.5 1.4 copy-done.7
  80.8 1.4 shard_map.162
  82.3 1.1 copy-done.4
  83.4 0.7 copy-done.23
  84.1 0.9 copy-done.30
  84.9 3.3 %all-to-all-start.4 = ((f32[32,8,128]{2,1,0:T(8,128)}), f32[32,8,128]{2,1,0:T(8,128)}, u32[]{:S(2)}, u32[]{:S(2)}) async-start(f32[32,8,128]{2,1,0:T(8,128)} %copy-done.23), calls=%async_computation.4 | async-start | bytes 262144 | tf_op jit(solution)/shard_map/all_to_all | solution.py:386
  88.3 1.1 copy-done.9
  89.4 1.1 copy-done.31
  90.5 1.0 copy-done.33
  91.5 4.1 %shard_map.163 = (bf16[32,64,128]{2,1,0:T(8,128)(2,1)}, bf16[16,72,128]{2,1,0:T(8,128)(2,1)S(1)}) custom-call(bf16[3072,128]{1,0:T(8,128)(2,1)S(1)} %copy-done.31, bf16[3072,128]{1,0:T(8,128)(2,1)S(1)} %copy-done.9, bf16[32,64,128]{2,1,0:T(8,128)(2,1)S(1)} %copy-done, bf16[3,3,128,128]{3,2,1,0:T(8,128)(2,1)S(1)} %copy-done.33), custom_call_target="tpu_custom_call" | custom-call | flops 1651507200 | bytes 4194304 | tf_op jit(solution)/shard_map/pallas_call | solution.py:41
  95.6 0.0 copy-start.17
  95.6 0.7 copy-done.17
  96.3 0.1 all-to-all-done.4.grad_stats
  96.5 1.1 copy-done.10
  97.6 1.0 copy-done.18
  98.6 3.1 %shard_map.164 = (bf16[32,72,128]{2,1,0:T(8,128)(2,1)S(1)}, bf16[2816,128]{1,0:T(8,128)(2,1)S(1)}) custom-call(f32[32,8,128]{2,1,0:T(8,128)S(1)} %all-to-all-done.3.stats, f32[32,8,128]{2,1,0:T(8,128)} %all-to-all-done.4.grad_stats, f32[2800,128]{1,0:T(8,128)S(1)} %get-tuple-element.33.normed_ref, f32[2800,128]{1,0:T(8,128)S(1)} %copy-done.5, ...), custom_call_target="tpu_custom_call" | custom-call | flops 825753600 | bytes 4194304 | tf_op jit(solution)/shard_map/pallas_call | solution.py:41
  101.7 0.9 copy-done.11
  102.6 22.2 %all_to_all.35.received = bf16[32,72,128]{2,1,0:T(8,128)(2,1)S(1)} all-to-all(bf16[32,72,128]{2,1,0:T(8,128)(2,1)S(1)} %get-tuple-element.36), channel_id=1, replica_groups=mesh['rows'=4,'cols'=8] {'rows','cols'}, dimensions={0} | all-to-all | bytes 1179648 | tf_op jit(solution)/shard_map/all_to_all | solution.py:386
  124.8 0.9 shard_map.165
  125.7 3.3 %all-to-all-start.6 = ((bf16[32,72,128]{2,1,0:T(8,128)(2,1)}), bf16[32,72,128]{2,1,0:T(8,128)(2,1)S(1)}, u32[]{:S(2)}, u32[]{:S(2)}) async-start(bf16[32,72,128]{2,1,0:T(8,128)(2,1)} %shard_map.165), calls=%async_computation.6 | async-start | bytes 1179648 | tf_op jit(solution)/shard_map/all_to_all | solution.py:386
  129.0 1.9 %shard_map.167 = f32[8,128]{1,0:T(8,128)} custom-call(bf16[2816,128]{1,0:T(8,128)(2,1)S(1)} %copy-done.12, bf16[72,2816]{1,0:T(8,128)(2,1)S(1)} %copy-done.16, bf16[32,64,128]{2,1,0:T(8,128)(2,1)S(1)} %copy-done, bf16[3,3,128,128]{3,2,1,0:T(8,128)(2,1)S(1)} %copy-done.20), custom_call_target="tpu_custom_call" | custom-call | bytes 4194304 | tf_op jit(solution)/shard_map/pallas_call | solution.py:41
  130.9 14.8 %all-to-all-done.6.received = bf16[32,72,128]{2,1,0:T(8,128)(2,1)S(1)} async-done(((bf16[32,72,128]{2,1,0:T(8,128)(2,1)}), bf16[32,72,128]{2,1,0:T(8,128)(2,1)S(1)}, u32[]{:S(2)}, u32[]{:S(2)}) %all-to-all-start.6) | async-done | bytes 589856 | tf_op jit(solution)/shard_map/all_to_all | solution.py:386
  145.7 1.0 shard_map.166
  (49 shorter events, 0.1 us)
Async XLA Ops:
  0.6 24.9 %copy-start.13 = (bf16[32,64,128]{2,1,0:T(8,128)(2,1)S(1)}, bf16[32,64,128]{2,1,0:T(8,128)(2,1)}, u32[]{:S(2)}) copy-start(bf16[32,64,128]{2,1,0:T(8,128)(2,1)} %main.4) | copy-start | bytes 1572868
  0.6 24.9 %copy-start = (bf16[32,64,128]{2,1,0:T(8,128)(2,1)S(1)}, bf16[32,64,128]{2,1,0:T(8,128)(2,1)}, u32[]{:S(2)}) copy-start(bf16[32,64,128]{2,1,0:T(8,128)(2,1)} %main.7) | copy-start | bytes 1572868
  2.3 0.9 copy-start.22
  3.3 0.7 copy-start.26
  4.0 0.7 copy-start.27
  6.0 25.3 %all-to-all-start = ((bf16[32,72,128]{2,1,0:T(8,128)(2,1)}), bf16[32,72,128]{2,1,0:T(8,128)(2,1)S(1)}, u32[]{:S(2)}, u32[]{:S(2)}) async-start(bf16[32,72,128]{2,1,0:T(8,128)(2,1)} %shard_map.156), calls=%async_computation | async-start | bytes 1179648 | tf_op jit(solution)/shard_map/all_to_all | solution.py:386
  13.3 11.6 %collective-permute-start = (bf16[2,2,64,128]{3,2,1,0:T(8,128)(2,1)S(1)}, bf16[2,2,64,128]{3,2,1,0:T(8,128)(2,1)S(1)}, u32[]{:S(2)}, u32[]{:S(2)}) collective-permute-start(bf16[2,2,64,128]{3,2,1,0:T(8,128)(2,1)S(1)} %get-tuple-element.22), channel_id=1, source_target_pairs={{0,8},{8,16},{16,24},{1,9},{9,17},{17,25},{2,10},{10,18},{18,26},{... | collective-permute-start | bytes 196616 | tf_op jit(solution)/shard_map/ppermute | solution.py:598
  17.0 7.9 %collective-permute-start.1 = (bf16[2,2,64,128]{3,2,1,0:T(8,128)(2,1)S(1)}, bf16[2,2,64,128]{3,2,1,0:T(8,128)(2,1)S(1)}, u32[]{:S(2)}, u32[]{:S(2)}) collective-permute-start(bf16[2,2,64,128]{3,2,1,0:T(8,128)(2,1)S(1)} %get-tuple-element.23), channel_id=1, source_target_pairs={{8,0},{16,8},{24,16},{9,1},{17,9},{25,17},{10,2},{18,10},{26,18},{... | collective-permute-start | bytes 196616 | tf_op jit(solution)/shard_map/ppermute | solution.py:599
  24.9 0.6 copy-start.34
  26.3 14.1 %collective-permute-start.2 = (bf16[2,36,8,128]{3,2,1,0:T(8,128)(2,1)}, bf16[2,36,8,128]{3,2,1,0:T(8,128)(2,1)}, u32[]{:S(2)}, u32[]{:S(2)}) collective-permute-start(bf16[2,36,8,128]{3,2,1,0:T(8,128)(2,1)} %get-tuple-element.40), channel_id=1, source_target_pairs={{1,0},{2,1},{3,2},{4,3},{5,4},{6,5},{7,6},{9,8},{10,9},{11,10},{12... | collective-permute-start | bytes 442376 | tf_op jit(solution)/shard_map/ppermute | solution.py:604
  27.6 12.8 %collective-permute-start.3 = (bf16[2,36,8,128]{3,2,1,0:T(8,128)(2,1)}, bf16[2,36,8,128]{3,2,1,0:T(8,128)(2,1)}, u32[]{:S(2)}, u32[]{:S(2)}) collective-permute-start(bf16[2,36,8,128]{3,2,1,0:T(8,128)(2,1)} %get-tuple-element.41), channel_id=1, source_target_pairs={{0,1},{1,2},{2,3},{3,4},{4,5},{5,6},{6,7},{8,9},{9,10},{10,11},{11... | collective-permute-start | bytes 442376 | tf_op jit(solution)/shard_map/ppermute | solution.py:603
  31.3 1.7 %copy-start.2 = (bf16[3,3,1024,128]{3,2,1,0:T(8,128)(2,1)S(1)}, bf16[3,3,1024,128]{3,2,1,0:T(8,128)(2,1)}, u32[]{:S(2)}) copy-start(bf16[3,3,1024,128]{3,2,1,0:T(8,128)(2,1)} %weight.7) | copy-start | bytes 7077892
  33.0 14.4 %copy-start.1 = (bf16[3,3,1024,128]{3,2,1,0:T(8,128)(2,1)S(1)}, bf16[3,3,1024,128]{3,2,1,0:T(8,128)(2,1)}, u32[]{:S(2)}) copy-start(bf16[3,3,1024,128]{3,2,1,0:T(8,128)(2,1)} %weight.8) | copy-start | bytes 7077892
  34.1 0.7 copy-start.3
  34.9 12.5 %all-to-all-start.1 = ((bf16[8,192,128]{2,1,0:T(8,128)(2,1)}), bf16[8,192,128]{2,1,0:T(8,128)(2,1)}, u32[]{:S(2)}, u32[]{:S(2)}) async-start(bf16[8,192,128]{2,1,0:T(8,128)(2,1)} %copy-done.3), calls=%async_computation.1 | async-start | bytes 786432 | tf_op jit(solution)/shard_map/all_to_all | solution.py:386
  47.3 1.0 copy-start.21
  48.3 7.0 %copy-start.28 = (f32[16,128]{1,0:T(8,128)S(1)}, f32[16,128]{1,0:T(8,128)}, u32[]{:S(2)}) copy-start(f32[16,128]{1,0:T(8,128)} %weight.9) | copy-start | bytes 24580
  48.3 7.0 %copy-start.29 = (s32[8,256]{1,0:T(8,128)S(1)}, s32[8,256]{1,0:T(8,128)}, u32[]{:S(2)}) copy-start(s32[8,256]{1,0:T(8,128)} %constant.7.clone.places) | copy-start | bytes 24580
  50.1 0.7 copy-start.15
  50.7 9.0 %copy-start.14 = (bf16[32,64,128]{2,1,0:T(8,128)(2,1)S(1)}, bf16[32,64,128]{2,1,0:T(8,128)(2,1)}, u32[]{:S(2)}) copy-start(bf16[32,64,128]{2,1,0:T(8,128)(2,1)} %main.4) | copy-start | bytes 1572868
  50.7 9.0 %copy-start.19 = (bf16[3,3,128,128]{3,2,1,0:T(8,128)(2,1)S(1)}, bf16[3,3,128,128]{3,2,1,0:T(8,128)(2,1)}, u32[]{:S(2)}) copy-start(bf16[3,3,128,128]{3,2,1,0:T(8,128)(2,1)} %weight.13) | copy-start | bytes 884740
  50.7 9.0 %copy-start.25 = (bf16[2,64,128]{2,1,0:T(8,128)(2,1)S(1)}, bf16[2,64,128]{2,1,0:T(8,128)(2,1)}, u32[]{:S(2)}) copy-start(bf16[2,64,128]{2,1,0:T(8,128)(2,1)} %get-tuple-element.49.bottom) | copy-start | bytes 98308
  50.7 9.0 %all-to-all-start.2 = ((f32[8,4,8,128]{3,2,1,0:T(8,128)}), f32[8,4,8,128]{3,2,1,0:T(8,128)S(1)}, u32[]{:S(2)}, u32[]{:S(2)}) async-start(f32[8,4,8,128]{3,2,1,0:T(8,128)} %copy-done.15), calls=%async_computation.2 | async-start | bytes 262144 | tf_op jit(solution)/shard_map/all_to_all | solution.py:386
  59.7 11.5 %copy-start.24 = (bf16[2,64,128]{2,1,0:T(8,128)(2,1)S(1)}, bf16[2,64,128]{2,1,0:T(8,128)(2,1)}, u32[]{:S(2)}) copy-start(bf16[2,64,128]{2,1,0:T(8,128)(2,1)} %get-tuple-element.48.bottom) | copy-start | bytes 98308
  63.2 0.9 copy-start.8
  64.1 15.3 %all-to-all-start.3 = ((f32[32,8,128]{2,1,0:T(8,128)}), f32[32,8,128]{2,1,0:T(8,128)S(1)}, u32[]{:S(2)}, u32[]{:S(2)}) async-start(f32[32,8,128]{2,1,0:T(8,128)} %get-tuple-element.28), calls=%async_computation.3 | async-start | bytes 262144 | tf_op jit(solution)/shard_map/all_to_all | solution.py:386
  71.3 1.0 copy-start.32
  74.9 1.1 copy-start.6
  79.5 1.4 copy-start.7
  82.3 1.1 copy-start.4
  83.4 0.7 copy-start.23
  84.1 0.9 copy-start.30
  84.9 11.5 %all-to-all-start.4 = ((f32[32,8,128]{2,1,0:T(8,128)}), f32[32,8,128]{2,1,0:T(8,128)}, u32[]{:S(2)}, u32[]{:S(2)}) async-start(f32[32,8,128]{2,1,0:T(8,128)} %copy-done.23), calls=%async_computation.4 | async-start | bytes 262144 | tf_op jit(solution)/shard_map/all_to_all | solution.py:386
  88.3 1.1 copy-start.9
  89.4 1.1 copy-start.31
  90.5 1.0 copy-start.33
  91.5 5.0 %copy-start.5 = (f32[2800,128]{1,0:T(8,128)S(1)}, f32[2800,128]{1,0:T(8,128)}, u32[]{:S(2)}) copy-start(f32[2800,128]{1,0:T(8,128)} %copy-done.4) | copy-start | bytes 4300804
  95.6 0.7 copy-start.17
  96.5 1.1 copy-start.10
  97.6 1.0 copy-start.18
  101.7 0.9 copy-start.11
  124.8 4.2 %copy-start.12 = (bf16[2816,128]{1,0:T(8,128)(2,1)S(1)}, bf16[2816,128]{1,0:T(8,128)(2,1)}, u32[]{:S(2)}) copy-start(bf16[2816,128]{1,0:T(8,128)(2,1)} %copy-done.11) | copy-start | bytes 2162692
  124.8 4.2 %copy-start.16 = (bf16[72,2816]{1,0:T(8,128)(2,1)S(1)}, bf16[72,2816]{1,0:T(8,128)(2,1)}, u32[]{:S(2)}) copy-start(bf16[72,2816]{1,0:T(8,128)(2,1)} %constant.8.clone.picked) | copy-start | bytes 1216516
  124.8 4.2 %copy-start.20 = (bf16[3,3,128,128]{3,2,1,0:T(8,128)(2,1)S(1)}, bf16[3,3,128,128]{3,2,1,0:T(8,128)(2,1)}, u32[]{:S(2)}) copy-start(bf16[3,3,128,128]{3,2,1,0:T(8,128)(2,1)} %weight.13) | copy-start | bytes 884740
  125.7 20.0 %all-to-all-start.6 = ((bf16[32,72,128]{2,1,0:T(8,128)(2,1)}), bf16[32,72,128]{2,1,0:T(8,128)(2,1)S(1)}, u32[]{:S(2)}, u32[]{:S(2)}) async-start(bf16[32,72,128]{2,1,0:T(8,128)(2,1)} %shard_map.165), calls=%async_computation.6 | async-start | bytes 1179648 | tf_op jit(solution)/shard_map/all_to_all | solution.py:386

commit v5 on v4

--- a/solution.py
+++ b/solution.py
@@ -359,11 +359,20 @@
         sent[d] = total
 
 
-def join_kernel(received, first, second, *, chunk):
-    half = received.shape[0] // 2
-    for out, begin in ((first, 0), (second, half)):
-        for d in range(half):
-            out[d * chunk : (d + 1) * chunk] = received[begin + d].astype(jnp.float32)[:chunk]
+def join_kernel(mine, other, first, second, *, chunk, grid):
+    row_devices, col_devices = grid
+    half, pairs = row_devices * col_devices // 2, col_devices // 2
+    core = lax.axis_index("cols") & 1
+    for k in range(2):
+
+        @pl.when(core == k)
+        def _():
+            for source, side in ((mine, k), (other, 1 - k)):
+                for d in range(half):
+                    owner = d // pairs * col_devices + d % pairs * 2 + side
+                    out = first if owner < half else second
+                    begin = owner % half * chunk
+                    out[begin : begin + chunk] = source[d].astype(jnp.float32)[:chunk]
 
 
 def window_picks(lay):
@@ -386,6 +395,16 @@
     return lax.all_to_all(payload, axis, 0, 0)
 
 
+def from_all(payload, row_devices, col_devices):
+    groups = [
+        [r * col_devices + 2 * h + k for r in range(row_devices) for h in range(col_devices // 2)]
+        for k in range(2)
+    ]
+    mine = lax.all_to_all(payload, BOTH, 0, 0, axis_index_groups=groups)
+    swap = [(c, c ^ 1) for c in range(col_devices)]
+    return mine, lax.ppermute(mine, "cols", swap)
+
+
 def pieces(array):
     high = array.astype(jnp.bfloat16)
     rest = array - high.astype(jnp.float32)
@@ -430,14 +449,16 @@
         sent[d] = value
 
 
-def pool_kernel(received, places, weight, pooled, valid, table, *, near, coarse):
+def pool_kernel(mine_ref, other_ref, places, weight, pooled, valid, table, *, near, coarse):
     block_rows, block_cols = near
     coarse_rows, coarse_cols = coarse
     encoder_width = weight.shape[0]
-    devices, rows, _ = received.shape
+    half, rows, _ = mine_ref.shape
+    devices = 2 * half
     lane = lax.broadcasted_iota(jnp.int32, (8, 128), 1)
     for d in range(devices):
-        packed = received[d].astype(jnp.float32)[rows - 8 :]
+        part = mine_ref[d] if d < half else other_ref[d - half]
+        packed = part.astype(jnp.float32)[rows - 8 :]
         value = packed + lane_roll(packed, -32) + lane_roll(packed, -64)
         table[d * 8 : (d + 1) * 8] = jnp.where(lane <= encoder_width, value, 0.0)
     exact = dict(precision=lax.Precision.HIGHEST, preferred_element_type=jnp.float32)
@@ -450,7 +471,9 @@
 
     count = pooled.shape[0]
     row, col = position((count, devices * 8))
-    chosen = ((row == places[0:1]) & (col == places[1:2])).astype(jnp.float32)
+    core = lax.axis_index("cols") & 1
+    column = places[1:2] + block_cols * jnp.where(places[2:3] == 1, core, 1 - core)
+    chosen = ((row == places[0:1]) & (col == column)).astype(jnp.float32)
     mine = jnp.dot(chosen, table[...], **exact)[:, encoder_width : encoder_width + 1]
     pick = (lane == encoder_width).astype(jnp.float32)
     every = lax.dot_general(pick, table[...], (((1,), (1,)), ((), ())), **exact)[0:1]
@@ -488,21 +511,24 @@
     return total
 
 
-def hidden_kernel(source, weight, sent, rows_ref, shifted, kept, *, grid, band, direct):
+def hidden_kernel(mine, other, weight, sent, rows_ref, shifted, kept, *, grid, band, direct):
     row_devices, col_devices = grid
     band_rows, cols = band
     coarse_rows = row_devices * band_rows
     width = weight.shape[3]
     rows_ref[...] = jnp.zeros_like(rows_ref)
     if direct:
-        for d in range(row_devices * col_devices):
-            r, c = d // col_devices, d % col_devices
-            begin = (1 + r * band_rows) * cols
-            rows_ref[begin : begin + band_rows * cols, c * width : (c + 1) * width] = source[
-                d, : band_rows * cols
-            ]
+        pairs = col_devices // 2
+        core = lax.axis_index("cols") & 1
+        for source, side in ((mine, core), (other, 1 - core)):
+            for d in range(row_devices * pairs):
+                begin = (1 + d // pairs * band_rows) * cols
+                lanes = pl.multiple_of((d % pairs * 2 + side) * width, width)
+                rows_ref[begin : begin + band_rows * cols, pl.ds(lanes, width)] = source[
+                    d, : band_rows * cols
+                ]
     else:
-        rows_ref[cols : cols + coarse_rows * cols] = source[...]
+        rows_ref[cols : cols + coarse_rows * cols] = mine[...]
     raw = channel_conv(rows_ref, weight, shifted, coarse_rows, cols)
     pixels = coarse_rows * cols
     mean = jnp.sum(raw, 0, keepdims=True) / pixels
@@ -531,7 +557,7 @@
     if direct:
         residual[...] = jnp.zeros_like(residual)
         for r in range(row_devices):
-            piece = source[r * col_devices + my_col, : band_rows * cols]
+            piece = source[r * (col_devices // 2) + (my_col >> 1), : band_rows * cols]
             residual[1 + r * band_rows : 1 + (r + 1) * band_rows] = piece.reshape(
                 band_rows, cols, width
             )
@@ -582,14 +608,16 @@
     main_rows = main.shape[0]
     sent_input = call(
         pack_kernel,
-        jax.ShapeDtypeStruct((devices, main_rows + 8, 128), jnp.bfloat16),
+        jax.ShapeDtypeStruct((devices // 2, main_rows + 8, 128), jnp.bfloat16),
         (encoder_features, instance_map, main),
         [pltpu.VMEM((128, tile_cols), jnp.float32)],
     )
-    tops = jnp.stack([enhancer_input[-2:], output_cotangent[-2:]])
-    bottoms = jnp.stack([enhancer_input[:2], output_cotangent[:2]])
-    sent_input, tops, bottoms = lax.optimization_barrier((sent_input, tops, bottoms))
-    everything = to_all(sent_input, BOTH)
+    mine, other = from_all(sent_input, row_devices, col_devices)
+    late_input, late_cotangent, _ = lax.optimization_barrier(
+        (enhancer_input, output_cotangent, sent_input)
+    )
+    tops = jnp.stack([late_input[-2:], late_cotangent[-2:]])
+    bottoms = jnp.stack([late_input[:2], late_cotangent[:2]])
 
     row_up = [(i, i + 1) for i in range(row_devices - 1)]
     row_down = [(j, i) for i, j in row_up]
@@ -597,18 +625,6 @@
     col_down = [(j, i) for i, j in col_up]
     top = lax.ppermute(tops, "rows", row_up)
     bottom = lax.ppermute(bottoms, "rows", row_down)
-    both = jnp.stack([enhancer_input, output_cotangent])
-    tall_last = jnp.concatenate([top[:, :, -RIM:], both[:, :, -RIM:], bottom[:, :, -RIM:]], 1)
-    tall_first = jnp.concatenate([top[:, :, :RIM], both[:, :, :RIM], bottom[:, :, :RIM]], 1)
-    left = lax.ppermute(tall_last, "cols", col_up)
-    right = lax.ppermute(tall_first, "cols", col_down)
-    strip = jnp.concatenate(
-        [
-            jnp.pad(right, ((0, 0), (1, 0), (0, 0), (0, 0))),
-            jnp.pad(left, ((0, 0), (0, 1), (0, 0), (0, 0))),
-        ],
-        2,
-    )
     pixel_total = float(tile_rows * tile_cols * devices)
     chunk = 18 * width // devices
     padded_chunk = -(-chunk // 8) * 8
@@ -623,48 +639,44 @@
     half_shape = jax.ShapeDtypeStruct((devices // 2, padded_chunk, width), jnp.bfloat16)
     conv_flops = 18 * width * width * lay.out
 
-    act_grad = call(
-        cot_kernel,
-        out_shape,
-        (output_cotangent, top[1], bottom[1], strip[1], enhancer_second),
-        [pltpu.VMEM((lay.flat, width), jnp.bfloat16), square, *z],
-        conv_flops,
-        lay=lay,
-    )
-
     place = np.arange(devices * blocks)
-    owner, slot = place // blocks, place % blocks
+    owner, slot = place // blocks % (devices // 2), place % blocks
+    pairs = col_devices // 2
     places = np.zeros((8, devices * blocks), np.int32)
-    places[0] = owner // col_devices * block_rows + slot // block_cols
-    places[1] = owner % col_devices * block_cols + slot % block_cols
+    places[0] = owner // pairs * block_rows + slot // block_cols
+    places[1] = owner % pairs * 2 * block_cols + slot % block_cols
+    places[2] = place // blocks < devices // 2
     near_shape = jax.ShapeDtypeStruct(((block_rows + 2) * 8, width), jnp.float32)
     pooled, valid = call(
         pool_kernel,
         (near_shape, near_shape),
-        (everything, jnp.asarray(places), instance_weight),
+        (mine, other, jnp.asarray(places), instance_weight),
         [pltpu.VMEM((devices * 8, 128), jnp.float32)],
         near=(block_rows, block_cols),
         coarse=(coarse_rows, band_cols),
     )
     channels = width_share * col_devices
     if direct:
-        source = base = everything
+        sources, base = (mine, other), mine
     else:
-        gathered = everything[:, :main_rows].reshape(
+        even = my_col % 2 == 0
+        sides = [jnp.where(even, mine, other), jnp.where(even, other, mine)]
+        gathered = jnp.stack([side[:, :main_rows] for side in sides], 1).reshape(
             row_devices, col_devices, band_rows, band_cols, width_share
         )
         source = gathered.transpose(0, 2, 3, 1, 4).reshape(coarse_rows * band_cols, channels)
-        mine = lax.dynamic_index_in_dim(gathered, my_col, 1, keepdims=False)
-        mine = jnp.pad(
-            mine.reshape(coarse_rows, band_cols, width_share), ((1, 1), (0, 0), (0, 0))
-        )
-        base = lax.dynamic_slice_in_dim(mine, my_row * band_rows, band_rows + 2, 0)
+        sources = (source, source)
+        column = lax.dynamic_index_in_dim(gathered, my_col, 1, keepdims=False)
+        column = jnp.pad(
+            column.reshape(coarse_rows, band_cols, width_share), ((1, 1), (0, 0), (0, 0))
+        )
+        base = lax.dynamic_slice_in_dim(column, my_row * band_rows, band_rows + 2, 0)
         base = base.reshape(-1, width_share)
     near_rows = band_rows + 4
     sent_hidden = call(
         hidden_kernel,
         jax.ShapeDtypeStruct((col_devices, near_rows * band_cols, width_share), jnp.bfloat16),
-        (source, global_first),
+        (*sources, global_first),
         [
             pltpu.VMEM(((coarse_rows + 2) * band_cols, channels), jnp.bfloat16),
             pltpu.VMEM((coarse_rows, band_cols + 16, width_share), jnp.float32),
@@ -676,6 +688,30 @@
         direct=direct,
     )
     near_hidden = to_all(sent_hidden, "cols")
+    late_input, late_cotangent, top, bottom, _ = lax.optimization_barrier(
+        (enhancer_input, output_cotangent, top, bottom, sent_hidden)
+    )
+    both = jnp.stack([late_input, late_cotangent])
+    tall_last = jnp.concatenate([top[:, :, -RIM:], both[:, :, -RIM:], bottom[:, :, -RIM:]], 1)
+    tall_first = jnp.concatenate([top[:, :, :RIM], both[:, :, :RIM], bottom[:, :, :RIM]], 1)
+    left = lax.ppermute(tall_last, "cols", col_up)
+    right = lax.ppermute(tall_first, "cols", col_down)
+    strip = jnp.concatenate(
+        [
+            jnp.pad(right, ((0, 0), (1, 0), (0, 0), (0, 0))),
+            jnp.pad(left, ((0, 0), (0, 1), (0, 0), (0, 0))),
+        ],
+        2,
+    )
+    act_grad = call(
+        cot_kernel,
+        out_shape,
+        (output_cotangent, top[1], bottom[1], strip[1], enhancer_second),
+        [pltpu.VMEM((lay.flat, width), jnp.bfloat16), square, *z],
+        conv_flops,
+        lay=lay,
+    )
+
     sent_coarse = call(
         project_kernel,
         jax.ShapeDtypeStruct((col_devices, band_rows + 2, 8, width), jnp.float32),
@@ -741,10 +777,11 @@
         (),
         lay=lay,
     )
-    share = to_all(call(share_kernel, sent_shape, (part,), rescale=rescale), BOTH)
+    share = call(share_kernel, half_shape, (part,), rescale=rescale)
+    shares = from_all(share, row_devices, col_devices)
     whole_shape = jax.ShapeDtypeStruct((9 * width, width), jnp.float32)
     first_total, second_total = call(
-        join_kernel, (whole_shape, whole_shape), (share,), chunk=chunk
+        join_kernel, (whole_shape, whole_shape), shares, chunk=chunk, grid=grid
     )
     return (
         enhanced,

time: 148 us -> 143 us (0.966)
  waiting for transfers between devices: 33.9 us -> 20.7 us
  blocking collectives: 22.2 us -> 35.3 us
  starting transfers between devices: 38.6 us -> 33.3 us
  local copies, waits for them, and re-layouts: 25 us -> 26.5 us
    all_to_all x6 -> x4, waiting for transfers between devices: 27.2 us -> 10 us  [to_all(): return lax.all_to_all(payload, axis, 0, 0)]
    all_to_all x0 -> x1, blocking collectives: none -> 14.9 us  [from_all(): mine = lax.all_to_all(payload, BOTH, 0, 0, axis_index_groups=groups)]
    all_to_all x6 -> x4, starting transfers between devices: 28.6 us -> 16.4 us  [to_all(): return lax.all_to_all(payload, axis, 0, 0)]
    all_to_all x0 -> x1, waiting for transfers between devices: none -> 10.7 us  [from_all(): mine = lax.all_to_all(payload, BOTH, 0, 0, axis_index_groups=groups)]
    all_to_all x0 -> x1, starting transfers between devices: none -> 8.31 us  [from_all(): mine = lax.all_to_all(payload, BOTH, 0, 0, axis_index_groups=groups)]
    ppermute x1, waiting for transfers between devices: 6.64 us -> 0.01 us  [per_device(): top = lax.ppermute(tops, 'rows', row_up)]
    all_to_all x1, blocking collectives: 22.2 us -> 20.4 us  [to_all(): return lax.all_to_all(payload, axis, 0, 0)]
    unnamed x70 -> x64, local copies, waits for them, and re-layouts: 21 us -> 21.6 us
  transfers between devices with their start and end apart: 10 -> 11, of which waited for: 6 -> 4; matrix products, arithmetic and copies ran while one was open for 3% -> 5% of each run, Pallas kernels for 7% -> 8%
where the time goes in v5:
time: 143 us; the launch traced here: 142 us
  blocking collectives  35.3 us (25%)
  starting transfers between devices  33.3 us (23%)
  local copies, waits for them, and re-layouts  26.5 us (19%)
  Pallas kernels  23.3 us (16%)
  waiting for transfers between devices  20.7 us (14%)
  other arithmetic  1.69 us (1%)
    pallas_call x12, Pallas kernels, call(): pl.pallas_call(functools.partial(body, **fixed), out_shape=outs, in_specs...  23.3 us
    unnamed x64, local copies, waits for them, and re-layouts  21.6 us
    all_to_all x1, blocking collectives, to_all(): return lax.all_to_all(payload, axis, 0, 0)  20.4 us
    all_to_all x4, starting transfers between devices, to_all(): return lax.all_to_all(payload, axis, 0, 0)  16.4 us
    all_to_all x1, blocking collectives, from_all(): mine = lax.all_to_all(payload, BOTH, 0, 0, axis_index_groups=groups)  14.9 us
    all_to_all x1, waiting for transfers between devices, from_all(): mine = lax.all_to_all(payload, BOTH, 0, 0, axis_index_groups=groups)  10.7 us
    all_to_all x4, waiting for transfers between devices, to_all(): return lax.all_to_all(payload, axis, 0, 0)  10 us
    all_to_all x1, starting transfers between devices, from_all(): mine = lax.all_to_all(payload, BOTH, 0, 0, axis_index_groups=groups)  8.31 us
  transfers between devices with their start and end apart: 11, of which 4 were waited for; matrix products, arithmetic and copies ran while one was open for 5% of the time, Pallas kernels for 8%

profile of v5, /device:TPU:0, one launch (start us, length us, event | category | flops | bytes accessed | tf_op | source)
XLA Modules:
  0.0 141.8 jit_solution(12436010360639082653)
XLA Ops:
  0.6 0.9 copy-done.14
  1.6 0.7 copy-done.18
  2.3 0.7 copy-done.19
  3.0 1.2 shard_map.156
  4.2 8.3 %all-to-all-start = ((bf16[16,72,128]{2,1,0:T(8,128)(2,1)}), bf16[16,72,128]{2,1,0:T(8,128)(2,1)S(1)}, u32[]{:S(2)}, u32[]{:S(2)}) async-start(bf16[16,72,128]{2,1,0:T(8,128)(2,1)} %shard_map.156), calls=%async_computation | async-start | bytes 589824 | tf_op jit(solution)/shard_map/all_to_all | solution.py:403
  12.5 10.7 %all-to-all-done.mine.source.mine_ref = bf16[16,72,128]{2,1,0:T(8,128)(2,1)S(1)} async-done(((bf16[16,72,128]{2,1,0:T(8,128)(2,1)}), bf16[16,72,128]{2,1,0:T(8,128)(2,1)S(1)}, u32[]{:S(2)}, u32[]{:S(2)}) %all-to-all-start) | async-done | bytes 294944 | tf_op jit(solution)/shard_map/all_to_all | solution.py:403
  23.2 0.8 slice_bitcast_fusion.6
  24.0 2.9 %collective-permute-start = (bf16[2,2,64,128]{3,2,1,0:T(8,128)(2,1)S(1)}, bf16[2,2,64,128]{3,2,1,0:T(8,128)(2,1)S(1)}, u32[]{:S(2)}, u32[]{:S(2)}) collective-permute-start(bf16[2,2,64,128]{3,2,1,0:T(8,128)(2,1)S(1)} %pad_maximum_fusion.2), channel_id=1, source_target_pairs={{0,8},{8,16},{16,24},{1,9},{9,17},{17,25},{2,10},{10,18},{18,26},{... | collective-permute-start | bytes 196616 | tf_op jit(solution)/shard_map/ppermute | solution.py:626
  26.9 0.0 copy-start
  26.9 1.4 %collective-permute-start.1 = (bf16[2,2,64,128]{3,2,1,0:T(8,128)(2,1)S(1)}, bf16[2,2,64,128]{3,2,1,0:T(8,128)(2,1)S(1)}, u32[]{:S(2)}, u32[]{:S(2)}) collective-permute-start(bf16[2,2,64,128]{3,2,1,0:T(8,128)(2,1)S(1)} %pad_maximum_fusion.3), channel_id=1, source_target_pairs={{8,0},{16,8},{24,16},{9,1},{17,9},{25,17},{10,2},{18,10},{26,18},{... | collective-permute-start | bytes 196616 | tf_op jit(solution)/shard_map/ppermute | solution.py:627
  28.4 0.0 copy-start.1
  28.4 1.7 %copy-done.1 = bf16[3,3,1024,128]{3,2,1,0:T(8,128)(2,1)S(1)} copy-done((bf16[3,3,1024,128]{3,2,1,0:T(8,128)(2,1)S(1)}, bf16[3,3,1024,128]{3,2,1,0:T(8,128)(2,1)}, u32[]{:S(2)}) %copy-start.1) | copy-done | bytes 2359320
  30.0 1.9 %shard_map.157 = bf16[8,192,128]{2,1,0:T(8,128)(2,1)} custom-call(bf16[16,72,128]{2,1,0:T(8,128)(2,1)S(1)} %all-to-all-done.mine.source.mine_ref, bf16[16,72,128]{2,1,0:T(8,128)(2,1)S(1)} %collective-permute-done.2.other.other_ref, bf16[3,3,1024,128]{3,2,1,0:T(8,128)(2,1)S(1)} %copy-done.1), custom_call_target="tpu_custom_call" | custom-call | flops 603979776 | bytes 4194304 | tf_op jit(solution)/shard_map/pallas_call | solution.py:41
  31.9 4.2 %all-to-all-start.1 = ((bf16[8,192,128]{2,1,0:T(8,128)(2,1)}), bf16[8,192,128]{2,1,0:T(8,128)(2,1)}, u32[]{:S(2)}, u32[]{:S(2)}) async-start(bf16[8,192,128]{2,1,0:T(8,128)(2,1)} %shard_map.157), calls=%async_computation.1 | async-start | bytes 786432 | tf_op jit(solution)/shard_map/all_to_all | solution.py:395
  36.2 0.0 copy-start.31
  36.2 0.6 copy-done.31
  36.8 0.6 copy-done.30
  37.5 0.9 slice_bitcast_fusion.3
  38.4 0.7 fusion.8
  39.1 0.9 fusion.6
  40.0 1.3 collective-permute-start.3
  41.3 3.0 %collective-permute-start.4 = (bf16[2,36,8,128]{3,2,1,0:T(8,128)(2,1)S(1)}, bf16[2,36,8,128]{3,2,1,0:T(8,128)(2,1)S(1)}, u32[]{:S(2)}, u32[]{:S(2)}) collective-permute-start(bf16[2,36,8,128]{3,2,1,0:T(8,128)(2,1)S(1)} %get-tuple-element.47), channel_id=1, source_target_pairs={{0,1},{1,2},{2,3},{3,4},{4,5},{5,6},{6,7},{8,9},{9,10},{10,11},{11... | collective-permute-start | bytes 442376 | tf_op jit(solution)/shard_map/ppermute | solution.py:697
  44.4 0.8 shard_map.159
  45.2 0.6 copy-done.26
  45.8 0.6 copy-done.28
  46.4 1.4 slice_bitcast_fusion.2
  47.8 0.8 fusion.2
  48.6 0.9 copy-done.15
  49.5 1.8 %shard_map.158 = f32[8,4,8,128]{3,2,1,0:T(8,128)S(1)} custom-call(bf16[8,192,128]{2,1,0:T(8,128)(2,1)} %all-to-all-done.1.received, bf16[3,3,1024,128]{3,2,1,0:T(8,128)(2,1)S(1)} %copy-done.2, bf16[16,72,128]{2,1,0:T(8,128)(2,1)S(1)} %all-to-all-done.mine.source.mine_ref, bf16[1024,128]{1,0:T(8,128)(2,1)S(1)} %copy-done.15), custom_call_target="tpu_custom_call" | custom-call | flops 301989888 | bytes 4194304 | tf_op jit(solution)/shard_map/pallas_call | solution.py:41
  51.3 0.0 copy-start.10
  51.3 0.6 copy-done.10
  52.0 5.9 %all-to-all-start.2 = ((f32[8,4,8,128]{3,2,1,0:T(8,128)}), f32[8,4,8,128]{3,2,1,0:T(8,128)S(1)}, u32[]{:S(2)}, u32[]{:S(2)}) async-start(f32[8,4,8,128]{3,2,1,0:T(8,128)} %copy-done.10), calls=%async_computation.2 | async-start | bytes 262144 | tf_op jit(solution)/shard_map/all_to_all | solution.py:395
  57.8 1.0 slice_bitcast_fusion
  58.9 4.5 %all-to-all-done.2.coarse = f32[8,4,8,128]{3,2,1,0:T(8,128)S(1)} async-done(((f32[8,4,8,128]{3,2,1,0:T(8,128)}), f32[8,4,8,128]{3,2,1,0:T(8,128)S(1)}, u32[]{:S(2)}, u32[]{:S(2)}) %all-to-all-start.2) | async-done | bytes 131104 | tf_op jit(solution)/shard_map/all_to_all | solution.py:395
  63.4 1.0 copy-done.9
  64.4 1.0 copy-done.12
  65.4 0.8 copy-done.17
  66.1 0.7 copy-done.29
  66.9 3.5 %shard_map.160 = (bf16[3072,128]{1,0:T(8,128)(2,1)S(1)}, f32[2800,128]{1,0:T(8,128)S(1)}, f32[32,8,128]{2,1,0:T(8,128)}) custom-call(bf16[32,64,128]{2,1,0:T(8,128)(2,1)S(1)} %copy-done.9, bf16[2,64,128]{2,1,0:T(8,128)(2,1)S(1)} %get-tuple-element.57.top, bf16[2,64,128]{2,1,0:T(8,128)(2,1)S(1)} %copy-done.17, ...), custom_call_target="tpu_custom_call" | custom-call | flops 825753600 | bytes 4194304 | tf_op jit(solution)/shard_map/pallas_call | solution.py:41
  70.4 3.7 %all-to-all-start.3 = ((f32[32,8,128]{2,1,0:T(8,128)}), f32[32,8,128]{2,1,0:T(8,128)S(1)}, u32[]{:S(2)}, u32[]{:S(2)}) async-start(f32[32,8,128]{2,1,0:T(8,128)} %get-tuple-element.34), calls=%async_computation.3 | async-start | bytes 262144 | tf_op jit(solution)/shard_map/all_to_all | solution.py:395
  74.1 0.0 copy-start.24
  74.1 1.0 copy-done.24
  75.1 2.6 %shard_map.161.act_grad = f32[2800,128]{1,0:T(8,128)S(1)} custom-call(bf16[32,64,128]{2,1,0:T(8,128)(2,1)S(1)} %copy-done, bf16[2,64,128]{2,1,0:T(8,128)(2,1)S(1)} %get-tuple-element.56.top, bf16[2,64,128]{2,1,0:T(8,128)(2,1)S(1)} %copy-done.16, bf16[37,16,128]{2,1,0:T(8,128)(2,1)S(1)} %get-tuple-element.52.strip, bf16[3,3,128,128]{3,2,1,0:T(8,128)(2,1)S(1)} %copy-done.24), custom_call_target="tpu_custom_call" | custom-call | flops 825753600 | bytes 4194304 | tf_op jit(solution)/shard_map/pallas_call | solution.py:41
  77.7 1.1 copy-done.7
  78.8 3.5 %all-to-all-done.3.stats = f32[32,8,128]{2,1,0:T(8,128)S(1)} async-done(((f32[32,8,128]{2,1,0:T(8,128)}), f32[32,8,128]{2,1,0:T(8,128)S(1)}, u32[]{:S(2)}, u32[]{:S(2)}) %all-to-all-start.3) | async-done | bytes 131104 | tf_op jit(solution)/shard_map/all_to_all | solution.py:395
  82.3 1.4 copy-done.8
  83.7 2.1 %shard_map.162 = (bf16[3072,128]{1,0:T(8,128)(2,1)S(1)}, f32[2800,128]{1,0:T(8,128)S(1)}, f32[2800,128]{1,0:T(8,128)S(1)}, f32[32,8,128]{2,1,0:T(8,128)}) custom-call(f32[2800,128]{1,0:T(8,128)S(1)} %get-tuple-element.33.act, f32[32,8,128]{2,1,0:T(8,128)S(1)} %all-to-all-done.3.stats, f32[2800,128]{1,0:T(8,128)S(1)} %copy-done.8), custom_call_target="tpu_custom_call" | custom-call | bytes 4194304 | tf_op jit(solution)/shard_map/pallas_call | solution.py:41
  85.8 1.1 copy-done.3
  86.9 1.1 copy-done.5
  88.0 0.9 copy-done.22
  88.9 2.6 %all-to-all-start.4 = ((f32[32,8,128]{2,1,0:T(8,128)}), f32[32,8,128]{2,1,0:T(8,128)S(1)}, u32[]{:S(2)}, u32[]{:S(2)}) async-start(f32[32,8,128]{2,1,0:T(8,128)} %get-tuple-element.38), calls=%async_computation.4 | async-start | bytes 262144 | tf_op jit(solution)/shard_map/all_to_all | solution.py:395
  91.5 1.1 copy-done.23
  92.6 1.0 copy-done.25
  93.6 4.1 %shard_map.163 = (bf16[32,64,128]{2,1,0:T(8,128)(2,1)}, bf16[16,72,128]{2,1,0:T(8,128)(2,1)S(1)}) custom-call(bf16[3072,128]{1,0:T(8,128)(2,1)S(1)} %copy-done.23, bf16[3072,128]{1,0:T(8,128)(2,1)S(1)} %get-tuple-element.36.mixed, bf16[32,64,128]{2,1,0:T(8,128)(2,1)S(1)} %copy-done, bf16[3,3,128,128]{3,2,1,0:T(8,128)(2,1)S(1)} %copy-done.25), custom_call_target="tpu_custom_call" | custom-call | flops 1651507200 | bytes 4194304 | tf_op jit(solution)/shard_map/pallas_call | solution.py:41
  97.7 2.0 %all-to-all-done.4.grad_stats = f32[32,8,128]{2,1,0:T(8,128)S(1)} async-done(((f32[32,8,128]{2,1,0:T(8,128)}), f32[32,8,128]{2,1,0:T(8,128)S(1)}, u32[]{:S(2)}, u32[]{:S(2)}) %all-to-all-start.4) | async-done | bytes 131104 | tf_op jit(solution)/shard_map/all_to_all | solution.py:395
  99.7 1.4 copy-done.6
  101.1 2.2 %shard_map.164 = (bf16[32,72,128]{2,1,0:T(8,128)(2,1)S(1)}, bf16[2816,128]{1,0:T(8,128)(2,1)S(1)}) custom-call(f32[32,8,128]{2,1,0:T(8,128)S(1)} %all-to-all-done.3.stats, f32[32,8,128]{2,1,0:T(8,128)S(1)} %all-to-all-done.4.grad_stats, f32[2800,128]{1,0:T(8,128)S(1)} %copy-done.4, f32[2800,128]{1,0:T(8,128)S(1)} %copy-done.6, ...), custom_call_target="tpu_custom_call" | custom-call | flops 825753600 | bytes 4194304 | tf_op jit(solution)/shard_map/pallas_call | solution.py:41
  103.3 0.0 copy-start.11
  103.3 0.0 copy-start.13
  103.3 20.4 %all_to_all.35.received = bf16[32,72,128]{2,1,0:T(8,128)(2,1)S(1)} all-to-all(bf16[32,72,128]{2,1,0:T(8,128)(2,1)S(1)} %get-tuple-element.42), channel_id=1, replica_groups=mesh['rows'=4,'cols'=8] {'rows','cols'}, dimensions={0} | all-to-all | bytes 1179648 | tf_op jit(solution)/shard_map/all_to_all | solution.py:395
  123.7 0.1 shard_map.165
  123.8 14.9 %all_to_all.36.mine = bf16[16,72,128]{2,1,0:T(8,128)(2,1)S(1)} all-to-all(bf16[16,72,128]{2,1,0:T(8,128)(2,1)S(1)} %shard_map.165), channel_id=1, replica_groups={{0,2,4,6,8,10,12,14,16,18,20,22,24,26,28,30},{1,3,5,7,9,11,13,15,17,19,..., dimensions={0} | all-to-all | bytes 589824 | tf_op jit(solution)/shard_map/all_to_all | solution.py:403
  138.8 1.9 %shard_map.167 = f32[8,128]{1,0:T(8,128)} custom-call(bf16[2816,128]{1,0:T(8,128)(2,1)S(1)} %get-tuple-element.45.kept, bf16[72,2816]{1,0:T(8,128)(2,1)S(1)} %copy-done.11, bf16[32,64,128]{2,1,0:T(8,128)(2,1)S(1)} %copy-done, bf16[3,3,128,128]{3,2,1,0:T(8,128)(2,1)S(1)} %copy-done.13), custom_call_target="tpu_custom_call" | custom-call | bytes 4194304 | tf_op jit(solution)/shard_map/pallas_call | solution.py:41
  140.7 1.1 shard_map.166
  (46 shorter events, 0.1 us)
Async XLA Ops:
  0.6 1.0 copy-start.14
  1.6 0.7 copy-start.18
  2.3 0.7 copy-start.19
  4.2 19.0 %all-to-all-start = ((bf16[16,72,128]{2,1,0:T(8,128)(2,1)}), bf16[16,72,128]{2,1,0:T(8,128)(2,1)S(1)}, u32[]{:S(2)}, u32[]{:S(2)}) async-start(bf16[16,72,128]{2,1,0:T(8,128)(2,1)} %shard_map.156), calls=%async_computation | async-start | bytes 589824 | tf_op jit(solution)/shard_map/all_to_all | solution.py:403
  23.2 5.2 %collective-permute-start.2 = (bf16[16,72,128]{2,1,0:T(8,128)(2,1)S(1)}, bf16[16,72,128]{2,1,0:T(8,128)(2,1)S(1)}, u32[]{:S(2)}, u32[]{:S(2)}) collective-permute-start(bf16[16,72,128]{2,1,0:T(8,128)(2,1)S(1)} %all-to-all-done.mine.source.mine_ref), channel_id=1, source_target_pairs={{0,1},{1,0},{2,3},{3,2},{4,5},{5,4},{6,7},{7,6},{8,9},{9,8},{10,11... | collective-permute-start | bytes 884744 | tf_op jit(solution)/shard_map/ppermute | solution.py:405
  24.0 12.2 %collective-permute-start = (bf16[2,2,64,128]{3,2,1,0:T(8,128)(2,1)S(1)}, bf16[2,2,64,128]{3,2,1,0:T(8,128)(2,1)S(1)}, u32[]{:S(2)}, u32[]{:S(2)}) collective-permute-start(bf16[2,2,64,128]{3,2,1,0:T(8,128)(2,1)S(1)} %pad_maximum_fusion.2), channel_id=1, source_target_pairs={{0,8},{8,16},{16,24},{1,9},{9,17},{17,25},{2,10},{10,18},{18,26},{... | collective-permute-start | bytes 196616 | tf_op jit(solution)/shard_map/ppermute | solution.py:626
  26.9 12.2 %copy-start = (bf16[32,64,128]{2,1,0:T(8,128)(2,1)S(1)}, bf16[32,64,128]{2,1,0:T(8,128)(2,1)}, u32[]{:S(2)}) copy-start(bf16[32,64,128]{2,1,0:T(8,128)(2,1)} %main.7) | copy-start | bytes 1572868
  26.9 9.3 %collective-permute-start.1 = (bf16[2,2,64,128]{3,2,1,0:T(8,128)(2,1)S(1)}, bf16[2,2,64,128]{3,2,1,0:T(8,128)(2,1)S(1)}, u32[]{:S(2)}, u32[]{:S(2)}) collective-permute-start(bf16[2,2,64,128]{3,2,1,0:T(8,128)(2,1)S(1)} %pad_maximum_fusion.3), channel_id=1, source_target_pairs={{8,0},{16,8},{24,16},{9,1},{17,9},{25,17},{10,2},{18,10},{26,18},{... | collective-permute-start | bytes 196616 | tf_op jit(solution)/shard_map/ppermute | solution.py:627
  28.4 1.7 %copy-start.1 = (bf16[3,3,1024,128]{3,2,1,0:T(8,128)(2,1)S(1)}, bf16[3,3,1024,128]{3,2,1,0:T(8,128)(2,1)}, u32[]{:S(2)}) copy-start(bf16[3,3,1024,128]{3,2,1,0:T(8,128)(2,1)} %weight.7) | copy-start | bytes 7077892
  31.9 12.4 %copy-start.20 = (f32[16,128]{1,0:T(8,128)S(1)}, f32[16,128]{1,0:T(8,128)}, u32[]{:S(2)}) copy-start(f32[16,128]{1,0:T(8,128)} %weight.9) | copy-start | bytes 24580
  31.9 12.4 %copy-start.21 = (s32[8,256]{1,0:T(8,128)S(1)}, s32[8,256]{1,0:T(8,128)}, u32[]{:S(2)}) copy-start(s32[8,256]{1,0:T(8,128)} %constant.7.clone.places) | copy-start | bytes 24580
  31.9 16.6 %all-to-all-start.1 = ((bf16[8,192,128]{2,1,0:T(8,128)(2,1)}), bf16[8,192,128]{2,1,0:T(8,128)(2,1)}, u32[]{:S(2)}, u32[]{:S(2)}) async-start(bf16[8,192,128]{2,1,0:T(8,128)(2,1)} %shard_map.157), calls=%async_computation.1 | async-start | bytes 786432 | tf_op jit(solution)/shard_map/all_to_all | solution.py:395
  36.2 0.6 copy-start.31
  36.8 0.6 copy-start.30
  37.5 11.1 %copy-start.2 = (bf16[3,3,1024,128]{3,2,1,0:T(8,128)(2,1)S(1)}, bf16[3,3,1024,128]{3,2,1,0:T(8,128)(2,1)}, u32[]{:S(2)}) copy-start(bf16[3,3,1024,128]{3,2,1,0:T(8,128)(2,1)} %weight.8) | copy-start | bytes 7077892
  40.0 7.8 %collective-permute-start.3 = (bf16[2,36,8,128]{3,2,1,0:T(8,128)(2,1)S(1)}, bf16[2,36,8,128]{3,2,1,0:T(8,128)(2,1)S(1)}, u32[]{:S(2)}, u32[]{:S(2)}) collective-permute-start(bf16[2,36,8,128]{3,2,1,0:T(8,128)(2,1)S(1)} %get-tuple-element.46), channel_id=1, source_target_pairs={{1,0},{2,1},{3,2},{4,3},{5,4},{6,5},{7,6},{9,8},{10,9},{11,10},{12... | collective-permute-start | bytes 442376 | tf_op jit(solution)/shard_map/ppermute | solution.py:698
  41.3 6.5 %collective-permute-start.4 = (bf16[2,36,8,128]{3,2,1,0:T(8,128)(2,1)S(1)}, bf16[2,36,8,128]{3,2,1,0:T(8,128)(2,1)S(1)}, u32[]{:S(2)}, u32[]{:S(2)}) collective-permute-start(bf16[2,36,8,128]{3,2,1,0:T(8,128)(2,1)S(1)} %get-tuple-element.47), channel_id=1, source_target_pairs={{0,1},{1,2},{2,3},{3,4},{4,5},{5,6},{6,7},{8,9},{9,10},{10,11},{11... | collective-permute-start | bytes 442376 | tf_op jit(solution)/shard_map/ppermute | solution.py:697
  45.2 0.6 copy-start.26
  45.8 0.6 copy-start.28
  48.6 1.0 copy-start.15
  49.5 13.8 %copy-start.27 = (f32[32,128]{1,0:T(8,128)S(1)}, f32[32,128]{1,0:T(8,128)}, u32[]{:S(2)}) copy-start(f32[32,128]{1,0:T(8,128)} %copy-done.26) | copy-start | bytes 49156
  51.3 0.7 copy-start.10
  52.0 11.4 %all-to-all-start.2 = ((f32[8,4,8,128]{3,2,1,0:T(8,128)}), f32[8,4,8,128]{3,2,1,0:T(8,128)S(1)}, u32[]{:S(2)}, u32[]{:S(2)}) async-start(f32[8,4,8,128]{3,2,1,0:T(8,128)} %copy-done.10), calls=%async_computation.2 | async-start | bytes 262144 | tf_op jit(solution)/shard_map/all_to_all | solution.py:395
  63.4 1.0 copy-start.9
  64.4 1.0 copy-start.12
  65.4 0.8 copy-start.17
  66.1 0.7 copy-start.29
  66.9 7.2 %copy-start.16 = (bf16[2,64,128]{2,1,0:T(8,128)(2,1)S(1)}, bf16[2,64,128]{2,1,0:T(8,128)(2,1)}, u32[]{:S(2)}) copy-start(bf16[2,64,128]{2,1,0:T(8,128)(2,1)} %get-tuple-element.54.bottom) | copy-start | bytes 98308
  70.4 11.9 %all-to-all-start.3 = ((f32[32,8,128]{2,1,0:T(8,128)}), f32[32,8,128]{2,1,0:T(8,128)S(1)}, u32[]{:S(2)}, u32[]{:S(2)}) async-start(f32[32,8,128]{2,1,0:T(8,128)} %get-tuple-element.34), calls=%async_computation.3 | async-start | bytes 262144 | tf_op jit(solution)/shard_map/all_to_all | solution.py:395
  74.1 1.0 copy-start.24
  77.7 1.1 copy-start.7
  82.3 1.4 copy-start.8
  85.8 1.1 copy-start.3
  86.9 1.1 copy-start.5
  88.0 0.9 copy-start.22
  88.9 10.8 %all-to-all-start.4 = ((f32[32,8,128]{2,1,0:T(8,128)}), f32[32,8,128]{2,1,0:T(8,128)S(1)}, u32[]{:S(2)}, u32[]{:S(2)}) async-start(f32[32,8,128]{2,1,0:T(8,128)} %get-tuple-element.38), calls=%async_computation.4 | async-start | bytes 262144 | tf_op jit(solution)/shard_map/all_to_all | solution.py:395
  91.5 1.1 copy-start.23
  92.6 1.0 copy-start.25
  93.6 6.1 %copy-start.4 = (f32[2800,128]{1,0:T(8,128)S(1)}, f32[2800,128]{1,0:T(8,128)}, u32[]{:S(2)}) copy-start(f32[2800,128]{1,0:T(8,128)} %copy-done.3) | copy-start | bytes 4300804
  99.7 1.4 copy-start.6
  103.3 35.4 %copy-start.11 = (bf16[72,2816]{1,0:T(8,128)(2,1)S(1)}, bf16[72,2816]{1,0:T(8,128)(2,1)}, u32[]{:S(2)}) copy-start(bf16[72,2816]{1,0:T(8,128)(2,1)} %constant.8.clone.picked) | copy-start | bytes 1216516
  103.3 35.4 %copy-start.13 = (bf16[3,3,128,128]{3,2,1,0:T(8,128)(2,1)S(1)}, bf16[3,3,128,128]{3,2,1,0:T(8,128)(2,1)}, u32[]{:S(2)}) copy-start(bf16[3,3,128,128]{3,2,1,0:T(8,128)(2,1)} %weight.13) | copy-start | bytes 884740
  138.8 1.9 %collective-permute-start.5 = (bf16[16,72,128]{2,1,0:T(8,128)(2,1)S(1)}, bf16[16,72,128]{2,1,0:T(8,128)(2,1)S(1)}, u32[]{:S(2)}, u32[]{:S(2)}) collective-permute-start(bf16[16,72,128]{2,1,0:T(8,128)(2,1)S(1)} %all_to_all.36.mine), channel_id=1, source_target_pairs={{0,1},{1,0},{2,3},{3,2},{4,5},{5,4},{6,7},{7,6},{8,9},{9,8},{10,11... | collective-permute-start | bytes 884744 | tf_op jit(solution)/shard_map/ppermute | solution.py:405

commit v6 on v5

--- a/solution.py
+++ b/solution.py
@@ -1,4 +1,3 @@
-import functools
 import math
 
 import jax
@@ -33,20 +32,65 @@
         self.kept = -(-self.out // 128) * 128
 
 
-def vmem(count):
-    return [pl.BlockSpec(memory_space=pltpu.VMEM)] * count
-
-
-def call(body, outs, ins, scratch=(), flops=0, **fixed):
-    return pl.pallas_call(
-        functools.partial(body, **fixed),
+def call(body, outs, ins, scratch=(), flops=0, far=None, late=(), far_out=(), **fixed):
+    far = far or {}
+    single = not isinstance(outs, tuple)
+    outs = (outs,) if single else outs
+    n_in, n_out, n_own = len(ins), len(outs), len(scratch)
+    near = pl.BlockSpec(memory_space=pltpu.VMEM)
+    hbm = pl.BlockSpec(memory_space=pltpu.MemorySpace.HBM)
+    landing = [
+        pltpu.VMEM(ins[i].shape[0 if k is None else 1 :], ins[i].dtype) for i, k in far.items()
+    ]
+    leaving = [pltpu.VMEM(outs[j].shape, outs[j].dtype) for j in far_out]
+
+    def kernel(*refs):
+        in_refs, out_refs = list(refs[:n_in]), list(refs[n_in : n_in + n_out])
+        rest = refs[n_in + n_out :]
+        own, rest = rest[:n_own], rest[n_own:]
+        buffers, sems = rest[: len(far) + len(far_out)], rest[len(far) + len(far_out) :]
+        copies = {}
+        for slot, (i, k) in enumerate(far.items()):
+            source = in_refs[i] if k is None else in_refs[i].at[k]
+            copies[i] = pltpu.make_async_copy(source, buffers[slot], sems[slot])
+            copies[i].start()
+            in_refs[i] = buffers[slot]
+        results = []
+        for slot, j in enumerate(far_out, len(far)):
+            results.append((buffers[slot], out_refs[j], sems[slot]))
+            out_refs[j] = buffers[slot]
+        for i, copy in copies.items():
+            if i not in late:
+                copy.wait()
+
+        def arrive():
+            for i in late:
+                copies[i].wait()
+
+        extra = {"arrive": arrive} if late else {}
+        body(*in_refs, *out_refs, *own, **fixed, **extra)
+        ends = [pltpu.make_async_copy(*triple) for triple in results]
+        for copy in ends:
+            copy.start()
+        for copy in ends:
+            copy.wait()
+
+    result = pl.pallas_call(
+        kernel,
         out_shape=outs,
-        in_specs=vmem(len(ins)),
-        out_specs=jax.tree.map(lambda _: pl.BlockSpec(memory_space=pltpu.VMEM), outs),
-        scratch_shapes=list(scratch),
+        in_specs=[hbm if i in far else near for i in range(n_in)],
+        out_specs=tuple(hbm if j in far_out else near for j in range(n_out)),
+        scratch_shapes=[
+            *scratch,
+            *landing,
+            *leaving,
+            *[pltpu.SemaphoreType.DMA] * (len(landing) + len(leaving)),
+        ],
         compiler_params=pltpu.CompilerParams(vmem_limit_bytes=KERNEL_VMEM),
         cost_estimate=pl.CostEstimate(flops=flops, bytes_accessed=4 << 20, transcendentals=0),
+        name=body.__name__,
     )(*ins)
+    return result[0] if single else result
 
 
 def put_tiles(flat_ref, lay, main_ref, top_ref, bottom_ref, strip_ref):
@@ -130,7 +174,7 @@
 
 def mixed_kernel(
     main, top, bottom, strip, coarse, pooled, valid, weight, flat, act_out, stats, square, terms, z0,
-    z1, z2, *, lay
+    z1, z2, *, lay, arrive
 ):
     width = main.shape[2]
     flat[...] = jnp.zeros_like(flat)
@@ -164,6 +208,7 @@
         flat[base + lay.cols : base + lay.wide] = (
             strip[k].astype(jnp.float32) + jnp.concatenate([right, left], 0)
         ).astype(jnp.bfloat16)
+    arrive()
     put_square(square, weight, False)
     taps_matmul(flat, square, (z0, z1, z2), lay, False)
 
@@ -204,7 +249,7 @@
 
 
 def norm_kernel(
-    act, stats, act_grad, activated, normed_out, grad_out, grad_stats, *, lay, grid, pixel_total
+    act, stats, act_grad, activated, grad_out, grad_stats, *, lay, grid, pixel_total
 ):
     width = act.shape[1]
     mean, inverse = act_moments(stats, pixel_total)
@@ -220,7 +265,6 @@
             normed * gate * inside
         ).astype(jnp.bfloat16)
         grad = act_grad[pl.ds(begin, lay.wide)] * gate * (1.0 + normed * (1.0 - gate))
-        normed_out[pl.ds(begin, lay.wide)] = normed
         grad_out[pl.ds(begin, lay.wide)] = grad
         mine = ((r >= 2) & (r < lay.rows + 2)).astype(jnp.float32)
         own_grad = grad[: lay.cols] * mine
@@ -269,10 +313,12 @@
 
 
 def second_kernel(
-    activated, mixed, main, weight, enhanced, sent, square, z0, z1, z2, own, total, *, lay, chunk
+    activated, mixed, main, weight, enhanced, sent, square, z0, z1, z2, own, total, *, lay, chunk,
+    arrive
 ):
     put_square(square, weight, False)
     taps_matmul(activated, square, (z0, z1, z2), lay, False)
+    arrive()
 
     @pl.loop(0, lay.rows)
     def _(i):
@@ -294,11 +340,11 @@
 
 
 def first_kernel(
-    stats, grad_stats, normed_ref, grad_ref, mixed, second, sent, kept, own, total, *, lay, grid,
-    chunk, pixel_total
+    stats, grad_stats, act, grad_ref, mixed, second, sent, kept, own, total, *, lay, grid,
+    chunk, pixel_total, arrive
 ):
-    width = normed_ref.shape[1]
-    _, inverse = act_moments(stats, pixel_total)
+    width = act.shape[1]
+    mean, inverse = act_moments(stats, pixel_total)
     sums = jnp.sum(grad_stats[...], 0)
     grad_mean, cross_mean = sums[0:1] / pixel_total, sums[1:2] / pixel_total
     mask = inside_masks(lay, width, *grid)
@@ -311,7 +357,7 @@
         value = inverse * (
             grad_ref[pl.ds(begin, lay.wide)]
             - grad_mean
-            - normed_ref[pl.ds(begin, lay.wide)] * cross_mean
+            - (act[pl.ds(begin, lay.wide)] - mean) * inverse * cross_mean
         )
         value = (value * mask(r)).astype(jnp.bfloat16)
         kept[pl.ds(begin, lay.wide)] = value
@@ -321,6 +367,7 @@
             place = pl.multiple_of((r - 2) * lay.wide + 2 * MARGIN, 16)
             own[pl.ds(place, lay.cols)] = value[: lay.cols].astype(jnp.float32)
 
+    arrive()
     weight_matmul(mixed, own, total, sent, lay, chunk)
     for d in range(second.shape[0]):
         sent[second.shape[0] + d] = second[d]
@@ -395,14 +442,16 @@
     return lax.all_to_all(payload, axis, 0, 0)
 
 
-def from_all(payload, row_devices, col_devices):
+def among_cores(payload, row_devices, col_devices):
     groups = [
         [r * col_devices + 2 * h + k for r in range(row_devices) for h in range(col_devices // 2)]
         for k in range(2)
     ]
-    mine = lax.all_to_all(payload, BOTH, 0, 0, axis_index_groups=groups)
-    swap = [(c, c ^ 1) for c in range(col_devices)]
-    return mine, lax.ppermute(mine, "cols", swap)
+    return lax.all_to_all(payload, BOTH, 0, 0, axis_index_groups=groups)
+
+
+def core_swap(array, col_devices):
+    return lax.ppermute(array, "cols", [(c, c ^ 1) for c in range(col_devices)])
 
 
 def pieces(array):
@@ -511,7 +560,7 @@
     return total
 
 
-def hidden_kernel(mine, other, weight, sent, rows_ref, shifted, kept, *, grid, band, direct):
+def hidden_kernel(mine, other, weight, sent, rows_ref, shifted, kept, *, grid, band, direct, arrive):
     row_devices, col_devices = grid
     band_rows, cols = band
     coarse_rows = row_devices * band_rows
@@ -529,6 +578,7 @@
                 ]
     else:
         rows_ref[cols : cols + coarse_rows * cols] = mine[...]
+    arrive()
     raw = channel_conv(rows_ref, weight, shifted, coarse_rows, cols)
     pixels = coarse_rows * cols
     mean = jnp.sum(raw, 0, keepdims=True) / pixels
@@ -544,7 +594,7 @@
 
 def project_kernel(
     received, weight, source, project, sent, rows_ref, shifted, residual, spread, *, grid, band,
-    direct
+    direct, arrive
 ):
     row_devices, col_devices = grid
     band_rows, cols = band
@@ -552,6 +602,7 @@
     my_col = lax.axis_index("cols")
     for c in range(col_devices):
         rows_ref[:, c * width : (c + 1) * width] = received[c]
+    arrive()
     raw = channel_conv(rows_ref, weight, shifted, band_rows + 2, cols)
     count = (band_rows + 2) * cols
     if direct:
@@ -611,8 +662,9 @@
         jax.ShapeDtypeStruct((devices // 2, main_rows + 8, 128), jnp.bfloat16),
         (encoder_features, instance_map, main),
         [pltpu.VMEM((128, tile_cols), jnp.float32)],
-    )
-    mine, other = from_all(sent_input, row_devices, col_devices)
+        far={0: None, 1: None, 2: None},
+    )
+    mine = among_cores(sent_input, row_devices, col_devices)
     late_input, late_cotangent, _ = lax.optimization_barrier(
         (enhancer_input, output_cotangent, sent_input)
     )
@@ -625,6 +677,11 @@
     col_down = [(j, i) for i, j in col_up]
     top = lax.ppermute(tops, "rows", row_up)
     bottom = lax.ppermute(bottoms, "rows", row_down)
+    both = jnp.stack([late_input, late_cotangent])
+    tall_last = jnp.concatenate([top[:, :, -RIM:], both[:, :, -RIM:], bottom[:, :, -RIM:]], 1)
+    tall_first = jnp.concatenate([top[:, :, :RIM], both[:, :, :RIM], bottom[:, :, :RIM]], 1)
+    mine, tall_last, tall_first = lax.optimization_barrier((mine, tall_last, tall_first))
+    other = core_swap(mine, col_devices)
     pixel_total = float(tile_rows * tile_cols * devices)
     chunk = 18 * width // devices
     padded_chunk = -(-chunk // 8) * 8
@@ -683,17 +740,15 @@
             pltpu.VMEM((coarse_rows + 4, band_cols, width_share), jnp.bfloat16),
         ],
         18 * coarse_rows * band_cols * channels * width_share,
+        far={2: None},
+        late=(2,),
+        far_out=(0,),
         grid=grid,
         band=band,
         direct=direct,
     )
     near_hidden = to_all(sent_hidden, "cols")
-    late_input, late_cotangent, top, bottom, _ = lax.optimization_barrier(
-        (enhancer_input, output_cotangent, top, bottom, sent_hidden)
-    )
-    both = jnp.stack([late_input, late_cotangent])
-    tall_last = jnp.concatenate([top[:, :, -RIM:], both[:, :, -RIM:], bottom[:, :, -RIM:]], 1)
-    tall_first = jnp.concatenate([top[:, :, :RIM], both[:, :, :RIM], bottom[:, :, :RIM]], 1)
+    tall_last, tall_first, _ = lax.optimization_barrier((tall_last, tall_first, sent_hidden))
     left = lax.ppermute(tall_last, "cols", col_up)
     right = lax.ppermute(tall_first, "cols", col_down)
     strip = jnp.concatenate(
@@ -706,9 +761,11 @@
     act_grad = call(
         cot_kernel,
         out_shape,
-        (output_cotangent, top[1], bottom[1], strip[1], enhancer_second),
+        (output_cotangent, top, bottom, strip, enhancer_second),
         [pltpu.VMEM((lay.flat, width), jnp.bfloat16), square, *z],
         conv_flops,
+        far={0: None, 1: 1, 2: 1, 3: 1, 4: None},
+        far_out=(0,),
         lay=lay,
     )
 
@@ -723,6 +780,9 @@
             pltpu.VMEM((band_rows + 2, band_cols + 16, width), jnp.float32),
         ],
         18 * (band_rows + 2) * band_cols * channels * width_share,
+        far={1: None, 2: None, 3: None},
+        late=(1, 2, 3),
+        far_out=(0,),
         grid=grid,
         band=band,
         direct=direct,
@@ -733,16 +793,21 @@
     mixed, first_act, stats = call(
         mixed_kernel,
         (flat_shape, out_shape, stats_shape),
-        (enhancer_input, top[0], bottom[0], strip[0], *terms, enhancer_first),
+        (enhancer_input, top, bottom, strip, *terms, enhancer_first),
         [square, pltpu.VMEM((block_rows + 2, 8, width), jnp.float32), *z],
         conv_flops,
+        far={0: None, 1: 0, 2: 0, 3: 0, 5: None, 6: None, 7: None},
+        late=(7,),
+        far_out=(0, 1, 2),
         lay=lay,
     )
     stats = to_all(stats, BOTH)
-    activated, normed_act, normed_grad, grad_stats = call(
+    activated, normed_grad, grad_stats = call(
         norm_kernel,
-        (flat_shape, out_shape, out_shape, stats_shape),
+        (flat_shape, out_shape, stats_shape),
         (first_act, stats, act_grad),
+        far={0: None, 2: None},
+        far_out=(0, 1, 2),
         lay=lay,
         grid=grid,
         pixel_total=pixel_total,
@@ -754,15 +819,19 @@
         (activated, mixed, output_cotangent, enhancer_second),
         [square, *z, own, total],
         2 * conv_flops,
+        far={0: None, 1: None, 2: None, 3: None},
+        late=(1, 2),
         lay=lay,
         chunk=chunk,
     )
     sent_both, kept = call(
         first_kernel,
         (sent_shape, jax.ShapeDtypeStruct((lay.kept, width), jnp.bfloat16)),
-        (stats, grad_stats, normed_act, normed_grad, mixed, second_sent),
+        (stats, grad_stats, first_act, normed_grad, mixed, second_sent),
         [own, total],
         conv_flops,
+        far={2: None, 3: None, 4: None},
+        late=(4,),
         lay=lay,
         grid=grid,
         chunk=chunk,
@@ -777,8 +846,10 @@
         (),
         lay=lay,
     )
+    part, global_gradient = lax.optimization_barrier((part, global_gradient))
     share = call(share_kernel, half_shape, (part,), rescale=rescale)
-    shares = from_all(share, row_devices, col_devices)
+    share = among_cores(share, row_devices, col_devices)
+    shares = (share, core_swap(share, col_devices))
     whole_shape = jax.ShapeDtypeStruct((9 * width, width), jnp.float32)
     first_total, second_total = call(
         join_kernel, (whole_shape, whole_shape), shares, chunk=chunk, grid=grid

time: 143 us -> 136 us (0.951)
  blocking collectives: 35.3 us -> 14.9 us
  waiting for transfers between devices: 20.7 us -> 31.7 us
  local copies, waits for them, and re-layouts: 26.5 us -> 21.2 us
  starting transfers between devices: 33.3 us -> 37.5 us
  Pallas kernels: 23.3 us -> 27.4 us
    all_to_all x2 -> x1, blocking collectives: 35.3 us -> 14.9 us  [among_cores(): return lax.all_to_all(payload, BOTH, 0, 0, axis_index_groups=groups)]
    all_to_all x4 -> x5, waiting for transfers between devices: 10 us -> 23.7 us  [to_all(): return lax.all_to_all(payload, axis, 0, 0)]
    all_to_all x1, waiting for transfers between devices: 10.7 us -> 0.01 us  [among_cores(): return lax.all_to_all(payload, BOTH, 0, 0, axis_index_groups=groups)]
    ppermute x1, waiting for transfers between devices: 0.01 us -> 4.29 us  [per_device(): bottom = lax.ppermute(bottoms, 'rows', row_down)]
    pallas_call x12, Pallas kernels: 23.3 us -> 27.4 us  [call(): pl.pallas_call(kernel, out_shape=outs, in_specs=[hbm if i in far else nea...]
    squeeze x3 -> x0, local copies, waits for them, and re-layouts: 3.33 us -> none  [the longest x1 1.4 us: per_device(): bottom[1]]
    ppermute x2, waiting for transfers between devices: 0.01 us -> 3.15 us  [core_swap(): return lax.ppermute(array, 'cols', [(c, c ^ 1) for c in range(col_devices)])]
    all_to_all x4 -> x5, starting transfers between devices: 16.4 us -> 19 us  [to_all(): return lax.all_to_all(payload, axis, 0, 0)]
  transfers between devices with their start and end apart: 11 -> 12, of which waited for: 4 -> 8; matrix products, arithmetic and copies ran while one was open for 5% -> 1% of each run, Pallas kernels for 8% -> 9%
where the time goes in v6:
time: 136 us; the launch traced here: 135 us
  starting transfers between devices  37.5 us (28%)
  waiting for transfers between devices  31.7 us (23%)
  Pallas kernels  27.4 us (20%)
  local copies, waits for them, and re-layouts  21.2 us (16%)
  blocking collectives  14.9 us (11%)
    pallas_call x12, Pallas kernels, call(): pl.pallas_call(kernel, out_shape=outs, in_specs=[hbm if i in far else nea...  27.4 us
    all_to_all x5, waiting for transfers between devices, to_all(): return lax.all_to_all(payload, axis, 0, 0)  23.7 us
    unnamed x56, local copies, waits for them, and re-layouts  20.3 us
    all_to_all x5, starting transfers between devices, to_all(): return lax.all_to_all(payload, axis, 0, 0)  19 us
    all_to_all x1, blocking collectives, among_cores(): return lax.all_to_all(payload, BOTH, 0, 0, axis_index_groups=groups)  14.9 us
    all_to_all x1, starting transfers between devices, among_cores(): return lax.all_to_all(payload, BOTH, 0, 0, axis_index_groups=groups)  8.32 us
    ppermute x1, waiting for transfers between devices, per_device(): bottom = lax.ppermute(bottoms, 'rows', row_down)  4.29 us
    ppermute x1, starting transfers between devices, per_device(): top = lax.ppermute(tops, 'rows', row_up)  3.83 us
  transfers between devices with their start and end apart: 12, of which 8 were waited for; matrix products, arithmetic and copies ran while one was open for 1% of the time, Pallas kernels for 9%

profile of v6, /device:TPU:0, one launch (start us, length us, event | category | flops | bytes accessed | tf_op | source)
XLA Modules:
  0.0 134.6 jit_solution(4168030701144643566)
XLA Ops:
  0.6 0.0 copy-start
  0.6 0.0 copy-start.10
  0.7 1.0 copy-done.17
  1.7 0.7 copy-done.20
  2.4 0.7 copy-done.21
  3.1 1.3 pack_kernel.1
  4.4 8.3 %all-to-all-start = ((bf16[16,72,128]{2,1,0:T(8,128)(2,1)}), bf16[16,72,128]{2,1,0:T(8,128)(2,1)S(1)}, u32[]{:S(2)}, u32[]{:S(2)}) async-start(bf16[16,72,128]{2,1,0:T(8,128)(2,1)} %pack_kernel.1), calls=%async_computation | async-start | bytes 589824 | tf_op jit(solution)/shard_map/all_to_all | solution.py:450
  12.7 0.8 slice_bitcast_fusion
  13.6 3.8 %collective-permute-start = (bf16[2,2,64,128]{3,2,1,0:T(8,128)(2,1)S(1)}, bf16[2,2,64,128]{3,2,1,0:T(8,128)(2,1)S(1)}, u32[]{:S(2)}, u32[]{:S(2)}) collective-permute-start(bf16[2,2,64,128]{3,2,1,0:T(8,128)(2,1)S(1)} %pad_maximum_fusion.2), channel_id=1, source_target_pairs={{0,8},{8,16},{16,24},{1,9},{9,17},{17,25},{2,10},{10,18},{18,26},{... | collective-permute-start | bytes 196616 | tf_op jit(solution)/shard_map/ppermute | solution.py:678
  17.4 1.3 collective-permute-start.1
  18.7 0.6 collective-permute-done.refs_1_
  19.3 4.3 %collective-permute-done.1.refs_2_ = bf16[2,2,64,128]{3,2,1,0:T(8,128)(2,1)S(1)} collective-permute-done((bf16[2,2,64,128]{3,2,1,0:T(8,128)(2,1)S(1)}, bf16[2,2,64,128]{3,2,1,0:T(8,128)(2,1)S(1)}, u32[]{:S(2)}, u32[]{:S(2)}) %collective-permute-start.1) | collective-permute-done | bytes 65568 | tf_op jit(solution)/shard_map/ppermute | solution.py:679
  23.6 0.1 fusion.4
  23.7 0.1 collective-permute-start.2
  23.7 1.6 %collective-permute-done.2.refs_1_ = bf16[16,72,128]{2,1,0:T(8,128)(2,1)S(1)} collective-permute-done((bf16[16,72,128]{2,1,0:T(8,128)(2,1)S(1)}, bf16[16,72,128]{2,1,0:T(8,128)(2,1)S(1)}, u32[]{:S(2)}, u32[]{:S(2)}) %collective-permute-start.2) | collective-permute-done | bytes 294944 | tf_op jit(solution)/shard_map/ppermute | solution.py:454
  25.3 1.7 %copy-done.1 = bf16[3,3,1024,128]{3,2,1,0:T(8,128)(2,1)S(1)} copy-done((bf16[3,3,1024,128]{3,2,1,0:T(8,128)(2,1)S(1)}, bf16[3,3,1024,128]{3,2,1,0:T(8,128)(2,1)}, u32[]{:S(2)}) %copy-start.1) | copy-done | bytes 2359320
  27.0 2.2 %hidden_kernel.1 = bf16[8,192,128]{2,1,0:T(8,128)(2,1)} custom-call(bf16[16,72,128]{2,1,0:T(8,128)(2,1)S(1)} %all-to-all-done.refs_0_.refs_2_, bf16[16,72,128]{2,1,0:T(8,128)(2,1)S(1)} %collective-permute-done.2.refs_1_, bf16[3,3,1024,128]{3,2,1,0:T(8,128)(2,1)S(1)} %copy-done.1), custom_call_target="tpu_custom_call" | custom-call | flops 603979776 | bytes 4194304 | tf_op jit(solution)/shard_map/hidden_kernel/pallas_call | solution.py:78
  29.1 0.0 copy-start.18
  29.2 3.8 %all-to-all-start.1 = ((bf16[8,192,128]{2,1,0:T(8,128)(2,1)}), bf16[8,192,128]{2,1,0:T(8,128)(2,1)S(1)}, u32[]{:S(2)}, u32[]{:S(2)}) async-start(bf16[8,192,128]{2,1,0:T(8,128)(2,1)} %hidden_kernel.1), calls=%async_computation.1 | async-start | bytes 786432 | tf_op jit(solution)/shard_map/all_to_all | solution.py:442
  32.9 1.3 collective-permute-start.3
  34.2 3.7 %collective-permute-start.4 = (bf16[2,36,8,128]{3,2,1,0:T(8,128)(2,1)S(1)}, bf16[2,36,8,128]{3,2,1,0:T(8,128)(2,1)}, u32[]{:S(2)}, u32[]{:S(2)}) collective-permute-start(bf16[2,36,8,128]{3,2,1,0:T(8,128)(2,1)S(1)} %get-tuple-element.33), channel_id=1, source_target_pairs={{0,1},{1,2},{2,3},{3,4},{4,5},{5,6},{6,7},{8,9},{9,10},{10,11},{11... | collective-permute-start | bytes 442376 | tf_op jit(solution)/shard_map/ppermute | solution.py:752
  37.9 0.8 pool_kernel.1
  38.7 2.5 %all-to-all-done.1.refs_0_ = bf16[8,192,128]{2,1,0:T(8,128)(2,1)S(1)} async-done(((bf16[8,192,128]{2,1,0:T(8,128)(2,1)}), bf16[8,192,128]{2,1,0:T(8,128)(2,1)S(1)}, u32[]{:S(2)}, u32[]{:S(2)}) %all-to-all-start.1) | async-done | bytes 393248 | tf_op jit(solution)/shard_map/all_to_all | solution.py:442
  41.3 1.7 %copy-done.2 = bf16[3,3,1024,128]{3,2,1,0:T(8,128)(2,1)S(1)} copy-done((bf16[3,3,1024,128]{3,2,1,0:T(8,128)(2,1)S(1)}, bf16[3,3,1024,128]{3,2,1,0:T(8,128)(2,1)}, u32[]{:S(2)}) %copy-start.2) | copy-done | bytes 2359320
  42.9 1.7 %project_kernel.1 = f32[8,4,8,128]{3,2,1,0:T(8,128)} custom-call(bf16[8,192,128]{2,1,0:T(8,128)(2,1)S(1)} %all-to-all-done.1.refs_0_, bf16[3,3,1024,128]{3,2,1,0:T(8,128)(2,1)S(1)} %copy-done.2, bf16[16,72,128]{2,1,0:T(8,128)(2,1)S(1)} %all-to-all-done.refs_0_.refs_2_, bf16[1024,128]{1,0:T(8,128)(2,1)S(1)} %copy-done.18), custom_call_target="tpu_custom_call" | custom-call | flops 301989888 | bytes 4194304 | tf_op jit(solution)/shard_map/project_kernel/pallas_call | solution.py:78
  44.7 3.4 %all-to-all-start.2 = ((f32[8,4,8,128]{3,2,1,0:T(8,128)}), f32[8,4,8,128]{3,2,1,0:T(8,128)S(1)}, u32[]{:S(2)}, u32[]{:S(2)}) async-start(f32[8,4,8,128]{3,2,1,0:T(8,128)} %project_kernel.1), calls=%async_computation.2 | async-start | bytes 262144 | tf_op jit(solution)/shard_map/all_to_all | solution.py:442
  48.1 0.0 collective-permute-done.4
  48.1 1.0 fusion.2.refs_3_
  49.1 4.5 %all-to-all-done.2.refs_4_ = f32[8,4,8,128]{3,2,1,0:T(8,128)S(1)} async-done(((f32[8,4,8,128]{3,2,1,0:T(8,128)}), f32[8,4,8,128]{3,2,1,0:T(8,128)S(1)}, u32[]{:S(2)}, u32[]{:S(2)}) %all-to-all-start.2) | async-done | bytes 131104 | tf_op jit(solution)/shard_map/all_to_all | solution.py:442
  53.6 4.3 %mixed_kernel.1 = (bf16[3072,128]{1,0:T(8,128)(2,1)S(1)}, f32[2800,128]{1,0:T(8,128)S(1)}, f32[32,8,128]{2,1,0:T(8,128)}) custom-call(bf16[32,64,128]{2,1,0:T(8,128)(2,1)S(1)} %copy-done.10, bf16[2,2,64,128]{3,2,1,0:T(8,128)(2,1)S(1)} %collective-permute-done.refs_1_, bf16[2,2,64,128]{3,2,1,0:T(8,128)(2,1)S(1)} %collective-permute-done.1.refs_2_, ...), custom_call_target="tpu_custom_call" | custom-call | flops 825753600 | bytes 4194304 | tf_op jit(solution)/shard_map/mixed_kernel/pallas_call | solution.py:78
  57.9 0.9 copy-done.5
  58.8 2.7 %all-to-all-start.3 = ((f32[32,8,128]{2,1,0:T(8,128)}), f32[32,8,128]{2,1,0:T(8,128)S(1)}, u32[]{:S(2)}, u32[]{:S(2)}) async-start(f32[32,8,128]{2,1,0:T(8,128)} %get-tuple-element.37), calls=%async_computation.3 | async-start | bytes 262144 | tf_op jit(solution)/shard_map/all_to_all | solution.py:442
  61.6 0.0 copy-start.26
  61.6 1.0 copy-done.26
  62.5 3.3 %cot_kernel.1.refs_2_ = f32[2800,128]{1,0:T(8,128)S(1)} custom-call(bf16[32,64,128]{2,1,0:T(8,128)(2,1)S(1)} %copy-done, bf16[2,2,64,128]{3,2,1,0:T(8,128)(2,1)S(1)} %collective-permute-done.refs_1_, bf16[2,2,64,128]{3,2,1,0:T(8,128)(2,1)S(1)} %collective-permute-done.1.refs_2_, bf16[2,37,16,128]{3,2,1,0:T(8,128)(2,1)S(1)} %fusion.2.refs_3_, ...), custom_call_target="tpu_custom_call" | custom-call | flops 825753600 | bytes 4194304 | tf_op jit(solution)/shard_map/cot_kernel/pallas_call | solution.py:78
  65.9 1.1 copy-done.3
  67.0 2.8 %all-to-all-done.3.refs_1_.refs_0_ = f32[32,8,128]{2,1,0:T(8,128)S(1)} async-done(((f32[32,8,128]{2,1,0:T(8,128)}), f32[32,8,128]{2,1,0:T(8,128)S(1)}, u32[]{:S(2)}, u32[]{:S(2)}) %all-to-all-start.3) | async-done | bytes 131104 | tf_op jit(solution)/shard_map/all_to_all | solution.py:442
  69.8 1.4 %copy-done.4 = f32[2800,128]{1,0:T(8,128)S(1)} copy-done((f32[2800,128]{1,0:T(8,128)S(1)}, f32[2800,128]{1,0:T(8,128)}, u32[]{:S(2)}) %copy-start.4) | copy-done | bytes 1433624
  71.1 2.5 %norm_kernel.1 = (bf16[3072,128]{1,0:T(8,128)(2,1)S(1)}, f32[2800,128]{1,0:T(8,128)S(1)}, f32[32,8,128]{2,1,0:T(8,128)S(1)}) custom-call(f32[2800,128]{1,0:T(8,128)S(1)} %get-tuple-element.36.refs_0_.refs_2_, f32[32,8,128]{2,1,0:T(8,128)S(1)} %all-to-all-done.3.refs_1_.refs_0_, f32[2800,128]{1,0:T(8,128)S(1)} %copy-done.4), custom_call_target="tpu_custom_call" | custom-call | bytes 4194304 | tf_op jit(solution)/shard_map/norm_kernel/pallas_call | solution.py:78
  73.6 0.0 copy-start.19
  73.6 0.6 copy-done.19
  74.3 0.9 copy-done.24
  75.2 3.3 %all-to-all-start.4 = ((f32[32,8,128]{2,1,0:T(8,128)}), f32[32,8,128]{2,1,0:T(8,128)}, u32[]{:S(2)}, u32[]{:S(2)}) async-start(f32[32,8,128]{2,1,0:T(8,128)} %copy-done.19), calls=%async_computation.4 | async-start | bytes 262144 | tf_op jit(solution)/shard_map/all_to_all | solution.py:442
  78.5 1.1 copy-done.6
  79.6 1.1 copy-done.25
  80.7 1.0 copy-done.27
  81.7 4.4 %second_kernel.1 = (bf16[32,64,128]{2,1,0:T(8,128)(2,1)}, bf16[16,72,128]{2,1,0:T(8,128)(2,1)S(1)}) custom-call(bf16[3072,128]{1,0:T(8,128)(2,1)S(1)} %copy-done.25, bf16[3072,128]{1,0:T(8,128)(2,1)S(1)} %copy-done.6, bf16[32,64,128]{2,1,0:T(8,128)(2,1)S(1)} %copy-done, bf16[3,3,128,128]{3,2,1,0:T(8,128)(2,1)S(1)} %copy-done.27), custom_call_target="tpu_custom_call" | custom-call | flops 1651507200 | bytes 4194304 | tf_op jit(solution)/shard_map/second_kernel/pallas_call | solution.py:78
  86.1 0.0 copy-start.13
  86.1 0.7 copy-done.13
  86.8 1.1 copy-done.7
  87.9 1.0 copy-done.14
  88.9 3.8 %first_kernel.1 = (bf16[32,72,128]{2,1,0:T(8,128)(2,1)S(1)}, bf16[2816,128]{1,0:T(8,128)(2,1)S(1)}) custom-call(f32[32,8,128]{2,1,0:T(8,128)S(1)} %all-to-all-done.3.refs_1_.refs_0_, f32[32,8,128]{2,1,0:T(8,128)} %all-to-all-done.4.refs_1_, f32[2800,128]{1,0:T(8,128)S(1)} %get-tuple-element.36.refs_0_.refs_2_, f32[2800,128]{1,0:T(8,128)S(1)} %get-tuple-element.42.refs_3_, ...), custom_call_target="tpu_custom_call" | custom-call | flops 825753600 | bytes 4194304 | tf_op jit(solution)/shard_map/first_kernel/pallas_call | solution.py:78
  92.7 0.9 copy-done.8
  93.6 0.8 copy-done.11
  94.4 5.8 %all-to-all-start.5 = ((bf16[32,72,128]{2,1,0:T(8,128)(2,1)}), bf16[32,72,128]{2,1,0:T(8,128)(2,1)S(1)}, u32[]{:S(2)}, u32[]{:S(2)}) async-start(bf16[32,72,128]{2,1,0:T(8,128)(2,1)} %copy-done.11), calls=%async_computation.5 | async-start | bytes 1179648 | tf_op jit(solution)/shard_map/all_to_all | solution.py:442
  100.2 0.0 copy-start.16
  100.2 1.0 copy-done.16
  101.2 1.9 %coarse_kernel.1 = f32[8,128]{1,0:T(8,128)} custom-call(bf16[2816,128]{1,0:T(8,128)(2,1)S(1)} %copy-done.9, bf16[72,2816]{1,0:T(8,128)(2,1)S(1)} %copy-done.12, bf16[32,64,128]{2,1,0:T(8,128)(2,1)S(1)} %copy-done, bf16[3,3,128,128]{3,2,1,0:T(8,128)(2,1)S(1)} %copy-done.16), custom_call_target="tpu_custom_call" | custom-call | bytes 4194304 | tf_op jit(solution)/shard_map/coarse_kernel/pallas_call | solution.py:78
  103.1 13.8 %all-to-all-done.5.refs_0_ = bf16[32,72,128]{2,1,0:T(8,128)(2,1)S(1)} async-done(((bf16[32,72,128]{2,1,0:T(8,128)(2,1)}), bf16[32,72,128]{2,1,0:T(8,128)(2,1)S(1)}, u32[]{:S(2)}, u32[]{:S(2)}) %all-to-all-start.5) | async-done | bytes 589856 | tf_op jit(solution)/shard_map/all_to_all | solution.py:442
  116.9 0.1 share_kernel.1
  117.0 14.9 %all_to_all.35.refs_0_ = bf16[16,72,128]{2,1,0:T(8,128)(2,1)S(1)} all-to-all(bf16[16,72,128]{2,1,0:T(8,128)(2,1)S(1)} %share_kernel.1), channel_id=1, replica_groups={{0,2,4,6,8,10,12,14,16,18,20,22,24,26,28,30},{1,3,5,7,9,11,13,15,17,19,..., dimensions={0} | all-to-all | bytes 589824 | tf_op jit(solution)/shard_map/all_to_all | solution.py:450
  131.9 0.0 collective-permute-start.5
  132.0 1.6 %collective-permute-done.5.refs_1_ = bf16[16,72,128]{2,1,0:T(8,128)(2,1)S(1)} collective-permute-done((bf16[16,72,128]{2,1,0:T(8,128)(2,1)S(1)}, bf16[16,72,128]{2,1,0:T(8,128)(2,1)S(1)}, u32[]{:S(2)}, u32[]{:S(2)}) %collective-permute-start.5) | collective-permute-done | bytes 294944 | tf_op jit(solution)/shard_map/ppermute | solution.py:454
  133.5 1.1 join_kernel.1
  (36 shorter events, 0.1 us)
Async XLA Ops:
  0.6 23.0 %copy-start = (bf16[32,64,128]{2,1,0:T(8,128)(2,1)S(1)}, bf16[32,64,128]{2,1,0:T(8,128)(2,1)}, u32[]{:S(2)}) copy-start(bf16[32,64,128]{2,1,0:T(8,128)(2,1)} %refs_2_.6) | copy-start | bytes 1572868
  0.6 22.9 %copy-start.10 = (bf16[32,64,128]{2,1,0:T(8,128)(2,1)S(1)}, bf16[32,64,128]{2,1,0:T(8,128)(2,1)}, u32[]{:S(2)}) copy-start(bf16[32,64,128]{2,1,0:T(8,128)(2,1)} %refs_0_.4) | copy-start | bytes 1572868
  0.7 1.0 copy-start.17
  1.7 0.7 copy-start.20
  2.4 0.7 copy-start.21
  4.4 19.3 %all-to-all-start = ((bf16[16,72,128]{2,1,0:T(8,128)(2,1)}), bf16[16,72,128]{2,1,0:T(8,128)(2,1)S(1)}, u32[]{:S(2)}, u32[]{:S(2)}) async-start(bf16[16,72,128]{2,1,0:T(8,128)(2,1)} %pack_kernel.1), calls=%async_computation | async-start | bytes 589824 | tf_op jit(solution)/shard_map/all_to_all | solution.py:450
  13.6 5.7 %collective-permute-start = (bf16[2,2,64,128]{3,2,1,0:T(8,128)(2,1)S(1)}, bf16[2,2,64,128]{3,2,1,0:T(8,128)(2,1)S(1)}, u32[]{:S(2)}, u32[]{:S(2)}) collective-permute-start(bf16[2,2,64,128]{3,2,1,0:T(8,128)(2,1)S(1)} %pad_maximum_fusion.2), channel_id=1, source_target_pairs={{0,8},{8,16},{16,24},{1,9},{9,17},{17,25},{2,10},{10,18},{18,26},{... | collective-permute-start | bytes 196616 | tf_op jit(solution)/shard_map/ppermute | solution.py:678
  17.4 6.2 %collective-permute-start.1 = (bf16[2,2,64,128]{3,2,1,0:T(8,128)(2,1)S(1)}, bf16[2,2,64,128]{3,2,1,0:T(8,128)(2,1)S(1)}, u32[]{:S(2)}, u32[]{:S(2)}) collective-permute-start(bf16[2,2,64,128]{3,2,1,0:T(8,128)(2,1)S(1)} %pad_maximum_fusion.3), channel_id=1, source_target_pairs={{8,0},{16,8},{24,16},{9,1},{17,9},{25,17},{10,2},{18,10},{26,18},{... | collective-permute-start | bytes 196616 | tf_op jit(solution)/shard_map/ppermute | solution.py:679
  23.7 1.6 %collective-permute-start.2 = (bf16[16,72,128]{2,1,0:T(8,128)(2,1)S(1)}, bf16[16,72,128]{2,1,0:T(8,128)(2,1)S(1)}, u32[]{:S(2)}, u32[]{:S(2)}) collective-permute-start(bf16[16,72,128]{2,1,0:T(8,128)(2,1)S(1)} %all-to-all-done.refs_0_.refs_2_), channel_id=1, source_target_pairs={{0,1},{1,0},{2,3},{3,2},{4,5},{5,4},{6,7},{7,6},{8,9},{9,8},{10,11... | collective-permute-start | bytes 884744 | tf_op jit(solution)/shard_map/ppermute | solution.py:454
  25.3 1.7 %copy-start.1 = (bf16[3,3,1024,128]{3,2,1,0:T(8,128)(2,1)S(1)}, bf16[3,3,1024,128]{3,2,1,0:T(8,128)(2,1)}, u32[]{:S(2)}) copy-start(bf16[3,3,1024,128]{3,2,1,0:T(8,128)(2,1)} %refs_2_.4) | copy-start | bytes 7077892
  27.0 11.0 %copy-start.22 = (f32[16,128]{1,0:T(8,128)S(1)}, f32[16,128]{1,0:T(8,128)}, u32[]{:S(2)}) copy-start(f32[16,128]{1,0:T(8,128)} %refs_3_.5) | copy-start | bytes 24580
  27.0 11.0 %copy-start.23 = (s32[8,256]{1,0:T(8,128)S(1)}, s32[8,256]{1,0:T(8,128)}, u32[]{:S(2)}) copy-start(s32[8,256]{1,0:T(8,128)} %constant.7.clone.refs_2_) | copy-start | bytes 24580
  29.1 12.1 %copy-start.18 = (bf16[1024,128]{1,0:T(8,128)(2,1)S(1)}, bf16[1024,128]{1,0:T(8,128)(2,1)}, u32[]{:S(2)}) copy-start(bf16[1024,128]{1,0:T(8,128)(2,1)} %refs_3_.4) | copy-start | bytes 786436
  29.2 12.1 %all-to-all-start.1 = ((bf16[8,192,128]{2,1,0:T(8,128)(2,1)}), bf16[8,192,128]{2,1,0:T(8,128)(2,1)S(1)}, u32[]{:S(2)}, u32[]{:S(2)}) async-start(bf16[8,192,128]{2,1,0:T(8,128)(2,1)} %hidden_kernel.1), calls=%async_computation.1 | async-start | bytes 786432 | tf_op jit(solution)/shard_map/all_to_all | solution.py:442
  32.9 15.2 %collective-permute-start.3 = (bf16[2,36,8,128]{3,2,1,0:T(8,128)(2,1)S(1)}, bf16[2,36,8,128]{3,2,1,0:T(8,128)(2,1)S(1)}, u32[]{:S(2)}, u32[]{:S(2)}) collective-permute-start(bf16[2,36,8,128]{3,2,1,0:T(8,128)(2,1)S(1)} %get-tuple-element.32), channel_id=1, source_target_pairs={{1,0},{2,1},{3,2},{4,3},{5,4},{6,5},{7,6},{9,8},{10,9},{11,10},{12... | collective-permute-start | bytes 442376 | tf_op jit(solution)/shard_map/ppermute | solution.py:753
  34.2 13.9 %collective-permute-start.4 = (bf16[2,36,8,128]{3,2,1,0:T(8,128)(2,1)S(1)}, bf16[2,36,8,128]{3,2,1,0:T(8,128)(2,1)}, u32[]{:S(2)}, u32[]{:S(2)}) collective-permute-start(bf16[2,36,8,128]{3,2,1,0:T(8,128)(2,1)S(1)} %get-tuple-element.33), channel_id=1, source_target_pairs={{0,1},{1,2},{2,3},{3,4},{4,5},{5,6},{6,7},{8,9},{9,10},{10,11},{11... | collective-permute-start | bytes 442376 | tf_op jit(solution)/shard_map/ppermute | solution.py:752
  41.3 1.7 %copy-start.2 = (bf16[3,3,1024,128]{3,2,1,0:T(8,128)(2,1)S(1)}, bf16[3,3,1024,128]{3,2,1,0:T(8,128)(2,1)}, u32[]{:S(2)}) copy-start(bf16[3,3,1024,128]{3,2,1,0:T(8,128)(2,1)} %refs_1_.4) | copy-start | bytes 7077892
  42.9 10.6 %copy-start.15 = (bf16[3,3,128,128]{3,2,1,0:T(8,128)(2,1)S(1)}, bf16[3,3,128,128]{3,2,1,0:T(8,128)(2,1)}, u32[]{:S(2)}) copy-start(bf16[3,3,128,128]{3,2,1,0:T(8,128)(2,1)} %refs_3_.7) | copy-start | bytes 884740
  44.7 8.9 %all-to-all-start.2 = ((f32[8,4,8,128]{3,2,1,0:T(8,128)}), f32[8,4,8,128]{3,2,1,0:T(8,128)S(1)}, u32[]{:S(2)}, u32[]{:S(2)}) async-start(f32[8,4,8,128]{3,2,1,0:T(8,128)} %project_kernel.1), calls=%async_computation.2 | async-start | bytes 262144 | tf_op jit(solution)/shard_map/all_to_all | solution.py:442
  57.9 0.9 copy-start.5
  58.8 11.0 %all-to-all-start.3 = ((f32[32,8,128]{2,1,0:T(8,128)}), f32[32,8,128]{2,1,0:T(8,128)S(1)}, u32[]{:S(2)}, u32[]{:S(2)}) async-start(f32[32,8,128]{2,1,0:T(8,128)} %get-tuple-element.37), calls=%async_computation.3 | async-start | bytes 262144 | tf_op jit(solution)/shard_map/all_to_all | solution.py:442
  61.6 1.0 copy-start.26
  65.8 1.1 copy-start.3
  69.8 1.4 %copy-start.4 = (f32[2800,128]{1,0:T(8,128)S(1)}, f32[2800,128]{1,0:T(8,128)}, u32[]{:S(2)}) copy-start(f32[2800,128]{1,0:T(8,128)} %copy-done.3) | copy-start | bytes 4300804
  73.6 0.7 copy-start.19
  74.3 0.9 copy-start.24
  75.2 11.6 %all-to-all-start.4 = ((f32[32,8,128]{2,1,0:T(8,128)}), f32[32,8,128]{2,1,0:T(8,128)}, u32[]{:S(2)}, u32[]{:S(2)}) async-start(f32[32,8,128]{2,1,0:T(8,128)} %copy-done.19), calls=%async_computation.4 | async-start | bytes 262144 | tf_op jit(solution)/shard_map/all_to_all | solution.py:442
  78.5 1.1 copy-start.6
  79.6 1.1 copy-start.25
  80.7 1.0 copy-start.27
  86.1 0.7 copy-start.13
  86.8 1.1 copy-start.7
  87.9 1.0 copy-start.14
  92.7 0.9 copy-start.8
  93.6 0.8 copy-start.11
  94.4 5.8 %copy-start.12 = (bf16[72,2816]{1,0:T(8,128)(2,1)S(1)}, bf16[72,2816]{1,0:T(8,128)(2,1)}, u32[]{:S(2)}) copy-start(bf16[72,2816]{1,0:T(8,128)(2,1)} %constant.8.clone.refs_1_) | copy-start | bytes 1216516
  94.4 5.8 %copy-start.9 = (bf16[2816,128]{1,0:T(8,128)(2,1)S(1)}, bf16[2816,128]{1,0:T(8,128)(2,1)}, u32[]{:S(2)}) copy-start(bf16[2816,128]{1,0:T(8,128)(2,1)} %copy-done.8) | copy-start | bytes 2162692
  94.4 22.5 %all-to-all-start.5 = ((bf16[32,72,128]{2,1,0:T(8,128)(2,1)}), bf16[32,72,128]{2,1,0:T(8,128)(2,1)S(1)}, u32[]{:S(2)}, u32[]{:S(2)}) async-start(bf16[32,72,128]{2,1,0:T(8,128)(2,1)} %copy-done.11), calls=%async_computation.5 | async-start | bytes 1179648 | tf_op jit(solution)/shard_map/all_to_all | solution.py:442
  100.2 1.0 copy-start.16
  131.9 1.6 %collective-permute-start.5 = (bf16[16,72,128]{2,1,0:T(8,128)(2,1)S(1)}, bf16[16,72,128]{2,1,0:T(8,128)(2,1)S(1)}, u32[]{:S(2)}, u32[]{:S(2)}) collective-permute-start(bf16[16,72,128]{2,1,0:T(8,128)(2,1)S(1)} %all_to_all.35.refs_0_), channel_id=1, source_target_pairs={{0,1},{1,0},{2,3},{3,2},{4,5},{5,4},{6,7},{7,6},{8,9},{9,8},{10,11... | collective-permute-start | bytes 884744 | tf_op jit(solution)/shard_map/ppermute | solution.py:454

commit v7 on v6

--- a/solution.py
+++ b/solution.py
@@ -17,7 +17,7 @@
 
 RIM = 8
 MARGIN = 16
-KERNEL_VMEM = 20 * 1024 * 1024
+KERNEL_VMEM = 62 * 1024 * 1024
 
 
 class Layout:
@@ -821,6 +821,7 @@
         2 * conv_flops,
         far={0: None, 1: None, 2: None, 3: None},
         late=(1, 2),
+        far_out=(1,),
         lay=lay,
         chunk=chunk,
     )
@@ -830,8 +831,9 @@
         (stats, grad_stats, first_act, normed_grad, mixed, second_sent),
         [own, total],
         conv_flops,
-        far={2: None, 3: None, 4: None},
-        late=(4,),
+        far={2: None, 3: None, 4: None, 5: None},
+        late=(4, 5),
+        far_out=(1,),
         lay=lay,
         grid=grid,
         chunk=chunk,
@@ -843,7 +845,7 @@
         coarse_kernel,
         jax.ShapeDtypeStruct((blocks, width), jnp.float32),
         (kept, window_picks(lay), output_cotangent, enhancer_first),
-        (),
+        far={0: None, 1: None, 2: None, 3: None},
         lay=lay,
     )
     part, global_gradient = lax.optimization_barrier((part, global_gradient))

time: 136 us -> 142 us (1.044)
  Pallas kernels: 27.4 us -> 51 us
  local copies, waits for them, and re-layouts: 21.2 us -> 5.81 us
  starting transfers between devices: 37.5 us -> 35.7 us
    pallas_call x12, Pallas kernels: 27.4 us -> 51 us  [call(): pl.pallas_call(kernel, out_shape=outs, in_specs=[hbm if i in far else nea...]
    unnamed x56 -> x26, local copies, waits for them, and re-layouts: 20.3 us -> 4.98 us
  transfers between devices with their start and end apart: 12 -> 12, of which waited for: 8 -> 9; matrix products, arithmetic and copies ran while one was open for 1% -> 1% of each run, Pallas kernels for 9% -> 16%
where the time goes in v7:
time: 142 us; the launch traced here: 141 us
  Pallas kernels  51 us (36%)
  starting transfers between devices  35.7 us (25%)
  waiting for transfers between devices  31.8 us (22%)
  blocking collectives  15.1 us (11%)
  local copies, waits for them, and re-layouts  5.81 us (4%)
    pallas_call x12, Pallas kernels, call(): pl.pallas_call(kernel, out_shape=outs, in_specs=[hbm if i in far else nea...  51 us
    all_to_all x5, waiting for transfers between devices, to_all(): return lax.all_to_all(payload, axis, 0, 0)  23.8 us
    all_to_all x5, starting transfers between devices, to_all(): return lax.all_to_all(payload, axis, 0, 0)  17.8 us
    all_to_all x1, blocking collectives, among_cores(): return lax.all_to_all(payload, BOTH, 0, 0, axis_index_groups=groups)  15.1 us
    all_to_all x1, starting transfers between devices, among_cores(): return lax.all_to_all(payload, BOTH, 0, 0, axis_index_groups=groups)  8.32 us
    unnamed x26, local copies, waits for them, and re-layouts  4.98 us
    ppermute x1, waiting for transfers between devices, per_device(): bottom = lax.ppermute(bottoms, 'rows', row_down)  4.28 us
    ppermute x1, starting transfers between devices, per_device(): top = lax.ppermute(tops, 'rows', row_up)  3.83 us
  transfers between devices with their start and end apart: 12, of which 9 were waited for; matrix products, arithmetic and copies ran while one was open for 1% of the time, Pallas kernels for 16%

profile of v7, /device:TPU:0, one launch (start us, length us, event | category | flops | bytes accessed | tf_op | source)
XLA Modules:
  0.0 141.1 jit_solution(8109599066817732725)
XLA Ops:
  0.6 0.0 copy-start.1
  0.6 0.0 copy-start.7
  0.7 2.2 %pack_kernel.1 = bf16[16,72,128]{2,1,0:T(8,128)(2,1)} custom-call(f32[16,32,64]{2,1,0:T(8,128)} %refs_0_.3, s32[32,64]{1,0:T(8,128)} %refs_1_.3, bf16[64,128]{1,0:T(8,128)(2,1)} %bitcast.18), custom_call_target="tpu_custom_call" | custom-call | bytes 4194304 | tf_op jit(solution)/shard_map/pack_kernel/pallas_call | solution.py:78
  2.9 8.3 %all-to-all-start = ((bf16[16,72,128]{2,1,0:T(8,128)(2,1)}), bf16[16,72,128]{2,1,0:T(8,128)(2,1)S(1)}, u32[]{:S(2)}, u32[]{:S(2)}) async-start(bf16[16,72,128]{2,1,0:T(8,128)(2,1)} %pack_kernel.1), calls=%async_computation | async-start | bytes 589824 | tf_op jit(solution)/shard_map/all_to_all | solution.py:450
  11.2 0.8 slice_bitcast_fusion
  12.1 3.8 %collective-permute-start = (bf16[2,2,64,128]{3,2,1,0:T(8,128)(2,1)S(1)}, bf16[2,2,64,128]{3,2,1,0:T(8,128)(2,1)S(1)}, u32[]{:S(2)}, u32[]{:S(2)}) collective-permute-start(bf16[2,2,64,128]{3,2,1,0:T(8,128)(2,1)S(1)} %pad_maximum_fusion.2), channel_id=1, source_target_pairs={{0,8},{8,16},{16,24},{1,9},{9,17},{17,25},{2,10},{10,18},{18,26},{... | collective-permute-start | bytes 196616 | tf_op jit(solution)/shard_map/ppermute | solution.py:678
  15.9 1.3 collective-permute-start.1
  17.2 0.6 collective-permute-done.refs_1_
  17.8 4.3 %collective-permute-done.1.refs_2_ = bf16[2,2,64,128]{3,2,1,0:T(8,128)(2,1)S(1)} collective-permute-done((bf16[2,2,64,128]{3,2,1,0:T(8,128)(2,1)S(1)}, bf16[2,2,64,128]{3,2,1,0:T(8,128)(2,1)S(1)}, u32[]{:S(2)}, u32[]{:S(2)}) %collective-permute-start.1) | collective-permute-done | bytes 65568 | tf_op jit(solution)/shard_map/ppermute | solution.py:679
  22.1 0.0 copy-start.12
  22.1 0.0 copy-done.1
  22.1 0.0 copy-done.7
  22.1 0.1 fusion.4
  22.2 0.0 all-to-all-done.refs_0_.refs_2_
  22.2 0.0 copy-start
  22.2 0.1 collective-permute-start.2
  22.3 1.6 %collective-permute-done.2.refs_1_ = bf16[16,72,128]{2,1,0:T(8,128)(2,1)S(1)} collective-permute-done((bf16[16,72,128]{2,1,0:T(8,128)(2,1)S(1)}, bf16[16,72,128]{2,1,0:T(8,128)(2,1)S(1)}, u32[]{:S(2)}, u32[]{:S(2)}) %collective-permute-start.2) | collective-permute-done | bytes 294944 | tf_op jit(solution)/shard_map/ppermute | solution.py:454
  23.8 0.0 copy-done
  23.8 0.0 copy-start.4
  23.8 0.7 copy-done.4
  24.6 4.6 %hidden_kernel.1 = bf16[8,192,128]{2,1,0:T(8,128)(2,1)} custom-call(bf16[16,72,128]{2,1,0:T(8,128)(2,1)} %copy-done, bf16[16,72,128]{2,1,0:T(8,128)(2,1)} %copy-done.4, bf16[3,3,1024,128]{3,2,1,0:T(8,128)(2,1)} %refs_2_.4), custom_call_target="tpu_custom_call" | custom-call | flops 603979776 | bytes 4194304 | tf_op jit(solution)/shard_map/hidden_kernel/pallas_call | solution.py:78
  29.1 0.0 copy-done.11
  29.1 0.0 copy-done.12
  29.2 3.7 %all-to-all-start.1 = ((bf16[8,192,128]{2,1,0:T(8,128)(2,1)}), bf16[8,192,128]{2,1,0:T(8,128)(2,1)S(1)}, u32[]{:S(2)}, u32[]{:S(2)}) async-start(bf16[8,192,128]{2,1,0:T(8,128)(2,1)} %hidden_kernel.1), calls=%async_computation.1 | async-start | bytes 786432 | tf_op jit(solution)/shard_map/all_to_all | solution.py:442
  32.8 1.3 collective-permute-start.3
  34.1 3.0 %collective-permute-start.4 = (bf16[2,36,8,128]{3,2,1,0:T(8,128)(2,1)S(1)}, bf16[2,36,8,128]{3,2,1,0:T(8,128)(2,1)S(1)}, u32[]{:S(2)}, u32[]{:S(2)}) collective-permute-start(bf16[2,36,8,128]{3,2,1,0:T(8,128)(2,1)S(1)} %get-tuple-element.33), channel_id=1, source_target_pairs={{0,1},{1,2},{2,3},{3,4},{4,5},{5,6},{6,7},{8,9},{9,10},{10,11},{11... | collective-permute-start | bytes 442376 | tf_op jit(solution)/shard_map/ppermute | solution.py:752
  37.2 2.5 %pool_kernel.1 = (f32[32,128]{1,0:T(8,128)}, f32[32,128]{1,0:T(8,128)}) custom-call(bf16[16,72,128]{2,1,0:T(8,128)(2,1)} %copy-done, bf16[16,72,128]{2,1,0:T(8,128)(2,1)} %copy-done.4, s32[8,256]{1,0:T(8,128)} %constant.7.clone.refs_2_, f32[16,128]{1,0:T(8,128)} %refs_3_.5), custom_call_target="tpu_custom_call" | custom-call | bytes 4194304 | tf_op jit(solution)/shard_map/pool_kernel/pallas_call | solution.py:78
  39.6 1.5 %all-to-all-done.1.refs_0_ = bf16[8,192,128]{2,1,0:T(8,128)(2,1)S(1)} async-done(((bf16[8,192,128]{2,1,0:T(8,128)(2,1)}), bf16[8,192,128]{2,1,0:T(8,128)(2,1)S(1)}, u32[]{:S(2)}, u32[]{:S(2)}) %all-to-all-start.1) | async-done | bytes 393248 | tf_op jit(solution)/shard_map/all_to_all | solution.py:442
  41.2 0.7 copy-done.3
  41.9 4.1 %project_kernel.1 = f32[8,4,8,128]{3,2,1,0:T(8,128)} custom-call(bf16[8,192,128]{2,1,0:T(8,128)(2,1)} %copy-done.3, bf16[3,3,1024,128]{3,2,1,0:T(8,128)(2,1)} %refs_1_.4, bf16[16,72,128]{2,1,0:T(8,128)(2,1)} %copy-done, bf16[1024,128]{1,0:T(8,128)(2,1)} %refs_3_.4), custom_call_target="tpu_custom_call" | custom-call | flops 301989888 | bytes 4194304 | tf_op jit(solution)/shard_map/project_kernel/pallas_call | solution.py:78
  46.1 3.7 %all-to-all-start.2 = ((f32[8,4,8,128]{3,2,1,0:T(8,128)}), f32[8,4,8,128]{3,2,1,0:T(8,128)S(1)}, u32[]{:S(2)}, u32[]{:S(2)}) async-start(f32[8,4,8,128]{3,2,1,0:T(8,128)} %project_kernel.1), calls=%async_computation.2 | async-start | bytes 262144 | tf_op jit(solution)/shard_map/all_to_all | solution.py:442
  49.7 0.0 collective-permute-done.3
  49.7 0.0 collective-permute-done.4
  49.7 0.8 fusion.2.refs_3_
  50.5 4.7 %all-to-all-done.2.refs_4_ = f32[8,4,8,128]{3,2,1,0:T(8,128)S(1)} async-done(((f32[8,4,8,128]{3,2,1,0:T(8,128)}), f32[8,4,8,128]{3,2,1,0:T(8,128)S(1)}, u32[]{:S(2)}, u32[]{:S(2)}) %all-to-all-start.2) | async-done | bytes 131104 | tf_op jit(solution)/shard_map/all_to_all | solution.py:442
  55.3 0.0 copy-start.10
  55.3 0.7 copy-done.10
  55.9 6.3 %mixed_kernel.1 = (bf16[3072,128]{1,0:T(8,128)(2,1)}, f32[2800,128]{1,0:T(8,128)}, f32[32,8,128]{2,1,0:T(8,128)}) custom-call(bf16[32,64,128]{2,1,0:T(8,128)(2,1)} %refs_0_.4, bf16[2,2,64,128]{3,2,1,0:T(8,128)(2,1)} %copy-done.11, bf16[2,2,64,128]{3,2,1,0:T(8,128)(2,1)} %copy-done.12, bf16[2,37,16,128]{3,2,1,0:T(8,128)(2,1)} %fusion.2.refs_3_, ...), custom_call_target="tpu_custom_call" | custom-call | flops 825753600 | bytes 4194304 | tf_op jit(solution)/shard_map/mixed_kernel/pallas_call | solution.py:78
  62.2 3.0 %all-to-all-start.3 = ((f32[32,8,128]{2,1,0:T(8,128)}), f32[32,8,128]{2,1,0:T(8,128)S(1)}, u32[]{:S(2)}, u32[]{:S(2)}) async-start(f32[32,8,128]{2,1,0:T(8,128)} %get-tuple-element.37), calls=%async_computation.3 | async-start | bytes 262144 | tf_op jit(solution)/shard_map/all_to_all | solution.py:442
  65.2 5.0 %cot_kernel.1.refs_2_ = f32[2800,128]{1,0:T(8,128)} custom-call(bf16[32,64,128]{2,1,0:T(8,128)(2,1)} %refs_2_.6, bf16[2,2,64,128]{3,2,1,0:T(8,128)(2,1)} %copy-done.11, bf16[2,2,64,128]{3,2,1,0:T(8,128)(2,1)} %copy-done.12, bf16[2,37,16,128]{3,2,1,0:T(8,128)(2,1)} %fusion.2.refs_3_, bf16[3,3,128,128]{3,2,1,0:T(8,128)(2,1)} %refs_3_.6), custom_call_target="tpu_custom_call" | custom-call | flops 825753600 | bytes 4194304 | tf_op jit(solution)/shard_map/cot_kernel/pallas_call | solution.py:78
  70.2 3.2 %all-to-all-done.3.refs_1_.refs_0_ = f32[32,8,128]{2,1,0:T(8,128)S(1)} async-done(((f32[32,8,128]{2,1,0:T(8,128)}), f32[32,8,128]{2,1,0:T(8,128)S(1)}, u32[]{:S(2)}, u32[]{:S(2)}) %all-to-all-start.3) | async-done | bytes 131104 | tf_op jit(solution)/shard_map/all_to_all | solution.py:442
  73.5 0.0 copy-start.5
  73.5 0.6 copy-done.5
  74.1 5.5 %norm_kernel.1 = (bf16[3072,128]{1,0:T(8,128)(2,1)}, f32[2800,128]{1,0:T(8,128)}, f32[32,8,128]{2,1,0:T(8,128)}) custom-call(f32[2800,128]{1,0:T(8,128)} %get-tuple-element.36.refs_0_.refs_2_, f32[32,8,128]{2,1,0:T(8,128)} %copy-done.5, f32[2800,128]{1,0:T(8,128)} %cot_kernel.1.refs_2_), custom_call_target="tpu_custom_call" | custom-call | bytes 4194304 | tf_op jit(solution)/shard_map/norm_kernel/pallas_call | solution.py:78
  79.7 2.6 %all-to-all-start.4 = ((f32[32,8,128]{2,1,0:T(8,128)}), f32[32,8,128]{2,1,0:T(8,128)S(1)}, u32[]{:S(2)}, u32[]{:S(2)}) async-start(f32[32,8,128]{2,1,0:T(8,128)} %get-tuple-element.41), calls=%async_computation.4 | async-start | bytes 262144 | tf_op jit(solution)/shard_map/all_to_all | solution.py:442
  82.3 7.3 %second_kernel.1 = (bf16[32,64,128]{2,1,0:T(8,128)(2,1)}, bf16[16,72,128]{2,1,0:T(8,128)(2,1)}) custom-call(bf16[3072,128]{1,0:T(8,128)(2,1)} %get-tuple-element.38.refs_0_, bf16[3072,128]{1,0:T(8,128)(2,1)} %get-tuple-element.39.refs_1_.refs_4_, bf16[32,64,128]{2,1,0:T(8,128)(2,1)} %refs_2_.6, bf16[3,3,128,128]{3,2,1,0:T(8,128)(2,1)} %refs_3_.6), custom_call_target="tpu_custom_call" | custom-call | flops 1651507200 | bytes 4194304 | tf_op jit(solution)/shard_map/second_kernel/pallas_call | solution.py:78
  89.6 1.0 all-to-all-done.4.refs_1_
  90.5 0.0 copy-start.8
  90.5 0.6 copy-done.8
  91.2 6.0 %first_kernel.1 = (bf16[32,72,128]{2,1,0:T(8,128)(2,1)}, bf16[2816,128]{1,0:T(8,128)(2,1)}) custom-call(f32[32,8,128]{2,1,0:T(8,128)} %copy-done.5, f32[32,8,128]{2,1,0:T(8,128)} %copy-done.8, f32[2800,128]{1,0:T(8,128)} %get-tuple-element.36.refs_0_.refs_2_, f32[2800,128]{1,0:T(8,128)} %get-tuple-element.42.refs_3_, ...), custom_call_target="tpu_custom_call" | custom-call | flops 825753600 | bytes 4194304 | tf_op jit(solution)/shard_map/first_kernel/pallas_call | solution.py:78
  97.2 4.9 %all-to-all-start.5 = ((bf16[32,72,128]{2,1,0:T(8,128)(2,1)}), bf16[32,72,128]{2,1,0:T(8,128)(2,1)S(1)}, u32[]{:S(2)}, u32[]{:S(2)}) async-start(bf16[32,72,128]{2,1,0:T(8,128)(2,1)} %get-tuple-element.44), calls=%async_computation.5 | async-start | bytes 1179648 | tf_op jit(solution)/shard_map/all_to_all | solution.py:442
  102.1 3.4 %coarse_kernel.1 = f32[8,128]{1,0:T(8,128)} custom-call(bf16[2816,128]{1,0:T(8,128)(2,1)} %get-tuple-element.45.refs_0_, bf16[72,2816]{1,0:T(8,128)(2,1)} %constant.8.clone.refs_1_, bf16[32,64,128]{2,1,0:T(8,128)(2,1)} %refs_2_.6, bf16[3,3,128,128]{3,2,1,0:T(8,128)(2,1)} %refs_3_.7), custom_call_target="tpu_custom_call" | custom-call | bytes 4194304 | tf_op jit(solution)/shard_map/coarse_kernel/pallas_call | solution.py:78
  105.5 13.3 %all-to-all-done.5.refs_0_ = bf16[32,72,128]{2,1,0:T(8,128)(2,1)S(1)} async-done(((bf16[32,72,128]{2,1,0:T(8,128)(2,1)}), bf16[32,72,128]{2,1,0:T(8,128)(2,1)S(1)}, u32[]{:S(2)}, u32[]{:S(2)}) %all-to-all-start.5) | async-done | bytes 589856 | tf_op jit(solution)/shard_map/all_to_all | solution.py:442
  118.8 0.0 copy-start.2
  118.8 0.8 copy-done.2
  119.6 1.9 %share_kernel.1 = bf16[16,72,128]{2,1,0:T(8,128)(2,1)} custom-call(bf16[32,72,128]{2,1,0:T(8,128)(2,1)} %copy-done.2), custom_call_target="tpu_custom_call" | custom-call | bytes 4194304 | tf_op jit(solution)/shard_map/share_kernel/pallas_call | solution.py:78
  121.5 15.1 %all_to_all.35.refs_0_ = bf16[16,72,128]{2,1,0:T(8,128)(2,1)S(1)} all-to-all(bf16[16,72,128]{2,1,0:T(8,128)(2,1)} %share_kernel.1), channel_id=1, replica_groups={{0,2,4,6,8,10,12,14,16,18,20,22,24,26,28,30},{1,3,5,7,9,11,13,15,17,19,..., dimensions={0} | all-to-all | bytes 589824 | tf_op jit(solution)/shard_map/all_to_all | solution.py:450
  136.6 0.0 copy-start.6
  136.6 0.0 collective-permute-start.5
  136.6 1.6 %collective-permute-done.5.refs_1_ = bf16[16,72,128]{2,1,0:T(8,128)(2,1)S(1)} collective-permute-done((bf16[16,72,128]{2,1,0:T(8,128)(2,1)S(1)}, bf16[16,72,128]{2,1,0:T(8,128)(2,1)S(1)}, u32[]{:S(2)}, u32[]{:S(2)}) %collective-permute-start.5) | collective-permute-done | bytes 294944 | tf_op jit(solution)/shard_map/ppermute | solution.py:454
  138.2 0.0 copy-done.6
  138.2 0.0 copy-start.9
  138.2 0.7 copy-done.9
  138.9 2.1 %join_kernel.1 = (f32[1152,128]{1,0:T(8,128)}, f32[1152,128]{1,0:T(8,128)}) custom-call(bf16[16,72,128]{2,1,0:T(8,128)(2,1)} %copy-done.6, bf16[16,72,128]{2,1,0:T(8,128)(2,1)} %copy-done.9), custom_call_target="tpu_custom_call" | custom-call | bytes 4194304 | tf_op jit(solution)/shard_map/join_kernel/pallas_call | solution.py:78
  (6 shorter events, 0.0 us)
Async XLA Ops:
  0.6 21.5 %copy-start.1 = (bf16[32,64,128]{2,1,0:T(8,128)(2,1)S(1)}, bf16[32,64,128]{2,1,0:T(8,128)(2,1)}, u32[]{:S(2)}) copy-start(bf16[32,64,128]{2,1,0:T(8,128)(2,1)} %refs_2_.6) | copy-start | bytes 1572868
  0.6 21.5 %copy-start.7 = (bf16[32,64,128]{2,1,0:T(8,128)(2,1)S(1)}, bf16[32,64,128]{2,1,0:T(8,128)(2,1)}, u32[]{:S(2)}) copy-start(bf16[32,64,128]{2,1,0:T(8,128)(2,1)} %refs_0_.4) | copy-start | bytes 1572868
  2.9 19.3 %all-to-all-start = ((bf16[16,72,128]{2,1,0:T(8,128)(2,1)}), bf16[16,72,128]{2,1,0:T(8,128)(2,1)S(1)}, u32[]{:S(2)}, u32[]{:S(2)}) async-start(bf16[16,72,128]{2,1,0:T(8,128)(2,1)} %pack_kernel.1), calls=%async_computation | async-start | bytes 589824 | tf_op jit(solution)/shard_map/all_to_all | solution.py:450
  12.1 5.7 %collective-permute-start = (bf16[2,2,64,128]{3,2,1,0:T(8,128)(2,1)S(1)}, bf16[2,2,64,128]{3,2,1,0:T(8,128)(2,1)S(1)}, u32[]{:S(2)}, u32[]{:S(2)}) collective-permute-start(bf16[2,2,64,128]{3,2,1,0:T(8,128)(2,1)S(1)} %pad_maximum_fusion.2), channel_id=1, source_target_pairs={{0,8},{8,16},{16,24},{1,9},{9,17},{17,25},{2,10},{10,18},{18,26},{... | collective-permute-start | bytes 196616 | tf_op jit(solution)/shard_map/ppermute | solution.py:678
  15.9 6.2 %collective-permute-start.1 = (bf16[2,2,64,128]{3,2,1,0:T(8,128)(2,1)S(1)}, bf16[2,2,64,128]{3,2,1,0:T(8,128)(2,1)S(1)}, u32[]{:S(2)}, u32[]{:S(2)}) collective-permute-start(bf16[2,2,64,128]{3,2,1,0:T(8,128)(2,1)S(1)} %pad_maximum_fusion.3), channel_id=1, source_target_pairs={{8,0},{16,8},{24,16},{9,1},{17,9},{25,17},{10,2},{18,10},{26,18},{... | collective-permute-start | bytes 196616 | tf_op jit(solution)/shard_map/ppermute | solution.py:679
  17.8 11.3 %copy-start.11 = (bf16[2,2,64,128]{3,2,1,0:T(8,128)(2,1)}, bf16[2,2,64,128]{3,2,1,0:T(8,128)(2,1)S(1)}, u32[]{:S(2)}) copy-start(bf16[2,2,64,128]{3,2,1,0:T(8,128)(2,1)S(1)} %collective-permute-done.refs_1_) | copy-start | bytes 196612
  22.1 7.1 %copy-start.12 = (bf16[2,2,64,128]{3,2,1,0:T(8,128)(2,1)}, bf16[2,2,64,128]{3,2,1,0:T(8,128)(2,1)S(1)}, u32[]{:S(2)}) copy-start(bf16[2,2,64,128]{3,2,1,0:T(8,128)(2,1)S(1)} %collective-permute-done.1.refs_2_) | copy-start | bytes 196612
  22.2 1.7 %copy-start = (bf16[16,72,128]{2,1,0:T(8,128)(2,1)}, bf16[16,72,128]{2,1,0:T(8,128)(2,1)S(1)}, u32[]{:S(2)}) copy-start(bf16[16,72,128]{2,1,0:T(8,128)(2,1)S(1)} %all-to-all-done.refs_0_.refs_2_) | copy-start | bytes 884740
  22.2 1.6 %collective-permute-start.2 = (bf16[16,72,128]{2,1,0:T(8,128)(2,1)S(1)}, bf16[16,72,128]{2,1,0:T(8,128)(2,1)S(1)}, u32[]{:S(2)}, u32[]{:S(2)}) collective-permute-start(bf16[16,72,128]{2,1,0:T(8,128)(2,1)S(1)} %all-to-all-done.refs_0_.refs_2_), channel_id=1, source_target_pairs={{0,1},{1,0},{2,3},{3,2},{4,5},{5,4},{6,7},{7,6},{8,9},{9,8},{10,11... | collective-permute-start | bytes 884744 | tf_op jit(solution)/shard_map/ppermute | solution.py:454
  23.8 0.7 copy-start.4
  29.2 12.0 %all-to-all-start.1 = ((bf16[8,192,128]{2,1,0:T(8,128)(2,1)}), bf16[8,192,128]{2,1,0:T(8,128)(2,1)S(1)}, u32[]{:S(2)}, u32[]{:S(2)}) async-start(bf16[8,192,128]{2,1,0:T(8,128)(2,1)} %hidden_kernel.1), calls=%async_computation.1 | async-start | bytes 786432 | tf_op jit(solution)/shard_map/all_to_all | solution.py:442
  32.8 16.9 %collective-permute-start.3 = (bf16[2,36,8,128]{3,2,1,0:T(8,128)(2,1)S(1)}, bf16[2,36,8,128]{3,2,1,0:T(8,128)(2,1)S(1)}, u32[]{:S(2)}, u32[]{:S(2)}) collective-permute-start(bf16[2,36,8,128]{3,2,1,0:T(8,128)(2,1)S(1)} %get-tuple-element.32), channel_id=1, source_target_pairs={{1,0},{2,1},{3,2},{4,3},{5,4},{6,5},{7,6},{9,8},{10,9},{11,10},{12... | collective-permute-start | bytes 442376 | tf_op jit(solution)/shard_map/ppermute | solution.py:753
  34.1 15.6 %collective-permute-start.4 = (bf16[2,36,8,128]{3,2,1,0:T(8,128)(2,1)S(1)}, bf16[2,36,8,128]{3,2,1,0:T(8,128)(2,1)S(1)}, u32[]{:S(2)}, u32[]{:S(2)}) collective-permute-start(bf16[2,36,8,128]{3,2,1,0:T(8,128)(2,1)S(1)} %get-tuple-element.33), channel_id=1, source_target_pairs={{0,1},{1,2},{2,3},{3,4},{4,5},{5,6},{6,7},{8,9},{9,10},{10,11},{11... | collective-permute-start | bytes 442376 | tf_op jit(solution)/shard_map/ppermute | solution.py:752
  41.2 0.7 copy-start.3
  46.1 9.2 %all-to-all-start.2 = ((f32[8,4,8,128]{3,2,1,0:T(8,128)}), f32[8,4,8,128]{3,2,1,0:T(8,128)S(1)}, u32[]{:S(2)}, u32[]{:S(2)}) async-start(f32[8,4,8,128]{3,2,1,0:T(8,128)} %project_kernel.1), calls=%async_computation.2 | async-start | bytes 262144 | tf_op jit(solution)/shard_map/all_to_all | solution.py:442
  55.3 0.7 copy-start.10
  62.2 11.2 %all-to-all-start.3 = ((f32[32,8,128]{2,1,0:T(8,128)}), f32[32,8,128]{2,1,0:T(8,128)S(1)}, u32[]{:S(2)}, u32[]{:S(2)}) async-start(f32[32,8,128]{2,1,0:T(8,128)} %get-tuple-element.37), calls=%async_computation.3 | async-start | bytes 262144 | tf_op jit(solution)/shard_map/all_to_all | solution.py:442
  73.5 0.7 copy-start.5
  79.7 10.9 %all-to-all-start.4 = ((f32[32,8,128]{2,1,0:T(8,128)}), f32[32,8,128]{2,1,0:T(8,128)S(1)}, u32[]{:S(2)}, u32[]{:S(2)}) async-start(f32[32,8,128]{2,1,0:T(8,128)} %get-tuple-element.41), calls=%async_computation.4 | async-start | bytes 262144 | tf_op jit(solution)/shard_map/all_to_all | solution.py:442
  90.5 0.6 copy-start.8
  97.2 21.6 %all-to-all-start.5 = ((bf16[32,72,128]{2,1,0:T(8,128)(2,1)}), bf16[32,72,128]{2,1,0:T(8,128)(2,1)S(1)}, u32[]{:S(2)}, u32[]{:S(2)}) async-start(bf16[32,72,128]{2,1,0:T(8,128)(2,1)} %get-tuple-element.44), calls=%async_computation.5 | async-start | bytes 1179648 | tf_op jit(solution)/shard_map/all_to_all | solution.py:442
  118.8 0.8 copy-start.2
  136.6 1.6 %copy-start.6 = (bf16[16,72,128]{2,1,0:T(8,128)(2,1)}, bf16[16,72,128]{2,1,0:T(8,128)(2,1)S(1)}, u32[]{:S(2)}) copy-start(bf16[16,72,128]{2,1,0:T(8,128)(2,1)S(1)} %all_to_all.35.refs_0_) | copy-start | bytes 884740
  136.6 1.6 %collective-permute-start.5 = (bf16[16,72,128]{2,1,0:T(8,128)(2,1)S(1)}, bf16[16,72,128]{2,1,0:T(8,128)(2,1)S(1)}, u32[]{:S(2)}, u32[]{:S(2)}) collective-permute-start(bf16[16,72,128]{2,1,0:T(8,128)(2,1)S(1)} %all_to_all.35.refs_0_), channel_id=1, source_target_pairs={{0,1},{1,0},{2,3},{3,2},{4,5},{5,4},{6,7},{7,6},{8,9},{9,8},{10,11... | collective-permute-start | bytes 884744 | tf_op jit(solution)/shard_map/ppermute | solution.py:454
  138.2 0.7 copy-start.9

commit v8 on v6

--- a/solution.py
+++ b/solution.py
@@ -32,16 +32,16 @@
         self.kept = -(-self.out // 128) * 128
 
 
-def call(body, outs, ins, scratch=(), flops=0, far=None, late=(), far_out=(), **fixed):
-    far = far or {}
+def call(
+    body, outs, ins, scratch=(), flops=0, far=(), pick=None, far_out=(), limit=KERNEL_VMEM, **fixed
+):
+    pick = pick or {}
     single = not isinstance(outs, tuple)
     outs = (outs,) if single else outs
     n_in, n_out, n_own = len(ins), len(outs), len(scratch)
     near = pl.BlockSpec(memory_space=pltpu.VMEM)
     hbm = pl.BlockSpec(memory_space=pltpu.MemorySpace.HBM)
-    landing = [
-        pltpu.VMEM(ins[i].shape[0 if k is None else 1 :], ins[i].dtype) for i, k in far.items()
-    ]
+    landing = [pltpu.VMEM(ins[i].shape, ins[i].dtype) for i in far]
     leaving = [pltpu.VMEM(outs[j].shape, outs[j].dtype) for j in far_out]
 
     def kernel(*refs):
@@ -49,26 +49,19 @@
         rest = refs[n_in + n_out :]
         own, rest = rest[:n_own], rest[n_own:]
         buffers, sems = rest[: len(far) + len(far_out)], rest[len(far) + len(far_out) :]
-        copies = {}
-        for slot, (i, k) in enumerate(far.items()):
-            source = in_refs[i] if k is None else in_refs[i].at[k]
-            copies[i] = pltpu.make_async_copy(source, buffers[slot], sems[slot])
-            copies[i].start()
+        starts, results = [], []
+        for slot, i in enumerate(far):
+            starts.append(pltpu.make_async_copy(in_refs[i], buffers[slot], sems[slot]))
+            starts[-1].start()
             in_refs[i] = buffers[slot]
-        results = []
         for slot, j in enumerate(far_out, len(far)):
             results.append((buffers[slot], out_refs[j], sems[slot]))
             out_refs[j] = buffers[slot]
-        for i, copy in copies.items():
-            if i not in late:
-                copy.wait()
-
-        def arrive():
-            for i in late:
-                copies[i].wait()
-
-        extra = {"arrive": arrive} if late else {}
-        body(*in_refs, *out_refs, *own, **fixed, **extra)
+        for i, k in pick.items():
+            in_refs[i] = in_refs[i].at[k]
+        for copy in starts:
+            copy.wait()
+        body(*in_refs, *out_refs, *own, **fixed)
         ends = [pltpu.make_async_copy(*triple) for triple in results]
         for copy in ends:
             copy.start()
@@ -86,7 +79,7 @@
             *leaving,
             *[pltpu.SemaphoreType.DMA] * (len(landing) + len(leaving)),
         ],
-        compiler_params=pltpu.CompilerParams(vmem_limit_bytes=KERNEL_VMEM),
+        compiler_params=pltpu.CompilerParams(vmem_limit_bytes=limit),
         cost_estimate=pl.CostEstimate(flops=flops, bytes_accessed=4 << 20, transcendentals=0),
         name=body.__name__,
     )(*ins)
@@ -169,12 +162,13 @@
     @pl.loop(0, lay.out_rows)
     def _(r):
         begin = pl.multiple_of(r * lay.wide, 16)
-        grad_out[pl.ds(begin, lay.wide)] = taken((z0, z1, z2), begin, lay.wide, True)
+        value = taken((z0, z1, z2), begin, lay.wide, True)
+        grad_out[pl.ds(begin, lay.wide)] = value.astype(jnp.bfloat16)
 
 
 def mixed_kernel(
     main, top, bottom, strip, coarse, pooled, valid, weight, flat, act_out, stats, square, terms, z0,
-    z1, z2, *, lay, arrive
+    z1, z2, *, lay
 ):
     width = main.shape[2]
     flat[...] = jnp.zeros_like(flat)
@@ -208,7 +202,6 @@
         flat[base + lay.cols : base + lay.wide] = (
             strip[k].astype(jnp.float32) + jnp.concatenate([right, left], 0)
         ).astype(jnp.bfloat16)
-    arrive()
     put_square(square, weight, False)
     taps_matmul(flat, square, (z0, z1, z2), lay, False)
 
@@ -248,30 +241,24 @@
     return lambda r: near * row_inside(r - 2) + following * row_inside(r - 1)
 
 
-def norm_kernel(
-    act, stats, act_grad, activated, grad_out, grad_stats, *, lay, grid, pixel_total
-):
+def gated(value):
+    gate = 1.0 / (1.0 + jnp.exp(-value))
+    return gate, gate * (1.0 + value * (1.0 - gate))
+
+
+def norm_kernel(act, stats, act_grad, grad_stats, *, lay, pixel_total):
     width = act.shape[1]
     mean, inverse = act_moments(stats, pixel_total)
-    mask = inside_masks(lay, width, *grid)
-    activated[...] = jnp.zeros_like(activated)
-
-    def step(r, sums):
-        begin = pl.multiple_of(r * lay.wide, 16)
-        normed = (act[pl.ds(begin, lay.wide)] - mean) * inverse
-        gate = 1.0 / (1.0 + jnp.exp(-normed))
-        inside = mask(r)
-        activated[pl.ds(pl.multiple_of(begin + MARGIN + lay.wide, 16), lay.wide)] = (
-            normed * gate * inside
-        ).astype(jnp.bfloat16)
-        grad = act_grad[pl.ds(begin, lay.wide)] * gate * (1.0 + normed * (1.0 - gate))
-        grad_out[pl.ds(begin, lay.wide)] = grad
-        mine = ((r >= 2) & (r < lay.rows + 2)).astype(jnp.float32)
-        own_grad = grad[: lay.cols] * mine
-        return sums[0] + folded(own_grad), sums[1] + folded(own_grad * normed[: lay.cols])
+
+    def step(i, sums):
+        begin = pl.multiple_of((i + 2) * lay.wide, 16)
+        normed = (act[pl.ds(begin, lay.cols)] - mean) * inverse
+        _, slope = gated(normed)
+        grad = act_grad[pl.ds(begin, lay.cols)].astype(jnp.float32) * slope
+        return sums[0] + folded(grad), sums[1] + folded(grad * normed)
 
     zero = jnp.zeros((8, width), jnp.float32)
-    sums = lax.fori_loop(0, lay.out_rows, step, (zero, zero))
+    sums = lax.fori_loop(0, lay.rows, step, (zero, zero))
     send_stats(grad_stats, *sums)
 
 
@@ -313,12 +300,25 @@
 
 
 def second_kernel(
-    activated, mixed, main, weight, enhanced, sent, square, z0, z1, z2, own, total, *, lay, chunk,
-    arrive
+    act, stats, mixed, main, weight, enhanced, sent, activated, square, z0, z1, z2, own, total, *, lay, chunk,
+    grid, pixel_total
 ):
+    width = act.shape[1]
+    mean, inverse = act_moments(stats, pixel_total)
+    mask = inside_masks(lay, width, *grid)
+    activated[...] = jnp.zeros_like(activated)
+
+    @pl.loop(0, lay.out_rows)
+    def _(r):
+        begin = pl.multiple_of(r * lay.wide, 16)
+        normed = (act[pl.ds(begin, lay.wide)] - mean) * inverse
+        gate, _ = gated(normed)
+        activated[pl.ds(pl.multiple_of(begin + MARGIN + lay.wide, 16), lay.wide)] = (
+            normed * gate * mask(r)
+        ).astype(jnp.bfloat16)
+
     put_square(square, weight, False)
     taps_matmul(activated, square, (z0, z1, z2), lay, False)
-    arrive()
 
     @pl.loop(0, lay.rows)
     def _(i):
@@ -340,8 +340,8 @@
 
 
 def first_kernel(
-    stats, grad_stats, act, grad_ref, mixed, second, sent, kept, own, total, *, lay, grid,
-    chunk, pixel_total, arrive
+    stats, grad_stats, act, act_grad, mixed, second, sent, kept, own, total, *, lay, grid,
+    chunk, pixel_total
 ):
     width = act.shape[1]
     mean, inverse = act_moments(stats, pixel_total)
@@ -354,11 +354,10 @@
     @pl.loop(0, lay.out_rows)
     def _(r):
         begin = pl.multiple_of(r * lay.wide, 16)
-        value = inverse * (
-            grad_ref[pl.ds(begin, lay.wide)]
-            - grad_mean
-            - (act[pl.ds(begin, lay.wide)] - mean) * inverse * cross_mean
-        )
+        normed = (act[pl.ds(begin, lay.wide)] - mean) * inverse
+        _, slope = gated(normed)
+        grad = act_grad[pl.ds(begin, lay.wide)].astype(jnp.float32) * slope
+        value = inverse * (grad - grad_mean - normed * cross_mean)
         value = (value * mask(r)).astype(jnp.bfloat16)
         kept[pl.ds(begin, lay.wide)] = value
 
@@ -367,7 +366,6 @@
             place = pl.multiple_of((r - 2) * lay.wide + 2 * MARGIN, 16)
             own[pl.ds(place, lay.cols)] = value[: lay.cols].astype(jnp.float32)
 
-    arrive()
     weight_matmul(mixed, own, total, sent, lay, chunk)
     for d in range(second.shape[0]):
         sent[second.shape[0] + d] = second[d]
@@ -560,7 +558,7 @@
     return total
 
 
-def hidden_kernel(mine, other, weight, sent, rows_ref, shifted, kept, *, grid, band, direct, arrive):
+def hidden_kernel(mine, other, weight, sent, rows_ref, shifted, kept, *, grid, band, direct):
     row_devices, col_devices = grid
     band_rows, cols = band
     coarse_rows = row_devices * band_rows
@@ -578,7 +576,6 @@
                 ]
     else:
         rows_ref[cols : cols + coarse_rows * cols] = mine[...]
-    arrive()
     raw = channel_conv(rows_ref, weight, shifted, coarse_rows, cols)
     pixels = coarse_rows * cols
     mean = jnp.sum(raw, 0, keepdims=True) / pixels
@@ -594,7 +591,7 @@
 
 def project_kernel(
     received, weight, source, project, sent, rows_ref, shifted, residual, spread, *, grid, band,
-    direct, arrive
+    direct
 ):
     row_devices, col_devices = grid
     band_rows, cols = band
@@ -602,7 +599,6 @@
     my_col = lax.axis_index("cols")
     for c in range(col_devices):
         rows_ref[:, c * width : (c + 1) * width] = received[c]
-    arrive()
     raw = channel_conv(rows_ref, weight, shifted, band_rows + 2, cols)
     count = (band_rows + 2) * cols
     if direct:
@@ -662,7 +658,8 @@
         jax.ShapeDtypeStruct((devices // 2, main_rows + 8, 128), jnp.bfloat16),
         (encoder_features, instance_map, main),
         [pltpu.VMEM((128, tile_cols), jnp.float32)],
-        far={0: None, 1: None, 2: None},
+        far=(0, 1, 2),
+        limit=62 * 1024 * 1024,
     )
     mine = among_cores(sent_input, row_devices, col_devices)
     late_input, late_cotangent, _ = lax.optimization_barrier(
@@ -740,8 +737,6 @@
             pltpu.VMEM((coarse_rows + 4, band_cols, width_share), jnp.bfloat16),
         ],
         18 * coarse_rows * band_cols * channels * width_share,
-        far={2: None},
-        late=(2,),
         far_out=(0,),
         grid=grid,
         band=band,
@@ -760,12 +755,11 @@
     )
     act_grad = call(
         cot_kernel,
-        out_shape,
+        jax.ShapeDtypeStruct((lay.out, width), jnp.bfloat16),
         (output_cotangent, top, bottom, strip, enhancer_second),
         [pltpu.VMEM((lay.flat, width), jnp.bfloat16), square, *z],
         conv_flops,
-        far={0: None, 1: 1, 2: 1, 3: 1, 4: None},
-        far_out=(0,),
+        pick={1: 1, 2: 1, 3: 1},
         lay=lay,
     )
 
@@ -780,8 +774,6 @@
             pltpu.VMEM((band_rows + 2, band_cols + 16, width), jnp.float32),
         ],
         18 * (band_rows + 2) * band_cols * channels * width_share,
-        far={1: None, 2: None, 3: None},
-        late=(1, 2, 3),
         far_out=(0,),
         grid=grid,
         band=band,
@@ -796,42 +788,38 @@
         (enhancer_input, top, bottom, strip, *terms, enhancer_first),
         [square, pltpu.VMEM((block_rows + 2, 8, width), jnp.float32), *z],
         conv_flops,
-        far={0: None, 1: 0, 2: 0, 3: 0, 5: None, 6: None, 7: None},
-        late=(7,),
-        far_out=(0, 1, 2),
+        pick={1: 0, 2: 0, 3: 0},
+        far_out=(2,),
         lay=lay,
     )
     stats = to_all(stats, BOTH)
-    activated, normed_grad, grad_stats = call(
+    grad_stats = call(
         norm_kernel,
-        (flat_shape, out_shape, stats_shape),
+        stats_shape,
         (first_act, stats, act_grad),
-        far={0: None, 2: None},
-        far_out=(0, 1, 2),
+        far_out=(0,),
         lay=lay,
-        grid=grid,
         pixel_total=pixel_total,
     )
     grad_stats = to_all(grad_stats, BOTH)
     enhanced, second_sent = call(
         second_kernel,
         (jax.ShapeDtypeStruct((tile_rows, tile_cols, width), jnp.bfloat16), half_shape),
-        (activated, mixed, output_cotangent, enhancer_second),
-        [square, *z, own, total],
+        (first_act, stats, mixed, output_cotangent, enhancer_second),
+        [pltpu.VMEM((lay.flat, width), jnp.bfloat16), square, *z, own, total],
         2 * conv_flops,
-        far={0: None, 1: None, 2: None, 3: None},
-        late=(1, 2),
         lay=lay,
         chunk=chunk,
+        grid=grid,
+        pixel_total=pixel_total,
     )
     sent_both, kept = call(
         first_kernel,
         (sent_shape, jax.ShapeDtypeStruct((lay.kept, width), jnp.bfloat16)),
-        (stats, grad_stats, first_act, normed_grad, mixed, second_sent),
+        (stats, grad_stats, first_act, act_grad, mixed, second_sent),
         [own, total],
         conv_flops,
-        far={2: None, 3: None, 4: None},
-        late=(4,),
+        far_out=(0,),
         lay=lay,
         grid=grid,
         chunk=chunk,

time: 136 us -> 129 us (0.949)
  local copies, waits for them, and re-layouts: 21.2 us -> 13.6 us
  waiting for transfers between devices: 31.7 us -> 33.4 us
  Pallas kernels: 27.4 us -> 25.9 us
    unnamed x56 -> x38, local copies, waits for them, and re-layouts: 20.3 us -> 12.7 us
    all_to_all x5, waiting for transfers between devices: 23.7 us -> 27.7 us  [to_all(): return lax.all_to_all(payload, axis, 0, 0)]
    ppermute x1, waiting for transfers between devices: 4.29 us -> 1.12 us  [per_device(): bottom = lax.ppermute(bottoms, 'rows', row_down)]
    concatenate x1, other arithmetic: 0.05 us -> 1.67 us  [per_device(): jnp.concatenate([top[:, :, :RIM], both[:, :, :RIM], bottom[:, :, :RIM]], 1)]
    pallas_call x12, Pallas kernels: 27.4 us -> 25.9 us  [call(): pl.pallas_call(kernel, out_shape=outs, in_specs=[hbm if i in far else nea...]
  transfers between devices with their start and end apart: 12 -> 12, of which waited for: 8 -> 10; matrix products, arithmetic and copies ran while one was open for 1% -> 2% of each run, Pallas kernels for 9% -> 9%
where the time goes in v8:
time: 129 us; the launch traced here: 128 us
  starting transfers between devices  37 us (29%)
  waiting for transfers between devices  33.4 us (26%)
  Pallas kernels  25.9 us (20%)
  blocking collectives  14.9 us (12%)
  local copies, waits for them, and re-layouts  13.6 us (11%)
  other arithmetic  1.74 us (1%)
    all_to_all x5, waiting for transfers between devices, to_all(): return lax.all_to_all(payload, axis, 0, 0)  27.7 us
    pallas_call x12, Pallas kernels, call(): pl.pallas_call(kernel, out_shape=outs, in_specs=[hbm if i in far else nea...  25.9 us
    all_to_all x5, starting transfers between devices, to_all(): return lax.all_to_all(payload, axis, 0, 0)  18.9 us
    all_to_all x1, blocking collectives, among_cores(): return lax.all_to_all(payload, BOTH, 0, 0, axis_index_groups=groups)  14.9 us
    unnamed x38, local copies, waits for them, and re-layouts  12.7 us
    all_to_all x1, starting transfers between devices, among_cores(): return lax.all_to_all(payload, BOTH, 0, 0, axis_index_groups=groups)  8.46 us
    ppermute x1, starting transfers between devices, per_device(): top = lax.ppermute(tops, 'rows', row_up)  4.55 us
    ppermute x2, waiting for transfers between devices, core_swap(): return lax.ppermute(array, 'cols', [(c, c ^ 1) for c in range(col_devices)])  3.16 us
  transfers between devices with their start and end apart: 12, of which 10 were waited for; matrix products, arithmetic and copies ran while one was open for 2% of the time, Pallas kernels for 9%

profile of v8, /device:TPU:0, one launch (start us, length us, event | category | flops | bytes accessed | tf_op | source)
XLA Modules:
  0.0 127.5 jit_solution(6944529501097594451)
XLA Ops:
  0.6 2.1 %pack_kernel.1 = bf16[16,72,128]{2,1,0:T(8,128)(2,1)} custom-call(f32[16,32,64]{2,1,0:T(8,128)} %refs_0_.3, s32[32,64]{1,0:T(8,128)} %refs_1_.3, bf16[64,128]{1,0:T(8,128)(2,1)} %bitcast.20), custom_call_target="tpu_custom_call" | custom-call | bytes 4194304 | tf_op jit(solution)/shard_map/pack_kernel/pallas_call | solution.py:71
  2.8 0.0 copy-start.1
  2.8 8.5 %all-to-all-start = ((bf16[16,72,128]{2,1,0:T(8,128)(2,1)}), bf16[16,72,128]{2,1,0:T(8,128)(2,1)S(1)}, u32[]{:S(2)}, u32[]{:S(2)}) async-start(bf16[16,72,128]{2,1,0:T(8,128)(2,1)} %pack_kernel.1), calls=%async_computation | async-start | bytes 589824 | tf_op jit(solution)/shard_map/all_to_all | solution.py:448
  11.3 0.8 slice_bitcast_fusion
  12.1 1.3 %collective-permute-start.1 = (bf16[2,2,64,128]{3,2,1,0:T(8,128)(2,1)S(1)}, bf16[2,2,64,128]{3,2,1,0:T(8,128)(2,1)S(1)}, u32[]{:S(2)}, u32[]{:S(2)}) collective-permute-start(bf16[2,2,64,128]{3,2,1,0:T(8,128)(2,1)S(1)} %pad_maximum_fusion.3), channel_id=1, source_target_pairs={{8,0},{16,8},{24,16},{9,1},{17,9},{25,17},{10,2},{18,10},{26,18},{... | collective-permute-start | bytes 196616 | tf_op jit(solution)/shard_map/ppermute | solution.py:676
  13.4 4.5 %collective-permute-start = (bf16[2,2,64,128]{3,2,1,0:T(8,128)(2,1)S(1)}, bf16[2,2,64,128]{3,2,1,0:T(8,128)(2,1)S(1)}, u32[]{:S(2)}, u32[]{:S(2)}) collective-permute-start(bf16[2,2,64,128]{3,2,1,0:T(8,128)(2,1)S(1)} %pad_maximum_fusion.2), channel_id=1, source_target_pairs={{0,8},{8,16},{16,24},{1,9},{9,17},{17,25},{2,10},{10,18},{18,26},{... | collective-permute-start | bytes 196616 | tf_op jit(solution)/shard_map/ppermute | solution.py:675
  18.0 1.1 collective-permute-done.1.refs_2_
  19.1 0.8 collective-permute-done.refs_1_
  19.9 1.7 %fusion.4 = (bf16[2,36,8,128]{3,2,1,0:T(8,128)(2,1)}, bf16[2,36,8,128]{3,2,1,0:T(8,128)(2,1)}) fusion(bf16[1,32,64,128]{3,2,1,0:T(8,128)(2,1)} %bitcast.16, bf16[1,32,64,128]{3,2,1,0:T(8,128)(2,1)} %bitcast.17, bf16[2,2,8,128]{3,2,1,0:T(8,128)(2,1)S(1)} %get-tuple-element.52, bf16[2,2,8,128]{3,2,1,0:T(8,128)(2,1)S(1)} %get-tuple-element.50, ...), kind=kLoop, calls=%fused_computation.7 | loop fusion | flops 1179648 | bytes 1376256 | tf_op jit(solution)/shard_map/concatenate | solution.py:679
  21.5 0.7 all-to-all-done.refs_0_.refs_2_
  22.2 0.0 collective-permute-start.2
  22.2 1.6 %collective-permute-done.2.refs_1_ = bf16[16,72,128]{2,1,0:T(8,128)(2,1)S(1)} collective-permute-done((bf16[16,72,128]{2,1,0:T(8,128)(2,1)S(1)}, bf16[16,72,128]{2,1,0:T(8,128)(2,1)S(1)}, u32[]{:S(2)}, u32[]{:S(2)}) %collective-permute-start.2) | collective-permute-done | bytes 294944 | tf_op jit(solution)/shard_map/ppermute | solution.py:452
  23.8 0.0 copy-done.1
  23.8 1.9 %hidden_kernel.1 = bf16[8,192,128]{2,1,0:T(8,128)(2,1)} custom-call(bf16[16,72,128]{2,1,0:T(8,128)(2,1)S(1)} %all-to-all-done.refs_0_.refs_2_, bf16[16,72,128]{2,1,0:T(8,128)(2,1)S(1)} %collective-permute-done.2.refs_1_, bf16[3,3,1024,128]{3,2,1,0:T(8,128)(2,1)S(1)} %copy-done.1), custom_call_target="tpu_custom_call" | custom-call | flops 603979776 | bytes 4194304 | tf_op jit(solution)/shard_map/hidden_kernel/pallas_call | solution.py:71
  25.7 0.0 copy-start.13
  25.7 3.6 %all-to-all-start.1 = ((bf16[8,192,128]{2,1,0:T(8,128)(2,1)}), bf16[8,192,128]{2,1,0:T(8,128)(2,1)S(1)}, u32[]{:S(2)}, u32[]{:S(2)}) async-start(bf16[8,192,128]{2,1,0:T(8,128)(2,1)} %hidden_kernel.1), calls=%async_computation.1 | async-start | bytes 786432 | tf_op jit(solution)/shard_map/all_to_all | solution.py:440
  29.4 2.5 %collective-permute-start.4 = (bf16[2,36,8,128]{3,2,1,0:T(8,128)(2,1)}, bf16[2,36,8,128]{3,2,1,0:T(8,128)(2,1)S(1)}, u32[]{:S(2)}, u32[]{:S(2)}) collective-permute-start(bf16[2,36,8,128]{3,2,1,0:T(8,128)(2,1)} %get-tuple-element.30), channel_id=1, source_target_pairs={{0,1},{1,2},{2,3},{3,4},{4,5},{5,6},{6,7},{8,9},{9,10},{10,11},{11... | collective-permute-start | bytes 442376 | tf_op jit(solution)/shard_map/ppermute | solution.py:747
  31.9 1.3 %collective-permute-start.3 = (bf16[2,36,8,128]{3,2,1,0:T(8,128)(2,1)}, bf16[2,36,8,128]{3,2,1,0:T(8,128)(2,1)S(1)}, u32[]{:S(2)}, u32[]{:S(2)}) collective-permute-start(bf16[2,36,8,128]{3,2,1,0:T(8,128)(2,1)} %get-tuple-element.29), channel_id=1, source_target_pairs={{1,0},{2,1},{3,2},{4,3},{5,4},{6,5},{7,6},{9,8},{10,9},{11,10},{12... | collective-permute-start | bytes 442376 | tf_op jit(solution)/shard_map/ppermute | solution.py:748
  33.2 0.0 copy-done.16
  33.2 0.0 copy-done.17
  33.2 0.8 pool_kernel.1
  34.0 3.7 %all-to-all-done.1.refs_0_ = bf16[8,192,128]{2,1,0:T(8,128)(2,1)S(1)} async-done(((bf16[8,192,128]{2,1,0:T(8,128)(2,1)}), bf16[8,192,128]{2,1,0:T(8,128)(2,1)S(1)}, u32[]{:S(2)}, u32[]{:S(2)}) %all-to-all-start.1) | async-done | bytes 393248 | tf_op jit(solution)/shard_map/all_to_all | solution.py:440
  37.7 1.7 %copy-done.2 = bf16[3,3,1024,128]{3,2,1,0:T(8,128)(2,1)S(1)} copy-done((bf16[3,3,1024,128]{3,2,1,0:T(8,128)(2,1)S(1)}, bf16[3,3,1024,128]{3,2,1,0:T(8,128)(2,1)}, u32[]{:S(2)}) %copy-start.2) | copy-done | bytes 2359320
  39.4 0.9 copy-done.15
  40.3 1.4 %project_kernel.1 = f32[8,4,8,128]{3,2,1,0:T(8,128)} custom-call(bf16[8,192,128]{2,1,0:T(8,128)(2,1)S(1)} %all-to-all-done.1.refs_0_, bf16[3,3,1024,128]{3,2,1,0:T(8,128)(2,1)S(1)} %copy-done.2, bf16[16,72,128]{2,1,0:T(8,128)(2,1)S(1)} %all-to-all-done.refs_0_.refs_2_, bf16[1024,128]{1,0:T(8,128)(2,1)S(1)} %copy-done.15), custom_call_target="tpu_custom_call" | custom-call | flops 301989888 | bytes 4194304 | tf_op jit(solution)/shard_map/project_kernel/pallas_call | solution.py:71
  41.7 0.0 copy-start
  41.7 3.5 %all-to-all-start.2 = ((f32[8,4,8,128]{3,2,1,0:T(8,128)}), f32[8,4,8,128]{3,2,1,0:T(8,128)S(1)}, u32[]{:S(2)}, u32[]{:S(2)}) async-start(f32[8,4,8,128]{3,2,1,0:T(8,128)} %project_kernel.1), calls=%async_computation.2 | async-start | bytes 262144 | tf_op jit(solution)/shard_map/all_to_all | solution.py:440
  45.3 0.0 collective-permute-done.4
  45.3 0.0 collective-permute-done.3
  45.3 0.1 fusion.2.refs_3_
  45.3 5.4 %all-to-all-done.2.refs_4_ = f32[8,4,8,128]{3,2,1,0:T(8,128)S(1)} async-done(((f32[8,4,8,128]{3,2,1,0:T(8,128)}), f32[8,4,8,128]{3,2,1,0:T(8,128)S(1)}, u32[]{:S(2)}, u32[]{:S(2)}) %all-to-all-start.2) | async-done | bytes 131104 | tf_op jit(solution)/shard_map/all_to_all | solution.py:440
  50.7 0.0 copy-done.13
  50.7 3.5 %mixed_kernel.1 = (bf16[3072,128]{1,0:T(8,128)(2,1)S(1)}, f32[2800,128]{1,0:T(8,128)S(1)}, f32[32,8,128]{2,1,0:T(8,128)}) custom-call(bf16[32,64,128]{2,1,0:T(8,128)(2,1)S(1)} %copy-done.6, bf16[2,2,64,128]{3,2,1,0:T(8,128)(2,1)S(1)} %collective-permute-done.refs_1_, bf16[2,2,64,128]{3,2,1,0:T(8,128)(2,1)S(1)} %collective-permute-done.1.refs_2_, ...), custom_call_target="tpu_custom_call" | custom-call | flops 825753600 | bytes 4194304 | tf_op jit(solution)/shard_map/mixed_kernel/pallas_call | solution.py:71
  54.3 0.9 copy-done.3
  55.2 4.5 %all-to-all-start.3 = ((f32[32,8,128]{2,1,0:T(8,128)}), f32[32,8,128]{2,1,0:T(8,128)S(1)}, u32[]{:S(2)}, u32[]{:S(2)}) async-start(f32[32,8,128]{2,1,0:T(8,128)} %get-tuple-element.34), calls=%async_computation.3 | async-start | bytes 262144 | tf_op jit(solution)/shard_map/all_to_all | solution.py:440
  59.7 0.0 copy-start.18
  59.7 1.0 copy-done.18
  60.7 2.6 %cot_kernel.1.refs_2_.refs_3_ = bf16[2800,128]{1,0:T(8,128)(2,1)S(1)} custom-call(bf16[32,64,128]{2,1,0:T(8,128)(2,1)S(1)} %copy-done, bf16[2,2,64,128]{3,2,1,0:T(8,128)(2,1)S(1)} %collective-permute-done.refs_1_, bf16[2,2,64,128]{3,2,1,0:T(8,128)(2,1)S(1)} %collective-permute-done.1.refs_2_, bf16[2,37,16,128]{3,2,1,0:T(8,128)(2,1)S(1)} %fusion.2.refs_3_, ...), custom_call_target="tpu_custom_call" | custom-call | flops 825753600 | bytes 4194304 | tf_op jit(solution)/shard_map/cot_kernel/pallas_call | solution.py:71
  63.3 4.6 %all-to-all-done.3.refs_1_.refs_0_ = f32[32,8,128]{2,1,0:T(8,128)S(1)} async-done(((f32[32,8,128]{2,1,0:T(8,128)}), f32[32,8,128]{2,1,0:T(8,128)S(1)}, u32[]{:S(2)}, u32[]{:S(2)}) %all-to-all-start.3) | async-done | bytes 131104 | tf_op jit(solution)/shard_map/all_to_all | solution.py:440
  67.9 1.8 %norm_kernel.1 = f32[32,8,128]{2,1,0:T(8,128)} custom-call(f32[2800,128]{1,0:T(8,128)S(1)} %get-tuple-element.33.refs_0_.refs_2_, f32[32,8,128]{2,1,0:T(8,128)S(1)} %all-to-all-done.3.refs_1_.refs_0_, bf16[2800,128]{1,0:T(8,128)(2,1)S(1)} %cot_kernel.1.refs_2_.refs_3_), custom_call_target="tpu_custom_call" | custom-call | bytes 4194304 | tf_op jit(solution)/shard_map/norm_kernel/pallas_call | solution.py:71
  69.8 2.6 %all-to-all-start.4 = ((f32[32,8,128]{2,1,0:T(8,128)}), f32[32,8,128]{2,1,0:T(8,128)S(1)}, u32[]{:S(2)}, u32[]{:S(2)}) async-start(f32[32,8,128]{2,1,0:T(8,128)} %norm_kernel.1), calls=%async_computation.4 | async-start | bytes 262144 | tf_op jit(solution)/shard_map/all_to_all | solution.py:440
  72.4 1.1 copy-done.4
  73.5 5.2 %second_kernel.1 = (bf16[32,64,128]{2,1,0:T(8,128)(2,1)}, bf16[16,72,128]{2,1,0:T(8,128)(2,1)S(1)}) custom-call(f32[2800,128]{1,0:T(8,128)S(1)} %get-tuple-element.33.refs_0_.refs_2_, f32[32,8,128]{2,1,0:T(8,128)S(1)} %all-to-all-done.3.refs_1_.refs_0_, bf16[3072,128]{1,0:T(8,128)(2,1)S(1)} %copy-done.4, bf16[32,64,128]{2,1,0:T(8,128)(2,1)S(1)} %copy-done, ...), custom_call_target="tpu_custom_call" | custom-call | flops 1651507200 | bytes 4194304 | tf_op jit(solution)/shard_map/second_kernel/pallas_call | solution.py:71
  78.7 0.0 copy-start.11
  78.7 0.7 copy-done.11
  79.4 1.2 all-to-all-done.4.refs_1_
  80.6 0.7 copy-done.8
  81.3 1.1 copy-done.5
  82.4 0.9 copy-done.9
  83.3 1.0 copy-done.12
  84.2 3.4 %first_kernel.1 = (bf16[32,72,128]{2,1,0:T(8,128)(2,1)S(1)}, bf16[2816,128]{1,0:T(8,128)(2,1)S(1)}) custom-call(f32[32,8,128]{2,1,0:T(8,128)S(1)} %all-to-all-done.3.refs_1_.refs_0_, f32[32,8,128]{2,1,0:T(8,128)S(1)} %copy-done.9, f32[2800,128]{1,0:T(8,128)S(1)} %get-tuple-element.33.refs_0_.refs_2_, bf16[2800,128]{1,0:T(8,128)(2,1)S(1)} %cot_kernel.1.refs_2_.refs_3_, ...), custom_call_target="tpu_custom_call" | custom-call | flops 825753600 | bytes 4194304 | tf_op jit(solution)/shard_map/first_kernel/pallas_call | solution.py:71
  87.6 0.0 copy-start.7
  87.7 0.8 copy-done.7
  88.5 4.6 %all-to-all-start.5 = ((bf16[32,72,128]{2,1,0:T(8,128)(2,1)}), bf16[32,72,128]{2,1,0:T(8,128)(2,1)S(1)}, u32[]{:S(2)}, u32[]{:S(2)}) async-start(bf16[32,72,128]{2,1,0:T(8,128)(2,1)} %copy-done.7), calls=%async_computation.5 | async-start | bytes 1179648 | tf_op jit(solution)/shard_map/all_to_all | solution.py:440
  93.1 0.0 copy-start.10
  93.1 1.0 copy-done.10
  94.1 1.0 copy-done.14
  95.1 1.9 %coarse_kernel.1 = f32[8,128]{1,0:T(8,128)} custom-call(bf16[2816,128]{1,0:T(8,128)(2,1)S(1)} %get-tuple-element.39.refs_0_, bf16[72,2816]{1,0:T(8,128)(2,1)S(1)} %copy-done.10, bf16[32,64,128]{2,1,0:T(8,128)(2,1)S(1)} %copy-done, bf16[3,3,128,128]{3,2,1,0:T(8,128)(2,1)S(1)} %copy-done.14), custom_call_target="tpu_custom_call" | custom-call | bytes 4194304 | tf_op jit(solution)/shard_map/coarse_kernel/pallas_call | solution.py:71
  97.0 12.8 %all-to-all-done.5.refs_0_ = bf16[32,72,128]{2,1,0:T(8,128)(2,1)S(1)} async-done(((bf16[32,72,128]{2,1,0:T(8,128)(2,1)}), bf16[32,72,128]{2,1,0:T(8,128)(2,1)S(1)}, u32[]{:S(2)}, u32[]{:S(2)}) %all-to-all-start.5) | async-done | bytes 589856 | tf_op jit(solution)/shard_map/all_to_all | solution.py:440
  109.8 0.1 share_kernel.1
  109.9 14.9 %all_to_all.35.refs_0_ = bf16[16,72,128]{2,1,0:T(8,128)(2,1)S(1)} all-to-all(bf16[16,72,128]{2,1,0:T(8,128)(2,1)S(1)} %share_kernel.1), channel_id=1, replica_groups={{0,2,4,6,8,10,12,14,16,18,20,22,24,26,28,30},{1,3,5,7,9,11,13,15,17,19,..., dimensions={0} | all-to-all | bytes 589824 | tf_op jit(solution)/shard_map/all_to_all | solution.py:448
  124.9 0.0 collective-permute-start.5
  124.9 1.6 %collective-permute-done.5.refs_1_ = bf16[16,72,128]{2,1,0:T(8,128)(2,1)S(1)} collective-permute-done((bf16[16,72,128]{2,1,0:T(8,128)(2,1)S(1)}, bf16[16,72,128]{2,1,0:T(8,128)(2,1)S(1)}, u32[]{:S(2)}, u32[]{:S(2)}) %collective-permute-start.5) | collective-permute-done | bytes 294944 | tf_op jit(solution)/shard_map/ppermute | solution.py:452
  126.4 1.1 join_kernel.1
  (18 shorter events, 0.0 us)
Async XLA Ops:
  2.8 21.0 %copy-start.1 = (bf16[3,3,1024,128]{3,2,1,0:T(8,128)(2,1)S(1)}, bf16[3,3,1024,128]{3,2,1,0:T(8,128)(2,1)}, u32[]{:S(2)}) copy-start(bf16[3,3,1024,128]{3,2,1,0:T(8,128)(2,1)} %refs_2_.3) | copy-start | bytes 7077892
  2.8 19.4 %all-to-all-start = ((bf16[16,72,128]{2,1,0:T(8,128)(2,1)}), bf16[16,72,128]{2,1,0:T(8,128)(2,1)S(1)}, u32[]{:S(2)}, u32[]{:S(2)}) async-start(bf16[16,72,128]{2,1,0:T(8,128)(2,1)} %pack_kernel.1), calls=%async_computation | async-start | bytes 589824 | tf_op jit(solution)/shard_map/all_to_all | solution.py:448
  12.1 7.0 %collective-permute-start.1 = (bf16[2,2,64,128]{3,2,1,0:T(8,128)(2,1)S(1)}, bf16[2,2,64,128]{3,2,1,0:T(8,128)(2,1)S(1)}, u32[]{:S(2)}, u32[]{:S(2)}) collective-permute-start(bf16[2,2,64,128]{3,2,1,0:T(8,128)(2,1)S(1)} %pad_maximum_fusion.3), channel_id=1, source_target_pairs={{8,0},{16,8},{24,16},{9,1},{17,9},{25,17},{10,2},{18,10},{26,18},{... | collective-permute-start | bytes 196616 | tf_op jit(solution)/shard_map/ppermute | solution.py:676
  13.4 6.4 %collective-permute-start = (bf16[2,2,64,128]{3,2,1,0:T(8,128)(2,1)S(1)}, bf16[2,2,64,128]{3,2,1,0:T(8,128)(2,1)S(1)}, u32[]{:S(2)}, u32[]{:S(2)}) collective-permute-start(bf16[2,2,64,128]{3,2,1,0:T(8,128)(2,1)S(1)} %pad_maximum_fusion.2), channel_id=1, source_target_pairs={{0,8},{8,16},{16,24},{1,9},{9,17},{17,25},{2,10},{10,18},{18,26},{... | collective-permute-start | bytes 196616 | tf_op jit(solution)/shard_map/ppermute | solution.py:675
  21.5 11.7 %copy-start.16 = (f32[16,128]{1,0:T(8,128)S(1)}, f32[16,128]{1,0:T(8,128)}, u32[]{:S(2)}) copy-start(f32[16,128]{1,0:T(8,128)} %refs_3_.5) | copy-start | bytes 24580
  21.5 11.7 %copy-start.17 = (s32[8,256]{1,0:T(8,128)S(1)}, s32[8,256]{1,0:T(8,128)}, u32[]{:S(2)}) copy-start(s32[8,256]{1,0:T(8,128)} %constant.7.clone.refs_2_) | copy-start | bytes 24580
  22.2 1.6 %collective-permute-start.2 = (bf16[16,72,128]{2,1,0:T(8,128)(2,1)S(1)}, bf16[16,72,128]{2,1,0:T(8,128)(2,1)S(1)}, u32[]{:S(2)}, u32[]{:S(2)}) collective-permute-start(bf16[16,72,128]{2,1,0:T(8,128)(2,1)S(1)} %all-to-all-done.refs_0_.refs_2_), channel_id=1, source_target_pairs={{0,1},{1,0},{2,3},{3,2},{4,5},{5,4},{6,7},{7,6},{8,9},{9,8},{10,11... | collective-permute-start | bytes 884744 | tf_op jit(solution)/shard_map/ppermute | solution.py:452
  25.7 25.0 %copy-start.13 = (bf16[3,3,128,128]{3,2,1,0:T(8,128)(2,1)S(1)}, bf16[3,3,128,128]{3,2,1,0:T(8,128)(2,1)}, u32[]{:S(2)}) copy-start(bf16[3,3,128,128]{3,2,1,0:T(8,128)(2,1)} %refs_3_.7) | copy-start | bytes 884740
  25.7 12.0 %all-to-all-start.1 = ((bf16[8,192,128]{2,1,0:T(8,128)(2,1)}), bf16[8,192,128]{2,1,0:T(8,128)(2,1)S(1)}, u32[]{:S(2)}, u32[]{:S(2)}) async-start(bf16[8,192,128]{2,1,0:T(8,128)(2,1)} %hidden_kernel.1), calls=%async_computation.1 | async-start | bytes 786432 | tf_op jit(solution)/shard_map/all_to_all | solution.py:440
  29.4 21.4 %copy-start.6 = (bf16[32,64,128]{2,1,0:T(8,128)(2,1)S(1)}, bf16[32,64,128]{2,1,0:T(8,128)(2,1)}, u32[]{:S(2)}) copy-start(bf16[32,64,128]{2,1,0:T(8,128)(2,1)} %refs_0_.4) | copy-start | bytes 1572868
  29.4 15.9 %collective-permute-start.4 = (bf16[2,36,8,128]{3,2,1,0:T(8,128)(2,1)}, bf16[2,36,8,128]{3,2,1,0:T(8,128)(2,1)S(1)}, u32[]{:S(2)}, u32[]{:S(2)}) collective-permute-start(bf16[2,36,8,128]{3,2,1,0:T(8,128)(2,1)} %get-tuple-element.30), channel_id=1, source_target_pairs={{0,1},{1,2},{2,3},{3,4},{4,5},{5,6},{6,7},{8,9},{9,10},{10,11},{11... | collective-permute-start | bytes 442376 | tf_op jit(solution)/shard_map/ppermute | solution.py:747
  31.9 13.4 %collective-permute-start.3 = (bf16[2,36,8,128]{3,2,1,0:T(8,128)(2,1)}, bf16[2,36,8,128]{3,2,1,0:T(8,128)(2,1)S(1)}, u32[]{:S(2)}, u32[]{:S(2)}) collective-permute-start(bf16[2,36,8,128]{3,2,1,0:T(8,128)(2,1)} %get-tuple-element.29), channel_id=1, source_target_pairs={{1,0},{2,1},{3,2},{4,3},{5,4},{6,5},{7,6},{9,8},{10,9},{11,10},{12... | collective-permute-start | bytes 442376 | tf_op jit(solution)/shard_map/ppermute | solution.py:748
  37.7 1.7 %copy-start.2 = (bf16[3,3,1024,128]{3,2,1,0:T(8,128)(2,1)S(1)}, bf16[3,3,1024,128]{3,2,1,0:T(8,128)(2,1)}, u32[]{:S(2)}) copy-start(bf16[3,3,1024,128]{3,2,1,0:T(8,128)(2,1)} %refs_1_.4) | copy-start | bytes 7077892
  39.4 0.9 copy-start.15
  41.7 18.0 %copy-start = (bf16[32,64,128]{2,1,0:T(8,128)(2,1)S(1)}, bf16[32,64,128]{2,1,0:T(8,128)(2,1)}, u32[]{:S(2)}) copy-start(bf16[32,64,128]{2,1,0:T(8,128)(2,1)} %refs_2_.4) | copy-start | bytes 1572868
  41.7 9.0 %all-to-all-start.2 = ((f32[8,4,8,128]{3,2,1,0:T(8,128)}), f32[8,4,8,128]{3,2,1,0:T(8,128)S(1)}, u32[]{:S(2)}, u32[]{:S(2)}) async-start(f32[8,4,8,128]{3,2,1,0:T(8,128)} %project_kernel.1), calls=%async_computation.2 | async-start | bytes 262144 | tf_op jit(solution)/shard_map/all_to_all | solution.py:440
  54.3 0.9 copy-start.3
  55.2 12.8 %all-to-all-start.3 = ((f32[32,8,128]{2,1,0:T(8,128)}), f32[32,8,128]{2,1,0:T(8,128)S(1)}, u32[]{:S(2)}, u32[]{:S(2)}) async-start(f32[32,8,128]{2,1,0:T(8,128)} %get-tuple-element.34), calls=%async_computation.3 | async-start | bytes 262144 | tf_op jit(solution)/shard_map/all_to_all | solution.py:440
  59.7 1.0 copy-start.18
  69.8 10.8 %all-to-all-start.4 = ((f32[32,8,128]{2,1,0:T(8,128)}), f32[32,8,128]{2,1,0:T(8,128)S(1)}, u32[]{:S(2)}, u32[]{:S(2)}) async-start(f32[32,8,128]{2,1,0:T(8,128)} %norm_kernel.1), calls=%async_computation.4 | async-start | bytes 262144 | tf_op jit(solution)/shard_map/all_to_all | solution.py:440
  72.4 1.1 copy-start.4
  78.7 0.7 copy-start.11
  80.6 0.7 copy-start.8
  81.2 1.1 copy-start.5
  82.4 0.9 copy-start.9
  83.3 1.0 copy-start.12
  87.6 0.8 copy-start.7
  88.5 21.4 %all-to-all-start.5 = ((bf16[32,72,128]{2,1,0:T(8,128)(2,1)}), bf16[32,72,128]{2,1,0:T(8,128)(2,1)S(1)}, u32[]{:S(2)}, u32[]{:S(2)}) async-start(bf16[32,72,128]{2,1,0:T(8,128)(2,1)} %copy-done.7), calls=%async_computation.5 | async-start | bytes 1179648 | tf_op jit(solution)/shard_map/all_to_all | solution.py:440
  93.1 1.0 copy-start.10
  94.1 1.0 copy-start.14
  124.9 1.6 %collective-permute-start.5 = (bf16[16,72,128]{2,1,0:T(8,128)(2,1)S(1)}, bf16[16,72,128]{2,1,0:T(8,128)(2,1)S(1)}, u32[]{:S(2)}, u32[]{:S(2)}) collective-permute-start(bf16[16,72,128]{2,1,0:T(8,128)(2,1)S(1)} %all_to_all.35.refs_0_), channel_id=1, source_target_pairs={{0,1},{1,0},{2,3},{3,2},{4,5},{5,4},{6,7},{7,6},{8,9},{9,8},{10,11... | collective-permute-start | bytes 884744 | tf_op jit(solution)/shard_map/ppermute | solution.py:452

commit v9 on v8

--- a/solution.py
+++ b/solution.py
@@ -33,7 +33,8 @@
 
 
 def call(
-    body, outs, ins, scratch=(), flops=0, far=(), pick=None, far_out=(), limit=KERNEL_VMEM, **fixed
+    body, outs, ins, scratch=(), flops=0, far=(), stream=None, pick=None, far_out=(),
+    limit=KERNEL_VMEM, **fixed
 ):
     pick = pick or {}
     single = not isinstance(outs, tuple)
@@ -42,6 +43,8 @@
     near = pl.BlockSpec(memory_space=pltpu.VMEM)
     hbm = pl.BlockSpec(memory_space=pltpu.MemorySpace.HBM)
     landing = [pltpu.VMEM(ins[i].shape, ins[i].dtype) for i in far]
+    flow = [] if stream is None else [pltpu.VMEM(ins[stream].shape, ins[stream].dtype)]
+    parts = 0 if stream is None else ins[stream].shape[0]
     leaving = [pltpu.VMEM(outs[j].shape, outs[j].dtype) for j in far_out]
 
     def kernel(*refs):
@@ -49,11 +52,23 @@
         rest = refs[n_in + n_out :]
         own, rest = rest[:n_own], rest[n_own:]
         buffers, sems = rest[: len(far) + len(far_out)], rest[len(far) + len(far_out) :]
+        sems, flow_sems = sems[: len(far) + len(far_out)], sems[len(far) + len(far_out) :]
+        extra, flowing = {}, []
+        if stream is not None:
+            target, flow_sems = flow_sems[0], flow_sems[1:]
+            for k in range(parts):
+                flowing.append(
+                    pltpu.make_async_copy(in_refs[stream].at[k], target.at[k], flow_sems[k])
+                )
+            in_refs[stream] = target
+            extra["arrive"] = lambda k: flowing[k].wait()
         starts, results = [], []
         for slot, i in enumerate(far):
             starts.append(pltpu.make_async_copy(in_refs[i], buffers[slot], sems[slot]))
             starts[-1].start()
             in_refs[i] = buffers[slot]
+        for copy in flowing:
+            copy.start()
         for slot, j in enumerate(far_out, len(far)):
             results.append((buffers[slot], out_refs[j], sems[slot]))
             out_refs[j] = buffers[slot]
@@ -61,7 +76,7 @@
             in_refs[i] = in_refs[i].at[k]
         for copy in starts:
             copy.wait()
-        body(*in_refs, *out_refs, *own, **fixed)
+        body(*in_refs, *out_refs, *own, **fixed, **extra)
         ends = [pltpu.make_async_copy(*triple) for triple in results]
         for copy in ends:
             copy.start()
@@ -71,13 +86,15 @@
     result = pl.pallas_call(
         kernel,
         out_shape=outs,
-        in_specs=[hbm if i in far else near for i in range(n_in)],
+        in_specs=[hbm if i in far or i == stream else near for i in range(n_in)],
         out_specs=tuple(hbm if j in far_out else near for j in range(n_out)),
         scratch_shapes=[
             *scratch,
             *landing,
             *leaving,
             *[pltpu.SemaphoreType.DMA] * (len(landing) + len(leaving)),
+            *flow,
+            *[pltpu.SemaphoreType.DMA] * parts,
         ],
         compiler_params=pltpu.CompilerParams(vmem_limit_bytes=limit),
         cost_estimate=pl.CostEstimate(flops=flops, bytes_accessed=4 << 20, transcendentals=0),
@@ -299,10 +316,7 @@
         sent_ref[d] = total_ref[d * chunk : d * chunk + padded].astype(jnp.bfloat16)
 
 
-def second_kernel(
-    act, stats, mixed, main, weight, enhanced, sent, activated, square, z0, z1, z2, own, total, *, lay, chunk,
-    grid, pixel_total
-):
+def activate(activated, act, stats, lay, grid, pixel_total):
     width = act.shape[1]
     mean, inverse = act_moments(stats, pixel_total)
     mask = inside_masks(lay, width, *grid)
@@ -317,6 +331,25 @@
             normed * gate * mask(r)
         ).astype(jnp.bfloat16)
 
+
+def second_kernel(
+    act, stats, main, sent, activated, own, total, *, lay, chunk, grid, pixel_total
+):
+    activate(activated, act, stats, lay, grid, pixel_total)
+    own[...] = jnp.zeros_like(own)
+
+    @pl.loop(0, lay.rows)
+    def _(i):
+        place = pl.multiple_of(i * lay.wide + 2 * MARGIN, 16)
+        own[pl.ds(place, lay.cols)] = main[i].astype(jnp.float32)
+
+    weight_matmul(activated, own, total, sent, lay, chunk)
+
+
+def enhanced_kernel(
+    act, stats, mixed, weight, enhanced, activated, square, z0, z1, z2, *, lay, grid, pixel_total
+):
+    activate(activated, act, stats, lay, grid, pixel_total)
     put_square(square, weight, False)
     taps_matmul(activated, square, (z0, z1, z2), lay, False)
 
@@ -328,15 +361,6 @@
         enhanced[i] = (mixed[pl.ds(place, lay.cols)].astype(jnp.float32) + value).astype(
             jnp.bfloat16
         )
-
-    own[...] = jnp.zeros_like(own)
-
-    @pl.loop(0, lay.rows)
-    def _(i):
-        place = pl.multiple_of(i * lay.wide + 2 * MARGIN, 16)
-        own[pl.ds(place, lay.cols)] = main[i].astype(jnp.float32)
-
-    weight_matmul(activated, own, total, sent, lay, chunk)
 
 
 def first_kernel(
@@ -535,12 +559,14 @@
     valid[...] = inside.astype(jnp.float32)
 
 
-def channel_conv(rows_ref, weight, shifted, out_rows, cols):
+def channel_conv(rows_ref, weight, shifted, out_rows, cols, arrive=None):
     width = weight.shape[3]
     count = out_rows * cols
     sums = None
     for a in range(3):
         left = rows_ref[a * cols : a * cols + count]
+        if arrive is not None:
+            arrive(a)
         if width % 128:
             part = [
                 jnp.dot(left, weight[a, b], preferred_element_type=jnp.float32) for b in range(3)
@@ -591,7 +617,7 @@
 
 def project_kernel(
     received, weight, source, project, sent, rows_ref, shifted, residual, spread, *, grid, band,
-    direct
+    direct, arrive
 ):
     row_devices, col_devices = grid
     band_rows, cols = band
@@ -599,7 +625,7 @@
     my_col = lax.axis_index("cols")
     for c in range(col_devices):
         rows_ref[:, c * width : (c + 1) * width] = received[c]
-    raw = channel_conv(rows_ref, weight, shifted, band_rows + 2, cols)
+    raw = channel_conv(rows_ref, weight, shifted, band_rows + 2, cols, arrive)
     count = (band_rows + 2) * cols
     if direct:
         residual[...] = jnp.zeros_like(residual)
@@ -774,6 +800,9 @@
             pltpu.VMEM((band_rows + 2, band_cols + 16, width), jnp.float32),
         ],
         18 * (band_rows + 2) * band_cols * channels * width_share,
+        far=(3,),
+        stream=1,
+        limit=63438848,
         far_out=(0,),
         grid=grid,
         band=band,
@@ -802,12 +831,13 @@
         pixel_total=pixel_total,
     )
     grad_stats = to_all(grad_stats, BOTH)
-    enhanced, second_sent = call(
+    flat_scratch = pltpu.VMEM((lay.flat, width), jnp.bfloat16)
+    second_sent = call(
         second_kernel,
-        (jax.ShapeDtypeStruct((tile_rows, tile_cols, width), jnp.bfloat16), half_shape),
-        (first_act, stats, mixed, output_cotangent, enhancer_second),
-        [pltpu.VMEM((lay.flat, width), jnp.bfloat16), square, *z, own, total],
-        2 * conv_flops,
+        half_shape,
+        (first_act, stats, output_cotangent),
+        [flat_scratch, own, total],
+        conv_flops,
         lay=lay,
         chunk=chunk,
         grid=grid,
@@ -826,6 +856,17 @@
         pixel_total=pixel_total,
     )
     part = to_all(sent_both, BOTH)
+    late_stats, _ = lax.optimization_barrier((stats, sent_both))
+    enhanced = call(
+        enhanced_kernel,
+        jax.ShapeDtypeStruct((tile_rows, tile_cols, width), jnp.bfloat16),
+        (first_act, late_stats, mixed, enhancer_second),
+        [flat_scratch, square, *z],
+        conv_flops,
+        lay=lay,
+        grid=grid,
+        pixel_total=pixel_total,
+    )
     rescale = 1.0 / math.sqrt(pixel_total)
     global_gradient = call(
         coarse_kernel,
@@ -834,7 +875,7 @@
         (),
         lay=lay,
     )
-    part, global_gradient = lax.optimization_barrier((part, global_gradient))
+    part, global_gradient, enhanced = lax.optimization_barrier((part, global_gradient, enhanced))
     share = call(share_kernel, half_shape, (part,), rescale=rescale)
     share = among_cores(share, row_devices, col_devices)
     shares = (share, core_swap(share, col_devices))

time: 129 us -> 132 us (1.023)
  Pallas kernels: 25.9 us -> 33.4 us
  waiting for transfers between devices: 33.4 us -> 28.7 us
  local copies, waits for them, and re-layouts: 13.6 us -> 16.3 us
  starting transfers between devices: 37 us -> 34.5 us
    pallas_call x12 -> x13, Pallas kernels: 25.9 us -> 33.4 us  [call(): pl.pallas_call(kernel, out_shape=outs, in_specs=[hbm if i in far or i ==...]
    all_to_all x5, waiting for transfers between devices: 27.7 us -> 20.6 us  [to_all(): return lax.all_to_all(payload, axis, 0, 0)]
    ppermute x1, waiting for transfers between devices: 1.12 us -> 4.29 us  [per_device(): bottom = lax.ppermute(bottoms, 'rows', row_down)]
    unnamed x38 -> x52, local copies, waits for them, and re-layouts: 12.7 us -> 15.5 us
    all_to_all x5, starting transfers between devices: 18.9 us -> 16.4 us  [to_all(): return lax.all_to_all(payload, axis, 0, 0)]
  transfers between devices with their start and end apart: 12 -> 12, of which waited for: 10 -> 9; matrix products, arithmetic and copies ran while one was open for 2% -> 2% of each run, Pallas kernels for 9% -> 14%
where the time goes in v9:
time: 132 us; the launch traced here: 130 us
  starting transfers between devices  34.5 us (26%)
  Pallas kernels  33.4 us (25%)
  waiting for transfers between devices  28.7 us (22%)
  local copies, waits for them, and re-layouts  16.3 us (12%)
  blocking collectives  14.8 us (11%)
  other arithmetic  1.73 us (1%)
    pallas_call x13, Pallas kernels, call(): pl.pallas_call(kernel, out_shape=outs, in_specs=[hbm if i in far or i ==...  33.4 us
    all_to_all x5, waiting for transfers between devices, to_all(): return lax.all_to_all(payload, axis, 0, 0)  20.6 us
    all_to_all x5, starting transfers between devices, to_all(): return lax.all_to_all(payload, axis, 0, 0)  16.4 us
    unnamed x52, local copies, waits for them, and re-layouts  15.5 us
    all_to_all x1, blocking collectives, among_cores(): return lax.all_to_all(payload, BOTH, 0, 0, axis_index_groups=groups)  14.8 us
    all_to_all x1, starting transfers between devices, among_cores(): return lax.all_to_all(payload, BOTH, 0, 0, axis_index_groups=groups)  8.46 us
    ppermute x1, waiting for transfers between devices, per_device(): bottom = lax.ppermute(bottoms, 'rows', row_down)  4.29 us
    ppermute x1, starting transfers between devices, per_device(): top = lax.ppermute(tops, 'rows', row_up)  3.83 us
  transfers between devices with their start and end apart: 12, of which 9 were waited for; matrix products, arithmetic and copies ran while one was open for 2% of the time, Pallas kernels for 14%

profile of v9, /device:TPU:0, one launch (start us, length us, event | category | flops | bytes accessed | tf_op | source)
XLA Modules:
  0.0 130.3 jit_solution(7024445794410938365)
XLA Ops:
  0.6 2.1 %pack_kernel.1 = bf16[16,72,128]{2,1,0:T(8,128)(2,1)} custom-call(f32[16,32,64]{2,1,0:T(8,128)} %refs_0_.3, s32[32,64]{1,0:T(8,128)} %refs_1_.3, bf16[64,128]{1,0:T(8,128)(2,1)} %bitcast.20), custom_call_target="tpu_custom_call" | custom-call | bytes 4194304 | tf_op jit(solution)/shard_map/pack_kernel/pallas_call | solution.py:86
  2.8 0.0 copy-start.2
  2.8 8.5 %all-to-all-start = ((bf16[16,72,128]{2,1,0:T(8,128)(2,1)}), bf16[16,72,128]{2,1,0:T(8,128)(2,1)S(1)}, u32[]{:S(2)}, u32[]{:S(2)}) async-start(bf16[16,72,128]{2,1,0:T(8,128)(2,1)} %pack_kernel.1), calls=%async_computation | async-start | bytes 589824 | tf_op jit(solution)/shard_map/all_to_all | solution.py:472
  11.3 0.8 slice_bitcast_fusion
  12.1 3.8 %collective-permute-start = (bf16[2,2,64,128]{3,2,1,0:T(8,128)(2,1)S(1)}, bf16[2,2,64,128]{3,2,1,0:T(8,128)(2,1)S(1)}, u32[]{:S(2)}, u32[]{:S(2)}) collective-permute-start(bf16[2,2,64,128]{3,2,1,0:T(8,128)(2,1)S(1)} %pad_maximum_fusion.2), channel_id=1, source_target_pairs={{0,8},{8,16},{16,24},{1,9},{9,17},{17,25},{2,10},{10,18},{18,26},{... | collective-permute-start | bytes 196616 | tf_op jit(solution)/shard_map/ppermute | solution.py:701
  16.0 1.3 collective-permute-start.1
  17.3 0.6 collective-permute-done.refs_1_
  17.8 4.3 %collective-permute-done.1.refs_2_ = bf16[2,2,64,128]{3,2,1,0:T(8,128)(2,1)S(1)} collective-permute-done((bf16[2,2,64,128]{3,2,1,0:T(8,128)(2,1)S(1)}, bf16[2,2,64,128]{3,2,1,0:T(8,128)(2,1)S(1)}, u32[]{:S(2)}, u32[]{:S(2)}) %collective-permute-start.1) | collective-permute-done | bytes 65568 | tf_op jit(solution)/shard_map/ppermute | solution.py:702
  22.1 0.6 copy-done.20
  22.7 1.7 %fusion.4 = (bf16[2,36,8,128]{3,2,1,0:T(8,128)(2,1)}, bf16[2,36,8,128]{3,2,1,0:T(8,128)(2,1)}) fusion(bf16[1,32,64,128]{3,2,1,0:T(8,128)(2,1)} %bitcast.16, bf16[1,32,64,128]{3,2,1,0:T(8,128)(2,1)} %bitcast.17, bf16[2,2,8,128]{3,2,1,0:T(8,128)(2,1)S(1)} %get-tuple-element.52, bf16[2,2,8,128]{3,2,1,0:T(8,128)(2,1)S(1)} %get-tuple-element.50, ...), kind=kLoop, calls=%fused_computation.7 | loop fusion | flops 1179648 | bytes 1376256 | tf_op jit(solution)/shard_map/concatenate | solution.py:705
  24.4 0.0 all-to-all-done.refs_0_.refs_2_
  24.4 0.0 copy-start
  24.4 0.1 collective-permute-start.2
  24.5 1.6 %collective-permute-done.2.refs_1_ = bf16[16,72,128]{2,1,0:T(8,128)(2,1)S(1)} collective-permute-done((bf16[16,72,128]{2,1,0:T(8,128)(2,1)S(1)}, bf16[16,72,128]{2,1,0:T(8,128)(2,1)S(1)}, u32[]{:S(2)}, u32[]{:S(2)}) %collective-permute-start.2) | collective-permute-done | bytes 294944 | tf_op jit(solution)/shard_map/ppermute | solution.py:476
  26.1 1.9 %hidden_kernel.1 = bf16[8,192,128]{2,1,0:T(8,128)(2,1)} custom-call(bf16[16,72,128]{2,1,0:T(8,128)(2,1)S(1)} %all-to-all-done.refs_0_.refs_2_, bf16[16,72,128]{2,1,0:T(8,128)(2,1)S(1)} %collective-permute-done.2.refs_1_, bf16[3,3,1024,128]{3,2,1,0:T(8,128)(2,1)S(1)} %copy-done.2), custom_call_target="tpu_custom_call" | custom-call | flops 603979776 | bytes 4194304 | tf_op jit(solution)/shard_map/hidden_kernel/pallas_call | solution.py:86
  28.0 3.7 %all-to-all-start.1 = ((bf16[8,192,128]{2,1,0:T(8,128)(2,1)}), bf16[8,192,128]{2,1,0:T(8,128)(2,1)S(1)}, u32[]{:S(2)}, u32[]{:S(2)}) async-start(bf16[8,192,128]{2,1,0:T(8,128)(2,1)} %hidden_kernel.1), calls=%async_computation.1 | async-start | bytes 786432 | tf_op jit(solution)/shard_map/all_to_all | solution.py:464
  31.6 1.4 %collective-permute-start.3 = (bf16[2,36,8,128]{3,2,1,0:T(8,128)(2,1)}, bf16[2,36,8,128]{3,2,1,0:T(8,128)(2,1)S(1)}, u32[]{:S(2)}, u32[]{:S(2)}) collective-permute-start(bf16[2,36,8,128]{3,2,1,0:T(8,128)(2,1)} %get-tuple-element.29), channel_id=1, source_target_pairs={{1,0},{2,1},{3,2},{4,3},{5,4},{6,5},{7,6},{9,8},{10,9},{11,10},{12... | collective-permute-start | bytes 442376 | tf_op jit(solution)/shard_map/ppermute | solution.py:774
  33.1 3.0 %collective-permute-start.4 = (bf16[2,36,8,128]{3,2,1,0:T(8,128)(2,1)}, bf16[2,36,8,128]{3,2,1,0:T(8,128)(2,1)S(1)}, u32[]{:S(2)}, u32[]{:S(2)}) collective-permute-start(bf16[2,36,8,128]{3,2,1,0:T(8,128)(2,1)} %get-tuple-element.30), channel_id=1, source_target_pairs={{0,1},{1,2},{2,3},{3,4},{4,5},{5,6},{6,7},{8,9},{9,10},{10,11},{11... | collective-permute-start | bytes 442376 | tf_op jit(solution)/shard_map/ppermute | solution.py:773
  36.1 0.8 pool_kernel.1
  36.9 3.0 %all-to-all-done.1.refs_0_ = bf16[8,192,128]{2,1,0:T(8,128)(2,1)S(1)} async-done(((bf16[8,192,128]{2,1,0:T(8,128)(2,1)}), bf16[8,192,128]{2,1,0:T(8,128)(2,1)S(1)}, u32[]{:S(2)}, u32[]{:S(2)}) %all-to-all-start.1) | async-done | bytes 393248 | tf_op jit(solution)/shard_map/all_to_all | solution.py:464
  40.0 0.7 copy-done.25
  40.7 4.4 %project_kernel.1 = f32[8,4,8,128]{3,2,1,0:T(8,128)} custom-call(bf16[8,192,128]{2,1,0:T(8,128)(2,1)} %copy-done.25, bf16[3,3,1024,128]{3,2,1,0:T(8,128)(2,1)} %refs_1_.4, bf16[16,72,128]{2,1,0:T(8,128)(2,1)} %copy-done, bf16[1024,128]{1,0:T(8,128)(2,1)} %refs_3_.4), custom_call_target="tpu_custom_call" | custom-call | flops 301989888 | bytes 4194304 | tf_op jit(solution)/shard_map/project_kernel/pallas_call | solution.py:86
  45.1 0.0 copy-start.1
  45.1 3.5 %all-to-all-start.2 = ((f32[8,4,8,128]{3,2,1,0:T(8,128)}), f32[8,4,8,128]{3,2,1,0:T(8,128)S(1)}, u32[]{:S(2)}, u32[]{:S(2)}) async-start(f32[8,4,8,128]{3,2,1,0:T(8,128)} %project_kernel.1), calls=%async_computation.2 | async-start | bytes 262144 | tf_op jit(solution)/shard_map/all_to_all | solution.py:464
  48.6 0.1 fusion.2.refs_3_
  48.7 0.0 copy-start.9
  48.7 5.4 %all-to-all-done.2.refs_4_ = f32[8,4,8,128]{3,2,1,0:T(8,128)S(1)} async-done(((f32[8,4,8,128]{3,2,1,0:T(8,128)}), f32[8,4,8,128]{3,2,1,0:T(8,128)S(1)}, u32[]{:S(2)}, u32[]{:S(2)}) %all-to-all-start.2) | async-done | bytes 131104 | tf_op jit(solution)/shard_map/all_to_all | solution.py:464
  54.1 1.0 copy-done.5
  55.1 0.8 copy-done.21
  56.0 0.7 copy-done.24
  56.7 3.0 %mixed_kernel.1 = (bf16[3072,128]{1,0:T(8,128)(2,1)S(1)}, f32[2800,128]{1,0:T(8,128)S(1)}, f32[32,8,128]{2,1,0:T(8,128)S(1)}) custom-call(bf16[32,64,128]{2,1,0:T(8,128)(2,1)S(1)} %copy-done.5, bf16[2,2,64,128]{3,2,1,0:T(8,128)(2,1)S(1)} %collective-permute-done.refs_1_, bf16[2,2,64,128]{3,2,1,0:T(8,128)(2,1)S(1)} %copy-done.21, ...), custom_call_target="tpu_custom_call" | custom-call | flops 825753600 | bytes 4194304 | tf_op jit(solution)/shard_map/mixed_kernel/pallas_call | solution.py:86
  59.7 0.0 copy-start.17
  59.8 0.6 copy-done.17
  60.4 3.3 %all-to-all-start.3 = ((f32[32,8,128]{2,1,0:T(8,128)}), f32[32,8,128]{2,1,0:T(8,128)}, u32[]{:S(2)}, u32[]{:S(2)}) async-start(f32[32,8,128]{2,1,0:T(8,128)} %copy-done.17), calls=%async_computation.3 | async-start | bytes 262144 | tf_op jit(solution)/shard_map/all_to_all | solution.py:464
  63.7 0.0 copy-start.10
  63.7 1.0 copy-done.10
  64.7 1.0 copy-done.11
  65.6 0.8 copy-done.22
  66.5 2.6 %cot_kernel.1.refs_2_.refs_3_ = bf16[2800,128]{1,0:T(8,128)(2,1)S(1)} custom-call(bf16[32,64,128]{2,1,0:T(8,128)(2,1)S(1)} %copy-done.1, bf16[2,2,64,128]{3,2,1,0:T(8,128)(2,1)S(1)} %collective-permute-done.refs_1_, bf16[2,2,64,128]{3,2,1,0:T(8,128)(2,1)S(1)} %copy-done.22, bf16[2,37,16,128]{3,2,1,0:T(8,128)(2,1)S(1)} %copy-done.10, ...), custom_call_target="tpu_custom_call" | custom-call | flops 825753600 | bytes 4194304 | tf_op jit(solution)/shard_map/cot_kernel/pallas_call | solution.py:86
  69.1 2.8 %all-to-all-done.3.refs_1_.refs_0_ = f32[32,8,128]{2,1,0:T(8,128)} async-done(((f32[32,8,128]{2,1,0:T(8,128)}), f32[32,8,128]{2,1,0:T(8,128)}, u32[]{:S(2)}, u32[]{:S(2)}) %all-to-all-start.3) | async-done | bytes 131104 | tf_op jit(solution)/shard_map/all_to_all | solution.py:464
  71.9 2.2 %norm_kernel.1 = f32[32,8,128]{2,1,0:T(8,128)S(1)} custom-call(f32[2800,128]{1,0:T(8,128)S(1)} %get-tuple-element.34.refs_0_.refs_2_, f32[32,8,128]{2,1,0:T(8,128)} %all-to-all-done.3.refs_1_.refs_0_, bf16[2800,128]{1,0:T(8,128)(2,1)S(1)} %cot_kernel.1.refs_2_.refs_3_), custom_call_target="tpu_custom_call" | custom-call | bytes 4194304 | tf_op jit(solution)/shard_map/norm_kernel/pallas_call | solution.py:86
  74.1 0.0 copy-start.7
  74.2 0.6 copy-done.7
  74.8 3.3 %all-to-all-start.4 = ((f32[32,8,128]{2,1,0:T(8,128)}), f32[32,8,128]{2,1,0:T(8,128)}, u32[]{:S(2)}, u32[]{:S(2)}) async-start(f32[32,8,128]{2,1,0:T(8,128)} %copy-done.7), calls=%async_computation.4 | async-start | bytes 262144 | tf_op jit(solution)/shard_map/all_to_all | solution.py:464
  78.1 3.6 %second_kernel.1.refs_5_ = bf16[16,72,128]{2,1,0:T(8,128)(2,1)S(1)} custom-call(f32[2800,128]{1,0:T(8,128)S(1)} %get-tuple-element.34.refs_0_.refs_2_, f32[32,8,128]{2,1,0:T(8,128)} %all-to-all-done.3.refs_1_.refs_0_, bf16[32,64,128]{2,1,0:T(8,128)(2,1)S(1)} %copy-done.1), custom_call_target="tpu_custom_call" | custom-call | flops 825753600 | bytes 4194304 | tf_op jit(solution)/shard_map/second_kernel/pallas_call | solution.py:86
  81.7 0.0 copy-start.13
  81.7 0.7 copy-done.13
  82.4 3.9 %all-to-all-done.4.refs_1_ = f32[32,8,128]{2,1,0:T(8,128)} async-done(((f32[32,8,128]{2,1,0:T(8,128)}), f32[32,8,128]{2,1,0:T(8,128)}, u32[]{:S(2)}, u32[]{:S(2)}) %all-to-all-start.4) | async-done | bytes 131104 | tf_op jit(solution)/shard_map/all_to_all | solution.py:464
  86.3 1.0 copy-done.14
  87.3 4.4 %first_kernel.1 = (bf16[32,72,128]{2,1,0:T(8,128)(2,1)S(1)}, bf16[2816,128]{1,0:T(8,128)(2,1)S(1)}) custom-call(f32[32,8,128]{2,1,0:T(8,128)} %all-to-all-done.3.refs_1_.refs_0_, f32[32,8,128]{2,1,0:T(8,128)} %all-to-all-done.4.refs_1_, f32[2800,128]{1,0:T(8,128)S(1)} %get-tuple-element.34.refs_0_.refs_2_, bf16[2800,128]{1,0:T(8,128)(2,1)S(1)} %cot_kernel.1.refs_2_.refs_3_, ...), custom_call_target="tpu_custom_call" | custom-call | flops 825753600 | bytes 4194304 | tf_op jit(solution)/shard_map/first_kernel/pallas_call | solution.py:86
  91.7 0.9 copy-done.3
  92.5 0.8 copy-done.6
  93.3 2.6 %all-to-all-start.5 = ((bf16[32,72,128]{2,1,0:T(8,128)(2,1)}), bf16[32,72,128]{2,1,0:T(8,128)(2,1)S(1)}, u32[]{:S(2)}, u32[]{:S(2)}) async-start(bf16[32,72,128]{2,1,0:T(8,128)(2,1)} %copy-done.6), calls=%async_computation.5 | async-start | bytes 1179648 | tf_op jit(solution)/shard_map/all_to_all | solution.py:464
  96.0 1.1 copy-done.4
  97.1 1.0 copy-done.8
  98.1 1.0 copy-done.16
  99.0 1.9 %coarse_kernel.1 = f32[8,128]{1,0:T(8,128)} custom-call(bf16[2816,128]{1,0:T(8,128)(2,1)S(1)} %copy-done.4, bf16[72,2816]{1,0:T(8,128)(2,1)S(1)} %copy-done.8, bf16[32,64,128]{2,1,0:T(8,128)(2,1)S(1)} %copy-done.1, bf16[3,3,128,128]{3,2,1,0:T(8,128)(2,1)S(1)} %copy-done.16), custom_call_target="tpu_custom_call" | custom-call | bytes 4194304 | tf_op jit(solution)/shard_map/coarse_kernel/pallas_call | solution.py:86
  101.0 1.0 copy-done.12
  101.9 5.2 %enhanced_kernel.1 = bf16[32,64,128]{2,1,0:T(8,128)(2,1)} custom-call(f32[2800,128]{1,0:T(8,128)S(1)} %get-tuple-element.34.refs_0_.refs_2_, f32[32,8,128]{2,1,0:T(8,128)} %all-to-all-done.3.refs_1_.refs_0_, bf16[3072,128]{1,0:T(8,128)(2,1)S(1)} %get-tuple-element.35.refs_4_.refs_2_, bf16[3,3,128,128]{3,2,1,0:T(8,128)(2,1)S(1)} %copy-done.12), custom_call_target="tpu_custom_call" | custom-call | flops 825753600 | bytes 4194304 | tf_op jit(solution)/shard_map/enhanced_kernel/pallas_call | solution.py:86
  107.1 5.6 %all-to-all-done.5.refs_0_ = bf16[32,72,128]{2,1,0:T(8,128)(2,1)S(1)} async-done(((bf16[32,72,128]{2,1,0:T(8,128)(2,1)}), bf16[32,72,128]{2,1,0:T(8,128)(2,1)S(1)}, u32[]{:S(2)}, u32[]{:S(2)}) %all-to-all-start.5) | async-done | bytes 589856 | tf_op jit(solution)/shard_map/all_to_all | solution.py:464
  112.7 0.1 share_kernel.1
  112.8 14.8 %all_to_all.35.refs_0_ = bf16[16,72,128]{2,1,0:T(8,128)(2,1)S(1)} all-to-all(bf16[16,72,128]{2,1,0:T(8,128)(2,1)S(1)} %share_kernel.1), channel_id=1, replica_groups={{0,2,4,6,8,10,12,14,16,18,20,22,24,26,28,30},{1,3,5,7,9,11,13,15,17,19,..., dimensions={0} | all-to-all | bytes 589824 | tf_op jit(solution)/shard_map/all_to_all | solution.py:472
  127.6 1.6 %collective-permute-done.5.refs_1_ = bf16[16,72,128]{2,1,0:T(8,128)(2,1)S(1)} collective-permute-done((bf16[16,72,128]{2,1,0:T(8,128)(2,1)S(1)}, bf16[16,72,128]{2,1,0:T(8,128)(2,1)S(1)}, u32[]{:S(2)}, u32[]{:S(2)}) %collective-permute-start.5) | collective-permute-done | bytes 294944 | tf_op jit(solution)/shard_map/ppermute | solution.py:476
  129.2 1.1 join_kernel.1
  (33 shorter events, 0.1 us)
Async XLA Ops:
  2.8 23.3 %copy-start.2 = (bf16[3,3,1024,128]{3,2,1,0:T(8,128)(2,1)S(1)}, bf16[3,3,1024,128]{3,2,1,0:T(8,128)(2,1)}, u32[]{:S(2)}) copy-start(bf16[3,3,1024,128]{3,2,1,0:T(8,128)(2,1)} %refs_2_.4) | copy-start | bytes 7077892
  2.8 21.6 %all-to-all-start = ((bf16[16,72,128]{2,1,0:T(8,128)(2,1)}), bf16[16,72,128]{2,1,0:T(8,128)(2,1)S(1)}, u32[]{:S(2)}, u32[]{:S(2)}) async-start(bf16[16,72,128]{2,1,0:T(8,128)(2,1)} %pack_kernel.1), calls=%async_computation | async-start | bytes 589824 | tf_op jit(solution)/shard_map/all_to_all | solution.py:472
  12.1 5.7 %collective-permute-start = (bf16[2,2,64,128]{3,2,1,0:T(8,128)(2,1)S(1)}, bf16[2,2,64,128]{3,2,1,0:T(8,128)(2,1)S(1)}, u32[]{:S(2)}, u32[]{:S(2)}) collective-permute-start(bf16[2,2,64,128]{3,2,1,0:T(8,128)(2,1)S(1)} %pad_maximum_fusion.2), channel_id=1, source_target_pairs={{0,8},{8,16},{16,24},{1,9},{9,17},{17,25},{2,10},{10,18},{18,26},{... | collective-permute-start | bytes 196616 | tf_op jit(solution)/shard_map/ppermute | solution.py:701
  16.0 6.2 %collective-permute-start.1 = (bf16[2,2,64,128]{3,2,1,0:T(8,128)(2,1)S(1)}, bf16[2,2,64,128]{3,2,1,0:T(8,128)(2,1)S(1)}, u32[]{:S(2)}, u32[]{:S(2)}) collective-permute-start(bf16[2,2,64,128]{3,2,1,0:T(8,128)(2,1)S(1)} %pad_maximum_fusion.3), channel_id=1, source_target_pairs={{8,0},{16,8},{24,16},{9,1},{17,9},{25,17},{10,2},{18,10},{26,18},{... | collective-permute-start | bytes 196616 | tf_op jit(solution)/shard_map/ppermute | solution.py:702
  22.1 0.6 copy-start.20
  24.4 11.7 %copy-start.18 = (f32[16,128]{1,0:T(8,128)S(1)}, f32[16,128]{1,0:T(8,128)}, u32[]{:S(2)}) copy-start(f32[16,128]{1,0:T(8,128)} %refs_3_.5) | copy-start | bytes 24580
  24.4 11.7 %copy-start.19 = (s32[8,256]{1,0:T(8,128)S(1)}, s32[8,256]{1,0:T(8,128)}, u32[]{:S(2)}) copy-start(s32[8,256]{1,0:T(8,128)} %constant.7.clone.refs_2_) | copy-start | bytes 24580
  24.4 12.5 %copy-start = (bf16[16,72,128]{2,1,0:T(8,128)(2,1)}, bf16[16,72,128]{2,1,0:T(8,128)(2,1)S(1)}, u32[]{:S(2)}) copy-start(bf16[16,72,128]{2,1,0:T(8,128)(2,1)S(1)} %all-to-all-done.refs_0_.refs_2_) | copy-start | bytes 884740
  24.4 1.6 %collective-permute-start.2 = (bf16[16,72,128]{2,1,0:T(8,128)(2,1)S(1)}, bf16[16,72,128]{2,1,0:T(8,128)(2,1)S(1)}, u32[]{:S(2)}, u32[]{:S(2)}) collective-permute-start(bf16[16,72,128]{2,1,0:T(8,128)(2,1)S(1)} %all-to-all-done.refs_0_.refs_2_), channel_id=1, source_target_pairs={{0,1},{1,0},{2,3},{3,2},{4,5},{5,4},{6,7},{7,6},{8,9},{9,8},{10,11... | collective-permute-start | bytes 884744 | tf_op jit(solution)/shard_map/ppermute | solution.py:476
  28.0 12.0 %all-to-all-start.1 = ((bf16[8,192,128]{2,1,0:T(8,128)(2,1)}), bf16[8,192,128]{2,1,0:T(8,128)(2,1)S(1)}, u32[]{:S(2)}, u32[]{:S(2)}) async-start(bf16[8,192,128]{2,1,0:T(8,128)(2,1)} %hidden_kernel.1), calls=%async_computation.1 | async-start | bytes 786432 | tf_op jit(solution)/shard_map/all_to_all | solution.py:464
  31.6 22.4 %copy-start.15 = (bf16[3,3,128,128]{3,2,1,0:T(8,128)(2,1)S(1)}, bf16[3,3,128,128]{3,2,1,0:T(8,128)(2,1)}, u32[]{:S(2)}) copy-start(bf16[3,3,128,128]{3,2,1,0:T(8,128)(2,1)} %refs_3_.6) | copy-start | bytes 884740
  31.6 17.0 %collective-permute-start.3 = (bf16[2,36,8,128]{3,2,1,0:T(8,128)(2,1)}, bf16[2,36,8,128]{3,2,1,0:T(8,128)(2,1)S(1)}, u32[]{:S(2)}, u32[]{:S(2)}) collective-permute-start(bf16[2,36,8,128]{3,2,1,0:T(8,128)(2,1)} %get-tuple-element.29), channel_id=1, source_target_pairs={{1,0},{2,1},{3,2},{4,3},{5,4},{6,5},{7,6},{9,8},{10,9},{11,10},{12... | collective-permute-start | bytes 442376 | tf_op jit(solution)/shard_map/ppermute | solution.py:774
  33.1 15.6 %collective-permute-start.4 = (bf16[2,36,8,128]{3,2,1,0:T(8,128)(2,1)}, bf16[2,36,8,128]{3,2,1,0:T(8,128)(2,1)S(1)}, u32[]{:S(2)}, u32[]{:S(2)}) collective-permute-start(bf16[2,36,8,128]{3,2,1,0:T(8,128)(2,1)} %get-tuple-element.30), channel_id=1, source_target_pairs={{0,1},{1,2},{2,3},{3,4},{4,5},{5,6},{6,7},{8,9},{9,10},{10,11},{11... | collective-permute-start | bytes 442376 | tf_op jit(solution)/shard_map/ppermute | solution.py:773
  36.9 17.1 %copy-start.23 = (f32[32,128]{1,0:T(8,128)}, f32[32,128]{1,0:T(8,128)S(1)}, u32[]{:S(2)}) copy-start(f32[32,128]{1,0:T(8,128)S(1)} %get-tuple-element.32) | copy-start | bytes 49156
  40.0 0.7 copy-start.25
  45.1 18.6 %copy-start.1 = (bf16[32,64,128]{2,1,0:T(8,128)(2,1)S(1)}, bf16[32,64,128]{2,1,0:T(8,128)(2,1)}, u32[]{:S(2)}) copy-start(bf16[32,64,128]{2,1,0:T(8,128)(2,1)} %refs_2_.6) | copy-start | bytes 1572868
  45.1 9.0 %all-to-all-start.2 = ((f32[8,4,8,128]{3,2,1,0:T(8,128)}), f32[8,4,8,128]{3,2,1,0:T(8,128)S(1)}, u32[]{:S(2)}, u32[]{:S(2)}) async-start(f32[8,4,8,128]{3,2,1,0:T(8,128)} %project_kernel.1), calls=%async_computation.2 | async-start | bytes 262144 | tf_op jit(solution)/shard_map/all_to_all | solution.py:464
  48.7 11.7 %copy-start.9 = (bf16[2,37,16,128]{3,2,1,0:T(8,128)(2,1)}, bf16[2,37,16,128]{3,2,1,0:T(8,128)(2,1)S(1)}, u32[]{:S(2)}) copy-start(bf16[2,37,16,128]{3,2,1,0:T(8,128)(2,1)S(1)} %fusion.2.refs_3_) | copy-start | bytes 909316
  54.1 1.0 copy-start.5
  55.1 0.8 copy-start.21
  56.0 0.7 copy-start.24
  59.7 0.7 copy-start.17
  60.4 11.5 %all-to-all-start.3 = ((f32[32,8,128]{2,1,0:T(8,128)}), f32[32,8,128]{2,1,0:T(8,128)}, u32[]{:S(2)}, u32[]{:S(2)}) async-start(f32[32,8,128]{2,1,0:T(8,128)} %copy-done.17), calls=%async_computation.3 | async-start | bytes 262144 | tf_op jit(solution)/shard_map/all_to_all | solution.py:464
  63.7 1.0 copy-start.10
  64.7 1.0 copy-start.11
  65.6 0.8 copy-start.22
  74.1 0.7 copy-start.7
  74.8 11.5 %all-to-all-start.4 = ((f32[32,8,128]{2,1,0:T(8,128)}), f32[32,8,128]{2,1,0:T(8,128)}, u32[]{:S(2)}, u32[]{:S(2)}) async-start(f32[32,8,128]{2,1,0:T(8,128)} %copy-done.7), calls=%async_computation.4 | async-start | bytes 262144 | tf_op jit(solution)/shard_map/all_to_all | solution.py:464
  81.7 0.7 copy-start.13
  86.3 1.0 copy-start.14
  91.6 0.9 copy-start.3
  92.5 0.8 copy-start.6
  93.3 19.3 %all-to-all-start.5 = ((bf16[32,72,128]{2,1,0:T(8,128)(2,1)}), bf16[32,72,128]{2,1,0:T(8,128)(2,1)S(1)}, u32[]{:S(2)}, u32[]{:S(2)}) async-start(bf16[32,72,128]{2,1,0:T(8,128)(2,1)} %copy-done.6), calls=%async_computation.5 | async-start | bytes 1179648 | tf_op jit(solution)/shard_map/all_to_all | solution.py:464
  96.0 1.1 copy-start.4
  97.1 1.0 copy-start.8
  98.1 1.0 copy-start.16
  101.0 1.0 copy-start.12
  127.6 1.6 %collective-permute-start.5 = (bf16[16,72,128]{2,1,0:T(8,128)(2,1)S(1)}, bf16[16,72,128]{2,1,0:T(8,128)(2,1)S(1)}, u32[]{:S(2)}, u32[]{:S(2)}) collective-permute-start(bf16[16,72,128]{2,1,0:T(8,128)(2,1)S(1)} %all_to_all.35.refs_0_), channel_id=1, source_target_pairs={{0,1},{1,0},{2,3},{3,2},{4,5},{5,4},{6,7},{7,6},{8,9},{9,8},{10,11... | collective-permute-start | bytes 884744 | tf_op jit(solution)/shard_map/ppermute | solution.py:476

commit v10 on v9

--- a/solution.py
+++ b/solution.py
@@ -33,8 +33,7 @@
 
 
 def call(
-    body, outs, ins, scratch=(), flops=0, far=(), stream=None, pick=None, far_out=(),
-    limit=KERNEL_VMEM, **fixed
+    body, outs, ins, scratch=(), flops=0, far=(), pick=None, far_out=(), limit=KERNEL_VMEM, **fixed
 ):
     pick = pick or {}
     single = not isinstance(outs, tuple)
@@ -43,8 +42,6 @@
     near = pl.BlockSpec(memory_space=pltpu.VMEM)
     hbm = pl.BlockSpec(memory_space=pltpu.MemorySpace.HBM)
     landing = [pltpu.VMEM(ins[i].shape, ins[i].dtype) for i in far]
-    flow = [] if stream is None else [pltpu.VMEM(ins[stream].shape, ins[stream].dtype)]
-    parts = 0 if stream is None else ins[stream].shape[0]
     leaving = [pltpu.VMEM(outs[j].shape, outs[j].dtype) for j in far_out]
 
     def kernel(*refs):
@@ -52,23 +49,11 @@
         rest = refs[n_in + n_out :]
         own, rest = rest[:n_own], rest[n_own:]
         buffers, sems = rest[: len(far) + len(far_out)], rest[len(far) + len(far_out) :]
-        sems, flow_sems = sems[: len(far) + len(far_out)], sems[len(far) + len(far_out) :]
-        extra, flowing = {}, []
-        if stream is not None:
-            target, flow_sems = flow_sems[0], flow_sems[1:]
-            for k in range(parts):
-                flowing.append(
-                    pltpu.make_async_copy(in_refs[stream].at[k], target.at[k], flow_sems[k])
-                )
-            in_refs[stream] = target
-            extra["arrive"] = lambda k: flowing[k].wait()
         starts, results = [], []
         for slot, i in enumerate(far):
             starts.append(pltpu.make_async_copy(in_refs[i], buffers[slot], sems[slot]))
             starts[-1].start()
             in_refs[i] = buffers[slot]
-        for copy in flowing:
-            copy.start()
         for slot, j in enumerate(far_out, len(far)):
             results.append((buffers[slot], out_refs[j], sems[slot]))
             out_refs[j] = buffers[slot]
@@ -76,7 +61,7 @@
             in_refs[i] = in_refs[i].at[k]
         for copy in starts:
             copy.wait()
-        body(*in_refs, *out_refs, *own, **fixed, **extra)
+        body(*in_refs, *out_refs, *own, **fixed)
         ends = [pltpu.make_async_copy(*triple) for triple in results]
         for copy in ends:
             copy.start()
@@ -86,15 +71,13 @@
     result = pl.pallas_call(
         kernel,
         out_shape=outs,
-        in_specs=[hbm if i in far or i == stream else near for i in range(n_in)],
+        in_specs=[hbm if i in far else near for i in range(n_in)],
         out_specs=tuple(hbm if j in far_out else near for j in range(n_out)),
         scratch_shapes=[
             *scratch,
             *landing,
             *leaving,
             *[pltpu.SemaphoreType.DMA] * (len(landing) + len(leaving)),
-            *flow,
-            *[pltpu.SemaphoreType.DMA] * parts,
         ],
         compiler_params=pltpu.CompilerParams(vmem_limit_bytes=limit),
         cost_estimate=pl.CostEstimate(flops=flops, bytes_accessed=4 << 20, transcendentals=0),
@@ -363,40 +346,50 @@
         )
 
 
-def first_kernel(
-    stats, grad_stats, act, act_grad, mixed, second, sent, kept, own, total, *, lay, grid,
-    chunk, pixel_total
-):
-    width = act.shape[1]
+def first_gradient(act, act_grad, stats, grad_stats, pixel_total):
     mean, inverse = act_moments(stats, pixel_total)
     sums = jnp.sum(grad_stats[...], 0)
     grad_mean, cross_mean = sums[0:1] / pixel_total, sums[1:2] / pixel_total
+
+    def value(begin, count):
+        normed = (act[pl.ds(begin, count)] - mean) * inverse
+        _, slope = gated(normed)
+        grad = act_grad[pl.ds(begin, count)].astype(jnp.float32) * slope
+        return inverse * (grad - grad_mean - normed * cross_mean)
+
+    return value
+
+
+def first_kernel(
+    stats, grad_stats, act, act_grad, mixed, second, sent, own, total, *, lay, chunk, pixel_total
+):
+    value = first_gradient(act, act_grad, stats, grad_stats, pixel_total)
+    own[...] = jnp.zeros_like(own)
+
+    @pl.loop(0, lay.rows)
+    def _(i):
+        begin = pl.multiple_of((i + 2) * lay.wide, 16)
+        place = pl.multiple_of(i * lay.wide + 2 * MARGIN, 16)
+        own[pl.ds(place, lay.cols)] = value(begin, lay.cols)
+
+    weight_matmul(mixed, own, total, sent, lay, chunk)
+    for d in range(second.shape[0]):
+        sent[second.shape[0] + d] = second[d]
+
+
+def coarse_kernel(
+    stats, grad_stats, act, act_grad, picked, main, weight, out, kept, *, lay, grid, pixel_total
+):
+    width = weight.shape[2]
+    value = first_gradient(act, act_grad, stats, grad_stats, pixel_total)
     mask = inside_masks(lay, width, *grid)
-    own[...] = jnp.zeros_like(own)
     kept[...] = jnp.zeros_like(kept)
 
     @pl.loop(0, lay.out_rows)
     def _(r):
         begin = pl.multiple_of(r * lay.wide, 16)
-        normed = (act[pl.ds(begin, lay.wide)] - mean) * inverse
-        _, slope = gated(normed)
-        grad = act_grad[pl.ds(begin, lay.wide)].astype(jnp.float32) * slope
-        value = inverse * (grad - grad_mean - normed * cross_mean)
-        value = (value * mask(r)).astype(jnp.bfloat16)
-        kept[pl.ds(begin, lay.wide)] = value
-
-        @pl.when((r >= 2) & (r < lay.rows + 2))
-        def _():
-            place = pl.multiple_of((r - 2) * lay.wide + 2 * MARGIN, 16)
-            own[pl.ds(place, lay.cols)] = value[: lay.cols].astype(jnp.float32)
-
-    weight_matmul(mixed, own, total, sent, lay, chunk)
-    for d in range(second.shape[0]):
-        sent[second.shape[0] + d] = second[d]
-
-
-def coarse_kernel(kept, picked, main, weight, out, *, lay):
-    width = weight.shape[2]
+        kept[pl.ds(begin, lay.wide)] = (value(begin, lay.wide) * mask(r)).astype(jnp.bfloat16)
+
     windows = jnp.dot(picked[...], kept[...], preferred_element_type=jnp.float32)
     block_rows, block_cols = lay.rows // UPSCALE, lay.cols // UPSCALE
     blocks = block_rows * block_cols
@@ -559,14 +552,12 @@
     valid[...] = inside.astype(jnp.float32)
 
 
-def channel_conv(rows_ref, weight, shifted, out_rows, cols, arrive=None):
+def channel_conv(rows_ref, weight, shifted, out_rows, cols):
     width = weight.shape[3]
     count = out_rows * cols
     sums = None
     for a in range(3):
         left = rows_ref[a * cols : a * cols + count]
-        if arrive is not None:
-            arrive(a)
         if width % 128:
             part = [
                 jnp.dot(left, weight[a, b], preferred_element_type=jnp.float32) for b in range(3)
@@ -617,7 +608,7 @@
 
 def project_kernel(
     received, weight, source, project, sent, rows_ref, shifted, residual, spread, *, grid, band,
-    direct, arrive
+    direct
 ):
     row_devices, col_devices = grid
     band_rows, cols = band
@@ -625,7 +616,7 @@
     my_col = lax.axis_index("cols")
     for c in range(col_devices):
         rows_ref[:, c * width : (c + 1) * width] = received[c]
-    raw = channel_conv(rows_ref, weight, shifted, band_rows + 2, cols, arrive)
+    raw = channel_conv(rows_ref, weight, shifted, band_rows + 2, cols)
     count = (band_rows + 2) * cols
     if direct:
         residual[...] = jnp.zeros_like(residual)
@@ -800,9 +791,6 @@
             pltpu.VMEM((band_rows + 2, band_cols + 16, width), jnp.float32),
         ],
         18 * (band_rows + 2) * band_cols * channels * width_share,
-        far=(3,),
-        stream=1,
-        limit=63438848,
         far_out=(0,),
         grid=grid,
         band=band,
@@ -843,20 +831,19 @@
         grid=grid,
         pixel_total=pixel_total,
     )
-    sent_both, kept = call(
+    sent_both = call(
         first_kernel,
-        (sent_shape, jax.ShapeDtypeStruct((lay.kept, width), jnp.bfloat16)),
+        sent_shape,
         (stats, grad_stats, first_act, act_grad, mixed, second_sent),
         [own, total],
         conv_flops,
         far_out=(0,),
         lay=lay,
-        grid=grid,
         chunk=chunk,
         pixel_total=pixel_total,
     )
     part = to_all(sent_both, BOTH)
-    late_stats, _ = lax.optimization_barrier((stats, sent_both))
+    late_stats, late_grad_stats, _ = lax.optimization_barrier((stats, grad_stats, sent_both))
     enhanced = call(
         enhanced_kernel,
         jax.ShapeDtypeStruct((tile_rows, tile_cols, width), jnp.bfloat16),
@@ -871,9 +858,19 @@
     global_gradient = call(
         coarse_kernel,
         jax.ShapeDtypeStruct((blocks, width), jnp.float32),
-        (kept, window_picks(lay), output_cotangent, enhancer_first),
-        (),
+        (
+            late_stats,
+            late_grad_stats,
+            first_act,
+            act_grad,
+            window_picks(lay),
+            output_cotangent,
+            enhancer_first,
+        ),
+        [pltpu.VMEM((lay.kept, width), jnp.bfloat16)],
         lay=lay,
+        grid=grid,
+        pixel_total=pixel_total,
     )
     part, global_gradient, enhanced = lax.optimization_barrier((part, global_gradient, enhanced))
     share = call(share_kernel, half_shape, (part,), rescale=rescale)

time: 132 us -> 125 us (0.947)
  local copies, waits for them, and re-layouts: 16.3 us -> 12.2 us
  Pallas kernels: 33.4 us -> 29.7 us
    unnamed x52 -> x34, local copies, waits for them, and re-layouts: 15.5 us -> 11.4 us
    pallas_call x13, Pallas kernels: 33.4 us -> 29.7 us  [call(): pl.pallas_call(kernel, out_shape=outs, in_specs=[hbm if i in far else nea...]
  transfers between devices with their start and end apart: 12 -> 12, of which waited for: 9 -> 9; matrix products, arithmetic and copies ran while one was open for 2% -> 2% of each run, Pallas kernels for 14% -> 13%
where the time goes in v10:
time: 125 us; the launch traced here: 123 us
  starting transfers between devices  34.6 us (28%)
  Pallas kernels  29.7 us (24%)
  waiting for transfers between devices  29.3 us (23%)
  blocking collectives  14.8 us (12%)
  local copies, waits for them, and re-layouts  12.2 us (10%)
  other arithmetic  1.69 us (1%)
    pallas_call x13, Pallas kernels, call(): pl.pallas_call(kernel, out_shape=outs, in_specs=[hbm if i in far else nea...  29.7 us
    all_to_all x5, waiting for transfers between devices, to_all(): return lax.all_to_all(payload, axis, 0, 0)  21.3 us
    all_to_all x5, starting transfers between devices, to_all(): return lax.all_to_all(payload, axis, 0, 0)  16.5 us
    all_to_all x1, blocking collectives, among_cores(): return lax.all_to_all(payload, BOTH, 0, 0, axis_index_groups=groups)  14.8 us
    unnamed x34, local copies, waits for them, and re-layouts  11.4 us
    all_to_all x1, starting transfers between devices, among_cores(): return lax.all_to_all(payload, BOTH, 0, 0, axis_index_groups=groups)  8.46 us
    ppermute x1, waiting for transfers between devices, per_device(): bottom = lax.ppermute(bottoms, 'rows', row_down)  4.29 us
    ppermute x1, starting transfers between devices, per_device(): top = lax.ppermute(tops, 'rows', row_up)  3.83 us
  transfers between devices with their start and end apart: 12, of which 9 were waited for; matrix products, arithmetic and copies ran while one was open for 2% of the time, Pallas kernels for 13%

profile of v10, /device:TPU:0, one launch (start us, length us, event | category | flops | bytes accessed | tf_op | source)
XLA Modules:
  0.0 123.3 jit_solution(3848905861483118327)
XLA Ops:
  0.6 2.1 %pack_kernel.1 = bf16[16,72,128]{2,1,0:T(8,128)(2,1)} custom-call(f32[16,32,64]{2,1,0:T(8,128)} %refs_0_.3, s32[32,64]{1,0:T(8,128)} %refs_1_.2, bf16[64,128]{1,0:T(8,128)(2,1)} %bitcast.20), custom_call_target="tpu_custom_call" | custom-call | bytes 4194304 | tf_op jit(solution)/shard_map/pack_kernel/pallas_call | solution.py:71
  2.8 0.0 copy-start.4
  2.8 8.5 %all-to-all-start = ((bf16[16,72,128]{2,1,0:T(8,128)(2,1)}), bf16[16,72,128]{2,1,0:T(8,128)(2,1)S(1)}, u32[]{:S(2)}, u32[]{:S(2)}) async-start(bf16[16,72,128]{2,1,0:T(8,128)(2,1)} %pack_kernel.1), calls=%async_computation | async-start | bytes 589824 | tf_op jit(solution)/shard_map/all_to_all | solution.py:465
  11.3 0.8 slice_bitcast_fusion
  12.1 3.8 %collective-permute-start = (bf16[2,2,64,128]{3,2,1,0:T(8,128)(2,1)S(1)}, bf16[2,2,64,128]{3,2,1,0:T(8,128)(2,1)S(1)}, u32[]{:S(2)}, u32[]{:S(2)}) collective-permute-start(bf16[2,2,64,128]{3,2,1,0:T(8,128)(2,1)S(1)} %pad_maximum_fusion.2), channel_id=1, source_target_pairs={{0,8},{8,16},{16,24},{1,9},{9,17},{17,25},{2,10},{10,18},{18,26},{... | collective-permute-start | bytes 196616 | tf_op jit(solution)/shard_map/ppermute | solution.py:692
  16.0 1.3 %collective-permute-start.1 = (bf16[2,2,64,128]{3,2,1,0:T(8,128)(2,1)S(1)}, bf16[2,2,64,128]{3,2,1,0:T(8,128)(2,1)S(1)}, u32[]{:S(2)}, u32[]{:S(2)}) collective-permute-start(bf16[2,2,64,128]{3,2,1,0:T(8,128)(2,1)S(1)} %pad_maximum_fusion.3), channel_id=1, source_target_pairs={{8,0},{16,8},{24,16},{9,1},{17,9},{25,17},{10,2},{18,10},{26,18},{... | collective-permute-start | bytes 196616 | tf_op jit(solution)/shard_map/ppermute | solution.py:693
  17.3 0.6 collective-permute-done.refs_1_
  17.8 4.3 %collective-permute-done.1.refs_2_ = bf16[2,2,64,128]{3,2,1,0:T(8,128)(2,1)S(1)} collective-permute-done((bf16[2,2,64,128]{3,2,1,0:T(8,128)(2,1)S(1)}, bf16[2,2,64,128]{3,2,1,0:T(8,128)(2,1)S(1)}, u32[]{:S(2)}, u32[]{:S(2)}) %collective-permute-start.1) | collective-permute-done | bytes 65568 | tf_op jit(solution)/shard_map/ppermute | solution.py:693
  22.1 1.6 %fusion.4 = (bf16[2,36,8,128]{3,2,1,0:T(8,128)(2,1)}, bf16[2,36,8,128]{3,2,1,0:T(8,128)(2,1)S(1)}) fusion(bf16[1,32,64,128]{3,2,1,0:T(8,128)(2,1)} %bitcast.16, bf16[1,32,64,128]{3,2,1,0:T(8,128)(2,1)} %bitcast.17, bf16[2,2,8,128]{3,2,1,0:T(8,128)(2,1)S(1)} %get-tuple-element.50, bf16[2,2,8,128]{3,2,1,0:T(8,128)(2,1)S(1)} %get-tuple-element.48, ...), kind=kLoop, calls=%fused_computation.7 | loop fusion | flops 1179648 | bytes 1376256 | tf_op jit(solution)/shard_map/concatenate | solution.py:696
  23.7 0.0 all-to-all-done.refs_0_.refs_2_
  23.8 0.1 collective-permute-start.2
  23.8 1.6 %collective-permute-done.2.refs_1_ = bf16[16,72,128]{2,1,0:T(8,128)(2,1)S(1)} collective-permute-done((bf16[16,72,128]{2,1,0:T(8,128)(2,1)S(1)}, bf16[16,72,128]{2,1,0:T(8,128)(2,1)S(1)}, u32[]{:S(2)}, u32[]{:S(2)}) %collective-permute-start.2) | collective-permute-done | bytes 294944 | tf_op jit(solution)/shard_map/ppermute | solution.py:469
  25.4 0.0 copy-done.4
  25.4 1.9 %hidden_kernel.1 = bf16[8,192,128]{2,1,0:T(8,128)(2,1)} custom-call(bf16[16,72,128]{2,1,0:T(8,128)(2,1)S(1)} %all-to-all-done.refs_0_.refs_2_, bf16[16,72,128]{2,1,0:T(8,128)(2,1)S(1)} %collective-permute-done.2.refs_1_, bf16[3,3,1024,128]{3,2,1,0:T(8,128)(2,1)S(1)} %copy-done.4), custom_call_target="tpu_custom_call" | custom-call | flops 603979776 | bytes 4194304 | tf_op jit(solution)/shard_map/hidden_kernel/pallas_call | solution.py:71
  27.3 3.7 %all-to-all-start.1 = ((bf16[8,192,128]{2,1,0:T(8,128)(2,1)}), bf16[8,192,128]{2,1,0:T(8,128)(2,1)S(1)}, u32[]{:S(2)}, u32[]{:S(2)}) async-start(bf16[8,192,128]{2,1,0:T(8,128)(2,1)} %hidden_kernel.1), calls=%async_computation.1 | async-start | bytes 786432 | tf_op jit(solution)/shard_map/all_to_all | solution.py:457
  31.0 1.4 %collective-permute-start.3 = (bf16[2,36,8,128]{3,2,1,0:T(8,128)(2,1)}, bf16[2,36,8,128]{3,2,1,0:T(8,128)(2,1)S(1)}, u32[]{:S(2)}, u32[]{:S(2)}) collective-permute-start(bf16[2,36,8,128]{3,2,1,0:T(8,128)(2,1)} %get-tuple-element.28), channel_id=1, source_target_pairs={{1,0},{2,1},{3,2},{4,3},{5,4},{6,5},{7,6},{9,8},{10,9},{11,10},{12... | collective-permute-start | bytes 442376 | tf_op jit(solution)/shard_map/ppermute | solution.py:765
  32.4 3.0 %collective-permute-start.4 = (bf16[2,36,8,128]{3,2,1,0:T(8,128)(2,1)S(1)}, bf16[2,36,8,128]{3,2,1,0:T(8,128)(2,1)S(1)}, u32[]{:S(2)}, u32[]{:S(2)}) collective-permute-start(bf16[2,36,8,128]{3,2,1,0:T(8,128)(2,1)S(1)} %get-tuple-element.29), channel_id=1, source_target_pairs={{0,1},{1,2},{2,3},{3,4},{4,5},{5,6},{6,7},{8,9},{9,10},{10,11},{11... | collective-permute-start | bytes 442376 | tf_op jit(solution)/shard_map/ppermute | solution.py:764
  35.4 0.0 copy-done.15
  35.5 0.0 copy-done.16
  35.5 0.8 pool_kernel.1
  36.3 3.0 %all-to-all-done.1.refs_0_ = bf16[8,192,128]{2,1,0:T(8,128)(2,1)S(1)} async-done(((bf16[8,192,128]{2,1,0:T(8,128)(2,1)}), bf16[8,192,128]{2,1,0:T(8,128)(2,1)S(1)}, u32[]{:S(2)}, u32[]{:S(2)}) %all-to-all-start.1) | async-done | bytes 393248 | tf_op jit(solution)/shard_map/all_to_all | solution.py:457
  39.3 1.7 %copy-done.5 = bf16[3,3,1024,128]{3,2,1,0:T(8,128)(2,1)S(1)} copy-done((bf16[3,3,1024,128]{3,2,1,0:T(8,128)(2,1)S(1)}, bf16[3,3,1024,128]{3,2,1,0:T(8,128)(2,1)}, u32[]{:S(2)}) %copy-start.5) | copy-done | bytes 2359320
  41.0 0.9 copy-done.14
  41.9 1.4 %project_kernel.1 = f32[8,4,8,128]{3,2,1,0:T(8,128)} custom-call(bf16[8,192,128]{2,1,0:T(8,128)(2,1)S(1)} %all-to-all-done.1.refs_0_, bf16[3,3,1024,128]{3,2,1,0:T(8,128)(2,1)S(1)} %copy-done.5, bf16[16,72,128]{2,1,0:T(8,128)(2,1)S(1)} %all-to-all-done.refs_0_.refs_2_, bf16[1024,128]{1,0:T(8,128)(2,1)S(1)} %copy-done.14), custom_call_target="tpu_custom_call" | custom-call | flops 301989888 | bytes 4194304 | tf_op jit(solution)/shard_map/project_kernel/pallas_call | solution.py:71
  43.3 3.4 %all-to-all-start.2 = ((f32[8,4,8,128]{3,2,1,0:T(8,128)}), f32[8,4,8,128]{3,2,1,0:T(8,128)S(1)}, u32[]{:S(2)}, u32[]{:S(2)}) async-start(f32[8,4,8,128]{3,2,1,0:T(8,128)} %project_kernel.1), calls=%async_computation.2 | async-start | bytes 262144 | tf_op jit(solution)/shard_map/all_to_all | solution.py:457
  46.7 0.0 collective-permute-done.3
  46.7 0.0 collective-permute-done.4
  46.8 0.1 fusion.2.refs_3_
  46.8 0.0 copy-start.8
  46.8 5.4 %all-to-all-done.2.refs_4_ = f32[8,4,8,128]{3,2,1,0:T(8,128)S(1)} async-done(((f32[8,4,8,128]{3,2,1,0:T(8,128)}), f32[8,4,8,128]{3,2,1,0:T(8,128)S(1)}, u32[]{:S(2)}, u32[]{:S(2)}) %all-to-all-start.2) | async-done | bytes 131104 | tf_op jit(solution)/shard_map/all_to_all | solution.py:457
  52.2 0.0 copy-done.6
  52.2 1.0 copy-done.12
  53.2 3.5 %mixed_kernel.1 = (bf16[3072,128]{1,0:T(8,128)(2,1)S(1)}, f32[2800,128]{1,0:T(8,128)S(1)}, f32[32,8,128]{2,1,0:T(8,128)}) custom-call(bf16[32,64,128]{2,1,0:T(8,128)(2,1)S(1)} %copy-done.6, bf16[2,2,64,128]{3,2,1,0:T(8,128)(2,1)S(1)} %collective-permute-done.refs_1_, bf16[2,2,64,128]{3,2,1,0:T(8,128)(2,1)S(1)} %collective-permute-done.1.refs_2_, ...), custom_call_target="tpu_custom_call" | custom-call | flops 825753600 | bytes 4194304 | tf_op jit(solution)/shard_map/mixed_kernel/pallas_call | solution.py:71
  56.7 0.0 copy-done.8
  56.7 2.7 %all-to-all-start.3 = ((f32[32,8,128]{2,1,0:T(8,128)}), f32[32,8,128]{2,1,0:T(8,128)S(1)}, u32[]{:S(2)}, u32[]{:S(2)}) async-start(f32[32,8,128]{2,1,0:T(8,128)} %get-tuple-element.32), calls=%async_computation.3 | async-start | bytes 262144 | tf_op jit(solution)/shard_map/all_to_all | solution.py:457
  59.5 0.0 copy-start
  59.5 1.0 copy-done
  60.5 1.0 copy-done.9
  61.5 1.0 copy-done.10
  62.4 2.6 %cot_kernel.1.refs_2_.refs_3_ = bf16[2800,128]{1,0:T(8,128)(2,1)S(1)} custom-call(bf16[32,64,128]{2,1,0:T(8,128)(2,1)S(1)} %copy-done, bf16[2,2,64,128]{3,2,1,0:T(8,128)(2,1)S(1)} %collective-permute-done.refs_1_, bf16[2,2,64,128]{3,2,1,0:T(8,128)(2,1)S(1)} %collective-permute-done.1.refs_2_, bf16[2,37,16,128]{3,2,1,0:T(8,128)(2,1)S(1)} %copy-done.9, ...), custom_call_target="tpu_custom_call" | custom-call | flops 825753600 | bytes 4194304 | tf_op jit(solution)/shard_map/cot_kernel/pallas_call | solution.py:71
  65.1 2.6 %all-to-all-done.3.refs_1_.refs_0_ = f32[32,8,128]{2,1,0:T(8,128)S(1)} async-done(((f32[32,8,128]{2,1,0:T(8,128)}), f32[32,8,128]{2,1,0:T(8,128)S(1)}, u32[]{:S(2)}, u32[]{:S(2)}) %all-to-all-start.3) | async-done | bytes 131104 | tf_op jit(solution)/shard_map/all_to_all | solution.py:457
  67.7 1.8 %norm_kernel.1 = f32[32,8,128]{2,1,0:T(8,128)} custom-call(f32[2800,128]{1,0:T(8,128)S(1)} %get-tuple-element.33.refs_0_.refs_2_, f32[32,8,128]{2,1,0:T(8,128)S(1)} %all-to-all-done.3.refs_1_.refs_0_, bf16[2800,128]{1,0:T(8,128)(2,1)S(1)} %cot_kernel.1.refs_2_.refs_3_), custom_call_target="tpu_custom_call" | custom-call | bytes 4194304 | tf_op jit(solution)/shard_map/norm_kernel/pallas_call | solution.py:71
  69.5 3.2 %all-to-all-start.4 = ((f32[32,8,128]{2,1,0:T(8,128)}), f32[32,8,128]{2,1,0:T(8,128)S(1)}, u32[]{:S(2)}, u32[]{:S(2)}) async-start(f32[32,8,128]{2,1,0:T(8,128)} %norm_kernel.1), calls=%async_computation.4 | async-start | bytes 262144 | tf_op jit(solution)/shard_map/all_to_all | solution.py:457
  72.7 0.0 copy-start.1
  72.8 1.0 copy-done.1
  73.8 2.7 %second_kernel.1.refs_5_ = bf16[16,72,128]{2,1,0:T(8,128)(2,1)S(1)} custom-call(f32[2800,128]{1,0:T(8,128)S(1)} %get-tuple-element.33.refs_0_.refs_2_, f32[32,8,128]{2,1,0:T(8,128)S(1)} %all-to-all-done.3.refs_1_.refs_0_, bf16[32,64,128]{2,1,0:T(8,128)(2,1)S(1)} %copy-done.1), custom_call_target="tpu_custom_call" | custom-call | flops 825753600 | bytes 4194304 | tf_op jit(solution)/shard_map/second_kernel/pallas_call | solution.py:71
  76.5 4.5 %all-to-all-done.4.refs_1_ = f32[32,8,128]{2,1,0:T(8,128)S(1)} async-done(((f32[32,8,128]{2,1,0:T(8,128)}), f32[32,8,128]{2,1,0:T(8,128)S(1)}, u32[]{:S(2)}, u32[]{:S(2)}) %all-to-all-start.4) | async-done | bytes 131104 | tf_op jit(solution)/shard_map/all_to_all | solution.py:457
  81.0 2.6 %first_kernel.1 = bf16[32,72,128]{2,1,0:T(8,128)(2,1)S(1)} custom-call(f32[32,8,128]{2,1,0:T(8,128)S(1)} %all-to-all-done.3.refs_1_.refs_0_, f32[32,8,128]{2,1,0:T(8,128)S(1)} %all-to-all-done.4.refs_1_, f32[2800,128]{1,0:T(8,128)S(1)} %get-tuple-element.33.refs_0_.refs_2_, bf16[2800,128]{1,0:T(8,128)(2,1)S(1)} %cot_kernel.1.refs_2_.refs_3_, ...), custom_call_target="tpu_custom_call" | custom-call | flops 825753600 | bytes 4194304 | tf_op jit(solution)/shard_map/first_kernel/pallas_call | solution.py:71
  83.6 0.0 copy-start.3
  83.6 0.8 copy-done.3
  84.4 3.5 %all-to-all-start.5 = ((bf16[32,72,128]{2,1,0:T(8,128)(2,1)}), bf16[32,72,128]{2,1,0:T(8,128)(2,1)}, u32[]{:S(2)}, u32[]{:S(2)}) async-start(bf16[32,72,128]{2,1,0:T(8,128)(2,1)} %copy-done.3), calls=%async_computation.5 | async-start | bytes 1179648 | tf_op jit(solution)/shard_map/all_to_all | solution.py:457
  87.9 0.0 copy-start.2
  87.9 1.0 copy-done.2
  88.9 1.0 copy-done.7
  89.9 1.0 copy-done.13
  90.9 3.6 %coarse_kernel.1 = f32[8,128]{1,0:T(8,128)} custom-call(f32[32,8,128]{2,1,0:T(8,128)S(1)} %all-to-all-done.3.refs_1_.refs_0_, f32[32,8,128]{2,1,0:T(8,128)S(1)} %all-to-all-done.4.refs_1_, f32[2800,128]{1,0:T(8,128)S(1)} %get-tuple-element.33.refs_0_.refs_2_, bf16[2800,128]{1,0:T(8,128)(2,1)S(1)} %cot_kernel.1.refs_2_.refs_3_, ...), custom_call_target="tpu_custom_call" | custom-call | bytes 4194304 | tf_op jit(solution)/shard_map/coarse_kernel/pallas_call | solution.py:71
  94.5 0.0 copy-done.11
  94.5 4.3 %enhanced_kernel.1 = bf16[32,64,128]{2,1,0:T(8,128)(2,1)} custom-call(f32[2800,128]{1,0:T(8,128)S(1)} %get-tuple-element.33.refs_0_.refs_2_, f32[32,8,128]{2,1,0:T(8,128)S(1)} %all-to-all-done.3.refs_1_.refs_0_, bf16[3072,128]{1,0:T(8,128)(2,1)S(1)} %get-tuple-element.34.refs_4_.refs_2_, bf16[3,3,128,128]{3,2,1,0:T(8,128)(2,1)S(1)} %copy-done.11), custom_call_target="tpu_custom_call" | custom-call | flops 825753600 | bytes 4194304 | tf_op jit(solution)/shard_map/enhanced_kernel/pallas_call | solution.py:71
  98.8 5.8 %all-to-all-done.5.refs_0_ = bf16[32,72,128]{2,1,0:T(8,128)(2,1)} async-done(((bf16[32,72,128]{2,1,0:T(8,128)(2,1)}), bf16[32,72,128]{2,1,0:T(8,128)(2,1)}, u32[]{:S(2)}, u32[]{:S(2)}) %all-to-all-start.5) | async-done | bytes 589856 | tf_op jit(solution)/shard_map/all_to_all | solution.py:457
  104.6 1.2 share_kernel.1
  105.8 14.8 %all_to_all.35.refs_0_ = bf16[16,72,128]{2,1,0:T(8,128)(2,1)S(1)} all-to-all(bf16[16,72,128]{2,1,0:T(8,128)(2,1)S(1)} %share_kernel.1), channel_id=1, replica_groups={{0,2,4,6,8,10,12,14,16,18,20,22,24,26,28,30},{1,3,5,7,9,11,13,15,17,19,..., dimensions={0} | all-to-all | bytes 589824 | tf_op jit(solution)/shard_map/all_to_all | solution.py:465
  120.6 0.0 collective-permute-start.5
  120.6 1.6 %collective-permute-done.5.refs_1_ = bf16[16,72,128]{2,1,0:T(8,128)(2,1)S(1)} collective-permute-done((bf16[16,72,128]{2,1,0:T(8,128)(2,1)S(1)}, bf16[16,72,128]{2,1,0:T(8,128)(2,1)S(1)}, u32[]{:S(2)}, u32[]{:S(2)}) %collective-permute-start.5) | collective-permute-done | bytes 294944 | tf_op jit(solution)/shard_map/ppermute | solution.py:469
  122.2 1.1 join_kernel.1
  (15 shorter events, 0.0 us)
Async XLA Ops:
  2.8 22.6 %copy-start.4 = (bf16[3,3,1024,128]{3,2,1,0:T(8,128)(2,1)S(1)}, bf16[3,3,1024,128]{3,2,1,0:T(8,128)(2,1)}, u32[]{:S(2)}) copy-start(bf16[3,3,1024,128]{3,2,1,0:T(8,128)(2,1)} %refs_2_.3) | copy-start | bytes 7077892
  2.8 21.0 %all-to-all-start = ((bf16[16,72,128]{2,1,0:T(8,128)(2,1)}), bf16[16,72,128]{2,1,0:T(8,128)(2,1)S(1)}, u32[]{:S(2)}, u32[]{:S(2)}) async-start(bf16[16,72,128]{2,1,0:T(8,128)(2,1)} %pack_kernel.1), calls=%async_computation | async-start | bytes 589824 | tf_op jit(solution)/shard_map/all_to_all | solution.py:465
  12.1 5.7 %collective-permute-start = (bf16[2,2,64,128]{3,2,1,0:T(8,128)(2,1)S(1)}, bf16[2,2,64,128]{3,2,1,0:T(8,128)(2,1)S(1)}, u32[]{:S(2)}, u32[]{:S(2)}) collective-permute-start(bf16[2,2,64,128]{3,2,1,0:T(8,128)(2,1)S(1)} %pad_maximum_fusion.2), channel_id=1, source_target_pairs={{0,8},{8,16},{16,24},{1,9},{9,17},{17,25},{2,10},{10,18},{18,26},{... | collective-permute-start | bytes 196616 | tf_op jit(solution)/shard_map/ppermute | solution.py:692
  16.0 6.2 %collective-permute-start.1 = (bf16[2,2,64,128]{3,2,1,0:T(8,128)(2,1)S(1)}, bf16[2,2,64,128]{3,2,1,0:T(8,128)(2,1)S(1)}, u32[]{:S(2)}, u32[]{:S(2)}) collective-permute-start(bf16[2,2,64,128]{3,2,1,0:T(8,128)(2,1)S(1)} %pad_maximum_fusion.3), channel_id=1, source_target_pairs={{8,0},{16,8},{24,16},{9,1},{17,9},{25,17},{10,2},{18,10},{26,18},{... | collective-permute-start | bytes 196616 | tf_op jit(solution)/shard_map/ppermute | solution.py:693
  23.7 11.7 %copy-start.15 = (f32[16,128]{1,0:T(8,128)S(1)}, f32[16,128]{1,0:T(8,128)}, u32[]{:S(2)}) copy-start(f32[16,128]{1,0:T(8,128)} %refs_3_.4) | copy-start | bytes 24580
  23.7 11.7 %copy-start.16 = (s32[8,256]{1,0:T(8,128)S(1)}, s32[8,256]{1,0:T(8,128)}, u32[]{:S(2)}) copy-start(s32[8,256]{1,0:T(8,128)} %constant.7.clone.refs_2_) | copy-start | bytes 24580
  23.8 1.6 %collective-permute-start.2 = (bf16[16,72,128]{2,1,0:T(8,128)(2,1)S(1)}, bf16[16,72,128]{2,1,0:T(8,128)(2,1)S(1)}, u32[]{:S(2)}, u32[]{:S(2)}) collective-permute-start(bf16[16,72,128]{2,1,0:T(8,128)(2,1)S(1)} %all-to-all-done.refs_0_.refs_2_), channel_id=1, source_target_pairs={{0,1},{1,0},{2,3},{3,2},{4,5},{5,4},{6,7},{7,6},{8,9},{9,8},{10,11... | collective-permute-start | bytes 884744 | tf_op jit(solution)/shard_map/ppermute | solution.py:469
  27.3 12.0 %all-to-all-start.1 = ((bf16[8,192,128]{2,1,0:T(8,128)(2,1)}), bf16[8,192,128]{2,1,0:T(8,128)(2,1)S(1)}, u32[]{:S(2)}, u32[]{:S(2)}) async-start(bf16[8,192,128]{2,1,0:T(8,128)(2,1)} %hidden_kernel.1), calls=%async_computation.1 | async-start | bytes 786432 | tf_op jit(solution)/shard_map/all_to_all | solution.py:457
  31.0 21.2 %copy-start.6 = (bf16[32,64,128]{2,1,0:T(8,128)(2,1)S(1)}, bf16[32,64,128]{2,1,0:T(8,128)(2,1)}, u32[]{:S(2)}) copy-start(bf16[32,64,128]{2,1,0:T(8,128)(2,1)} %refs_0_.4) | copy-start | bytes 1572868
  31.0 15.8 %collective-permute-start.3 = (bf16[2,36,8,128]{3,2,1,0:T(8,128)(2,1)}, bf16[2,36,8,128]{3,2,1,0:T(8,128)(2,1)S(1)}, u32[]{:S(2)}, u32[]{:S(2)}) collective-permute-start(bf16[2,36,8,128]{3,2,1,0:T(8,128)(2,1)} %get-tuple-element.28), channel_id=1, source_target_pairs={{1,0},{2,1},{3,2},{4,3},{5,4},{6,5},{7,6},{9,8},{10,9},{11,10},{12... | collective-permute-start | bytes 442376 | tf_op jit(solution)/shard_map/ppermute | solution.py:765
  32.4 14.3 %collective-permute-start.4 = (bf16[2,36,8,128]{3,2,1,0:T(8,128)(2,1)S(1)}, bf16[2,36,8,128]{3,2,1,0:T(8,128)(2,1)S(1)}, u32[]{:S(2)}, u32[]{:S(2)}) collective-permute-start(bf16[2,36,8,128]{3,2,1,0:T(8,128)(2,1)S(1)} %get-tuple-element.29), channel_id=1, source_target_pairs={{0,1},{1,2},{2,3},{3,4},{4,5},{5,6},{6,7},{8,9},{9,10},{10,11},{11... | collective-permute-start | bytes 442376 | tf_op jit(solution)/shard_map/ppermute | solution.py:764
  39.3 1.7 %copy-start.5 = (bf16[3,3,1024,128]{3,2,1,0:T(8,128)(2,1)S(1)}, bf16[3,3,1024,128]{3,2,1,0:T(8,128)(2,1)}, u32[]{:S(2)}) copy-start(bf16[3,3,1024,128]{3,2,1,0:T(8,128)(2,1)} %refs_1_.3) | copy-start | bytes 7077892
  41.0 0.9 copy-start.14
  43.3 8.9 %all-to-all-start.2 = ((f32[8,4,8,128]{3,2,1,0:T(8,128)}), f32[8,4,8,128]{3,2,1,0:T(8,128)S(1)}, u32[]{:S(2)}, u32[]{:S(2)}) async-start(f32[8,4,8,128]{3,2,1,0:T(8,128)} %project_kernel.1), calls=%async_computation.2 | async-start | bytes 262144 | tf_op jit(solution)/shard_map/all_to_all | solution.py:457
  46.8 9.9 %copy-start.8 = (bf16[2,37,16,128]{3,2,1,0:T(8,128)(2,1)}, bf16[2,37,16,128]{3,2,1,0:T(8,128)(2,1)S(1)}, u32[]{:S(2)}) copy-start(bf16[2,37,16,128]{3,2,1,0:T(8,128)(2,1)S(1)} %fusion.2.refs_3_) | copy-start | bytes 909316
  52.2 1.0 copy-start.12
  56.7 11.0 %all-to-all-start.3 = ((f32[32,8,128]{2,1,0:T(8,128)}), f32[32,8,128]{2,1,0:T(8,128)S(1)}, u32[]{:S(2)}, u32[]{:S(2)}) async-start(f32[32,8,128]{2,1,0:T(8,128)} %get-tuple-element.32), calls=%async_computation.3 | async-start | bytes 262144 | tf_op jit(solution)/shard_map/all_to_all | solution.py:457
  59.5 1.0 copy-start
  60.5 1.0 copy-start.9
  61.5 1.0 copy-start.10
  69.5 11.5 %all-to-all-start.4 = ((f32[32,8,128]{2,1,0:T(8,128)}), f32[32,8,128]{2,1,0:T(8,128)S(1)}, u32[]{:S(2)}, u32[]{:S(2)}) async-start(f32[32,8,128]{2,1,0:T(8,128)} %norm_kernel.1), calls=%async_computation.4 | async-start | bytes 262144 | tf_op jit(solution)/shard_map/all_to_all | solution.py:457
  72.7 1.0 copy-start.1
  83.6 0.8 copy-start.3
  84.4 10.1 %copy-start.11 = (bf16[3,3,128,128]{3,2,1,0:T(8,128)(2,1)S(1)}, bf16[3,3,128,128]{3,2,1,0:T(8,128)(2,1)}, u32[]{:S(2)}) copy-start(bf16[3,3,128,128]{3,2,1,0:T(8,128)(2,1)} %refs_3_.5) | copy-start | bytes 884740
  84.4 20.2 %all-to-all-start.5 = ((bf16[32,72,128]{2,1,0:T(8,128)(2,1)}), bf16[32,72,128]{2,1,0:T(8,128)(2,1)}, u32[]{:S(2)}, u32[]{:S(2)}) async-start(bf16[32,72,128]{2,1,0:T(8,128)(2,1)} %copy-done.3), calls=%async_computation.5 | async-start | bytes 1179648 | tf_op jit(solution)/shard_map/all_to_all | solution.py:457
  87.9 1.0 copy-start.2
  88.9 1.0 copy-start.7
  89.9 1.0 copy-start.13
  120.6 1.6 %collective-permute-start.5 = (bf16[16,72,128]{2,1,0:T(8,128)(2,1)S(1)}, bf16[16,72,128]{2,1,0:T(8,128)(2,1)S(1)}, u32[]{:S(2)}, u32[]{:S(2)}) collective-permute-start(bf16[16,72,128]{2,1,0:T(8,128)(2,1)S(1)} %all_to_all.35.refs_0_), channel_id=1, source_target_pairs={{0,1},{1,0},{2,3},{3,2},{4,5},{5,4},{6,7},{7,6},{8,9},{9,8},{10,11... | collective-permute-start | bytes 884744 | tf_op jit(solution)/shard_map/ppermute | solution.py:469

commit v11 on v10

--- a/solution.py
+++ b/solution.py
@@ -361,7 +361,7 @@
 
 
 def first_kernel(
-    stats, grad_stats, act, act_grad, mixed, second, sent, own, total, *, lay, chunk, pixel_total
+    stats, grad_stats, act, act_grad, mixed, sent, own, total, *, lay, chunk, pixel_total
 ):
     value = first_gradient(act, act_grad, stats, grad_stats, pixel_total)
     own[...] = jnp.zeros_like(own)
@@ -373,8 +373,6 @@
         own[pl.ds(place, lay.cols)] = value(begin, lay.cols)
 
     weight_matmul(mixed, own, total, sent, lay, chunk)
-    for d in range(second.shape[0]):
-        sent[second.shape[0] + d] = second[d]
 
 
 def coarse_kernel(
@@ -412,6 +410,17 @@
             out[k : k + 1] = (cot + summed[k : k + 1]) / UPSCALE
 
 
+def pair_kernel(first, moved_first, second, moved_second, sent):
+    core = lax.axis_index("cols") & 1
+    for k, (mine, other) in enumerate(((first, moved_first), (second, moved_second))):
+
+        @pl.when(core == k)
+        def _():
+            for d in range(sent.shape[0]):
+                total = mine[d].astype(jnp.float32) + other[d].astype(jnp.float32)
+                sent[d] = total.astype(jnp.bfloat16)
+
+
 def share_kernel(received, sent, *, rescale):
     total = received[0].astype(jnp.float32)
     for d in range(1, received.shape[0]):
@@ -421,20 +430,15 @@
         sent[d] = total
 
 
-def join_kernel(mine, other, first, second, *, chunk, grid):
-    row_devices, col_devices = grid
-    half, pairs = row_devices * col_devices // 2, col_devices // 2
+def join_kernel(mine, other, first, second, *, chunk):
     core = lax.axis_index("cols") & 1
-    for k in range(2):
+    for k, (near, far) in enumerate(((first, second), (second, first))):
 
         @pl.when(core == k)
         def _():
-            for source, side in ((mine, k), (other, 1 - k)):
-                for d in range(half):
-                    owner = d // pairs * col_devices + d % pairs * 2 + side
-                    out = first if owner < half else second
-                    begin = owner % half * chunk
-                    out[begin : begin + chunk] = source[d].astype(jnp.float32)[:chunk]
+            for source, out in ((mine, near), (other, far)):
+                for d in range(source.shape[0]):
+                    out[d * chunk : (d + 1) * chunk] = source[d].astype(jnp.float32)[:chunk]
 
 
 def window_picks(lay):
@@ -706,7 +710,6 @@
     flat_shape = jax.ShapeDtypeStruct((lay.flat, width), jnp.bfloat16)
     out_shape = jax.ShapeDtypeStruct((lay.out, width), jnp.float32)
     stats_shape = jax.ShapeDtypeStruct((devices, 8, width), jnp.float32)
-    sent_shape = jax.ShapeDtypeStruct((devices, padded_chunk, width), jnp.bfloat16)
     half_shape = jax.ShapeDtypeStruct((devices // 2, padded_chunk, width), jnp.bfloat16)
     conv_flops = 18 * width * width * lay.out
 
@@ -831,19 +834,27 @@
         grid=grid,
         pixel_total=pixel_total,
     )
-    sent_both = call(
+    moved_second = lax.ppermute(
+        second_sent, "cols", [(c, c + 1) for c in range(0, col_devices, 2)]
+    )
+    first_sent = call(
         first_kernel,
-        sent_shape,
-        (stats, grad_stats, first_act, act_grad, mixed, second_sent),
+        half_shape,
+        (stats, grad_stats, first_act, act_grad, mixed),
         [own, total],
         conv_flops,
-        far_out=(0,),
         lay=lay,
         chunk=chunk,
         pixel_total=pixel_total,
     )
-    part = to_all(sent_both, BOTH)
-    late_stats, late_grad_stats, _ = lax.optimization_barrier((stats, grad_stats, sent_both))
+    moved_first = lax.ppermute(
+        first_sent, "cols", [(c + 1, c) for c in range(0, col_devices, 2)]
+    )
+    pair = call(
+        pair_kernel, half_shape, (first_sent, moved_first, second_sent, moved_second)
+    )
+    part = among_cores(pair, row_devices, col_devices)
+    late_stats, late_grad_stats, _ = lax.optimization_barrier((stats, grad_stats, pair))
     enhanced = call(
         enhanced_kernel,
         jax.ShapeDtypeStruct((tile_rows, tile_cols, width), jnp.bfloat16),
@@ -878,7 +889,7 @@
     shares = (share, core_swap(share, col_devices))
     whole_shape = jax.ShapeDtypeStruct((9 * width, width), jnp.float32)
     first_total, second_total = call(
-        join_kernel, (whole_shape, whole_shape), shares, chunk=chunk, grid=grid
+        join_kernel, (whole_shape, whole_shape), shares, chunk=chunk
     )
     return (
         enhanced,

time: 125 us -> 126 us (level)
  waiting for transfers between devices: 29.3 us -> 22.9 us
  starting transfers between devices: 34.6 us -> 40.4 us
  blocking collectives: 14.8 us -> 17.1 us
    all_to_all x5 -> x4, waiting for transfers between devices: 21.3 us -> 12.6 us  [to_all(): return lax.all_to_all(payload, axis, 0, 0)]
    all_to_all x1 -> x2, starting transfers between devices: 8.46 us -> 13.6 us  [among_cores(): return lax.all_to_all(payload, BOTH, 0, 0, axis_index_groups=groups)]
    ppermute x0 -> x2, starting transfers between devices: none -> 4.17 us  [the longest x1 2.88 us: per_device(): lax.ppermute(second_sent, 'cols', [(c, c + 1) for c in range(0, col_devic...]
    all_to_all x5 -> x4, starting transfers between devices: 16.5 us -> 13 us  [to_all(): return lax.all_to_all(payload, axis, 0, 0)]
    all_to_all x1, blocking collectives: 14.8 us -> 17.1 us  [among_cores(): return lax.all_to_all(payload, BOTH, 0, 0, axis_index_groups=groups)]
    ppermute x0 -> x2, waiting for transfers between devices: none -> 2.17 us  [the longest x1 2.17 us: per_device(): lax.ppermute(first_sent, 'cols', [(c + 1, c) for c in range(0, col_device...]
    pallas_call x13 -> x14, Pallas kernels: 29.7 us -> 29.5 us  [call(): pl.pallas_call(kernel, out_shape=outs, in_specs=[hbm if i in far else nea...]
  transfers between devices with their start and end apart: 12 -> 14, of which waited for: 9 -> 9; matrix products, arithmetic and copies ran while one was open for 2% -> 2% of each run, Pallas kernels for 13% -> 14%
where the time goes in v11:
time: 126 us; the launch traced here: 125 us
  starting transfers between devices  40.4 us (32%)
  Pallas kernels  29.5 us (23%)
  waiting for transfers between devices  22.9 us (18%)
  blocking collectives  17.1 us (14%)
  local copies, waits for them, and re-layouts  12.1 us (10%)
  other arithmetic  1.69 us (1%)
    pallas_call x14, Pallas kernels, call(): pl.pallas_call(kernel, out_shape=outs, in_specs=[hbm if i in far else nea...  29.5 us
    all_to_all x1, blocking collectives, among_cores(): return lax.all_to_all(payload, BOTH, 0, 0, axis_index_groups=groups)  17.1 us
    all_to_all x2, starting transfers between devices, among_cores(): return lax.all_to_all(payload, BOTH, 0, 0, axis_index_groups=groups)  13.6 us
    all_to_all x4, starting transfers between devices, to_all(): return lax.all_to_all(payload, axis, 0, 0)  13 us
    all_to_all x4, waiting for transfers between devices, to_all(): return lax.all_to_all(payload, axis, 0, 0)  12.6 us
    unnamed x34, local copies, waits for them, and re-layouts  11.3 us
    ppermute x1, waiting for transfers between devices, per_device(): bottom = lax.ppermute(bottoms, 'rows', row_down)  4.29 us
    ppermute x1, starting transfers between devices, per_device(): top = lax.ppermute(tops, 'rows', row_up)  3.83 us
  transfers between devices with their start and end apart: 14, of which 9 were waited for; matrix products, arithmetic and copies ran while one was open for 2% of the time, Pallas kernels for 14%

profile of v11, /device:TPU:0, one launch (start us, length us, event | category | flops | bytes accessed | tf_op | source)
XLA Modules:
  0.0 124.6 jit_solution(5350249563177136703)
XLA Ops:
  0.6 2.1 %pack_kernel.1 = bf16[16,72,128]{2,1,0:T(8,128)(2,1)} custom-call(f32[16,32,64]{2,1,0:T(8,128)} %refs_0_.3, s32[32,64]{1,0:T(8,128)} %refs_1_.2, bf16[64,128]{1,0:T(8,128)(2,1)} %bitcast.20), custom_call_target="tpu_custom_call" | custom-call | bytes 4194304 | tf_op jit(solution)/shard_map/pack_kernel/pallas_call | solution.py:71
  2.8 0.0 copy-start.3
  2.8 8.5 %all-to-all-start = ((bf16[16,72,128]{2,1,0:T(8,128)(2,1)}), bf16[16,72,128]{2,1,0:T(8,128)(2,1)S(1)}, u32[]{:S(2)}, u32[]{:S(2)}) async-start(bf16[16,72,128]{2,1,0:T(8,128)(2,1)} %pack_kernel.1), calls=%async_computation | async-start | bytes 589824 | tf_op jit(solution)/shard_map/all_to_all | solution.py:469
  11.3 0.8 slice_bitcast_fusion
  12.1 3.8 %collective-permute-start = (bf16[2,2,64,128]{3,2,1,0:T(8,128)(2,1)S(1)}, bf16[2,2,64,128]{3,2,1,0:T(8,128)(2,1)S(1)}, u32[]{:S(2)}, u32[]{:S(2)}) collective-permute-start(bf16[2,2,64,128]{3,2,1,0:T(8,128)(2,1)S(1)} %pad_maximum_fusion.2), channel_id=1, source_target_pairs={{0,8},{8,16},{16,24},{1,9},{9,17},{17,25},{2,10},{10,18},{18,26},{... | collective-permute-start | bytes 196616 | tf_op jit(solution)/shard_map/ppermute | solution.py:696
  16.0 1.3 %collective-permute-start.1 = (bf16[2,2,64,128]{3,2,1,0:T(8,128)(2,1)S(1)}, bf16[2,2,64,128]{3,2,1,0:T(8,128)(2,1)S(1)}, u32[]{:S(2)}, u32[]{:S(2)}) collective-permute-start(bf16[2,2,64,128]{3,2,1,0:T(8,128)(2,1)S(1)} %pad_maximum_fusion.3), channel_id=1, source_target_pairs={{8,0},{16,8},{24,16},{9,1},{17,9},{25,17},{10,2},{18,10},{26,18},{... | collective-permute-start | bytes 196616 | tf_op jit(solution)/shard_map/ppermute | solution.py:697
  17.3 0.6 collective-permute-done.refs_1_
  17.8 4.3 %collective-permute-done.1.refs_2_ = bf16[2,2,64,128]{3,2,1,0:T(8,128)(2,1)S(1)} collective-permute-done((bf16[2,2,64,128]{3,2,1,0:T(8,128)(2,1)S(1)}, bf16[2,2,64,128]{3,2,1,0:T(8,128)(2,1)S(1)}, u32[]{:S(2)}, u32[]{:S(2)}) %collective-permute-start.1) | collective-permute-done | bytes 65568 | tf_op jit(solution)/shard_map/ppermute | solution.py:697
  22.1 1.6 %fusion.4 = (bf16[2,36,8,128]{3,2,1,0:T(8,128)(2,1)}, bf16[2,36,8,128]{3,2,1,0:T(8,128)(2,1)S(1)}) fusion(bf16[1,32,64,128]{3,2,1,0:T(8,128)(2,1)} %bitcast.16, bf16[1,32,64,128]{3,2,1,0:T(8,128)(2,1)} %bitcast.17, bf16[2,2,8,128]{3,2,1,0:T(8,128)(2,1)S(1)} %get-tuple-element.50, bf16[2,2,8,128]{3,2,1,0:T(8,128)(2,1)S(1)} %get-tuple-element.48, ...), kind=kLoop, calls=%fused_computation.7 | loop fusion | flops 1179648 | bytes 1376256 | tf_op jit(solution)/shard_map/concatenate | solution.py:700
  23.7 0.0 all-to-all-done.refs_0_.refs_2_
  23.8 0.1 collective-permute-start.2
  23.8 1.6 %collective-permute-done.2.refs_1_ = bf16[16,72,128]{2,1,0:T(8,128)(2,1)S(1)} collective-permute-done((bf16[16,72,128]{2,1,0:T(8,128)(2,1)S(1)}, bf16[16,72,128]{2,1,0:T(8,128)(2,1)S(1)}, u32[]{:S(2)}, u32[]{:S(2)}) %collective-permute-start.2) | collective-permute-done | bytes 294944 | tf_op jit(solution)/shard_map/ppermute | solution.py:473
  25.4 1.9 %hidden_kernel.1 = bf16[8,192,128]{2,1,0:T(8,128)(2,1)} custom-call(bf16[16,72,128]{2,1,0:T(8,128)(2,1)S(1)} %all-to-all-done.refs_0_.refs_2_, bf16[16,72,128]{2,1,0:T(8,128)(2,1)S(1)} %collective-permute-done.2.refs_1_, bf16[3,3,1024,128]{3,2,1,0:T(8,128)(2,1)S(1)} %copy-done.3), custom_call_target="tpu_custom_call" | custom-call | flops 603979776 | bytes 4194304 | tf_op jit(solution)/shard_map/hidden_kernel/pallas_call | solution.py:71
  27.3 3.7 %all-to-all-start.1 = ((bf16[8,192,128]{2,1,0:T(8,128)(2,1)}), bf16[8,192,128]{2,1,0:T(8,128)(2,1)S(1)}, u32[]{:S(2)}, u32[]{:S(2)}) async-start(bf16[8,192,128]{2,1,0:T(8,128)(2,1)} %hidden_kernel.1), calls=%async_computation.1 | async-start | bytes 786432 | tf_op jit(solution)/shard_map/all_to_all | solution.py:461
  31.0 1.4 %collective-permute-start.3 = (bf16[2,36,8,128]{3,2,1,0:T(8,128)(2,1)}, bf16[2,36,8,128]{3,2,1,0:T(8,128)(2,1)S(1)}, u32[]{:S(2)}, u32[]{:S(2)}) collective-permute-start(bf16[2,36,8,128]{3,2,1,0:T(8,128)(2,1)} %get-tuple-element.28), channel_id=1, source_target_pairs={{1,0},{2,1},{3,2},{4,3},{5,4},{6,5},{7,6},{9,8},{10,9},{11,10},{12... | collective-permute-start | bytes 442376 | tf_op jit(solution)/shard_map/ppermute | solution.py:768
  32.4 3.0 %collective-permute-start.4 = (bf16[2,36,8,128]{3,2,1,0:T(8,128)(2,1)S(1)}, bf16[2,36,8,128]{3,2,1,0:T(8,128)(2,1)S(1)}, u32[]{:S(2)}, u32[]{:S(2)}) collective-permute-start(bf16[2,36,8,128]{3,2,1,0:T(8,128)(2,1)S(1)} %get-tuple-element.29), channel_id=1, source_target_pairs={{0,1},{1,2},{2,3},{3,4},{4,5},{5,6},{6,7},{8,9},{9,10},{10,11},{11... | collective-permute-start | bytes 442376 | tf_op jit(solution)/shard_map/ppermute | solution.py:767
  35.4 0.0 copy-done.15
  35.5 0.8 pool_kernel.1
  36.3 3.0 %all-to-all-done.1.refs_0_ = bf16[8,192,128]{2,1,0:T(8,128)(2,1)S(1)} async-done(((bf16[8,192,128]{2,1,0:T(8,128)(2,1)}), bf16[8,192,128]{2,1,0:T(8,128)(2,1)S(1)}, u32[]{:S(2)}, u32[]{:S(2)}) %all-to-all-start.1) | async-done | bytes 393248 | tf_op jit(solution)/shard_map/all_to_all | solution.py:461
  39.3 1.7 %copy-done.4 = bf16[3,3,1024,128]{3,2,1,0:T(8,128)(2,1)S(1)} copy-done((bf16[3,3,1024,128]{3,2,1,0:T(8,128)(2,1)S(1)}, bf16[3,3,1024,128]{3,2,1,0:T(8,128)(2,1)}, u32[]{:S(2)}) %copy-start.4) | copy-done | bytes 2359320
  41.0 0.9 copy-done.14
  41.9 1.4 %project_kernel.1 = f32[8,4,8,128]{3,2,1,0:T(8,128)} custom-call(bf16[8,192,128]{2,1,0:T(8,128)(2,1)S(1)} %all-to-all-done.1.refs_0_, bf16[3,3,1024,128]{3,2,1,0:T(8,128)(2,1)S(1)} %copy-done.4, bf16[16,72,128]{2,1,0:T(8,128)(2,1)S(1)} %all-to-all-done.refs_0_.refs_2_, bf16[1024,128]{1,0:T(8,128)(2,1)S(1)} %copy-done.14), custom_call_target="tpu_custom_call" | custom-call | flops 301989888 | bytes 4194304 | tf_op jit(solution)/shard_map/project_kernel/pallas_call | solution.py:71
  43.3 3.4 %all-to-all-start.2 = ((f32[8,4,8,128]{3,2,1,0:T(8,128)}), f32[8,4,8,128]{3,2,1,0:T(8,128)S(1)}, u32[]{:S(2)}, u32[]{:S(2)}) async-start(f32[8,4,8,128]{3,2,1,0:T(8,128)} %project_kernel.1), calls=%async_computation.2 | async-start | bytes 262144 | tf_op jit(solution)/shard_map/all_to_all | solution.py:461
  46.7 0.0 collective-permute-done.3
  46.7 0.0 collective-permute-done.4
  46.8 0.1 fusion.2.refs_3_
  46.8 0.0 copy-start.8
  46.8 5.4 %all-to-all-done.2.refs_4_ = f32[8,4,8,128]{3,2,1,0:T(8,128)S(1)} async-done(((f32[8,4,8,128]{3,2,1,0:T(8,128)}), f32[8,4,8,128]{3,2,1,0:T(8,128)S(1)}, u32[]{:S(2)}, u32[]{:S(2)}) %all-to-all-start.2) | async-done | bytes 131104 | tf_op jit(solution)/shard_map/all_to_all | solution.py:461
  52.2 1.0 copy-done.12
  53.2 3.5 %mixed_kernel.1 = (bf16[3072,128]{1,0:T(8,128)(2,1)S(1)}, f32[2800,128]{1,0:T(8,128)S(1)}, f32[32,8,128]{2,1,0:T(8,128)}) custom-call(bf16[32,64,128]{2,1,0:T(8,128)(2,1)S(1)} %copy-done.6, bf16[2,2,64,128]{3,2,1,0:T(8,128)(2,1)S(1)} %collective-permute-done.refs_1_, bf16[2,2,64,128]{3,2,1,0:T(8,128)(2,1)S(1)} %collective-permute-done.1.refs_2_, ...), custom_call_target="tpu_custom_call" | custom-call | flops 825753600 | bytes 4194304 | tf_op jit(solution)/shard_map/mixed_kernel/pallas_call | solution.py:71
  56.7 2.7 %all-to-all-start.3 = ((f32[32,8,128]{2,1,0:T(8,128)}), f32[32,8,128]{2,1,0:T(8,128)S(1)}, u32[]{:S(2)}, u32[]{:S(2)}) async-start(f32[32,8,128]{2,1,0:T(8,128)} %get-tuple-element.32), calls=%async_computation.3 | async-start | bytes 262144 | tf_op jit(solution)/shard_map/all_to_all | solution.py:461
  59.5 0.0 copy-start
  59.5 1.0 copy-done
  60.5 1.0 copy-done.9
  61.5 1.0 copy-done.10
  62.4 2.6 %cot_kernel.1.refs_2_.refs_3_ = bf16[2800,128]{1,0:T(8,128)(2,1)S(1)} custom-call(bf16[32,64,128]{2,1,0:T(8,128)(2,1)S(1)} %copy-done, bf16[2,2,64,128]{3,2,1,0:T(8,128)(2,1)S(1)} %collective-permute-done.refs_1_, bf16[2,2,64,128]{3,2,1,0:T(8,128)(2,1)S(1)} %collective-permute-done.1.refs_2_, bf16[2,37,16,128]{3,2,1,0:T(8,128)(2,1)S(1)} %copy-done.9, ...), custom_call_target="tpu_custom_call" | custom-call | flops 825753600 | bytes 4194304 | tf_op jit(solution)/shard_map/cot_kernel/pallas_call | solution.py:71
  65.1 2.6 %all-to-all-done.3.refs_1_.refs_0_ = f32[32,8,128]{2,1,0:T(8,128)S(1)} async-done(((f32[32,8,128]{2,1,0:T(8,128)}), f32[32,8,128]{2,1,0:T(8,128)S(1)}, u32[]{:S(2)}, u32[]{:S(2)}) %all-to-all-start.3) | async-done | bytes 131104 | tf_op jit(solution)/shard_map/all_to_all | solution.py:461
  67.7 1.8 %norm_kernel.1 = f32[32,8,128]{2,1,0:T(8,128)} custom-call(f32[2800,128]{1,0:T(8,128)S(1)} %get-tuple-element.33.refs_0_.refs_2_, f32[32,8,128]{2,1,0:T(8,128)S(1)} %all-to-all-done.3.refs_1_.refs_0_, bf16[2800,128]{1,0:T(8,128)(2,1)S(1)} %cot_kernel.1.refs_2_.refs_3_), custom_call_target="tpu_custom_call" | custom-call | bytes 4194304 | tf_op jit(solution)/shard_map/norm_kernel/pallas_call | solution.py:71
  69.5 3.2 %all-to-all-start.4 = ((f32[32,8,128]{2,1,0:T(8,128)}), f32[32,8,128]{2,1,0:T(8,128)S(1)}, u32[]{:S(2)}, u32[]{:S(2)}) async-start(f32[32,8,128]{2,1,0:T(8,128)} %norm_kernel.1), calls=%async_computation.4 | async-start | bytes 262144 | tf_op jit(solution)/shard_map/all_to_all | solution.py:461
  72.7 0.0 copy-start.1
  72.8 1.0 copy-done.1
  73.8 2.7 %second_kernel.1.refs_2_ = bf16[16,72,128]{2,1,0:T(8,128)(2,1)S(1)} custom-call(f32[2800,128]{1,0:T(8,128)S(1)} %get-tuple-element.33.refs_0_.refs_2_, f32[32,8,128]{2,1,0:T(8,128)S(1)} %all-to-all-done.3.refs_1_.refs_0_, bf16[32,64,128]{2,1,0:T(8,128)(2,1)S(1)} %copy-done.1), custom_call_target="tpu_custom_call" | custom-call | flops 825753600 | bytes 4194304 | tf_op jit(solution)/shard_map/second_kernel/pallas_call | solution.py:71
  76.5 2.9 %collective-permute-start.6 = (bf16[16,72,128]{2,1,0:T(8,128)(2,1)S(1)}, bf16[16,72,128]{2,1,0:T(8,128)(2,1)}, u32[]{:S(2)}, u32[]{:S(2)}) collective-permute-start(bf16[16,72,128]{2,1,0:T(8,128)(2,1)S(1)} %second_kernel.1.refs_2_), channel_id=1, source_target_pairs={{0,1},{2,3},{4,5},{6,7},{8,9},{10,11},{12,13},{14,15},{16,17},{18,... | collective-permute-start | bytes 884744 | tf_op jit(solution)/shard_map/ppermute | solution.py:837
  79.3 1.6 %all-to-all-done.4.refs_1_ = f32[32,8,128]{2,1,0:T(8,128)S(1)} async-done(((f32[32,8,128]{2,1,0:T(8,128)}), f32[32,8,128]{2,1,0:T(8,128)S(1)}, u32[]{:S(2)}, u32[]{:S(2)}) %all-to-all-start.4) | async-done | bytes 131104 | tf_op jit(solution)/shard_map/all_to_all | solution.py:461
  81.0 2.5 %first_kernel.1.refs_0_ = bf16[16,72,128]{2,1,0:T(8,128)(2,1)S(1)} custom-call(f32[32,8,128]{2,1,0:T(8,128)S(1)} %all-to-all-done.3.refs_1_.refs_0_, f32[32,8,128]{2,1,0:T(8,128)S(1)} %all-to-all-done.4.refs_1_, f32[2800,128]{1,0:T(8,128)S(1)} %get-tuple-element.33.refs_0_.refs_2_, bf16[2800,128]{1,0:T(8,128)(2,1)S(1)} %cot_kernel.1.refs_2_.refs_3_, ...), custom_call_target="tpu_custom_call" | custom-call | flops 825753600 | bytes 4194304 | tf_op jit(solution)/shard_map/first_kernel/pallas_call | solution.py:71
  83.5 1.3 %collective-permute-start.5 = (bf16[16,72,128]{2,1,0:T(8,128)(2,1)S(1)}, bf16[16,72,128]{2,1,0:T(8,128)(2,1)S(1)}, u32[]{:S(2)}, u32[]{:S(2)}) collective-permute-start(bf16[16,72,128]{2,1,0:T(8,128)(2,1)S(1)} %first_kernel.1.refs_0_), channel_id=1, source_target_pairs={{1,0},{3,2},{5,4},{7,6},{9,8},{11,10},{13,12},{15,14},{17,16},{19,... | collective-permute-start | bytes 884744 | tf_op jit(solution)/shard_map/ppermute | solution.py:850
  84.8 0.0 collective-permute-done.6.refs_3_
  84.8 2.2 %collective-permute-done.5.refs_1_ = bf16[16,72,128]{2,1,0:T(8,128)(2,1)S(1)} collective-permute-done((bf16[16,72,128]{2,1,0:T(8,128)(2,1)S(1)}, bf16[16,72,128]{2,1,0:T(8,128)(2,1)S(1)}, u32[]{:S(2)}, u32[]{:S(2)}) %collective-permute-start.5) | collective-permute-done | bytes 294944 | tf_op jit(solution)/shard_map/ppermute | solution.py:850
  86.9 1.0 pair_kernel.1
  88.0 0.0 copy-start.5
  88.0 0.7 copy-done.5
  88.7 5.1 %all-to-all-start.5 = ((bf16[16,72,128]{2,1,0:T(8,128)(2,1)}), bf16[16,72,128]{2,1,0:T(8,128)(2,1)S(1)}, u32[]{:S(2)}, u32[]{:S(2)}) async-start(bf16[16,72,128]{2,1,0:T(8,128)(2,1)} %copy-done.5), calls=%async_computation.5 | async-start | bytes 589824 | tf_op jit(solution)/shard_map/all_to_all | solution.py:469
  93.8 0.0 copy-start.2
  93.8 1.0 copy-done.2
  94.9 1.0 copy-done.7
  95.9 1.0 copy-done.13
  96.8 3.6 %coarse_kernel.1 = f32[8,128]{1,0:T(8,128)} custom-call(f32[32,8,128]{2,1,0:T(8,128)S(1)} %all-to-all-done.3.refs_1_.refs_0_, f32[32,8,128]{2,1,0:T(8,128)S(1)} %all-to-all-done.4.refs_1_, f32[2800,128]{1,0:T(8,128)S(1)} %get-tuple-element.33.refs_0_.refs_2_, bf16[2800,128]{1,0:T(8,128)(2,1)S(1)} %cot_kernel.1.refs_2_.refs_3_, ...), custom_call_target="tpu_custom_call" | custom-call | bytes 4194304 | tf_op jit(solution)/shard_map/coarse_kernel/pallas_call | solution.py:71
  100.4 4.3 %enhanced_kernel.1 = bf16[32,64,128]{2,1,0:T(8,128)(2,1)} custom-call(f32[2800,128]{1,0:T(8,128)S(1)} %get-tuple-element.33.refs_0_.refs_2_, f32[32,8,128]{2,1,0:T(8,128)S(1)} %all-to-all-done.3.refs_1_.refs_0_, bf16[3072,128]{1,0:T(8,128)(2,1)S(1)} %get-tuple-element.34.refs_4_.refs_2_, bf16[3,3,128,128]{3,2,1,0:T(8,128)(2,1)S(1)} %copy-done.11), custom_call_target="tpu_custom_call" | custom-call | flops 825753600 | bytes 4194304 | tf_op jit(solution)/shard_map/enhanced_kernel/pallas_call | solution.py:71
  104.8 0.0 all-to-all-done.5.refs_0_
  104.8 0.1 share_kernel.1
  104.9 17.1 %all_to_all.35.refs_0_ = bf16[16,72,128]{2,1,0:T(8,128)(2,1)S(1)} all-to-all(bf16[16,72,128]{2,1,0:T(8,128)(2,1)S(1)} %share_kernel.1), channel_id=1, replica_groups={{0,2,4,6,8,10,12,14,16,18,20,22,24,26,28,30},{1,3,5,7,9,11,13,15,17,19,..., dimensions={0} | all-to-all | bytes 589824 | tf_op jit(solution)/shard_map/all_to_all | solution.py:469
  121.9 0.0 collective-permute-start.7
  121.9 1.6 %collective-permute-done.7.refs_1_ = bf16[16,72,128]{2,1,0:T(8,128)(2,1)S(1)} collective-permute-done((bf16[16,72,128]{2,1,0:T(8,128)(2,1)S(1)}, bf16[16,72,128]{2,1,0:T(8,128)(2,1)S(1)}, u32[]{:S(2)}, u32[]{:S(2)}) %collective-permute-start.7) | collective-permute-done | bytes 294944 | tf_op jit(solution)/shard_map/ppermute | solution.py:473
  123.5 1.1 join_kernel.1
  (20 shorter events, 0.1 us)
Async XLA Ops:
  2.8 22.6 %copy-start.3 = (bf16[3,3,1024,128]{3,2,1,0:T(8,128)(2,1)S(1)}, bf16[3,3,1024,128]{3,2,1,0:T(8,128)(2,1)}, u32[]{:S(2)}) copy-start(bf16[3,3,1024,128]{3,2,1,0:T(8,128)(2,1)} %refs_2_.3) | copy-start | bytes 7077892
  2.8 21.0 %all-to-all-start = ((bf16[16,72,128]{2,1,0:T(8,128)(2,1)}), bf16[16,72,128]{2,1,0:T(8,128)(2,1)S(1)}, u32[]{:S(2)}, u32[]{:S(2)}) async-start(bf16[16,72,128]{2,1,0:T(8,128)(2,1)} %pack_kernel.1), calls=%async_computation | async-start | bytes 589824 | tf_op jit(solution)/shard_map/all_to_all | solution.py:469
  12.1 5.7 %collective-permute-start = (bf16[2,2,64,128]{3,2,1,0:T(8,128)(2,1)S(1)}, bf16[2,2,64,128]{3,2,1,0:T(8,128)(2,1)S(1)}, u32[]{:S(2)}, u32[]{:S(2)}) collective-permute-start(bf16[2,2,64,128]{3,2,1,0:T(8,128)(2,1)S(1)} %pad_maximum_fusion.2), channel_id=1, source_target_pairs={{0,8},{8,16},{16,24},{1,9},{9,17},{17,25},{2,10},{10,18},{18,26},{... | collective-permute-start | bytes 196616 | tf_op jit(solution)/shard_map/ppermute | solution.py:696
  16.0 6.2 %collective-permute-start.1 = (bf16[2,2,64,128]{3,2,1,0:T(8,128)(2,1)S(1)}, bf16[2,2,64,128]{3,2,1,0:T(8,128)(2,1)S(1)}, u32[]{:S(2)}, u32[]{:S(2)}) collective-permute-start(bf16[2,2,64,128]{3,2,1,0:T(8,128)(2,1)S(1)} %pad_maximum_fusion.3), channel_id=1, source_target_pairs={{8,0},{16,8},{24,16},{9,1},{17,9},{25,17},{10,2},{18,10},{26,18},{... | collective-permute-start | bytes 196616 | tf_op jit(solution)/shard_map/ppermute | solution.py:697
  23.7 11.7 %copy-start.15 = (f32[16,128]{1,0:T(8,128)S(1)}, f32[16,128]{1,0:T(8,128)}, u32[]{:S(2)}) copy-start(f32[16,128]{1,0:T(8,128)} %refs_3_.4) | copy-start | bytes 24580
  23.7 11.7 %copy-start.16 = (s32[8,256]{1,0:T(8,128)S(1)}, s32[8,256]{1,0:T(8,128)}, u32[]{:S(2)}) copy-start(s32[8,256]{1,0:T(8,128)} %constant.7.clone.refs_2_) | copy-start | bytes 24580
  23.8 1.6 %collective-permute-start.2 = (bf16[16,72,128]{2,1,0:T(8,128)(2,1)S(1)}, bf16[16,72,128]{2,1,0:T(8,128)(2,1)S(1)}, u32[]{:S(2)}, u32[]{:S(2)}) collective-permute-start(bf16[16,72,128]{2,1,0:T(8,128)(2,1)S(1)} %all-to-all-done.refs_0_.refs_2_), channel_id=1, source_target_pairs={{0,1},{1,0},{2,3},{3,2},{4,5},{5,4},{6,7},{7,6},{8,9},{9,8},{10,11... | collective-permute-start | bytes 884744 | tf_op jit(solution)/shard_map/ppermute | solution.py:473
  27.3 12.0 %all-to-all-start.1 = ((bf16[8,192,128]{2,1,0:T(8,128)(2,1)}), bf16[8,192,128]{2,1,0:T(8,128)(2,1)S(1)}, u32[]{:S(2)}, u32[]{:S(2)}) async-start(bf16[8,192,128]{2,1,0:T(8,128)(2,1)} %hidden_kernel.1), calls=%async_computation.1 | async-start | bytes 786432 | tf_op jit(solution)/shard_map/all_to_all | solution.py:461
  31.0 21.2 %copy-start.6 = (bf16[32,64,128]{2,1,0:T(8,128)(2,1)S(1)}, bf16[32,64,128]{2,1,0:T(8,128)(2,1)}, u32[]{:S(2)}) copy-start(bf16[32,64,128]{2,1,0:T(8,128)(2,1)} %refs_0_.4) | copy-start | bytes 1572868
  31.0 15.8 %collective-permute-start.3 = (bf16[2,36,8,128]{3,2,1,0:T(8,128)(2,1)}, bf16[2,36,8,128]{3,2,1,0:T(8,128)(2,1)S(1)}, u32[]{:S(2)}, u32[]{:S(2)}) collective-permute-start(bf16[2,36,8,128]{3,2,1,0:T(8,128)(2,1)} %get-tuple-element.28), channel_id=1, source_target_pairs={{1,0},{2,1},{3,2},{4,3},{5,4},{6,5},{7,6},{9,8},{10,9},{11,10},{12... | collective-permute-start | bytes 442376 | tf_op jit(solution)/shard_map/ppermute | solution.py:768
  32.4 14.3 %collective-permute-start.4 = (bf16[2,36,8,128]{3,2,1,0:T(8,128)(2,1)S(1)}, bf16[2,36,8,128]{3,2,1,0:T(8,128)(2,1)S(1)}, u32[]{:S(2)}, u32[]{:S(2)}) collective-permute-start(bf16[2,36,8,128]{3,2,1,0:T(8,128)(2,1)S(1)} %get-tuple-element.29), channel_id=1, source_target_pairs={{0,1},{1,2},{2,3},{3,4},{4,5},{5,6},{6,7},{8,9},{9,10},{10,11},{11... | collective-permute-start | bytes 442376 | tf_op jit(solution)/shard_map/ppermute | solution.py:767
  39.3 1.7 %copy-start.4 = (bf16[3,3,1024,128]{3,2,1,0:T(8,128)(2,1)S(1)}, bf16[3,3,1024,128]{3,2,1,0:T(8,128)(2,1)}, u32[]{:S(2)}) copy-start(bf16[3,3,1024,128]{3,2,1,0:T(8,128)(2,1)} %refs_1_.3) | copy-start | bytes 7077892
  41.0 0.9 copy-start.14
  43.3 8.9 %all-to-all-start.2 = ((f32[8,4,8,128]{3,2,1,0:T(8,128)}), f32[8,4,8,128]{3,2,1,0:T(8,128)S(1)}, u32[]{:S(2)}, u32[]{:S(2)}) async-start(f32[8,4,8,128]{3,2,1,0:T(8,128)} %project_kernel.1), calls=%async_computation.2 | async-start | bytes 262144 | tf_op jit(solution)/shard_map/all_to_all | solution.py:461
  46.8 9.9 %copy-start.8 = (bf16[2,37,16,128]{3,2,1,0:T(8,128)(2,1)}, bf16[2,37,16,128]{3,2,1,0:T(8,128)(2,1)S(1)}, u32[]{:S(2)}) copy-start(bf16[2,37,16,128]{3,2,1,0:T(8,128)(2,1)S(1)} %fusion.2.refs_3_) | copy-start | bytes 909316
  52.2 1.0 copy-start.12
  56.7 11.0 %all-to-all-start.3 = ((f32[32,8,128]{2,1,0:T(8,128)}), f32[32,8,128]{2,1,0:T(8,128)S(1)}, u32[]{:S(2)}, u32[]{:S(2)}) async-start(f32[32,8,128]{2,1,0:T(8,128)} %get-tuple-element.32), calls=%async_computation.3 | async-start | bytes 262144 | tf_op jit(solution)/shard_map/all_to_all | solution.py:461
  59.5 1.0 copy-start
  60.5 1.0 copy-start.9
  61.5 1.0 copy-start.10
  69.5 11.5 %all-to-all-start.4 = ((f32[32,8,128]{2,1,0:T(8,128)}), f32[32,8,128]{2,1,0:T(8,128)S(1)}, u32[]{:S(2)}, u32[]{:S(2)}) async-start(f32[32,8,128]{2,1,0:T(8,128)} %norm_kernel.1), calls=%async_computation.4 | async-start | bytes 262144 | tf_op jit(solution)/shard_map/all_to_all | solution.py:461
  72.7 1.0 copy-start.1
  76.5 8.3 %collective-permute-start.6 = (bf16[16,72,128]{2,1,0:T(8,128)(2,1)S(1)}, bf16[16,72,128]{2,1,0:T(8,128)(2,1)}, u32[]{:S(2)}, u32[]{:S(2)}) collective-permute-start(bf16[16,72,128]{2,1,0:T(8,128)(2,1)S(1)} %second_kernel.1.refs_2_), channel_id=1, source_target_pairs={{0,1},{2,3},{4,5},{6,7},{8,9},{10,11},{12,13},{14,15},{16,17},{18,... | collective-permute-start | bytes 884744 | tf_op jit(solution)/shard_map/ppermute | solution.py:837
  83.5 3.5 %collective-permute-start.5 = (bf16[16,72,128]{2,1,0:T(8,128)(2,1)S(1)}, bf16[16,72,128]{2,1,0:T(8,128)(2,1)S(1)}, u32[]{:S(2)}, u32[]{:S(2)}) collective-permute-start(bf16[16,72,128]{2,1,0:T(8,128)(2,1)S(1)} %first_kernel.1.refs_0_), channel_id=1, source_target_pairs={{1,0},{3,2},{5,4},{7,6},{9,8},{11,10},{13,12},{15,14},{17,16},{19,... | collective-permute-start | bytes 884744 | tf_op jit(solution)/shard_map/ppermute | solution.py:850
  88.0 0.7 copy-start.5
  88.7 16.1 %all-to-all-start.5 = ((bf16[16,72,128]{2,1,0:T(8,128)(2,1)}), bf16[16,72,128]{2,1,0:T(8,128)(2,1)S(1)}, u32[]{:S(2)}, u32[]{:S(2)}) async-start(bf16[16,72,128]{2,1,0:T(8,128)(2,1)} %copy-done.5), calls=%async_computation.5 | async-start | bytes 589824 | tf_op jit(solution)/shard_map/all_to_all | solution.py:469
  93.8 1.0 copy-start.2
  94.9 1.0 copy-start.7
  95.9 1.0 copy-start.13
  96.8 3.6 %copy-start.11 = (bf16[3,3,128,128]{3,2,1,0:T(8,128)(2,1)S(1)}, bf16[3,3,128,128]{3,2,1,0:T(8,128)(2,1)}, u32[]{:S(2)}) copy-start(bf16[3,3,128,128]{3,2,1,0:T(8,128)(2,1)} %refs_3_.5) | copy-start | bytes 884740
  121.9 1.6 %collective-permute-start.7 = (bf16[16,72,128]{2,1,0:T(8,128)(2,1)S(1)}, bf16[16,72,128]{2,1,0:T(8,128)(2,1)S(1)}, u32[]{:S(2)}, u32[]{:S(2)}) collective-permute-start(bf16[16,72,128]{2,1,0:T(8,128)(2,1)S(1)} %all_to_all.35.refs_0_), channel_id=1, source_target_pairs={{0,1},{1,0},{2,3},{3,2},{4,5},{5,4},{6,7},{7,6},{8,9},{9,8},{10,11... | collective-permute-start | bytes 884744 | tf_op jit(solution)/shard_map/ppermute | solution.py:473
